TPU v7x, 128 devices: a whole 4x4x4 slice. The times are simulated.
128 devices in a mesh: rep: 8 (over z, core), fsdp: 16 (over y, x).
Axes of the slice: x: 4, y: 4, z: 4, core: 2. Of those that a mesh axis runs over, the one named last changes fastest.
Arguments:
- partials: bfloat16 [8, 16, 64, 131072], P('rep', 'fsdp'), may hold values from -5 to 5
- momentum: float32 [8, 64, 131072], P('rep', None, 'fsdp'), may hold values from -6 to 6
- positions: int32 [8, 8, 131072], P('rep', None, 'fsdp'), may hold values from 0 to 63, as said below
Outputs:
- update: float32 [64, 131072], P(None, 'fsdp')
- new_momentum: float32 [8, 64, 131072], P('rep', None, 'fsdp')
Inputs may be any that keep to these rules, and one draw needn't show every extreme that they name: For each replica and span the 8 positions are different numbers.
All inputs are finite; a program needn't handle non-finite values.
Results may differ from a plain program's by a relative error of at most 0.0003.
Values sent between devices are 32-bit elements; how exact they have to be, the bound alone decides.
No kernel may reach another device: no remote copies, remote signals or barrier semaphores. Data moves between devices by JAX's collectives and lax.ppermute only.
A program may use at most 128 MiB of HBM per device.

v0:
```python
import jax
import jax.numpy as jnp
from jax import lax
from jax.sharding import PartitionSpec as P


def dct_matrix(order):
    freq = jnp.arange(order).astype(jnp.float32)[:, None]
    place = jnp.arange(order).astype(jnp.float32)[None, :]
    basis = jnp.cos(jnp.pi * (2.0 * place + 1.0) * freq / (2.0 * order))
    scale = jnp.where(freq == 0.0, jnp.sqrt(1.0 / order), jnp.sqrt(2.0 / order))
    return scale * basis


def on_device(partials, momentum, positions):
    order = momentum.shape[1]
    dct = dct_matrix(order)
    grad = lax.psum_scatter(partials.astype(jnp.float32), "fsdp", scatter_dimension=3, tiled=True)[
        0, 0
    ]
    moment = 0.9 * momentum[0] + grad
    coeff = jnp.dot(
        dct, moment, precision=lax.Precision.HIGHEST, preferred_element_type=jnp.float32
    )
    freq = jnp.arange(order)
    chosen = positions[0]
    hits = chosen[:, None, :] == freq[None, :, None]
    keep = jnp.any(hits, axis=0)
    own = jnp.where(keep, coeff, 0.0)
    fresh = moment - jnp.dot(
        dct.T, own, precision=lax.Precision.HIGHEST, preferred_element_type=jnp.float32
    )
    values = jnp.sum(jnp.where(hits, coeff[None, :, :], 0.0), axis=1)
    vals_piece = lax.all_gather(values[None], "rep", axis=0, tiled=True)
    pos_piece = lax.all_gather(chosen[None], "rep", axis=0, tiled=True)

    def add_one(index, acc):
        vals_row = lax.dynamic_index_in_dim(vals_piece, index, 0, keepdims=False)
        pos_row = lax.dynamic_index_in_dim(pos_piece, index, 0, keepdims=False)
        match = pos_row[:, None, :] == freq[None, :, None]
        return acc + jnp.sum(jnp.where(match, vals_row[:, None, :], 0.0), axis=0)

    total = lax.fori_loop(0, vals_piece.shape[0], add_one, jnp.zeros_like(own))
    update = jnp.dot(
        dct.T, total, precision=lax.Precision.HIGHEST, preferred_element_type=jnp.float32
    )
    return (update, fresh[None])


def solution(mesh):
    placed = (P("rep", "fsdp", None, None), P("rep", None, "fsdp"), P("rep", None, "fsdp"))
    return jax.shard_map(
        on_device,
        mesh=mesh,
        in_specs=placed,
        out_specs=(P(None, "fsdp"), P("rep", None, "fsdp")),
        check_vma=False,
    )
```

profile of v0, /device:TPU:1, one launch (start us, length us, event | category | flops | bytes accessed | tf_op | source)
XLA Modules:
  0.0 326.1 jit_solution(13740688146752338003)
XLA Ops:
  8.0 0.0 reduce-scatter.2.cloned.1.call-start
  8.0 18.2 %convert_element_type.23 = f32[1,1,64,131072]{3,2,1,0:T(8,128)} convert(bf16[1,1,64,131072]{3,2,1,0:T(8,128)(2,1)} %param.5) | non-fusion elementwise | flops 8388608 | bytes 50331648 | tf_op jit(solution)/shard_map/convert_element_type | solution.py:18
  26.2 0.0 reduce-scatter.2.cloned.1.call-update
  26.3 0.0 all-gather.4.cloned.1.call-start
  26.3 0.5 all-gather.4.cloned.1.call-update
  26.8 0.0 all-gather.6.cloned.1.call-start
  26.9 197.4 %reduce-scatter.2.cloned.1.call-done = f32[1,1,64,8192]{3,2,1,0:T(8,128)} async-done(((f32[1,1,64,131072]{3,2,1,0:T(8,128)}), f32[1,1,64,8192]{3,2,1,0:T(8,128)}) %reduce-scatter.2.cloned.1.call-update) | async-done | bytes 2097168 | tf_op jit(solution)/shard_map/reduce_scatter | solution.py:18
  224.3 0.0 copy-start
  224.3 4.3 %fusion.6 = f32[64,8192]{1,0:T(8,128)S(1)} fusion(f32[1,1,64,8192]{3,2,1,0:T(8,128)} %reduce-scatter.2.cloned.1.call-done, f32[1,64,8192]{2,1,0:T(8,128)} %param.6, f32[64]{0:T(128)S(1)} %iota_convert_fusion, f32[64]{0:T(128)S(1)} %get-tuple-element.123, f32[64]{0:T(128)S(1)} %get-tuple-element.122), kind=kOutput, calls=%fused_computation.14 | convolution fusion | flops 403714048 | bytes 6292224 | tf_op jit(solution)/shard_map/dot_general | solution.py:22
  228.6 0.0 copy-done
  228.6 3.6 %select_reduce_fusion.1 = f32[8,8192]{1,0:T(8,128)} fusion(f32[64,8192]{1,0:T(8,128)S(1)} %fusion.6, s32[8,8192]{1,0:T(8,128)S(1)} %bitcast.23), kind=kLoop, calls=%fused_computation.6 | loop fusion | flops 12517376 | bytes 2621440 | tf_op jit(solution)/shard_map/reduce_sum | solution.py:33
  232.2 0.0 all-gather.6.cloned.1.call-update
  232.2 2.3 fusion.2
  234.5 5.9 %fusion.3 = f32[1,64,8192]{2,1,0:T(8,128)} fusion(pred[64,8192]{1,0:T(8,128)(4,1)S(1)} %fusion.2, f32[64,8192]{1,0:T(8,128)S(1)} %fusion.6, f32[1,1,64,8192]{3,2,1,0:T(8,128)} %reduce-scatter.2.cloned.1.call-done, f32[1,64,8192]{2,1,0:T(8,128)} %param.6, f32[64]{0:T(128)S(1)} %iota_convert_fusion, f32[64]{0:T(128)S(1)} %get-tuple-element.123, ...), kind=kOutput, calls=%fused_computation.10 | convolution fusion | flops 404762624 | bytes 8913664 | tf_op jit(solution)/shard_map/dot_general | solution.py:30
  240.4 0.0 all-gather.4.cloned.1.call-done
  240.4 17.5 %all-gather.6.cloned.1.call-done = f32[64,8192]{1,0:T(8,128)} async-done(((f32[8,8192]{1,0:T(8,128)}), f32[64,8192]{1,0:T(8,128)}) %all-gather.6.cloned.1.call-update) | async-done | bytes 2097168 | tf_op jit(solution)/shard_map/all_gather | solution.py:34
  258.0 55.8 %while.14 = (s32[]{:T(128)}, f32[64,8192]{1,0:T(8,128)}, s32[8,8,8192]{2,1,0:T(8,128)}, f32[8,8,8192]{2,1,0:T(8,128)}, s32[]{:T(128)}, /*index=5*/s32[]{:T(128)}) while((s32[]{:T(128)}, f32[64,8192]{1,0:T(8,128)}, s32[8,8,8192]{2,1,0:T(8,128)}, f32[8,8,8192]{2,1,0:T(8,128)}, s32[]{:T(128)}, /*index=5*/s32[]{:T(128)}) %tuple.46), condition=%wide.region_4.5_spmd.clone, body=%wide.region_2.4_spmd.clone.sunk | while | flops 13107203 | bytes 9961559 | solution.py:43
  258.0 1.0 dynamic-slice_bitcast_fusion.4
  258.9 1.0 dynamic-slice_bitcast_fusion.5
  259.9 2.1 select_reduce_fusion.3
  262.0 1.5 select_add_fusion.2
  263.6 1.0 dynamic-slice_bitcast_fusion.4
  264.5 1.0 dynamic-slice_bitcast_fusion.5
  265.5 2.1 select_reduce_fusion.3
  267.6 3.1 select_add_fusion.2
  270.7 1.0 dynamic-slice_bitcast_fusion.4
  271.7 1.0 dynamic-slice_bitcast_fusion.5
  272.7 2.1 select_reduce_fusion.3
  274.8 3.1 select_add_fusion.2
  277.9 1.0 dynamic-slice_bitcast_fusion.4
  278.9 1.0 dynamic-slice_bitcast_fusion.5
  279.8 2.1 select_reduce_fusion.3
  281.9 3.1 select_add_fusion.2
  285.1 1.0 dynamic-slice_bitcast_fusion.4
  286.0 1.0 dynamic-slice_bitcast_fusion.5
  287.0 2.1 select_reduce_fusion.3
  289.1 3.1 select_add_fusion.2
  292.2 1.0 dynamic-slice_bitcast_fusion.4
  293.2 1.0 dynamic-slice_bitcast_fusion.5
  294.2 2.1 select_reduce_fusion.3
  296.3 3.1 select_add_fusion.2
  299.4 1.0 dynamic-slice_bitcast_fusion.4
  300.4 1.0 dynamic-slice_bitcast_fusion.5
  301.3 2.1 select_reduce_fusion.3
  303.4 3.1 select_add_fusion.2
  306.6 1.0 dynamic-slice_bitcast_fusion.4
  307.5 1.0 dynamic-slice_bitcast_fusion.5
  308.5 2.1 select_reduce_fusion.3
  310.6 3.1 select_add_fusion.2
  313.7 5.0 %fusion.7 = f32[64,8192]{1,0:T(8,128)} fusion(f32[64,8192]{1,0:T(8,128)} %get-tuple-element.96, f32[64]{0:T(128)S(1)} %iota_convert_fusion, f32[64]{0:T(128)S(1)} %get-tuple-element.123, f32[64]{0:T(128)S(1)} %get-tuple-element.122), kind=kOutput, calls=%fused_computation.16 | convolution fusion | flops 402665472 | bytes 4195072 | tf_op jit(solution)/shard_map/dot_general | solution.py:44
  (3 shorter events, 0.0 us)
Async XLA Ops:
  8.0 216.3 %reduce-scatter.2.cloned.1.call-start = ((), (), s32[]{:S(2)}) async-start(), calls=%async_computation.2 | async-start | bytes 35651584 | tf_op jit(solution)/shard_map/reduce_scatter | solution.py:18
  26.3 214.2 %all-gather.4.cloned.1.call-start = ((), (), s32[]{:S(2)}) async-start(), calls=%async_computation.1 | async-start | bytes 2359296 | tf_op jit(solution)/shard_map/all_gather | solution.py:35
  26.8 231.1 %all-gather.6.cloned.1.call-start = ((), (), s32[]{:S(2)}) async-start(), calls=%async_computation.3 | async-start | bytes 2359296 | tf_op jit(solution)/shard_map/all_gather | solution.py:34
  224.3 4.3 %copy-start = (s32[1,8,8192]{2,1,0:T(8,128)S(1)}, s32[1,8,8192]{2,1,0:T(8,128)}, u32[]{:S(2)}) copy-start(s32[1,8,8192]{2,1,0:T(8,128)} %param.7) | copy-start | bytes 786436
Sparse Core Ops, SparseCore 0:
  26.4 197.9 reduce-scatter.1
Sparse Core Ops, SparseCore 1:
  28.4 29.1 all-gather.3
  232.3 25.6 all-gather.5
where the time goes:
time: 327 us; the launch traced here: 326 us
  waiting for transfers between devices  216 us (66%)
  other arithmetic  64.2 us (20%)
  local copies, waits for them, and re-layouts  15.5 us (5%)
  between operations  15.5 us (5%)
  matrix products  15.1 us (5%)
    reduce_scatter x1, waiting for transfers between devices, on_device(): lax.psum_scatter(partials.astype(jnp.float32), 'fsdp', scatter_dimension=...  197 us
    add x8, other arithmetic, add_one(): return acc + jnp.sum(jnp.where(match, vals_row[:, None, :], 0.0), axis=0)  23.3 us
    convert_element_type x1, other arithmetic, on_device(): partials.astype(jnp.float32)  18.2 us
    all_gather x1, waiting for transfers between devices, on_device(): vals_piece = lax.all_gather(values[None], 'rep', axis=0, tiled=True)  17.5 us
    reduce_sum x8, other arithmetic, add_one(): return acc + jnp.sum(jnp.where(match, vals_row[:, None, :], 0.0), axis=0)  16.8 us
    eq x8, local copies, waits for them, and re-layouts, add_one(): match = pos_row[:, None, :] == freq[None, :, None]  7.79 us
    broadcast_in_dim x8, local copies, waits for them, and re-layouts, add_one(): return acc + jnp.sum(jnp.where(match, vals_row[:, None, :], 0.0), axis=0)  7.73 us
  transfers between devices with their start and end apart: 3, of which 2 were waited for; matrix products, arithmetic and copies ran while one was open for 5% of the time, Pallas kernels for 0%

commit v1 on v0

v1 whole, which is shorter than its diff:
```python
import functools

import jax
import jax.numpy as jnp
import ml_dtypes
import numpy as np
from jax import lax
from jax.experimental import pallas as pl
from jax.experimental.pallas import tpu as pltpu
from jax.sharding import PartitionSpec as P

BLOCK = 64
HALF = BLOCK // 2
KEEP = 8
SIDE = 4
WIDTHS = (2048, 1024, 1024)
VMEM_LIMIT = 48 * 1024 * 1024
F32 = jnp.float32
BF16 = jnp.bfloat16


def dct_parts():
    k = np.arange(BLOCK, dtype=np.float64)[:, None]
    n = np.arange(BLOCK, dtype=np.float64)[None, :]
    scale = np.where(k == 0, np.sqrt(1.0 / BLOCK), np.sqrt(2.0 / BLOCK))
    dct = scale * np.cos(np.pi * (2.0 * n + 1.0) * k / (2.0 * BLOCK))

    def wide(mat):
        high = mat.astype(ml_dtypes.bfloat16)
        low = (mat - high.astype(np.float64)).astype(ml_dtypes.bfloat16)
        return np.concatenate([high, high, low, low], axis=1)

    return wide(dct), wide(dct.T.copy())


def params():
    return pltpu.CompilerParams(vmem_limit_bytes=VMEM_LIMIT)


def cost(flops, nbytes):
    return pl.CostEstimate(flops=flops, bytes_accessed=nbytes, transcendentals=0)


def fold(coord, step):
    return lax.rem(coord + (step + SIDE), SIDE)


class Half:
    def __init__(self, x_first, offset, width, spans):
        self.x_first = x_first
        self.width = width
        self.first = offset // width
        self.per_target = spans // width

    def column(self, here, step, other):
        y, x = here[0], here[1]
        if self.x_first:
            target = other * SIDE + fold(x, step)
        else:
            target = fold(y, step) * SIDE + other
        return target * self.per_target + self.first

    def second(self, here, step):
        return fold(here[0] if self.x_first else here[1], step)

    def grid_block(self, step):
        return pl.BlockSpec((BLOCK, self.width), lambda i, here: (0, self.column(here, step, i)))

    def one_block(self, step):
        return pl.BlockSpec(
            (BLOCK, self.width), lambda i, here: (0, self.column(here, 0, self.second(here, step)))
        )

    def message_block(self, step):
        return pl.BlockSpec((1, BLOCK, self.width), lambda i, here: (self.second(here, step), 0, 0))


def whole(*shape):
    return pl.BlockSpec(shape, lambda i, here: (0,) * len(shape))


def call(body, grid, here, ins, in_specs, out_shape, out_specs, nbytes, flops=0, aliases=None, scratch=()):
    return pl.pallas_call(
        body,
        grid_spec=pltpu.PrefetchScalarGridSpec(
            num_scalar_prefetch=1,
            grid=(grid,),
            in_specs=in_specs,
            out_specs=out_specs,
            scratch_shapes=scratch,
        ),
        out_shape=out_shape,
        input_output_aliases=aliases or {},
        compiler_params=params(),
        cost_estimate=cost(flops, nbytes),
    )(here, *ins)


def far_body(here, part, up, down):
    up[0] = part[:HALF].astype(F32)
    down[0] = part[HALF:].astype(F32)


def send_far(half, here, partials):
    w = half.width
    shape = jax.ShapeDtypeStruct((SIDE, HALF, w), F32)
    spec = pl.BlockSpec((1, HALF, w), lambda i, here: (i, 0, 0))
    return call(
        far_body, SIDE, here, (partials,), [half.grid_block(2)], (shape, shape), (spec, spec),
        SIDE * BLOCK * w * 6,
    )


def near_body(here, part_up, part_down, got_up, got_down, up, down):
    up[0, :HALF] = part_up[:HALF].astype(F32) + got_up[0]
    up[0, HALF:] = part_up[HALF:].astype(F32)
    down[0, :HALF] = part_down[:HALF].astype(F32)
    down[0, HALF:] = part_down[HALF:].astype(F32) + got_down[0]


def send_near(half, here, partials, got_up, got_down):
    w = half.width
    shape = jax.ShapeDtypeStruct((SIDE, BLOCK, w), F32)
    got = pl.BlockSpec((1, HALF, w), lambda i, here: (i, 0, 0))
    spec = pl.BlockSpec((1, BLOCK, w), lambda i, here: (i, 0, 0))
    return call(
        near_body, SIDE, here, (partials, partials, got_up, got_down),
        [half.grid_block(1), half.grid_block(-1), got, got], (shape, shape), (spec, spec),
        SIDE * BLOCK * w * 16,
    )


def far2_body(here, part, left, right, up, down):
    up[...] = part[:HALF].astype(F32) + left[0, :HALF] + right[0, :HALF]
    down[...] = part[HALF:].astype(F32) + left[0, HALF:] + right[0, HALF:]


def send_far2(half, here, partials, left, right):
    w = half.width
    shape = jax.ShapeDtypeStruct((HALF, w), F32)
    return call(
        far2_body, 1, here, (partials, left, right),
        [half.one_block(2), half.message_block(2), half.message_block(2)],
        (shape, shape), (whole(HALF, w), whole(HALF, w)), BLOCK * w * 14,
    )


def near2_body(here, part_u, left_u, right_u, part_d, left_d, right_d, got_up, got_down, up, down):
    up[:HALF] = part_u[:HALF].astype(F32) + left_u[0, :HALF] + right_u[0, :HALF] + got_up[...]
    up[HALF:] = part_u[HALF:].astype(F32) + left_u[0, HALF:] + right_u[0, HALF:]
    down[:HALF] = part_d[:HALF].astype(F32) + left_d[0, :HALF] + right_d[0, :HALF]
    down[HALF:] = part_d[HALF:].astype(F32) + left_d[0, HALF:] + right_d[0, HALF:] + got_down[...]


def send_near2(half, here, partials, left, right, got_up, got_down):
    w = half.width
    shape = jax.ShapeDtypeStruct((BLOCK, w), F32)
    return call(
        near2_body, 1, here, (partials, left, right, partials, left, right, got_up, got_down),
        [half.one_block(1), half.message_block(1), half.message_block(1),
         half.one_block(-1), half.message_block(-1), half.message_block(-1),
         whole(HALF, w), whole(HALF, w)],
        (shape, shape), (whole(BLOCK, w), whole(BLOCK, w)), BLOCK * w * 32,
    )


def product(parts, value):
    high = value.astype(BF16)
    low = (value - high.astype(F32)).astype(BF16)
    return jnp.dot(
        parts, jnp.concatenate([high, low, high, low], axis=0), preferred_element_type=F32
    )


def finish_body(step, here, *refs):
    halves, (momentum, positions, forward, backward) = (refs[0:5], refs[5:10]), refs[10:14]
    fresh, values = refs[-2:]
    w = halves[0][0].shape[1]
    freq = lax.broadcasted_iota(jnp.int32, (BLOCK, step), 0)
    for number, (part, left, right, left2, right2) in enumerate(halves):

        @pl.loop(0, w // step)
        def _(tile):
            col = pl.ds(pl.multiple_of(tile * step, step), step)
            out = pl.ds(pl.multiple_of(number * w + tile * step, step), step)
            grad = part[:, col].astype(F32) + left[0, :, col] + right[0, :, col]
            grad = grad + left2[:, col] + right2[:, col]
            moment = 0.9 * momentum[0, :, out] + grad
            coeff = product(forward[...], moment)
            chosen = positions[0, :, out]
            own = jnp.zeros_like(coeff)
            rows = []
            for place in range(KEEP):
                hit = jnp.where(chosen[place : place + 1] == freq, coeff, 0.0)
                rows.append(jnp.sum(hit, axis=0, keepdims=True))
                own = own + hit
            values[:, out] = jnp.concatenate(rows, axis=0)
            fresh[0, :, out] = moment - product(backward[...], own)


def finish(pair, piece, here, partials, momentum, positions, got, tables, fresh_so_far):
    w = pair[0].width
    ins, specs = [], []
    for half, (left, right, left2, right2) in zip(pair, got):
        ins += [partials, left, right, left2, right2]
        specs += [half.one_block(0), half.message_block(0), half.message_block(0),
                  whole(BLOCK, w), whole(BLOCK, w)]
    ins += [momentum, positions, *tables]
    specs += [
        pl.BlockSpec((1, BLOCK, 2 * w), lambda i, here: (0, 0, piece)),
        pl.BlockSpec((1, KEEP, 2 * w), lambda i, here: (0, 0, piece)),
        whole(BLOCK, 4 * BLOCK),
        whole(BLOCK, 4 * BLOCK),
    ]
    aliases = {}
    if fresh_so_far is not None:
        ins.append(fresh_so_far)
        specs.append(pl.BlockSpec(memory_space=pl.ANY))
        aliases = {len(ins): 0}
    return call(
        functools.partial(finish_body, min(w, 512)), 1, here, ins, specs,
        (jax.ShapeDtypeStruct(momentum.shape, F32), jax.ShapeDtypeStruct((KEEP, 2 * w), F32)),
        (pl.BlockSpec((1, BLOCK, 2 * w), lambda i, here: (0, 0, piece)), whole(KEEP, 2 * w)),
        BLOCK * w * 2 * 26, flops=2 * 2 * BLOCK * 4 * BLOCK * w * 2, aliases=aliases,
    )


def spread_body(step, here, v0, v1, v2, v3, p0, p1, p2, p3, backward, out):
    freq = lax.broadcasted_iota(jnp.int32, (BLOCK, step), 0)

    @pl.loop(0, out.shape[1] // step)
    def _(tile):
        col = pl.ds(pl.multiple_of(tile * step, step), step)
        dense = []
        for vals, pos in ((v0, p0), (v1, p1), (v2, p2), (v3, p3)):
            row, chosen = vals[:, col], pos[0, :, col]
            acc = jnp.zeros((BLOCK, step), F32)
            for place in range(KEEP):
                acc = jnp.where(chosen[place : place + 1] == freq, row[place : place + 1], acc)
            dense.append(acc)
        total = (dense[0] + dense[1]) + (dense[2] + dense[3])
        out[:, col] = product(backward[...], total)


def spread(width, piece, here, vals, pos, table):
    spec = pl.BlockSpec((1, KEEP, width), lambda i, here: (0, 0, piece))
    return call(
        functools.partial(spread_body, min(width, 512)), 1, here, (*vals, *pos, table),
        [whole(KEEP, width)] * 4 + [spec] * 4 + [whole(BLOCK, 4 * BLOCK)],
        jax.ShapeDtypeStruct((BLOCK, width), F32), whole(BLOCK, width),
        width * 4 * (BLOCK + 64), flops=2 * BLOCK * 4 * BLOCK * width,
    )


def join_body(here, mine, other, *refs):
    refs[-1][...] = mine[...] + other[...]


def join(width, piece, here, mine, other, spans, so_far):
    ins, specs, aliases = [mine, other], [whole(BLOCK, width)] * 2, {}
    if so_far is not None:
        ins.append(so_far)
        specs.append(pl.BlockSpec(memory_space=pl.ANY))
        aliases = {3: 0}
    return call(
        join_body, 1, here, ins, specs, jax.ShapeDtypeStruct((BLOCK, spans), F32),
        pl.BlockSpec((BLOCK, width), lambda i, here: (0, piece)), BLOCK * width * 12, aliases=aliases,
    )


def shift(dy, dx):
    return [
        (y * SIDE + x, (y + dy) % SIDE * SIDE + (x + dx) % SIDE)
        for y in range(SIDE)
        for x in range(SIDE)
    ]


def along(x_first, value, step):
    return lax.ppermute(value, "fsdp", shift(0, step) if x_first else shift(step, 0))


def along_z(value, step):
    return lax.ppermute(
        value, "rep", [(z * 2 + c, (z + step) % SIDE * 2 + c) for z in range(SIDE) for c in range(2)]
    )


def other_core(value):
    return lax.ppermute(value, "rep", [(r, r ^ 1) for r in range(2 * SIDE)])


def both(x_first, up, down):
    return along(x_first, up, 1), along(x_first, down, -1)


def on_device(partials, momentum, positions):
    spans = momentum.shape[2]
    flat = partials.reshape(partials.shape[2:])
    me = lax.axis_index("fsdp")
    here = jnp.stack([me // SIDE, lax.rem(me, SIDE)]).astype(jnp.int32)
    forward, backward = (jnp.asarray(part) for part in dct_parts())

    pairs, pieces, start = [], [], 0
    for width in WIDTHS:
        pairs.append((Half(True, start, width, spans), Half(False, start + width, width, spans)))
        pieces.append(start // (2 * width))
        start += 2 * width

    count = len(pairs)
    far, near, far2, near2 = ([[None, None] for _ in pairs] for _ in range(4))
    pos = [positions] + [along_z(positions, step) for step in (2, 1, -1)]
    fresh = update = None
    for stage in range(count + 4):
        for p in range(count):
            phase = stage - p
            for h, half in enumerate(pairs[p]):
                xf = half.x_first
                if phase == 0:
                    far[p][h] = both(xf, *send_far(half, here, flat))
                elif phase == 1:
                    near[p][h] = both(xf, *send_near(half, here, flat, *far[p][h]))
                elif phase == 2:
                    far2[p][h] = both(not xf, *send_far2(half, here, flat, *near[p][h]))
                elif phase == 3:
                    near2[p][h] = both(
                        not xf, *send_near2(half, here, flat, *near[p][h], *far2[p][h])
                    )
            if phase == 4:
                got = [near[p][h] + near2[p][h] for h in range(2)]
                fresh, vals = finish(
                    pairs[p], pieces[p], here, flat, momentum, positions, got, (forward, backward), fresh
                )
                gathered = [vals] + [along_z(vals, step) for step in (2, 1, -1)]
                mine = spread(2 * WIDTHS[p], pieces[p], here, gathered, pos, backward)
                update = join(2 * WIDTHS[p], pieces[p], here, mine, other_core(mine), spans, update)
    return update, fresh


def solution(mesh):
    placed = (P("rep", "fsdp", None, None), P("rep", None, "fsdp"), P("rep", None, "fsdp"))
    return jax.shard_map(
        on_device,
        mesh=mesh,
        in_specs=placed,
        out_specs=(P(None, "fsdp"), P("rep", None, "fsdp")),
        check_vma=False,
    )
```

time: 327 us -> 299 us (0.914)
  waiting for transfers between devices: 216 us -> 110 us
  starting transfers between devices: 0.12 us -> 93.3 us
  Pallas kernels: 0 us -> 92.8 us
  other arithmetic: 64.2 us -> 0.07 us
  matrix products: 15.1 us -> 0 us
  local copies, waits for them, and re-layouts: 15.5 us -> 1.15 us
  between operations: 15.5 us -> 1.23 us
    reduce_scatter x1 -> x0, waiting for transfers between devices: 197 us -> none  [on_device(): lax.psum_scatter(partials.astype(jnp.float32), 'fsdp', scatter_dimension=...]
    ppermute x0 -> x63, waiting for transfers between devices: none -> 110 us  [the longest x48 109 us: along(): lax.ppermute(value, 'fsdp', shift(0, step) if x_first else shift(step, 0))]
    ppermute x0 -> x63, starting transfers between devices: none -> 93.3 us  [the longest x48 57.4 us: along(): lax.ppermute(value, 'fsdp', shift(0, step) if x_first else shift(step, 0))]
    pallas_call x0 -> x33, Pallas kernels: none -> 92.8 us  [call(): pl.pallas_call(body, grid_spec=pltpu.PrefetchScalarGridSpec(num_scalar_pr...]
    add x8 -> x0, other arithmetic: 23.3 us -> none  [add_one(): return acc + jnp.sum(jnp.where(match, vals_row[:, None, :], 0.0), axis=0)]
    reduce_sum x9 -> x0, other arithmetic: 20.3 us -> none  [the longest x8 16.8 us: add_one(): return acc + jnp.sum(jnp.where(match, vals_row[:, None, :], 0.0), axis=0)]
    convert_element_type x2 -> x0, other arithmetic: 18.2 us -> none  [the longest x1 18.2 us: on_device(): partials.astype(jnp.float32)]
    all_gather x2 -> x0, waiting for transfers between devices: 17.5 us -> none  [the longest x1 17.5 us: on_device(): vals_piece = lax.all_gather(values[None], 'rep', axis=0, tiled=True)]
  transfers between devices with their start and end apart: 3 -> 63, of which waited for: 2 -> 10; matrix products, arithmetic and copies ran while one was open for 5% -> 0% of each run, Pallas kernels for 0% -> 31%
where the time goes in v1:
time: 299 us; the launch traced here: 298 us
  waiting for transfers between devices  110 us (37%)
  starting transfers between devices  93.3 us (31%)
  Pallas kernels  92.8 us (31%)
    ppermute x48, waiting for transfers between devices, along(): lax.ppermute(value, 'fsdp', shift(0, step) if x_first else shift(step, 0))  109 us
    pallas_call x33, Pallas kernels, call(): pl.pallas_call(body, grid_spec=pltpu.PrefetchScalarGridSpec(num_scalar_pr...  92.8 us
    ppermute x48, starting transfers between devices, along(): lax.ppermute(value, 'fsdp', shift(0, step) if x_first else shift(step, 0))  57.4 us
    ppermute x3, starting transfers between devices, other_core(): return lax.ppermute(value, 'rep', [(r, r ^ 1) for r in range(2 * SIDE)])  18.6 us
    ppermute x12, starting transfers between devices, along_z(): lax.ppermute(value, 'rep', [(z * 2 + c, (z + step) % SIDE * 2 + c) for z...  17.3 us
  transfers between devices with their start and end apart: 63, of which 10 were waited for; matrix products, arithmetic and copies ran while one was open for 0% of the time, Pallas kernels for 31%

profile of v1, /device:TPU:1, one launch (start us, length us, event | category | flops | bytes accessed | tf_op | source)
XLA Modules:
  0.0 298.2 jit_solution(18387279039766248217)
XLA Ops:
  0.6 4.5 %collective-permute-start.51 = (s32[1,8,8192]{2,1,0:T(8,128)}, s32[1,8,8192]{2,1,0:T(8,128)S(1)}, u32[]{:S(2)}, u32[]{:S(2)}) collective-permute-start(s32[1,8,8192]{2,1,0:T(8,128)} %p0.5), channel_id=1, source_target_pairs={{0,64},{16,80},{32,96},{48,112},{64,0},{80,16},{96,32},{112,48},{1... | collective-permute-start | bytes 786440 | tf_op jit(solution)/shard_map/ppermute | solution.py:284
  5.9 1.9 collective-permute-start.53
  7.9 2.5 shard_map.80
  11.8 1.5 collective-permute-start.25
  13.3 2.5 shard_map.76
  17.7 2.5 collective-permute-start.17
  20.2 2.5 shard_map.72
  24.1 2.7 shard_map.88
  29.9 2.5 shard_map.68
  32.5 4.2 %collective-permute-done.8.got_up = f32[4,32,1024]{2,1,0:T(8,128)S(1)} collective-permute-done((f32[4,32,1024]{2,1,0:T(8,128)S(1)}, f32[4,32,1024]{2,1,0:T(8,128)S(1)}, u32[]{:S(2)}, u32[]{:S(2)}) %collective-permute-start.8) | collective-permute-done | bytes 524320 | tf_op jit(solution)/shard_map/ppermute | solution.py:280
  38.2 3.9 %shard_map.84 = (f32[4,32,2048]{2,1,0:T(8,128)}, f32[4,32,2048]{2,1,0:T(8,128)S(1)}) custom-call(s32[2]{0:T(128)S(1)} %pad_add_fusion.here, bf16[64,131072]{1,0:T(8,128)(2,1)} %bitcast.8), custom_call_target="tpu_custom_call" | custom-call | bytes 3145728 | tf_op jit(solution)/shard_map/pallas_call | solution.py:83
  42.1 20.7 %collective-permute-done.9.got_down = f32[4,32,1024]{2,1,0:T(8,128)S(1)} collective-permute-done((f32[4,32,1024]{2,1,0:T(8,128)S(1)}, f32[4,32,1024]{2,1,0:T(8,128)S(1)}, u32[]{:S(2)}, u32[]{:S(2)}) %collective-permute-start.9) | collective-permute-done | bytes 524320 | tf_op jit(solution)/shard_map/ppermute | solution.py:280
  62.8 2.7 collective-permute-start.33
  65.4 2.8 shard_map.81
  69.3 4.1 %shard_map.77 = (f32[4,64,1024]{2,1,0:T(8,128)S(1)}, f32[4,64,1024]{2,1,0:T(8,128)}) custom-call(s32[2]{0:T(128)S(1)} %pad_add_fusion.here, bf16[64,131072]{1,0:T(8,128)(2,1)} %bitcast.11, bf16[64,131072]{1,0:T(8,128)(2,1)} %bitcast.12, f32[4,32,1024]{2,1,0:T(8,128)S(1)} %collective-permute-done.16.got_up, f32[4,32,1024]{2,1,0:T(8,128)S(1)} %collective-permute-done.17.got_down), custom_call_target="tpu_custom_call" | custom-call | bytes 4194304 | tf_op jit(solution)/shard_map/pallas_call | solution.py:83
  73.4 1.7 collective-permute-start.27
  75.2 11.4 %collective-permute-done.32.got_up = f32[4,32,2048]{2,1,0:T(8,128)S(1)} collective-permute-done((f32[4,32,2048]{2,1,0:T(8,128)}, f32[4,32,2048]{2,1,0:T(8,128)S(1)}, u32[]{:S(2)}, u32[]{:S(2)}) %collective-permute-start.32) | collective-permute-done | bytes 1048608 | tf_op jit(solution)/shard_map/ppermute | solution.py:280
  86.6 4.8 %shard_map.89 = (f32[4,64,2048]{2,1,0:T(8,128)}, f32[4,64,2048]{2,1,0:T(8,128)}) custom-call(s32[2]{0:T(128)S(1)} %pad_add_fusion.here, bf16[64,131072]{1,0:T(8,128)(2,1)} %bitcast.13, bf16[64,131072]{1,0:T(8,128)(2,1)} %bitcast.14, f32[4,32,2048]{2,1,0:T(8,128)S(1)} %collective-permute-done.40.got_up, f32[4,32,2048]{2,1,0:T(8,128)S(1)} %collective-permute-done.41.got_down), custom_call_target="tpu_custom_call" | custom-call | bytes 8388608 | tf_op jit(solution)/shard_map/pallas_call | solution.py:83
  92.4 1.7 collective-permute-start.43
  94.1 4.8 %shard_map.85 = (f32[4,64,2048]{2,1,0:T(8,128)}, f32[4,64,2048]{2,1,0:T(8,128)}) custom-call(s32[2]{0:T(128)S(1)} %pad_add_fusion.here, bf16[64,131072]{1,0:T(8,128)(2,1)} %bitcast.15, bf16[64,131072]{1,0:T(8,128)(2,1)} %bitcast.16, f32[4,32,2048]{2,1,0:T(8,128)S(1)} %collective-permute-done.32.got_up, f32[4,32,2048]{2,1,0:T(8,128)S(1)} %collective-permute-done.33.got_down), custom_call_target="tpu_custom_call" | custom-call | bytes 8388608 | tf_op jit(solution)/shard_map/pallas_call | solution.py:83
  100.3 8.7 %collective-permute-done.18.left.left_u.left_d.refs_1_ = f32[4,64,1024]{2,1,0:T(8,128)S(1)} collective-permute-done((f32[4,64,1024]{2,1,0:T(8,128)S(1)}, f32[4,64,1024]{2,1,0:T(8,128)S(1)}, u32[]{:S(2)}, u32[]{:S(2)}) %collective-permute-start.18) | collective-permute-done | bytes 1048608 | tf_op jit(solution)/shard_map/ppermute | solution.py:280
  109.1 4.2 %shard_map.73 = (f32[4,64,1024]{2,1,0:T(8,128)}, f32[4,64,1024]{2,1,0:T(8,128)}) custom-call(s32[2]{0:T(128)S(1)} %pad_add_fusion.here, bf16[64,131072]{1,0:T(8,128)(2,1)} %bitcast.17, bf16[64,131072]{1,0:T(8,128)(2,1)} %bitcast.18, f32[4,32,1024]{2,1,0:T(8,128)S(1)} %copy-done.20, f32[4,32,1024]{2,1,0:T(8,128)S(1)} %copy-done.24), custom_call_target="tpu_custom_call" | custom-call | bytes 4194304 | tf_op jit(solution)/shard_map/pallas_call | solution.py:83
  115.4 4.2 %shard_map.69 = (f32[4,64,1024]{2,1,0:T(8,128)}, f32[4,64,1024]{2,1,0:T(8,128)}) custom-call(s32[2]{0:T(128)S(1)} %pad_add_fusion.here, bf16[64,131072]{1,0:T(8,128)(2,1)} %bitcast.19, bf16[64,131072]{1,0:T(8,128)(2,1)} %bitcast.20, f32[4,32,1024]{2,1,0:T(8,128)S(1)} %copy-done.22, f32[4,32,1024]{2,1,0:T(8,128)S(1)} %copy-done.26), custom_call_target="tpu_custom_call" | custom-call | bytes 4194304 | tf_op jit(solution)/shard_map/pallas_call | solution.py:83
  119.6 36.8 %collective-permute-done.10.left.left_u.left_d.refs_6_ = f32[4,64,1024]{2,1,0:T(8,128)S(1)} collective-permute-done((f32[4,64,1024]{2,1,0:T(8,128)}, f32[4,64,1024]{2,1,0:T(8,128)S(1)}, u32[]{:S(2)}, u32[]{:S(2)}) %collective-permute-start.10) | collective-permute-done | bytes 1048608 | tf_op jit(solution)/shard_map/ppermute | solution.py:280
  159.0 1.5 collective-permute-start.3
  160.5 1.6 shard_map.90
  162.2 2.6 collective-permute-start.45
  164.9 1.6 shard_map.86
  166.4 15.9 %collective-permute-done.44.got_up = f32[32,2048]{1,0:T(8,128)S(1)} collective-permute-done((f32[32,2048]{1,0:T(8,128)S(1)}, f32[32,2048]{1,0:T(8,128)S(1)}, u32[]{:S(2)}, u32[]{:S(2)}) %collective-permute-start.44) | collective-permute-done | bytes 262176 | tf_op jit(solution)/shard_map/ppermute | solution.py:280
  182.5 2.6 collective-permute-start.37
  185.1 2.7 shard_map.91
  189.1 2.7 collective-permute-start.47
  191.8 1.8 shard_map.87
  193.7 2.6 collective-permute-start.39
  196.3 1.5 shard_map.82
  197.9 5.9 %collective-permute-done.28.got_up = f32[32,1024]{1,0:T(8,128)S(1)} collective-permute-done((f32[32,1024]{1,0:T(8,128)S(1)}, f32[32,1024]{1,0:T(8,128)S(1)}, u32[]{:S(2)}, u32[]{:S(2)}) %collective-permute-start.28) | collective-permute-done | bytes 131104 | tf_op jit(solution)/shard_map/ppermute | solution.py:280
  203.8 1.6 shard_map.78
  205.4 4.0 %collective-permute-done.29.got_down = f32[32,1024]{1,0:T(8,128)S(1)} collective-permute-done((f32[32,1024]{1,0:T(8,128)S(1)}, f32[32,1024]{1,0:T(8,128)S(1)}, u32[]{:S(2)}, u32[]{:S(2)}) %collective-permute-start.29) | collective-permute-done | bytes 131104 | tf_op jit(solution)/shard_map/ppermute | solution.py:280
  209.4 1.5 shard_map.74
  210.9 2.7 collective-permute-start.21
  213.8 1.6 shard_map.70
  215.4 2.7 collective-permute-start.13
  218.2 7.8 %shard_map.92 = (f32[1,64,8192]{2,1,0:T(8,128)}, f32[8,4096]{1,0:T(8,128)S(1)}) custom-call(s32[2]{0:T(128)S(1)} %pad_add_fusion.here, bf16[64,131072]{1,0:T(8,128)(2,1)} %bitcast.31, f32[4,64,2048]{2,1,0:T(8,128)S(1)} %collective-permute-done.34.left.left_u.left_d.refs_1_, f32[4,64,2048]{2,1,0:T(8,128)} %copy-done.2, ...), custom_call_target="tpu_custom_call" | custom-call | flops 268435456 | bytes 6815744 | tf_op jit(solution)/shard_map/pallas_call | solution.py:83
  226.0 2.7 collective-permute-start.61
  228.7 1.6 shard_map.83
  230.4 2.7 collective-permute-start.31
  233.1 2.7 collective-permute-start.5
  235.8 1.8 shard_map.79
  237.7 2.7 collective-permute-start.23
  240.4 4.2 %shard_map.97.mine = f32[64,4096]{1,0:T(8,128)S(1)} custom-call(s32[2]{0:T(128)S(1)} %pad_add_fusion.here, f32[8,4096]{1,0:T(8,128)S(1)} %get-tuple-element.108.v0, f32[8,4096]{1,0:T(8,128)S(1)} %collective-permute-done.59.v1, f32[8,4096]{1,0:T(8,128)S(1)} %collective-permute-done.60.v2, f32[8,4096]{1,0:T(8,128)S(1)} %collective-permute-done.61.v3, ...), custom_call_target="tpu_custom_call" | custom-call | flops 134217728 | bytes 2097152 | tf_op jit(solution)/shard_map/pallas_call | solution.py:83
  244.6 15.4 %collective-permute-start.62 = (f32[64,4096]{1,0:T(8,128)S(1)}, f32[64,4096]{1,0:T(8,128)S(1)}, u32[]{:S(2)}, u32[]{:S(2)}) collective-permute-start(f32[64,4096]{1,0:T(8,128)S(1)} %shard_map.97.mine), channel_id=1, source_target_pairs={{0,16},{16,0},{32,48},{48,32},{64,80},{80,64},{96,112},{112,96},{1... | collective-permute-start | bytes 3145736 | tf_op jit(solution)/shard_map/ppermute | solution.py:290
  260.0 1.6 shard_map.75
  261.7 2.7 collective-permute-start.15
  264.4 1.8 shard_map.71
  266.3 2.7 collective-permute-start.7
  268.9 4.8 %shard_map.93 = (f32[1,64,8192]{2,1,0:T(8,128)}, f32[8,2048]{1,0:T(8,128)S(1)}) custom-call(s32[2]{0:T(128)S(1)} %pad_add_fusion.here, bf16[64,131072]{1,0:T(8,128)(2,1)} %bitcast.41, f32[4,64,1024]{2,1,0:T(8,128)S(1)} %copy-done.4, f32[4,64,1024]{2,1,0:T(8,128)} %collective-permute-done.19.right.right_u.right_d.refs_2_, ...), custom_call_target="tpu_custom_call", output_to_operand_aliasing={{0}: (15, {})} | custom-call | flops 134217728 | bytes 3407872 | tf_op jit(solution)/shard_map/pallas_call | solution.py:83
  273.7 2.0 collective-permute-start.55
  275.7 2.7 collective-permute-start.57
  278.4 4.8 %shard_map.94 = (f32[1,64,8192]{2,1,0:T(8,128)}, f32[8,2048]{1,0:T(8,128)S(1)}) custom-call(s32[2]{0:T(128)S(1)} %pad_add_fusion.here, bf16[64,131072]{1,0:T(8,128)(2,1)} %bitcast.43, f32[4,64,1024]{2,1,0:T(8,128)S(1)} %copy-done.10, f32[4,64,1024]{2,1,0:T(8,128)} %collective-permute-done.3.right.right_u.right_d.refs_2_, ...), custom_call_target="tpu_custom_call", output_to_operand_aliasing={{0}: (15, {})} | custom-call | flops 134217728 | bytes 3407872 | tf_op jit(solution)/shard_map/pallas_call | solution.py:83
  283.7 2.1 collective-permute-start.50
  285.9 2.4 shard_map.96.mine
  288.2 2.6 collective-permute-start.58
  290.9 2.4 shard_map.95.mine
  293.8 1.6 shard_map.98.refs_0_
  (152 shorter events, 24.5 us)
Async XLA Ops:
  0.6 15.2 %collective-permute-start.51 = (s32[1,8,8192]{2,1,0:T(8,128)}, s32[1,8,8192]{2,1,0:T(8,128)S(1)}, u32[]{:S(2)}, u32[]{:S(2)}) collective-permute-start(s32[1,8,8192]{2,1,0:T(8,128)} %p0.5), channel_id=1, source_target_pairs={{0,64},{16,80},{32,96},{48,112},{64,0},{80,16},{96,32},{112,48},{1... | collective-permute-start | bytes 786440 | tf_op jit(solution)/shard_map/ppermute | solution.py:284
  5.1 12.6 %collective-permute-start.52 = (s32[1,8,8192]{2,1,0:T(8,128)}, s32[1,8,8192]{2,1,0:T(8,128)S(1)}, u32[]{:S(2)}, u32[]{:S(2)}) collective-permute-start(s32[1,8,8192]{2,1,0:T(8,128)} %p0.5), channel_id=1, source_target_pairs={{0,32},{16,48},{32,64},{48,80},{64,96},{80,112},{96,0},{112,16},{1... | collective-permute-start | bytes 786440 | tf_op jit(solution)/shard_map/ppermute | solution.py:284
  5.9 16.9 %collective-permute-start.53 = (s32[1,8,8192]{2,1,0:T(8,128)}, s32[1,8,8192]{2,1,0:T(8,128)S(1)}, u32[]{:S(2)}, u32[]{:S(2)}) collective-permute-start(s32[1,8,8192]{2,1,0:T(8,128)} %p0.5), channel_id=1, source_target_pairs={{0,96},{16,112},{32,0},{48,16},{64,32},{80,48},{96,64},{112,80},{1... | collective-permute-start | bytes 786440 | tf_op jit(solution)/shard_map/ppermute | solution.py:284
  10.4 16.4 %collective-permute-start.24 = (f32[4,32,1024]{2,1,0:T(8,128)S(1)}, f32[4,32,1024]{2,1,0:T(8,128)S(1)}, u32[]{:S(2)}, u32[]{:S(2)}) collective-permute-start(f32[4,32,1024]{2,1,0:T(8,128)S(1)} %get-tuple-element.80), channel_id=1, source_target_pairs={{0,4},{1,5},{2,6},{3,7},{4,8},{5,9},{6,10},{7,11},{8,12},{9,13},{1... | collective-permute-start | bytes 1572872 | tf_op jit(solution)/shard_map/ppermute | solution.py:280
  11.8 16.4 %collective-permute-start.25 = (f32[4,32,1024]{2,1,0:T(8,128)S(1)}, f32[4,32,1024]{2,1,0:T(8,128)S(1)}, u32[]{:S(2)}, u32[]{:S(2)}) collective-permute-start(f32[4,32,1024]{2,1,0:T(8,128)S(1)} %get-tuple-element.81), channel_id=1, source_target_pairs={{0,12},{1,13},{2,14},{3,15},{4,0},{5,1},{6,2},{7,3},{8,4},{9,5},{1... | collective-permute-start | bytes 1572872 | tf_op jit(solution)/shard_map/ppermute | solution.py:280
  15.8 13.7 %collective-permute-start.16 = (f32[4,32,1024]{2,1,0:T(8,128)S(1)}, f32[4,32,1024]{2,1,0:T(8,128)S(1)}, u32[]{:S(2)}, u32[]{:S(2)}) collective-permute-start(f32[4,32,1024]{2,1,0:T(8,128)S(1)} %get-tuple-element.72), channel_id=1, source_target_pairs={{0,1},{1,2},{2,3},{3,0},{4,5},{5,6},{6,7},{7,4},{8,9},{9,10},{10,1... | collective-permute-start | bytes 1572872 | tf_op jit(solution)/shard_map/ppermute | solution.py:280
  17.7 14.7 %collective-permute-start.17 = (f32[4,32,1024]{2,1,0:T(8,128)S(1)}, f32[4,32,1024]{2,1,0:T(8,128)S(1)}, u32[]{:S(2)}, u32[]{:S(2)}) collective-permute-start(f32[4,32,1024]{2,1,0:T(8,128)S(1)} %get-tuple-element.73), channel_id=1, source_target_pairs={{0,3},{1,0},{2,1},{3,2},{4,7},{5,4},{6,5},{7,6},{8,11},{9,8},{10,9... | collective-permute-start | bytes 1572872 | tf_op jit(solution)/shard_map/ppermute | solution.py:280
  22.8 14.0 %collective-permute-start.8 = (f32[4,32,1024]{2,1,0:T(8,128)S(1)}, f32[4,32,1024]{2,1,0:T(8,128)S(1)}, u32[]{:S(2)}, u32[]{:S(2)}) collective-permute-start(f32[4,32,1024]{2,1,0:T(8,128)S(1)} %get-tuple-element.64), channel_id=1, source_target_pairs={{0,4},{1,5},{2,6},{3,7},{4,8},{5,9},{6,10},{7,11},{8,12},{9,13},{1... | collective-permute-start | bytes 1572872 | tf_op jit(solution)/shard_map/ppermute | solution.py:280
  26.8 46.6 %collective-permute-start.40 = (f32[4,32,2048]{2,1,0:T(8,128)S(1)}, f32[4,32,2048]{2,1,0:T(8,128)S(1)}, u32[]{:S(2)}, u32[]{:S(2)}) collective-permute-start(f32[4,32,2048]{2,1,0:T(8,128)S(1)} %get-tuple-element.96), channel_id=1, source_target_pairs={{0,4},{1,5},{2,6},{3,7},{4,8},{5,9},{6,10},{7,11},{8,12},{9,13},{1... | collective-permute-start | bytes 3145736 | tf_op jit(solution)/shard_map/ppermute | solution.py:280
  28.2 47.0 %collective-permute-start.41 = (f32[4,32,2048]{2,1,0:T(8,128)S(1)}, f32[4,32,2048]{2,1,0:T(8,128)S(1)}, u32[]{:S(2)}, u32[]{:S(2)}) collective-permute-start(f32[4,32,2048]{2,1,0:T(8,128)S(1)} %get-tuple-element.97), channel_id=1, source_target_pairs={{0,12},{1,13},{2,14},{3,15},{4,0},{5,1},{6,2},{7,3},{8,4},{9,5},{1... | collective-permute-start | bytes 3145736 | tf_op jit(solution)/shard_map/ppermute | solution.py:280
  29.6 33.2 %collective-permute-start.9 = (f32[4,32,1024]{2,1,0:T(8,128)S(1)}, f32[4,32,1024]{2,1,0:T(8,128)S(1)}, u32[]{:S(2)}, u32[]{:S(2)}) collective-permute-start(f32[4,32,1024]{2,1,0:T(8,128)S(1)} %get-tuple-element.65), channel_id=1, source_target_pairs={{0,12},{1,13},{2,14},{3,15},{4,0},{5,1},{6,2},{7,3},{8,4},{9,5},{1... | collective-permute-start | bytes 1572872 | tf_op jit(solution)/shard_map/ppermute | solution.py:280
  32.4 30.3 %collective-permute-start = (f32[4,32,1024]{2,1,0:T(8,128)S(1)}, f32[4,32,1024]{2,1,0:T(8,128)S(1)}, u32[]{:S(2)}, u32[]{:S(2)}) collective-permute-start(f32[4,32,1024]{2,1,0:T(8,128)S(1)} %get-tuple-element.56), channel_id=1, source_target_pairs={{0,1},{1,2},{2,3},{3,0},{4,5},{5,6},{6,7},{7,4},{8,9},{9,10},{10,1... | collective-permute-start | bytes 1572872 | tf_op jit(solution)/shard_map/ppermute | solution.py:280
  36.8 31.5 %collective-permute-start.1 = (f32[4,32,1024]{2,1,0:T(8,128)S(1)}, f32[4,32,1024]{2,1,0:T(8,128)S(1)}, u32[]{:S(2)}, u32[]{:S(2)}) collective-permute-start(f32[4,32,1024]{2,1,0:T(8,128)S(1)} %get-tuple-element.57), channel_id=1, source_target_pairs={{0,3},{1,0},{2,1},{3,2},{4,7},{5,4},{6,5},{7,6},{8,11},{9,8},{10,9... | collective-permute-start | bytes 1572872 | tf_op jit(solution)/shard_map/ppermute | solution.py:280
  62.8 23.8 %collective-permute-start.32 = (f32[4,32,2048]{2,1,0:T(8,128)}, f32[4,32,2048]{2,1,0:T(8,128)S(1)}, u32[]{:S(2)}, u32[]{:S(2)}) collective-permute-start(f32[4,32,2048]{2,1,0:T(8,128)} %get-tuple-element.88), channel_id=1, source_target_pairs={{0,1},{1,2},{2,3},{3,0},{4,5},{5,6},{6,7},{7,4},{8,9},{9,10},{10,1... | collective-permute-start | bytes 3145736 | tf_op jit(solution)/shard_map/ppermute | solution.py:280
  62.8 28.6 %collective-permute-start.33 = (f32[4,32,2048]{2,1,0:T(8,128)S(1)}, f32[4,32,2048]{2,1,0:T(8,128)S(1)}, u32[]{:S(2)}, u32[]{:S(2)}) collective-permute-start(f32[4,32,2048]{2,1,0:T(8,128)S(1)} %get-tuple-element.89), channel_id=1, source_target_pairs={{0,3},{1,0},{2,1},{3,2},{4,7},{5,4},{6,5},{7,6},{8,11},{9,8},{10,9... | collective-permute-start | bytes 3145736 | tf_op jit(solution)/shard_map/ppermute | solution.py:280
  68.3 24.1 %collective-permute-start.26 = (f32[4,64,1024]{2,1,0:T(8,128)S(1)}, f32[4,64,1024]{2,1,0:T(8,128)S(1)}, u32[]{:S(2)}, u32[]{:S(2)}) collective-permute-start(f32[4,64,1024]{2,1,0:T(8,128)S(1)} %get-tuple-element.82), channel_id=1, source_target_pairs={{0,4},{1,5},{2,6},{3,7},{4,8},{5,9},{6,10},{7,11},{8,12},{9,13},{1... | collective-permute-start | bytes 3145736 | tf_op jit(solution)/shard_map/ppermute | solution.py:280
  73.4 25.4 %collective-permute-start.27 = (f32[4,64,1024]{2,1,0:T(8,128)S(1)}, f32[4,64,1024]{2,1,0:T(8,128)S(1)}, u32[]{:S(2)}, u32[]{:S(2)}) collective-permute-start(f32[4,64,1024]{2,1,0:T(8,128)S(1)} %get-tuple-element.83), channel_id=1, source_target_pairs={{0,12},{1,13},{2,14},{3,15},{4,0},{5,1},{6,2},{7,3},{8,4},{9,5},{1... | collective-permute-start | bytes 3145736 | tf_op jit(solution)/shard_map/ppermute | solution.py:280
  75.2 33.9 %collective-permute-start.18 = (f32[4,64,1024]{2,1,0:T(8,128)S(1)}, f32[4,64,1024]{2,1,0:T(8,128)S(1)}, u32[]{:S(2)}, u32[]{:S(2)}) collective-permute-start(f32[4,64,1024]{2,1,0:T(8,128)S(1)} %get-tuple-element.74), channel_id=1, source_target_pairs={{0,1},{1,2},{2,3},{3,0},{4,5},{5,6},{6,7},{7,4},{8,9},{9,10},{10,1... | collective-permute-start | bytes 3145736 | tf_op jit(solution)/shard_map/ppermute | solution.py:280
  86.6 26.7 %collective-permute-start.19 = (f32[4,64,1024]{2,1,0:T(8,128)}, f32[4,64,1024]{2,1,0:T(8,128)}, u32[]{:S(2)}, u32[]{:S(2)}) collective-permute-start(f32[4,64,1024]{2,1,0:T(8,128)} %get-tuple-element.75), channel_id=1, source_target_pairs={{0,3},{1,0},{2,1},{3,2},{4,7},{5,4},{6,5},{7,6},{8,11},{9,8},{10,9... | collective-permute-start | bytes 3145736 | tf_op jit(solution)/shard_map/ppermute | solution.py:280
  91.4 66.4 %collective-permute-start.42 = (f32[4,64,2048]{2,1,0:T(8,128)}, f32[4,64,2048]{2,1,0:T(8,128)S(1)}, u32[]{:S(2)}, u32[]{:S(2)}) collective-permute-start(f32[4,64,2048]{2,1,0:T(8,128)} %get-tuple-element.98), channel_id=1, source_target_pairs={{0,4},{1,5},{2,6},{3,7},{4,8},{5,9},{6,10},{7,11},{8,12},{9,13},{1... | collective-permute-start | bytes 6291464 | tf_op jit(solution)/shard_map/ppermute | solution.py:280
  92.4 66.6 %collective-permute-start.43 = (f32[4,64,2048]{2,1,0:T(8,128)}, f32[4,64,2048]{2,1,0:T(8,128)S(1)}, u32[]{:S(2)}, u32[]{:S(2)}) collective-permute-start(f32[4,64,2048]{2,1,0:T(8,128)} %get-tuple-element.99), channel_id=1, source_target_pairs={{0,12},{1,13},{2,14},{3,15},{4,0},{5,1},{6,2},{7,3},{8,4},{9,5},{1... | collective-permute-start | bytes 6291464 | tf_op jit(solution)/shard_map/ppermute | solution.py:280
  98.9 63.2 %collective-permute-start.34 = (f32[4,64,2048]{2,1,0:T(8,128)}, f32[4,64,2048]{2,1,0:T(8,128)S(1)}, u32[]{:S(2)}, u32[]{:S(2)}) collective-permute-start(f32[4,64,2048]{2,1,0:T(8,128)} %get-tuple-element.90), channel_id=1, source_target_pairs={{0,1},{1,2},{2,3},{3,0},{4,5},{5,6},{6,7},{7,4},{8,9},{9,10},{10,1... | collective-permute-start | bytes 6291464 | tf_op jit(solution)/shard_map/ppermute | solution.py:280
  109.0 53.1 %collective-permute-start.35 = (f32[4,64,2048]{2,1,0:T(8,128)}, f32[4,64,2048]{2,1,0:T(8,128)S(1)}, u32[]{:S(2)}, u32[]{:S(2)}) collective-permute-start(f32[4,64,2048]{2,1,0:T(8,128)} %get-tuple-element.91), channel_id=1, source_target_pairs={{0,3},{1,0},{2,1},{3,2},{4,7},{5,4},{6,5},{7,6},{8,11},{9,8},{10,9... | collective-permute-start | bytes 6291464 | tf_op jit(solution)/shard_map/ppermute | solution.py:280
  113.3 43.1 %collective-permute-start.10 = (f32[4,64,1024]{2,1,0:T(8,128)}, f32[4,64,1024]{2,1,0:T(8,128)S(1)}, u32[]{:S(2)}, u32[]{:S(2)}) collective-permute-start(f32[4,64,1024]{2,1,0:T(8,128)} %get-tuple-element.66), channel_id=1, source_target_pairs={{0,4},{1,5},{2,6},{3,7},{4,8},{5,9},{6,10},{7,11},{8,12},{9,13},{1... | collective-permute-start | bytes 3145736 | tf_op jit(solution)/shard_map/ppermute | solution.py:280
  156.4 53.0 %copy-start.5 = (f32[4,64,1024]{2,1,0:T(8,128)}, f32[4,64,1024]{2,1,0:T(8,128)S(1)}, u32[]{:S(2)}) copy-start(f32[4,64,1024]{2,1,0:T(8,128)S(1)} %collective-permute-done.10.left.left_u.left_d.refs_6_) | copy-start | bytes 3145732
  156.4 37.1 %collective-permute-start.11 = (f32[4,64,1024]{2,1,0:T(8,128)}, f32[4,64,1024]{2,1,0:T(8,128)S(1)}, u32[]{:S(2)}, u32[]{:S(2)}) collective-permute-start(f32[4,64,1024]{2,1,0:T(8,128)} %get-tuple-element.67), channel_id=1, source_target_pairs={{0,12},{1,13},{2,14},{3,15},{4,0},{5,1},{6,2},{7,3},{8,4},{9,5},{1... | collective-permute-start | bytes 3145736 | tf_op jit(solution)/shard_map/ppermute | solution.py:280
  157.8 35.8 %collective-permute-start.2 = (f32[4,64,1024]{2,1,0:T(8,128)}, f32[4,64,1024]{2,1,0:T(8,128)S(1)}, u32[]{:S(2)}, u32[]{:S(2)}) collective-permute-start(f32[4,64,1024]{2,1,0:T(8,128)} %get-tuple-element.58), channel_id=1, source_target_pairs={{0,1},{1,2},{2,3},{3,0},{4,5},{5,6},{6,7},{7,4},{8,9},{9,10},{10,1... | collective-permute-start | bytes 3145736 | tf_op jit(solution)/shard_map/ppermute | solution.py:280
  159.0 38.8 %collective-permute-start.3 = (f32[4,64,1024]{2,1,0:T(8,128)}, f32[4,64,1024]{2,1,0:T(8,128)}, u32[]{:S(2)}, u32[]{:S(2)}) collective-permute-start(f32[4,64,1024]{2,1,0:T(8,128)} %get-tuple-element.59), channel_id=1, source_target_pairs={{0,3},{1,0},{2,1},{3,2},{4,7},{5,4},{6,5},{7,6},{8,11},{9,8},{10,9... | collective-permute-start | bytes 3145736 | tf_op jit(solution)/shard_map/ppermute | solution.py:280
  162.1 20.3 %collective-permute-start.44 = (f32[32,2048]{1,0:T(8,128)S(1)}, f32[32,2048]{1,0:T(8,128)S(1)}, u32[]{:S(2)}, u32[]{:S(2)}) collective-permute-start(f32[32,2048]{1,0:T(8,128)S(1)} %get-tuple-element.100), channel_id=1, source_target_pairs={{0,1},{1,2},{2,3},{3,0},{4,5},{5,6},{6,7},{7,4},{8,9},{9,10},{10,1... | collective-permute-start | bytes 786440 | tf_op jit(solution)/shard_map/ppermute | solution.py:280
  162.2 20.3 %collective-permute-start.45 = (f32[32,2048]{1,0:T(8,128)S(1)}, f32[32,2048]{1,0:T(8,128)S(1)}, u32[]{:S(2)}, u32[]{:S(2)}) collective-permute-start(f32[32,2048]{1,0:T(8,128)S(1)} %get-tuple-element.101), channel_id=1, source_target_pairs={{0,3},{1,0},{2,1},{3,2},{4,7},{5,4},{6,5},{7,6},{8,11},{9,8},{10,9... | collective-permute-start | bytes 786440 | tf_op jit(solution)/shard_map/ppermute | solution.py:280
  182.4 6.7 %collective-permute-start.36 = (f32[32,2048]{1,0:T(8,128)S(1)}, f32[32,2048]{1,0:T(8,128)S(1)}, u32[]{:S(2)}, u32[]{:S(2)}) collective-permute-start(f32[32,2048]{1,0:T(8,128)S(1)} %get-tuple-element.92), channel_id=1, source_target_pairs={{0,4},{1,5},{2,6},{3,7},{4,8},{5,9},{6,10},{7,11},{8,12},{9,13},{1... | collective-permute-start | bytes 786440 | tf_op jit(solution)/shard_map/ppermute | solution.py:280
  182.5 6.6 %collective-permute-start.37 = (f32[32,2048]{1,0:T(8,128)S(1)}, f32[32,2048]{1,0:T(8,128)S(1)}, u32[]{:S(2)}, u32[]{:S(2)}) collective-permute-start(f32[32,2048]{1,0:T(8,128)S(1)} %get-tuple-element.93), channel_id=1, source_target_pairs={{0,12},{1,13},{2,14},{3,15},{4,0},{5,1},{6,2},{7,3},{8,4},{9,5},{1... | collective-permute-start | bytes 786440 | tf_op jit(solution)/shard_map/ppermute | solution.py:280
  189.1 21.8 %collective-permute-start.46 = (f32[64,2048]{1,0:T(8,128)}, f32[64,2048]{1,0:T(8,128)S(1)}, u32[]{:S(2)}, u32[]{:S(2)}) collective-permute-start(f32[64,2048]{1,0:T(8,128)} %get-tuple-element.102), channel_id=1, source_target_pairs={{0,1},{1,2},{2,3},{3,0},{4,5},{5,6},{6,7},{7,4},{8,9},{9,10},{10,1... | collective-permute-start | bytes 1572872 | tf_op jit(solution)/shard_map/ppermute | solution.py:280
  189.1 24.6 %collective-permute-start.47 = (f32[64,2048]{1,0:T(8,128)}, f32[64,2048]{1,0:T(8,128)S(1)}, u32[]{:S(2)}, u32[]{:S(2)}) collective-permute-start(f32[64,2048]{1,0:T(8,128)} %get-tuple-element.103), channel_id=1, source_target_pairs={{0,3},{1,0},{2,1},{3,2},{4,7},{5,4},{6,5},{7,6},{8,11},{9,8},{10,9... | collective-permute-start | bytes 1572872 | tf_op jit(solution)/shard_map/ppermute | solution.py:280
  193.6 21.8 %collective-permute-start.38 = (f32[64,2048]{1,0:T(8,128)S(1)}, f32[64,2048]{1,0:T(8,128)S(1)}, u32[]{:S(2)}, u32[]{:S(2)}) collective-permute-start(f32[64,2048]{1,0:T(8,128)S(1)} %get-tuple-element.94), channel_id=1, source_target_pairs={{0,4},{1,5},{2,6},{3,7},{4,8},{5,9},{6,10},{7,11},{8,12},{9,13},{1... | collective-permute-start | bytes 1572872 | tf_op jit(solution)/shard_map/ppermute | solution.py:280
  193.7 24.5 %collective-permute-start.39 = (f32[64,2048]{1,0:T(8,128)S(1)}, f32[64,2048]{1,0:T(8,128)S(1)}, u32[]{:S(2)}, u32[]{:S(2)}) collective-permute-start(f32[64,2048]{1,0:T(8,128)S(1)} %get-tuple-element.95), channel_id=1, source_target_pairs={{0,12},{1,13},{2,14},{3,15},{4,0},{5,1},{6,2},{7,3},{8,4},{9,5},{1... | collective-permute-start | bytes 1572872 | tf_op jit(solution)/shard_map/ppermute | solution.py:280
  197.8 6.0 %collective-permute-start.28 = (f32[32,1024]{1,0:T(8,128)S(1)}, f32[32,1024]{1,0:T(8,128)S(1)}, u32[]{:S(2)}, u32[]{:S(2)}) collective-permute-start(f32[32,1024]{1,0:T(8,128)S(1)} %get-tuple-element.84), channel_id=1, source_target_pairs={{0,1},{1,2},{2,3},{3,0},{4,5},{5,6},{6,7},{7,4},{8,9},{9,10},{10,1... | collective-permute-start | bytes 393224 | tf_op jit(solution)/shard_map/ppermute | solution.py:280
  203.8 5.6 %collective-permute-start.29 = (f32[32,1024]{1,0:T(8,128)S(1)}, f32[32,1024]{1,0:T(8,128)S(1)}, u32[]{:S(2)}, u32[]{:S(2)}) collective-permute-start(f32[32,1024]{1,0:T(8,128)S(1)} %get-tuple-element.85), channel_id=1, source_target_pairs={{0,3},{1,0},{2,1},{3,2},{4,7},{5,4},{6,5},{7,6},{8,11},{9,8},{10,9... | collective-permute-start | bytes 393224 | tf_op jit(solution)/shard_map/ppermute | solution.py:280
  209.4 16.5 %collective-permute-start.20 = (f32[32,1024]{1,0:T(8,128)S(1)}, f32[32,1024]{1,0:T(8,128)S(1)}, u32[]{:S(2)}, u32[]{:S(2)}) collective-permute-start(f32[32,1024]{1,0:T(8,128)S(1)} %get-tuple-element.76), channel_id=1, source_target_pairs={{0,4},{1,5},{2,6},{3,7},{4,8},{5,9},{6,10},{7,11},{8,12},{9,13},{1... | collective-permute-start | bytes 393224 | tf_op jit(solution)/shard_map/ppermute | solution.py:280
  210.9 15.0 %collective-permute-start.21 = (f32[32,1024]{1,0:T(8,128)S(1)}, f32[32,1024]{1,0:T(8,128)S(1)}, u32[]{:S(2)}, u32[]{:S(2)}) collective-permute-start(f32[32,1024]{1,0:T(8,128)S(1)} %get-tuple-element.77), channel_id=1, source_target_pairs={{0,12},{1,13},{2,14},{3,15},{4,0},{5,1},{6,2},{7,3},{8,4},{9,5},{1... | collective-permute-start | bytes 393224 | tf_op jit(solution)/shard_map/ppermute | solution.py:280
  213.7 12.3 %collective-permute-start.12 = (f32[32,1024]{1,0:T(8,128)S(1)}, f32[32,1024]{1,0:T(8,128)S(1)}, u32[]{:S(2)}, u32[]{:S(2)}) collective-permute-start(f32[32,1024]{1,0:T(8,128)S(1)} %get-tuple-element.68), channel_id=1, source_target_pairs={{0,1},{1,2},{2,3},{3,0},{4,5},{5,6},{6,7},{7,4},{8,9},{9,10},{10,1... | collective-permute-start | bytes 393224 | tf_op jit(solution)/shard_map/ppermute | solution.py:280
  215.4 14.9 %collective-permute-start.13 = (f32[32,1024]{1,0:T(8,128)S(1)}, f32[32,1024]{1,0:T(8,128)S(1)}, u32[]{:S(2)}, u32[]{:S(2)}) collective-permute-start(f32[32,1024]{1,0:T(8,128)S(1)} %get-tuple-element.69), channel_id=1, source_target_pairs={{0,3},{1,0},{2,1},{3,2},{4,7},{5,4},{6,5},{7,6},{8,11},{9,8},{10,9... | collective-permute-start | bytes 393224 | tf_op jit(solution)/shard_map/ppermute | solution.py:280
  218.1 12.3 %collective-permute-start.4 = (f32[32,1024]{1,0:T(8,128)S(1)}, f32[32,1024]{1,0:T(8,128)S(1)}, u32[]{:S(2)}, u32[]{:S(2)}) collective-permute-start(f32[32,1024]{1,0:T(8,128)S(1)} %get-tuple-element.60), channel_id=1, source_target_pairs={{0,4},{1,5},{2,6},{3,7},{4,8},{5,9},{6,10},{7,11},{8,12},{9,13},{1... | collective-permute-start | bytes 393224 | tf_op jit(solution)/shard_map/ppermute | solution.py:280
  225.9 7.1 %collective-permute-start.59 = (f32[8,4096]{1,0:T(8,128)S(1)}, f32[8,4096]{1,0:T(8,128)S(1)}, u32[]{:S(2)}, u32[]{:S(2)}) collective-permute-start(f32[8,4096]{1,0:T(8,128)S(1)} %get-tuple-element.108.v0), channel_id=1, source_target_pairs={{0,64},{16,80},{32,96},{48,112},{64,0},{80,16},{96,32},{112,48},{1... | collective-permute-start | bytes 393224 | tf_op jit(solution)/shard_map/ppermute | solution.py:284
  225.9 11.7 %collective-permute-start.60 = (f32[8,4096]{1,0:T(8,128)S(1)}, f32[8,4096]{1,0:T(8,128)S(1)}, u32[]{:S(2)}, u32[]{:S(2)}) collective-permute-start(f32[8,4096]{1,0:T(8,128)S(1)} %get-tuple-element.108.v0), channel_id=1, source_target_pairs={{0,32},{16,48},{32,64},{48,80},{64,96},{80,112},{96,0},{112,16},{1... | collective-permute-start | bytes 393224 | tf_op jit(solution)/shard_map/ppermute | solution.py:284
  226.0 11.7 %collective-permute-start.61 = (f32[8,4096]{1,0:T(8,128)S(1)}, f32[8,4096]{1,0:T(8,128)S(1)}, u32[]{:S(2)}, u32[]{:S(2)}) collective-permute-start(f32[8,4096]{1,0:T(8,128)S(1)} %get-tuple-element.108.v0), channel_id=1, source_target_pairs={{0,96},{16,112},{32,0},{48,16},{64,32},{80,48},{96,64},{112,80},{1... | collective-permute-start | bytes 393224 | tf_op jit(solution)/shard_map/ppermute | solution.py:284
  230.3 31.3 %collective-permute-start.30 = (f32[64,1024]{1,0:T(8,128)S(1)}, f32[64,1024]{1,0:T(8,128)S(1)}, u32[]{:S(2)}, u32[]{:S(2)}) collective-permute-start(f32[64,1024]{1,0:T(8,128)S(1)} %get-tuple-element.86), channel_id=1, source_target_pairs={{0,1},{1,2},{2,3},{3,0},{4,5},{5,6},{6,7},{7,4},{8,9},{9,10},{10,1... | collective-permute-start | bytes 786440 | tf_op jit(solution)/shard_map/ppermute | solution.py:280
  230.4 31.3 %collective-permute-start.31 = (f32[64,1024]{1,0:T(8,128)S(1)}, f32[64,1024]{1,0:T(8,128)S(1)}, u32[]{:S(2)}, u32[]{:S(2)}) collective-permute-start(f32[64,1024]{1,0:T(8,128)S(1)} %get-tuple-element.87), channel_id=1, source_target_pairs={{0,3},{1,0},{2,1},{3,2},{4,7},{5,4},{6,5},{7,6},{8,11},{9,8},{10,9... | collective-permute-start | bytes 786440 | tf_op jit(solution)/shard_map/ppermute | solution.py:280
  233.1 11.5 %collective-permute-start.5 = (f32[32,1024]{1,0:T(8,128)S(1)}, f32[32,1024]{1,0:T(8,128)S(1)}, u32[]{:S(2)}, u32[]{:S(2)}) collective-permute-start(f32[32,1024]{1,0:T(8,128)S(1)} %get-tuple-element.61), channel_id=1, source_target_pairs={{0,12},{1,13},{2,14},{3,15},{4,0},{5,1},{6,2},{7,3},{8,4},{9,5},{1... | collective-permute-start | bytes 393224 | tf_op jit(solution)/shard_map/ppermute | solution.py:280
  237.6 28.5 %collective-permute-start.22 = (f32[64,1024]{1,0:T(8,128)S(1)}, f32[64,1024]{1,0:T(8,128)S(1)}, u32[]{:S(2)}, u32[]{:S(2)}) collective-permute-start(f32[64,1024]{1,0:T(8,128)S(1)} %get-tuple-element.78), channel_id=1, source_target_pairs={{0,4},{1,5},{2,6},{3,7},{4,8},{5,9},{6,10},{7,11},{8,12},{9,13},{1... | collective-permute-start | bytes 786440 | tf_op jit(solution)/shard_map/ppermute | solution.py:280
  237.7 28.5 %collective-permute-start.23 = (f32[64,1024]{1,0:T(8,128)S(1)}, f32[64,1024]{1,0:T(8,128)S(1)}, u32[]{:S(2)}, u32[]{:S(2)}) collective-permute-start(f32[64,1024]{1,0:T(8,128)S(1)} %get-tuple-element.79), channel_id=1, source_target_pairs={{0,12},{1,13},{2,14},{3,15},{4,0},{5,1},{6,2},{7,3},{8,4},{9,5},{1... | collective-permute-start | bytes 786440 | tf_op jit(solution)/shard_map/ppermute | solution.py:280
  244.6 49.3 %collective-permute-start.62 = (f32[64,4096]{1,0:T(8,128)S(1)}, f32[64,4096]{1,0:T(8,128)S(1)}, u32[]{:S(2)}, u32[]{:S(2)}) collective-permute-start(f32[64,4096]{1,0:T(8,128)S(1)} %shard_map.97.mine), channel_id=1, source_target_pairs={{0,16},{16,0},{32,48},{48,32},{64,80},{80,64},{96,112},{112,96},{1... | collective-permute-start | bytes 3145736 | tf_op jit(solution)/shard_map/ppermute | solution.py:290
  261.6 12.1 %collective-permute-start.14 = (f32[64,1024]{1,0:T(8,128)S(1)}, f32[64,1024]{1,0:T(8,128)S(1)}, u32[]{:S(2)}, u32[]{:S(2)}) collective-permute-start(f32[64,1024]{1,0:T(8,128)S(1)} %get-tuple-element.70), channel_id=1, source_target_pairs={{0,1},{1,2},{2,3},{3,0},{4,5},{5,6},{6,7},{7,4},{8,9},{9,10},{10,1... | collective-permute-start | bytes 786440 | tf_op jit(solution)/shard_map/ppermute | solution.py:280
  261.7 14.0 %collective-permute-start.15 = (f32[64,1024]{1,0:T(8,128)S(1)}, f32[64,1024]{1,0:T(8,128)S(1)}, u32[]{:S(2)}, u32[]{:S(2)}) collective-permute-start(f32[64,1024]{1,0:T(8,128)S(1)} %get-tuple-element.71), channel_id=1, source_target_pairs={{0,3},{1,0},{2,1},{3,2},{4,7},{5,4},{6,5},{7,6},{8,11},{9,8},{10,9... | collective-permute-start | bytes 786440 | tf_op jit(solution)/shard_map/ppermute | solution.py:280
  266.2 9.5 %collective-permute-start.6 = (f32[64,1024]{1,0:T(8,128)S(1)}, f32[64,1024]{1,0:T(8,128)S(1)}, u32[]{:S(2)}, u32[]{:S(2)}) collective-permute-start(f32[64,1024]{1,0:T(8,128)S(1)} %get-tuple-element.62), channel_id=1, source_target_pairs={{0,4},{1,5},{2,6},{3,7},{4,8},{5,9},{6,10},{7,11},{8,12},{9,13},{1... | collective-permute-start | bytes 786440 | tf_op jit(solution)/shard_map/ppermute | solution.py:280
  266.3 12.1 %collective-permute-start.7 = (f32[64,1024]{1,0:T(8,128)S(1)}, f32[64,1024]{1,0:T(8,128)S(1)}, u32[]{:S(2)}, u32[]{:S(2)}) collective-permute-start(f32[64,1024]{1,0:T(8,128)S(1)} %get-tuple-element.63), channel_id=1, source_target_pairs={{0,12},{1,13},{2,14},{3,15},{4,0},{5,1},{6,2},{7,3},{8,4},{9,5},{1... | collective-permute-start | bytes 786440 | tf_op jit(solution)/shard_map/ppermute | solution.py:280
  273.7 9.4 %collective-permute-start.55 = (f32[8,2048]{1,0:T(8,128)S(1)}, f32[8,2048]{1,0:T(8,128)S(1)}, u32[]{:S(2)}, u32[]{:S(2)}) collective-permute-start(f32[8,2048]{1,0:T(8,128)S(1)} %get-tuple-element.107.v0), channel_id=1, source_target_pairs={{0,64},{16,80},{32,96},{48,112},{64,0},{80,16},{96,32},{112,48},{1... | collective-permute-start | bytes 196616 | tf_op jit(solution)/shard_map/ppermute | solution.py:284
  275.7 8.1 %collective-permute-start.56 = (f32[8,2048]{1,0:T(8,128)S(1)}, f32[8,2048]{1,0:T(8,128)S(1)}, u32[]{:S(2)}, u32[]{:S(2)}) collective-permute-start(f32[8,2048]{1,0:T(8,128)S(1)} %get-tuple-element.107.v0), channel_id=1, source_target_pairs={{0,32},{16,48},{32,64},{48,80},{64,96},{80,112},{96,0},{112,16},{1... | collective-permute-start | bytes 196616 | tf_op jit(solution)/shard_map/ppermute | solution.py:284
  275.7 10.2 %collective-permute-start.57 = (f32[8,2048]{1,0:T(8,128)S(1)}, f32[8,2048]{1,0:T(8,128)S(1)}, u32[]{:S(2)}, u32[]{:S(2)}) collective-permute-start(f32[8,2048]{1,0:T(8,128)S(1)} %get-tuple-element.107.v0), channel_id=1, source_target_pairs={{0,96},{16,112},{32,0},{48,16},{64,32},{80,48},{96,64},{112,80},{1... | collective-permute-start | bytes 196616 | tf_op jit(solution)/shard_map/ppermute | solution.py:284
  283.1 7.8 %collective-permute-start.48 = (f32[8,2048]{1,0:T(8,128)S(1)}, f32[8,2048]{1,0:T(8,128)S(1)}, u32[]{:S(2)}, u32[]{:S(2)}) collective-permute-start(f32[8,2048]{1,0:T(8,128)S(1)} %get-tuple-element.106.v0), channel_id=1, source_target_pairs={{0,64},{16,80},{32,96},{48,112},{64,0},{80,16},{96,32},{112,48},{1... | collective-permute-start | bytes 196616 | tf_op jit(solution)/shard_map/ppermute | solution.py:284
  283.1 7.7 %collective-permute-start.49 = (f32[8,2048]{1,0:T(8,128)S(1)}, f32[8,2048]{1,0:T(8,128)S(1)}, u32[]{:S(2)}, u32[]{:S(2)}) collective-permute-start(f32[8,2048]{1,0:T(8,128)S(1)} %get-tuple-element.106.v0), channel_id=1, source_target_pairs={{0,32},{16,48},{32,64},{48,80},{64,96},{80,112},{96,0},{112,16},{1... | collective-permute-start | bytes 196616 | tf_op jit(solution)/shard_map/ppermute | solution.py:284
  283.7 7.2 %collective-permute-start.50 = (f32[8,2048]{1,0:T(8,128)S(1)}, f32[8,2048]{1,0:T(8,128)S(1)}, u32[]{:S(2)}, u32[]{:S(2)}) collective-permute-start(f32[8,2048]{1,0:T(8,128)S(1)} %get-tuple-element.106.v0), channel_id=1, source_target_pairs={{0,96},{16,112},{32,0},{48,16},{64,32},{80,48},{96,64},{112,80},{1... | collective-permute-start | bytes 196616 | tf_op jit(solution)/shard_map/ppermute | solution.py:284
  288.2 7.2 %collective-permute-start.58 = (f32[64,2048]{1,0:T(8,128)S(1)}, f32[64,2048]{1,0:T(8,128)S(1)}, u32[]{:S(2)}, u32[]{:S(2)}) collective-permute-start(f32[64,2048]{1,0:T(8,128)S(1)} %shard_map.96.mine), channel_id=1, source_target_pairs={{0,16},{16,0},{32,48},{48,32},{64,80},{80,64},{96,112},{112,96},{1... | collective-permute-start | bytes 1572872 | tf_op jit(solution)/shard_map/ppermute | solution.py:290
  293.3 3.6 %collective-permute-start.54 = (f32[64,2048]{1,0:T(8,128)S(1)}, f32[64,2048]{1,0:T(8,128)S(1)}, u32[]{:S(2)}, u32[]{:S(2)}) collective-permute-start(f32[64,2048]{1,0:T(8,128)S(1)} %shard_map.95.mine), channel_id=1, source_target_pairs={{0,16},{16,0},{32,48},{48,32},{64,80},{80,64},{96,112},{112,96},{1... | collective-permute-start | bytes 1572872 | tf_op jit(solution)/shard_map/ppermute | solution.py:290
  (27 other events, 278.9 us)

commit v2 on v0

v2 whole, which is shorter than its diff:
```python
import jax
import jax.numpy as jnp
import ml_dtypes
import numpy as np
from jax import lax
from jax.experimental import pallas as pl
from jax.experimental.pallas import tpu as pltpu
from jax.sharding import PartitionSpec as P

BLOCK = 64
HALF = BLOCK // 2
KEEP = 8
SIDE = 4
TILE = 512
PIECES = {"a": (0, 2560), "b": (5120, 1536)}
ORDER = "a1 a2 a3 b1 b2a b3 a5 b4 a6 b5 a7 b6 a8 b7 b8"
PLACES_WITH = ("a2", "a3", "b1")
VMEM_LIMIT = 48 * 1024 * 1024
F32 = jnp.float32
BF16 = jnp.bfloat16


def dct_parts():
    k = np.arange(BLOCK, dtype=np.float64)[:, None]
    n = np.arange(BLOCK, dtype=np.float64)[None, :]
    scale = np.where(k == 0, np.sqrt(1.0 / BLOCK), np.sqrt(2.0 / BLOCK))
    dct = scale * np.cos(np.pi * (2.0 * n + 1.0) * k / (2.0 * BLOCK))

    def wide(mat):
        high = mat.astype(ml_dtypes.bfloat16)
        low = (mat - high.astype(np.float64)).astype(ml_dtypes.bfloat16)
        return np.concatenate([high, high, low, low], axis=1)

    return wide(dct), wide(dct.T.copy())


def fold(coord, step):
    return lax.rem(coord + (step + SIDE), SIDE)


class Half:
    def __init__(self, x_first, start, width, spans):
        self.x_first = x_first
        self.width = width
        self.count = width // TILE
        self.first = start // TILE
        self.per_target = spans // TILE

    def column(self, here, step, other):
        y, x = here[0], here[1]
        if self.x_first:
            target = other * SIDE + fold(x, step)
        else:
            target = fold(y, step) * SIDE + other
        return target * self.per_target + self.first

    def second(self, here, step):
        return fold(here[0] if self.x_first else here[1], step)

    def grid_blocks(self, step, rows):
        def spec(tile):
            return pl.BlockSpec(
                (HALF, TILE), lambda i, here: (rows, self.column(here, step, i) + tile)
            )

        return [spec(tile) for tile in range(self.count)]

    def one_blocks(self, step):
        def spec(tile):
            return pl.BlockSpec(
                (BLOCK, TILE),
                lambda i, here: (0, self.column(here, 0, self.second(here, step)) + tile),
            )

        return [spec(tile) for tile in range(self.count)]

    def message_blocks(self, step):
        def spec(tile):
            return pl.BlockSpec(
                (HALF, TILE), lambda i, here: (0, self.second(here, step) * self.count + tile)
            )

        return [spec(tile) for tile in range(self.count)]


def whole(*shape):
    return pl.BlockSpec(shape, lambda i, here: (0,) * len(shape))


class Line:
    def __init__(self, here):
        self.here = here
        self.token = None
        self.arrived = []

    def call(self, body, grid, ins, in_specs, out_shape, out_specs, aliases=None):
        ins, in_specs = list(ins), list(in_specs)
        count = len(ins)
        order = ([] if self.token is None else [self.token]) + self.arrived
        taken = len(order)
        ins += order
        in_specs += [whole(*(1,) * (array.ndim - 2), 8, 128) for array in order]

        def run(here, *refs):
            refs[-1][...] = jnp.zeros((8, 128), F32)
            body(here, *refs[:count], *refs[count + taken : -1])

        *outs, self.token = pl.pallas_call(
            run,
            grid_spec=pltpu.PrefetchScalarGridSpec(
                num_scalar_prefetch=1,
                grid=(grid,),
                in_specs=in_specs,
                out_specs=(*out_specs, whole(8, 128)),
            ),
            out_shape=(*out_shape, jax.ShapeDtypeStruct((8, 128), F32)),
            input_output_aliases=aliases or {},
            compiler_params=pltpu.CompilerParams(vmem_limit_bytes=VMEM_LIMIT),
            cost_estimate=pl.CostEstimate(flops=0, bytes_accessed=0, transcendentals=0),
        )(self.here, *ins)
        return outs


def tiles(n, *groups):
    for tile in range(n):
        yield slice(tile * TILE, (tile + 1) * TILE), [group[tile] for group in groups]


def groups(refs, n):
    return [refs[k : k + n] for k in range(0, len(refs), n)]


def send_part(line, half, partials, up_from, down_from, extra):
    w, n = half.width, half.count

    def body(here, *refs):
        up, down = refs[2 * n :]
        for col, (part_up, part_down) in tiles(n, *groups(refs[: 2 * n], n)):
            up[:, col] = part_up[...].astype(F32)
            down[:, col] = part_down[...].astype(F32)

    shape = jax.ShapeDtypeStruct((HALF, SIDE * w + extra), F32)
    spec = pl.BlockSpec((HALF, w), lambda i, here: (0, i))
    return line.call(
        body, SIDE, [partials] * (2 * n), half.grid_blocks(*up_from) + half.grid_blocks(*down_from),
        (shape, shape), (spec, spec),
    )


def send_far(line, half, partials):
    return send_part(line, half, partials, (2, 0), (2, 1), 0)


def send_raw(line, half, partials, extra):
    return send_part(line, half, partials, (1, 1), (-1, 0), extra)


def send_near(line, half, partials, far_up, far_down):
    w, n = half.width, half.count

    def body(here, *refs):
        far_up, far_down, up, down = refs[2 * n :]
        for col, (part_up, part_down) in tiles(n, *groups(refs[: 2 * n], n)):
            up[:, col] = part_up[...].astype(F32) + far_up[:, col]
            down[:, col] = part_down[...].astype(F32) + far_down[:, col]

    shape = jax.ShapeDtypeStruct((HALF, SIDE * w), F32)
    spec = pl.BlockSpec((HALF, w), lambda i, here: (0, i))
    return line.call(
        body, SIDE, [partials] * (2 * n) + [far_up, far_down],
        half.grid_blocks(1, 0) + half.grid_blocks(-1, 1) + [spec, spec],
        (shape, shape), (spec, spec),
    )


def repeat(arrays, n):
    return [array for array in arrays for _ in range(n)]


def high_low(part, raw_up, raw_down, near_up, near_down):
    high = part[:HALF].astype(F32) + near_up[...] + raw_down[...]
    low = part[HALF:].astype(F32) + near_down[...] + raw_up[...]
    return high, low


def send_far2(line, half, partials, got, into=None, first=0):
    w, n = half.width, half.count

    def body(here, *refs):
        up, down = refs[-2:]
        for col, blocks in tiles(n, *groups(refs[: 5 * n], n)):
            up[:, col], down[:, col] = high_low(*blocks)

    ins = [partials] * n + repeat(got, n)
    specs = half.one_blocks(2) + half.message_blocks(2) * 4
    shape = jax.ShapeDtypeStruct((HALF, w), F32)
    if into is None:
        return line.call(body, 1, ins, specs, (shape, shape), (whole(HALF, w), whole(HALF, w)))

    def by_tile(here, *refs):
        up, down = refs[-2:]
        for tile in range(n):

            @pl.when(pl.program_id(0) == tile)
            def _():
                up[...], down[...] = high_low(*(group[tile] for group in groups(refs[: 5 * n], n)))

    shape = jax.ShapeDtypeStruct(into[0].shape, F32)
    spec = pl.BlockSpec((HALF, TILE), lambda i, here: (0, first + i))
    return line.call(
        by_tile, n, ins + [*into], specs + [pl.BlockSpec(memory_space=pl.ANY)] * 2,
        (shape, shape), (spec, spec), aliases={len(ins) + 1: 0, len(ins) + 2: 1},
    )


def send_near2(line, half, partials, got, far, first=0):
    w, n = half.width, half.count

    def body(here, *refs):
        up, down = refs[-2:]
        for col, blocks in tiles(n, *groups(refs[: 12 * n], n)):
            high, low = high_low(*blocks[:5])
            up[:HALF, col] = high + blocks[10][...]
            up[HALF:, col] = low
            high, low = high_low(*blocks[5:10])
            down[:HALF, col] = high
            down[HALF:, col] = low + blocks[11][...]

    def far_spec(tile):
        return pl.BlockSpec((HALF, TILE), lambda i, here: (0, first + tile))

    shape = jax.ShapeDtypeStruct((BLOCK, w), F32)
    return line.call(
        body, 1,
        ([partials] * n + repeat(got, n)) * 2 + repeat(far, n),
        half.one_blocks(1) + half.message_blocks(1) * 4 + half.one_blocks(-1)
        + half.message_blocks(-1) * 4 + [far_spec(tile) for tile in range(n)] * 2,
        (shape, shape), (whole(BLOCK, w), whole(BLOCK, w)),
    )


def product(parts, value):
    high = value.astype(BF16)
    low = (value - high.astype(F32)).astype(BF16)
    return jnp.dot(
        parts[...], jnp.concatenate([high, low, high, low], axis=0), preferred_element_type=F32
    )


def finish(line, pair, partials, momentum, positions, got, tables, so_far):
    n = pair[0].count
    first = pair[0].first
    ins, specs = [], []
    for number, (half, arrays) in enumerate(zip(pair, got)):
        ins += [partials, *arrays]

        def tile(i, number=number):
            return jnp.minimum(i, n - 1) if number == 0 else jnp.maximum(i - n, 0)

        def part(i, here, half=half, tile=tile):
            return 0, half.column(here, 0, half.second(here, 0)) + tile(i)

        def message(i, here, half=half, tile=tile):
            return 0, half.second(here, 0) * n + tile(i)

        def flat(i, here, tile=tile):
            return 0, tile(i)

        specs += [pl.BlockSpec((BLOCK, TILE), part)]
        specs += [pl.BlockSpec((HALF, TILE), message)] * 4
        specs += [pl.BlockSpec((BLOCK, TILE), flat)] * 2
    along = lambda rows: pl.BlockSpec((1, rows, TILE), lambda i, here: (0, 0, first + i))
    ins += [momentum, positions, *tables]
    specs += [along(BLOCK), along(KEEP), whole(BLOCK, 4 * BLOCK), whole(BLOCK, 4 * BLOCK)]
    aliases = {}
    if so_far is not None:
        ins.append(so_far)
        specs.append(pl.BlockSpec(memory_space=pl.ANY))
        aliases = {len(ins): 0}

    def body(here, *refs):
        momentum, positions, forward, backward = refs[14:18]
        fresh, values = refs[-2:]
        freq = lax.broadcasted_iota(jnp.int32, (BLOCK, TILE), 0)

        def settle(part, raw_up, raw_down, near_up, near_down, left2, right2):
            grad = jnp.concatenate(high_low(part, raw_up, raw_down, near_up, near_down), axis=0)
            grad = grad + left2[...] + right2[...]
            moment = 0.9 * momentum[0] + grad
            coeff = product(forward, moment)
            chosen = positions[0]
            own = jnp.zeros_like(coeff)
            rows = []
            for place in range(KEEP):
                hit = jnp.where(chosen[place : place + 1] == freq, coeff, 0.0)
                rows.append(jnp.sum(hit, axis=0, keepdims=True))
                own = own + hit
            values[...] = jnp.concatenate(rows, axis=0)
            fresh[0] = moment - product(backward, own)

        @pl.when(pl.program_id(0) < n)
        def _():
            settle(*refs[0:7])

        @pl.when(pl.program_id(0) >= n)
        def _():
            settle(*refs[7:14])

    spans = 2 * n * TILE
    return line.call(
        body, 2 * n, ins, specs,
        (jax.ShapeDtypeStruct(momentum.shape, F32), jax.ShapeDtypeStruct((KEEP, spans), F32)),
        (along(BLOCK), pl.BlockSpec((KEEP, TILE), lambda i, here: (0, i))),
        aliases=aliases,
    )


def spread(line, first, lists, places, table):
    spans = lists[0].shape[1]

    def body(here, *refs):
        backward, out = refs[-2:]
        freq = lax.broadcasted_iota(jnp.int32, (BLOCK, TILE), 0)
        dense = []
        for values, chosen in zip(refs[:4], refs[4:8]):
            acc = jnp.zeros((BLOCK, TILE), F32)
            for place in range(KEEP):
                hit = chosen[0, place : place + 1] == freq
                acc = jnp.where(hit, values[place : place + 1], acc)
            dense.append(acc)
        out[...] = product(backward, (dense[0] + dense[3]) + (dense[1] + dense[2]))

    return line.call(
        body, spans // TILE, [*lists, *places, table],
        [pl.BlockSpec((KEEP, TILE), lambda i, here: (0, i))] * 4
        + [pl.BlockSpec((1, KEEP, TILE), lambda i, here: (0, 0, first + i))] * 4
        + [whole(BLOCK, 4 * BLOCK)],
        (jax.ShapeDtypeStruct((BLOCK, spans), F32),),
        (pl.BlockSpec((BLOCK, TILE), lambda i, here: (0, i)),),
    )[0]


def join(line, first, mine, other, spans, so_far):
    count = mine.shape[1] // TILE
    flat = pl.BlockSpec((BLOCK, TILE), lambda i, here: (0, i))
    ins, specs, aliases = [mine, other], [flat, flat], {}
    if so_far is not None:
        ins.append(so_far)
        specs.append(pl.BlockSpec(memory_space=pl.ANY))
        aliases = {3: 0}

    def body(here, *refs):
        refs[-1][...] = refs[0][...] + refs[1][...]

    return line.call(
        body, count, ins, specs, (jax.ShapeDtypeStruct((BLOCK, spans), F32),),
        (pl.BlockSpec((BLOCK, TILE), lambda i, here: (0, first + i)),),
        aliases=aliases,
    )[0]


def shift(dy, dx):
    return [
        (y * SIDE + x, (y + dy) % SIDE * SIDE + (x + dx) % SIDE)
        for y in range(SIDE)
        for x in range(SIDE)
    ]


def along(x_first, value, step):
    return lax.ppermute(value, "fsdp", shift(0, step) if x_first else shift(step, 0))


def along_z(value, step):
    return lax.ppermute(
        value, "rep", [(z * 2 + c, (z + step) % SIDE * 2 + c) for z in range(SIDE) for c in range(2)]
    )


def other_core(value):
    return lax.ppermute(value, "rep", [(r, r ^ 1) for r in range(2 * SIDE)])


def both(x_first, sent):
    return [along(x_first, sent[0], 1), along(x_first, sent[1], -1)]


def on_device(partials, momentum, positions):
    spans = momentum.shape[2]
    flat = partials.reshape(partials.shape[2:])
    me = lax.axis_index("fsdp")
    here = jnp.stack([me // SIDE, lax.rem(me, SIDE)]).astype(jnp.int32)
    tables = tuple(jnp.asarray(part) for part in dct_parts())
    line = Line(here)
    offset = dict.fromkeys(PIECES, 0)
    pairs = {
        name: (Half(True, start, width, spans), Half(False, start + width, width, spans))
        for name, (start, width) in PIECES.items()
    }
    places = [positions] + [along_z(positions, step) for step in (1, -1, 2)]
    got, sent = {}, []
    fresh = update = None
    for index, step in enumerate(ORDER.split()):
        name, stage, *guest = step
        pair = pairs[name]
        line.arrived = sent[index - 2] if index >= 2 else []
        before = lambda *stages, name=name: [
            [*sum((got[name, s][h] for s in stages), [])] for h in range(2)
        ]
        if stage == "1":
            out = [both(h.x_first, send_far(line, h, flat)) for h in pair]
        elif stage == "2" and not guest:
            out = [both(h.x_first, send_raw(line, h, flat, 0)) for h in pair]
        elif stage == "2":
            guests = pairs[guest[0]][::-1]
            out = []
            for half, other, g in zip(pair, guests, before(2, 3, name=guest[0])[::-1]):
                parts = send_raw(line, half, flat, other.width)
                parts = send_far2(line, other, flat, g, parts, SIDE * half.count)
                out.append(both(half.x_first, parts))
            got[guest[0], 4] = out[::-1]
            offset[guest[0]] = SIDE * pair[0].count
        elif stage == "3":
            out = [both(h.x_first, send_near(line, h, flat, *g)) for h, g in zip(pair, before(1))]
        elif stage == "4":
            out = [
                both(not h.x_first, send_far2(line, h, flat, g)) for h, g in zip(pair, before(2, 3))
            ]
        elif stage == "5":
            out = [
                both(not h.x_first, send_near2(line, h, flat, g, f, offset[name]))
                for h, g, f in zip(pair, before(2, 3), before(4))
            ]
        elif stage == "6":
            fresh, own = finish(
                line, pair, flat, momentum, positions, before(2, 3, 5), tables, fresh
            )
            lists = [own] + [along_z(own, step) for step in (1, -1, 2)]
            out = [lists[1:], lists]
        elif stage == "7":
            mine = spread(line, pair[0].first, got[name, 6][1], places, tables[1])
            out = [[other_core(mine)], [mine]]
        elif stage == "8":
            (other,), (mine,) = got[name, 7]
            update = join(line, pair[0].first, mine, other, spans, update)
            out = []
        got[name, int(stage)] = out
        sent.append(sum(out, []) if int(stage) < 6 else (out[0] if out else []))
        if step in PLACES_WITH:
            sent[-1] = sent[-1] + [places[1 + PLACES_WITH.index(step)]]
    return update, fresh


def solution(mesh):
    placed = (P("rep", "fsdp", None, None), P("rep", None, "fsdp"), P("rep", None, "fsdp"))
    return jax.shard_map(
        on_device,
        mesh=mesh,
        in_specs=placed,
        out_specs=(P(None, "fsdp"), P("rep", None, "fsdp")),
        check_vma=False,
    )
```

time: 327 us -> 268 us (0.82)
  waiting for transfers between devices: 216 us -> 87.2 us
  Pallas kernels: 0 us -> 103 us
  starting transfers between devices: 0.12 us -> 67.8 us
  other arithmetic: 64.2 us -> 0.08 us
  matrix products: 15.1 us -> 0 us
  between operations: 15.5 us -> 1.07 us
  local copies, waits for them, and re-layouts: 15.5 us -> 5.43 us
    reduce_scatter x1 -> x0, waiting for transfers between devices: 197 us -> none  [on_device(): lax.psum_scatter(partials.astype(jnp.float32), 'fsdp', scatter_dimension=...]
    pallas_call x0 -> x26, Pallas kernels: none -> 103 us  [call(): pl.pallas_call(run, grid_spec=pltpu.PrefetchScalarGridSpec(num_scalar_pre...]
    ppermute x0 -> x47, waiting for transfers between devices: none -> 87.2 us  [the longest x36 82.6 us: along(): lax.ppermute(value, 'fsdp', shift(0, step) if x_first else shift(step, 0))]
    ppermute x0 -> x47, starting transfers between devices: none -> 67.8 us  [the longest x36 41.5 us: along(): lax.ppermute(value, 'fsdp', shift(0, step) if x_first else shift(step, 0))]
    add x8 -> x0, other arithmetic: 23.3 us -> none  [add_one(): return acc + jnp.sum(jnp.where(match, vals_row[:, None, :], 0.0), axis=0)]
    reduce_sum x9 -> x0, other arithmetic: 20.3 us -> none  [the longest x8 16.8 us: add_one(): return acc + jnp.sum(jnp.where(match, vals_row[:, None, :], 0.0), axis=0)]
    convert_element_type x2 -> x0, other arithmetic: 18.2 us -> none  [the longest x1 18.2 us: on_device(): partials.astype(jnp.float32)]
    all_gather x2 -> x0, waiting for transfers between devices: 17.5 us -> none  [the longest x1 17.5 us: on_device(): vals_piece = lax.all_gather(values[None], 'rep', axis=0, tiled=True)]
  transfers between devices with their start and end apart: 3 -> 47, of which waited for: 2 -> 17; matrix products, arithmetic and copies ran while one was open for 5% -> 0% of each run, Pallas kernels for 0% -> 33%
where the time goes in v2:
time: 268 us; the launch traced here: 264 us
  Pallas kernels  103 us (38%)
  waiting for transfers between devices  87.2 us (33%)
  starting transfers between devices  67.8 us (25%)
  local copies, waits for them, and re-layouts  5.43 us (2%)
    pallas_call x26, Pallas kernels, call(): pl.pallas_call(run, grid_spec=pltpu.PrefetchScalarGridSpec(num_scalar_pre...  103 us
    ppermute x36, waiting for transfers between devices, along(): lax.ppermute(value, 'fsdp', shift(0, step) if x_first else shift(step, 0))  82.6 us
    ppermute x36, starting transfers between devices, along(): lax.ppermute(value, 'fsdp', shift(0, step) if x_first else shift(step, 0))  41.5 us
    ppermute x9, starting transfers between devices, along_z(): lax.ppermute(value, 'rep', [(z * 2 + c, (z + step) % SIDE * 2 + c) for z...  13.7 us
    ppermute x2, starting transfers between devices, other_core(): return lax.ppermute(value, 'rep', [(r, r ^ 1) for r in range(2 * SIDE)])  12.6 us
    unnamed x62, local copies, waits for them, and re-layouts  5.43 us
  transfers between devices with their start and end apart: 47, of which 17 were waited for; matrix products, arithmetic and copies ran while one was open for 0% of the time, Pallas kernels for 33%

profile of v2, /device:TPU:1, one launch (start us, length us, event | category | flops | bytes accessed | tf_op | source)
XLA Modules:
  0.0 264.4 jit_solution(13439561023231722100)
XLA Ops:
  0.7 3.1 %shard_map.68 = (f32[32,10240]{1,0:T(8,128)S(1)}, f32[32,10240]{1,0:T(8,128)S(1)}, f32[8,128]{1,0:T(8,128)S(1)}) custom-call(s32[2]{0:T(128)S(1)} %pad_add_fusion.here, bf16[64,131072]{1,0:T(8,128)(2,1)} %bitcast.3, bf16[64,131072]{1,0:T(8,128)(2,1)} %bitcast.4, bf16[64,131072]{1,0:T(8,128)(2,1)} %bitcast.5, bf16[64,131072]{1,0:T(8,128)(2,1)} %bitcast.6, ...), custom_call_target="tpu_custom_call" | custom-call | tf_op jit(solution)/shard_map/pallas_call | solution.py:108
  3.8 2.1 collective-permute-start.4
  6.0 1.3 collective-permute-start.5
  7.3 3.1 %shard_map.69 = (f32[32,10240]{1,0:T(8,128)S(1)}, f32[32,10240]{1,0:T(8,128)S(1)}, f32[8,128]{1,0:T(8,128)S(1)}) custom-call(s32[2]{0:T(128)S(1)} %pad_add_fusion.here, bf16[64,131072]{1,0:T(8,128)(2,1)} %bitcast.17, bf16[64,131072]{1,0:T(8,128)(2,1)} %bitcast.14, bf16[64,131072]{1,0:T(8,128)(2,1)} %bitcast.15, bf16[64,131072]{1,0:T(8,128)(2,1)} %bitcast.16, ...), custom_call_target="tpu_custom_call" | custom-call | tf_op jit(solution)/shard_map/pallas_call | solution.py:108
  10.4 1.5 collective-permute-start.2
  11.9 1.5 collective-permute-start.3
  13.4 4.2 %shard_map.70 = (f32[32,10240]{1,0:T(8,128)}, f32[32,10240]{1,0:T(8,128)}, f32[8,128]{1,0:T(8,128)S(1)}) custom-call(s32[2]{0:T(128)S(1)} %pad_add_fusion.here, bf16[64,131072]{1,0:T(8,128)(2,1)} %bitcast.23, bf16[64,131072]{1,0:T(8,128)(2,1)} %bitcast.24, bf16[64,131072]{1,0:T(8,128)(2,1)} %bitcast.25, bf16[64,131072]{1,0:T(8,128)(2,1)} %bitcast.26, ...), custom_call_target="tpu_custom_call" | custom-call | tf_op jit(solution)/shard_map/pallas_call | solution.py:108
  17.7 17.5 %collective-permute-done.4.refs_10_.refs_13_ = f32[32,10240]{1,0:T(8,128)S(1)} collective-permute-done((f32[32,10240]{1,0:T(8,128)S(1)}, f32[32,10240]{1,0:T(8,128)S(1)}, u32[]{:S(2)}, u32[]{:S(2)}) %collective-permute-start.4) | collective-permute-done | bytes 1310752 | tf_op jit(solution)/shard_map/ppermute | solution.py:371
  35.3 1.6 collective-permute-start.9
  36.9 4.3 %shard_map.71 = (f32[32,10240]{1,0:T(8,128)}, f32[32,10240]{1,0:T(8,128)}, f32[8,128]{1,0:T(8,128)S(1)}) custom-call(s32[2]{0:T(128)S(1)} %pad_add_fusion.here, bf16[64,131072]{1,0:T(8,128)(2,1)} %bitcast.38, bf16[64,131072]{1,0:T(8,128)(2,1)} %bitcast.34, bf16[64,131072]{1,0:T(8,128)(2,1)} %bitcast.35, bf16[64,131072]{1,0:T(8,128)(2,1)} %bitcast.36, ...), custom_call_target="tpu_custom_call" | custom-call | tf_op jit(solution)/shard_map/pallas_call | solution.py:108
  41.2 1.4 collective-permute-start
  42.6 1.5 collective-permute-start.1
  44.1 1.7 collective-permute-start.10
  45.8 4.1 %shard_map.72 = (f32[32,10240]{1,0:T(8,128)S(1)}, f32[32,10240]{1,0:T(8,128)}, f32[8,128]{1,0:T(8,128)S(1)}) custom-call(s32[2]{0:T(128)S(1)} %pad_add_fusion.here, bf16[64,131072]{1,0:T(8,128)(2,1)} %bitcast.43, bf16[64,131072]{1,0:T(8,128)(2,1)} %bitcast.44, bf16[64,131072]{1,0:T(8,128)(2,1)} %bitcast.45, bf16[64,131072]{1,0:T(8,128)(2,1)} %bitcast.46, ...), custom_call_target="tpu_custom_call" | custom-call | tf_op jit(solution)/shard_map/pallas_call | solution.py:108
  52.4 1.3 copy-done.20
  53.7 4.1 %shard_map.73 = (f32[32,10240]{1,0:T(8,128)S(1)}, f32[32,10240]{1,0:T(8,128)}, f32[8,128]{1,0:T(8,128)S(1)}) custom-call(s32[2]{0:T(128)S(1)} %pad_add_fusion.here, bf16[64,131072]{1,0:T(8,128)(2,1)} %bitcast.54, bf16[64,131072]{1,0:T(8,128)(2,1)} %bitcast.53, bf16[64,131072]{1,0:T(8,128)(2,1)} %bitcast.55, bf16[64,131072]{1,0:T(8,128)(2,1)} %bitcast.56, ...), custom_call_target="tpu_custom_call" | custom-call | tf_op jit(solution)/shard_map/pallas_call | solution.py:108
  58.5 4.9 %collective-permute-done.8.refs_7_.refs_5_.refs_6_.refs_8_.refs_9_.refs_30_.refs_31_.refs_32_.refs_33_.refs_34_.refs_1_ = f32[32,10240]{1,0:T(8,128)S(1)} collective-permute-done((f32[32,10240]{1,0:T(8,128)}, f32[32,10240]{1,0:T(8,128)S(1)}, u32[]{:S(2)}, u32[]{:S(2)}) %collective-permute-start.8) | collective-permute-done | bytes 1310752 | tf_op jit(solution)/shard_map/ppermute | solution.py:371
  63.4 3.1 %collective-permute-start.7 = (f32[32,10240]{1,0:T(8,128)}, f32[32,10240]{1,0:T(8,128)}, u32[]{:S(2)}, u32[]{:S(2)}) collective-permute-start(f32[32,10240]{1,0:T(8,128)} %get-tuple-element.87), channel_id=1, source_target_pairs={{0,12},{1,13},{2,14},{3,15},{4,0},{5,1},{6,2},{7,3},{8,4},{9,5},{1... | collective-permute-start | bytes 3932168 | tf_op jit(solution)/shard_map/ppermute | solution.py:371
  66.5 3.6 %collective-permute-done.refs_9_.refs_5_.refs_6_.refs_7_.refs_8_.refs_30_.refs_31_.refs_32_.refs_33_.refs_34_ = f32[32,10240]{1,0:T(8,128)S(1)} collective-permute-done((f32[32,10240]{1,0:T(8,128)}, f32[32,10240]{1,0:T(8,128)S(1)}, u32[]{:S(2)}, u32[]{:S(2)}) %collective-permute-start) | collective-permute-done | bytes 1310752 | tf_op jit(solution)/shard_map/ppermute | solution.py:371
  70.7 3.8 %collective-permute-start.13 = (s32[1,8,8192]{2,1,0:T(8,128)S(1)}, s32[1,8,8192]{2,1,0:T(8,128)S(1)}, u32[]{:S(2)}, u32[]{:S(2)}) collective-permute-start(s32[1,8,8192]{2,1,0:T(8,128)S(1)} %copy-done.23), channel_id=1, source_target_pairs={{0,96},{16,112},{32,0},{48,16},{64,32},{80,48},{96,64},{112,80},{1... | collective-permute-start | bytes 786440 | tf_op jit(solution)/shard_map/ppermute | solution.py:375
  75.4 3.9 %shard_map.74 = (f32[32,6144]{1,0:T(8,128)}, f32[32,6144]{1,0:T(8,128)}, f32[8,128]{1,0:T(8,128)S(1)}) custom-call(s32[2]{0:T(128)S(1)} %pad_add_fusion.here, bf16[64,131072]{1,0:T(8,128)(2,1)} %bitcast.63, bf16[64,131072]{1,0:T(8,128)(2,1)} %bitcast.64, bf16[64,131072]{1,0:T(8,128)(2,1)} %bitcast.65, bf16[64,131072]{1,0:T(8,128)(2,1)} %bitcast.66, ...), custom_call_target="tpu_custom_call" | custom-call | tf_op jit(solution)/shard_map/pallas_call | solution.py:108
  80.3 18.0 %collective-permute-done.6.refs_9_.refs_15_.refs_16_.refs_17_.refs_18_.refs_19_.refs_30_.refs_40_.refs_41_.refs_42_.refs_43_.refs_44_.refs_10_ = f32[32,10240]{1,0:T(8,128)} collective-permute-done((f32[32,10240]{1,0:T(8,128)S(1)}, f32[32,10240]{1,0:T(8,128)}, u32[]{:S(2)}, u32[]{:S(2)}) %collective-permute-start.6) | collective-permute-done | bytes 1310752 | tf_op jit(solution)/shard_map/ppermute | solution.py:371
  98.9 3.6 %collective-permute-start.20 = (s32[1,8,8192]{2,1,0:T(8,128)S(1)}, s32[1,8,8192]{2,1,0:T(8,128)S(1)}, u32[]{:S(2)}, u32[]{:S(2)}) collective-permute-start(s32[1,8,8192]{2,1,0:T(8,128)S(1)} %copy-done.23), channel_id=1, source_target_pairs={{0,64},{16,80},{32,96},{48,112},{64,0},{80,16},{96,32},{112,48},{1... | collective-permute-start | bytes 786440 | tf_op jit(solution)/shard_map/ppermute | solution.py:375
  102.5 3.9 %shard_map.75 = (f32[32,6144]{1,0:T(8,128)}, f32[32,6144]{1,0:T(8,128)}, f32[8,128]{1,0:T(8,128)S(1)}) custom-call(s32[2]{0:T(128)S(1)} %pad_add_fusion.here, bf16[64,131072]{1,0:T(8,128)(2,1)} %bitcast.69, bf16[64,131072]{1,0:T(8,128)(2,1)} %bitcast.70, bf16[64,131072]{1,0:T(8,128)(2,1)} %bitcast.71, bf16[64,131072]{1,0:T(8,128)(2,1)} %bitcast.72, ...), custom_call_target="tpu_custom_call" | custom-call | tf_op jit(solution)/shard_map/pallas_call | solution.py:108
  106.9 4.1 %shard_map.76 = (f32[32,8704]{1,0:T(8,128)S(1)}, f32[32,8704]{1,0:T(8,128)}, f32[8,128]{1,0:T(8,128)S(1)}) custom-call(s32[2]{0:T(128)S(1)} %pad_add_fusion.here, bf16[64,131072]{1,0:T(8,128)(2,1)} %bitcast.76, bf16[64,131072]{1,0:T(8,128)(2,1)} %bitcast.75, bf16[64,131072]{1,0:T(8,128)(2,1)} %bitcast.77, bf16[64,131072]{1,0:T(8,128)(2,1)} %bitcast.78, ...), custom_call_target="tpu_custom_call" | custom-call | tf_op jit(solution)/shard_map/pallas_call | solution.py:108
  111.1 4.6 %shard_map.77 = (f32[32,8704]{1,0:T(8,128)S(1)}, f32[32,8704]{1,0:T(8,128)}, f32[8,128]{1,0:T(8,128)S(1)}) custom-call(s32[2]{0:T(128)S(1)} %pad_add_fusion.here, bf16[64,131072]{1,0:T(8,128)(2,1)} %bitcast.81, bf16[64,131072]{1,0:T(8,128)(2,1)} %bitcast.82, bf16[64,131072]{1,0:T(8,128)(2,1)} %bitcast.83, ...), custom_call_target="tpu_custom_call", output_to_operand_aliasing={{0}: (26, {}), {1}: (27, {})} | custom-call | tf_op jit(solution)/shard_map/pallas_call | solution.py:108
  116.6 1.8 collective-permute-start.15
  118.4 2.2 collective-permute-start.19
  120.6 3.9 %shard_map.78 = (f32[32,8704]{1,0:T(8,128)}, f32[32,8704]{1,0:T(8,128)}, f32[8,128]{1,0:T(8,128)S(1)}) custom-call(s32[2]{0:T(128)S(1)} %pad_add_fusion.here, bf16[64,131072]{1,0:T(8,128)(2,1)} %bitcast.86, bf16[64,131072]{1,0:T(8,128)(2,1)} %bitcast.87, bf16[64,131072]{1,0:T(8,128)(2,1)} %bitcast.88, bf16[64,131072]{1,0:T(8,128)(2,1)} %bitcast.89, ...), custom_call_target="tpu_custom_call" | custom-call | tf_op jit(solution)/shard_map/pallas_call | solution.py:108
  124.5 4.6 %shard_map.79 = (f32[32,8704]{1,0:T(8,128)}, f32[32,8704]{1,0:T(8,128)}, f32[8,128]{1,0:T(8,128)S(1)}) custom-call(s32[2]{0:T(128)S(1)} %pad_add_fusion.here, bf16[64,131072]{1,0:T(8,128)(2,1)} %bitcast.92, bf16[64,131072]{1,0:T(8,128)(2,1)} %bitcast.93, bf16[64,131072]{1,0:T(8,128)(2,1)} %bitcast.94, ...), custom_call_target="tpu_custom_call", output_to_operand_aliasing={{0}: (26, {}), {1}: (27, {})} | custom-call | tf_op jit(solution)/shard_map/pallas_call | solution.py:108
  129.3 2.7 %collective-permute-start.24 = (f32[32,8704]{1,0:T(8,128)}, f32[32,8704]{1,0:T(8,128)S(1)}, u32[]{:S(2)}, u32[]{:S(2)}) collective-permute-start(f32[32,8704]{1,0:T(8,128)} %get-tuple-element.112), channel_id=1, source_target_pairs={{0,12},{1,13},{2,14},{3,15},{4,0},{5,1},{6,2},{7,3},{8,4},{9,5},{1... | collective-permute-start | bytes 3342344 | tf_op jit(solution)/shard_map/ppermute | solution.py:371
  132.5 4.3 %shard_map.80 = (f32[32,6144]{1,0:T(8,128)}, f32[32,6144]{1,0:T(8,128)}, f32[8,128]{1,0:T(8,128)S(1)}) custom-call(s32[2]{0:T(128)S(1)} %pad_add_fusion.here, bf16[64,131072]{1,0:T(8,128)(2,1)} %bitcast.97, bf16[64,131072]{1,0:T(8,128)(2,1)} %bitcast.98, bf16[64,131072]{1,0:T(8,128)(2,1)} %bitcast.99, bf16[64,131072]{1,0:T(8,128)(2,1)} %bitcast.100, ...), custom_call_target="tpu_custom_call" | custom-call | tf_op jit(solution)/shard_map/pallas_call | solution.py:108
  136.9 1.4 collective-permute-done.14.refs_61_.refs_50_.refs_51_.refs_52_.refs_53_.refs_54_.refs_3_.refs_4_.refs_5_.refs_18_.refs_19_.refs_20_.refs_1_
  138.2 1.3 collective-permute-start.22
  139.5 2.8 %shard_map.81 = (f32[32,6144]{1,0:T(8,128)S(1)}, f32[32,6144]{1,0:T(8,128)S(1)}, f32[8,128]{1,0:T(8,128)S(1)}) custom-call(s32[2]{0:T(128)S(1)} %pad_add_fusion.here, bf16[64,131072]{1,0:T(8,128)(2,1)} %bitcast.103, bf16[64,131072]{1,0:T(8,128)(2,1)} %bitcast.104, bf16[64,131072]{1,0:T(8,128)(2,1)} %bitcast.105, bf16[64,131072]{1,0:T(8,128)(2,1)} %bitcast.106, ...), custom_call_target="tpu_custom_call" | custom-call | tf_op jit(solution)/shard_map/pallas_call | solution.py:108
  143.2 8.0 %collective-permute-done.23.refs_50_.refs_51_.refs_52_.refs_53_.refs_54_.refs_63_.refs_3_.refs_4_.refs_5_.refs_18_.refs_19_.refs_20_.refs_8_ = f32[32,8704]{1,0:T(8,128)S(1)} collective-permute-done((f32[32,8704]{1,0:T(8,128)}, f32[32,8704]{1,0:T(8,128)S(1)}, u32[]{:S(2)}, u32[]{:S(2)}) %collective-permute-start.23) | collective-permute-done | bytes 1114144 | tf_op jit(solution)/shard_map/ppermute | solution.py:371
  151.2 5.5 %collective-permute-done.24.refs_55_.refs_56_.refs_57_.refs_58_.refs_59_.refs_64_.refs_6_.refs_7_.refs_8_.refs_21_.refs_22_.refs_23_.refs_9_ = f32[32,8704]{1,0:T(8,128)S(1)} collective-permute-done((f32[32,8704]{1,0:T(8,128)}, f32[32,8704]{1,0:T(8,128)S(1)}, u32[]{:S(2)}, u32[]{:S(2)}) %collective-permute-start.24) | collective-permute-done | bytes 1114144 | tf_op jit(solution)/shard_map/ppermute | solution.py:371
  156.7 3.4 %shard_map.82 = (f32[64,2560]{1,0:T(8,128)S(1)}, f32[64,2560]{1,0:T(8,128)}, f32[8,128]{1,0:T(8,128)S(1)}) custom-call(s32[2]{0:T(128)S(1)} %pad_add_fusion.here, bf16[64,131072]{1,0:T(8,128)(2,1)} %bitcast.113, bf16[64,131072]{1,0:T(8,128)(2,1)} %bitcast.110, bf16[64,131072]{1,0:T(8,128)(2,1)} %bitcast.111, bf16[64,131072]{1,0:T(8,128)(2,1)} %bitcast.112, ...), custom_call_target="tpu_custom_call" | custom-call | tf_op jit(solution)/shard_map/pallas_call | solution.py:108
  160.8 3.5 %shard_map.83 = (f32[64,2560]{1,0:T(8,128)S(1)}, f32[64,2560]{1,0:T(8,128)}, f32[8,128]{1,0:T(8,128)S(1)}) custom-call(s32[2]{0:T(128)S(1)} %pad_add_fusion.here, bf16[64,131072]{1,0:T(8,128)(2,1)} %bitcast.119, bf16[64,131072]{1,0:T(8,128)(2,1)} %bitcast.120, bf16[64,131072]{1,0:T(8,128)(2,1)} %bitcast.121, bf16[64,131072]{1,0:T(8,128)(2,1)} %bitcast.122, ...), custom_call_target="tpu_custom_call" | custom-call | tf_op jit(solution)/shard_map/pallas_call | solution.py:108
  164.3 3.0 %collective-permute-start.30 = (f32[64,2560]{1,0:T(8,128)}, f32[64,2560]{1,0:T(8,128)S(1)}, u32[]{:S(2)}, u32[]{:S(2)}) collective-permute-start(f32[64,2560]{1,0:T(8,128)} %get-tuple-element.122), channel_id=1, source_target_pairs={{0,12},{1,13},{2,14},{3,15},{4,0},{5,1},{6,2},{7,3},{8,4},{9,5},{1... | collective-permute-start | bytes 1966088 | tf_op jit(solution)/shard_map/ppermute | solution.py:371
  168.0 1.9 collective-permute-start.32
  170.0 3.5 %collective-permute-done.26.refs_19_.refs_12_.refs_13_.refs_14_.refs_27_.refs_28_.refs_29_.refs_11_ = f32[32,6144]{1,0:T(8,128)S(1)} collective-permute-done((f32[32,6144]{1,0:T(8,128)S(1)}, f32[32,6144]{1,0:T(8,128)S(1)}, u32[]{:S(2)}, u32[]{:S(2)}) %collective-permute-start.26) | collective-permute-done | bytes 786464 | tf_op jit(solution)/shard_map/ppermute | solution.py:371
  173.4 1.7 shard_map.84
  175.8 6.3 %collective-permute-done.29.refs_5_.refs_19_ = f32[64,2560]{1,0:T(8,128)S(1)} collective-permute-done((f32[64,2560]{1,0:T(8,128)S(1)}, f32[64,2560]{1,0:T(8,128)S(1)}, u32[]{:S(2)}, u32[]{:S(2)}) %collective-permute-start.29) | collective-permute-done | bytes 655392 | tf_op jit(solution)/shard_map/ppermute | solution.py:371
  182.1 1.8 shard_map.85
  183.9 3.7 %collective-permute-done.30.refs_6_.refs_20_ = f32[64,2560]{1,0:T(8,128)S(1)} collective-permute-done((f32[64,2560]{1,0:T(8,128)}, f32[64,2560]{1,0:T(8,128)S(1)}, u32[]{:S(2)}, u32[]{:S(2)}) %collective-permute-start.30) | collective-permute-done | bytes 655392 | tf_op jit(solution)/shard_map/ppermute | solution.py:371
  187.6 2.7 %collective-permute-start.34 = (f32[32,1536]{1,0:T(8,128)S(1)}, f32[32,1536]{1,0:T(8,128)S(1)}, u32[]{:S(2)}, u32[]{:S(2)}) collective-permute-start(f32[32,1536]{1,0:T(8,128)S(1)} %get-tuple-element.129), channel_id=1, source_target_pairs={{0,3},{1,0},{2,1},{3,2},{4,7},{5,4},{6,5},{7,6},{8,11},{9,8},{10,9... | collective-permute-start | bytes 589832 | tf_op jit(solution)/shard_map/ppermute | solution.py:371
  190.3 10.8 %shard_map.86 = (f32[1,64,8192]{2,1,0:T(8,128)}, f32[8,5120]{1,0:T(8,128)S(1)}, f32[8,128]{1,0:T(8,128)S(1)}) custom-call(s32[2]{0:T(128)S(1)} %pad_add_fusion.here, bf16[64,131072]{1,0:T(8,128)(2,1)} %bitcast.135, f32[32,10240]{1,0:T(8,128)S(1)} %copy-done.5, f32[32,10240]{1,0:T(8,128)S(1)} %copy-done.7, f32[32,10240]{1,0:T(8,128)} %copy-done, ...), custom_call_target="tpu_custom_call" | custom-call | tf_op jit(solution)/shard_map/pallas_call | solution.py:108
  201.1 3.1 %collective-permute-start.40 = (f32[8,5120]{1,0:T(8,128)S(1)}, f32[8,5120]{1,0:T(8,128)S(1)}, u32[]{:S(2)}, u32[]{:S(2)}) collective-permute-start(f32[8,5120]{1,0:T(8,128)S(1)} %get-tuple-element.136.refs_0_), channel_id=1, source_target_pairs={{0,96},{16,112},{32,0},{48,16},{64,32},{80,48},{96,64},{112,80},{1... | collective-permute-start | bytes 491528 | tf_op jit(solution)/shard_map/ppermute | solution.py:375
  204.3 2.0 shard_map.87
  206.3 1.7 shard_map.88
  208.1 1.5 collective-permute-done.39.refs_1_.refs_10_
  209.6 5.2 %shard_map.89 = (f32[64,5120]{1,0:T(8,128)S(1)}, f32[8,128]{1,0:T(8,128)S(1)}) custom-call(s32[2]{0:T(128)S(1)} %pad_add_fusion.here, f32[8,5120]{1,0:T(8,128)S(1)} %get-tuple-element.136.refs_0_, f32[8,5120]{1,0:T(8,128)S(1)} %collective-permute-done.39.refs_1_.refs_10_, f32[8,5120]{1,0:T(8,128)S(1)} %collective-permute-done.40.refs_2_.refs_11_, ...), custom_call_target="tpu_custom_call" | custom-call | tf_op jit(solution)/shard_map/pallas_call | solution.py:108
  214.8 10.3 %collective-permute-start.45 = (f32[64,5120]{1,0:T(8,128)S(1)}, f32[64,5120]{1,0:T(8,128)S(1)}, u32[]{:S(2)}, u32[]{:S(2)}) collective-permute-start(f32[64,5120]{1,0:T(8,128)S(1)} %get-tuple-element.140.refs_0_), channel_id=1, source_target_pairs={{0,16},{16,0},{32,48},{48,32},{64,80},{80,64},{96,112},{112,96},{1... | collective-permute-start | bytes 3932168 | tf_op jit(solution)/shard_map/ppermute | solution.py:381
  225.1 2.7 %collective-permute-start.38 = (f32[64,1536]{1,0:T(8,128)S(1)}, f32[64,1536]{1,0:T(8,128)S(1)}, u32[]{:S(2)}, u32[]{:S(2)}) collective-permute-start(f32[64,1536]{1,0:T(8,128)S(1)} %get-tuple-element.134), channel_id=1, source_target_pairs={{0,3},{1,0},{2,1},{3,2},{4,7},{5,4},{6,5},{7,6},{8,11},{9,8},{10,9... | collective-permute-start | bytes 1179656 | tf_op jit(solution)/shard_map/ppermute | solution.py:371
  228.7 2.5 collective-permute-start.36
  231.1 5.9 %collective-permute-done.37.refs_12_.refs_22_ = f32[64,1536]{1,0:T(8,128)S(1)} collective-permute-done((f32[64,1536]{1,0:T(8,128)S(1)}, f32[64,1536]{1,0:T(8,128)S(1)}, u32[]{:S(2)}, u32[]{:S(2)}) %collective-permute-start.37) | collective-permute-done | bytes 393248 | tf_op jit(solution)/shard_map/ppermute | solution.py:371
  237.0 3.0 %collective-permute-done.35.refs_5_.refs_20_ = f32[64,1536]{1,0:T(8,128)S(1)} collective-permute-done((f32[64,1536]{1,0:T(8,128)S(1)}, f32[64,1536]{1,0:T(8,128)S(1)}, u32[]{:S(2)}, u32[]{:S(2)}) %collective-permute-start.35) | collective-permute-done | bytes 393248 | tf_op jit(solution)/shard_map/ppermute | solution.py:371
  240.0 7.4 %shard_map.90 = (f32[1,64,8192]{2,1,0:T(8,128)}, f32[8,3072]{1,0:T(8,128)S(1)}, f32[8,128]{1,0:T(8,128)S(1)}) custom-call(s32[2]{0:T(128)S(1)} %pad_add_fusion.here, bf16[64,131072]{1,0:T(8,128)(2,1)} %bitcast.149, f32[32,8704]{1,0:T(8,128)} %copy-done.11, f32[32,8704]{1,0:T(8,128)} %copy-done.12, ...), custom_call_target="tpu_custom_call", output_to_operand_aliasing={{0}: (19, {})} | custom-call | tf_op jit(solution)/shard_map/pallas_call | solution.py:108
  248.9 4.1 %shard_map.91 = (f32[64,8192]{1,0:T(8,128)}, f32[8,128]{1,0:T(8,128)S(1)}) custom-call(s32[2]{0:T(128)S(1)} %pad_add_fusion.here, f32[64,5120]{1,0:T(8,128)S(1)} %get-tuple-element.140.refs_0_, f32[64,5120]{1,0:T(8,128)S(1)} %collective-permute-done.45.refs_1_.refs_3_, f32[8,128]{1,0:T(8,128)S(1)} %get-tuple-element.141.refs_2_, ...), custom_call_target="tpu_custom_call" | custom-call | tf_op jit(solution)/shard_map/pallas_call | solution.py:108
  254.2 3.3 %shard_map.92 = (f32[64,3072]{1,0:T(8,128)S(1)}, f32[8,128]{1,0:T(8,128)S(1)}) custom-call(s32[2]{0:T(128)S(1)} %pad_add_fusion.here, f32[8,3072]{1,0:T(8,128)S(1)} %get-tuple-element.139.refs_0_, f32[8,3072]{1,0:T(8,128)S(1)} %collective-permute-done.42.refs_1_.refs_10_, f32[8,3072]{1,0:T(8,128)S(1)} %collective-permute-done.43.refs_2_.refs_11_, ...), custom_call_target="tpu_custom_call" | custom-call | tf_op jit(solution)/shard_map/pallas_call | solution.py:108
  257.5 2.2 collective-permute-start.46
  259.8 1.9 collective-permute-done.46.refs_1_
  261.7 2.7 %shard_map.93 = (f32[64,8192]{1,0:T(8,128)}, f32[8,128]{1,0:T(8,128)}) custom-call(s32[2]{0:T(128)S(1)} %pad_add_fusion.here, f32[64,3072]{1,0:T(8,128)S(1)} %get-tuple-element.143.refs_0_, f32[64,3072]{1,0:T(8,128)S(1)} %collective-permute-done.46.refs_1_, f32[64,8192]{1,0:T(8,128)} %get-tuple-element.144.refs_2_, ...), custom_call_target="tpu_custom_call", output_to_operand_aliasing={{0}: (3, {})} | custom-call | tf_op jit(solution)/shard_map/pallas_call | solution.py:108
  (119 shorter events, 15.1 us)
Async XLA Ops:
  3.8 31.4 %collective-permute-start.4 = (f32[32,10240]{1,0:T(8,128)S(1)}, f32[32,10240]{1,0:T(8,128)S(1)}, u32[]{:S(2)}, u32[]{:S(2)}) collective-permute-start(f32[32,10240]{1,0:T(8,128)S(1)} %get-tuple-element.82), channel_id=1, source_target_pairs={{0,1},{1,2},{2,3},{3,0},{4,5},{5,6},{6,7},{7,4},{8,9},{9,10},{10,1... | collective-permute-start | bytes 3932168 | tf_op jit(solution)/shard_map/ppermute | solution.py:371
  6.0 35.2 %collective-permute-start.5 = (f32[32,10240]{1,0:T(8,128)S(1)}, f32[32,10240]{1,0:T(8,128)S(1)}, u32[]{:S(2)}, u32[]{:S(2)}) collective-permute-start(f32[32,10240]{1,0:T(8,128)S(1)} %get-tuple-element.83), channel_id=1, source_target_pairs={{0,3},{1,0},{2,1},{3,2},{4,7},{5,4},{6,5},{7,6},{8,11},{9,8},{10,9... | collective-permute-start | bytes 3932168 | tf_op jit(solution)/shard_map/ppermute | solution.py:371
  10.4 32.2 %collective-permute-start.2 = (f32[32,10240]{1,0:T(8,128)S(1)}, f32[32,10240]{1,0:T(8,128)S(1)}, u32[]{:S(2)}, u32[]{:S(2)}) collective-permute-start(f32[32,10240]{1,0:T(8,128)S(1)} %get-tuple-element.80), channel_id=1, source_target_pairs={{0,4},{1,5},{2,6},{3,7},{4,8},{5,9},{6,10},{7,11},{8,12},{9,13},{1... | collective-permute-start | bytes 3932168 | tf_op jit(solution)/shard_map/ppermute | solution.py:371
  11.9 32.2 %collective-permute-start.3 = (f32[32,10240]{1,0:T(8,128)S(1)}, f32[32,10240]{1,0:T(8,128)S(1)}, u32[]{:S(2)}, u32[]{:S(2)}) collective-permute-start(f32[32,10240]{1,0:T(8,128)S(1)} %get-tuple-element.81), channel_id=1, source_target_pairs={{0,12},{1,13},{2,14},{3,15},{4,0},{5,1},{6,2},{7,3},{8,4},{9,5},{1... | collective-permute-start | bytes 3932168 | tf_op jit(solution)/shard_map/ppermute | solution.py:371
  17.7 45.7 %collective-permute-start.8 = (f32[32,10240]{1,0:T(8,128)}, f32[32,10240]{1,0:T(8,128)S(1)}, u32[]{:S(2)}, u32[]{:S(2)}) collective-permute-start(f32[32,10240]{1,0:T(8,128)} %get-tuple-element.89), channel_id=1, source_target_pairs={{0,1},{1,2},{2,3},{3,0},{4,5},{5,6},{6,7},{7,4},{8,9},{9,10},{10,1... | collective-permute-start | bytes 3932168 | tf_op jit(solution)/shard_map/ppermute | solution.py:371
  35.3 10.6 %copy-start.15 = (f32[32,10240]{1,0:T(8,128)}, f32[32,10240]{1,0:T(8,128)S(1)}, u32[]{:S(2)}) copy-start(f32[32,10240]{1,0:T(8,128)S(1)} %collective-permute-done.4.refs_10_.refs_13_) | copy-start | bytes 3932164
  35.3 31.1 %collective-permute-start.9 = (f32[32,10240]{1,0:T(8,128)}, f32[32,10240]{1,0:T(8,128)S(1)}, u32[]{:S(2)}, u32[]{:S(2)}) collective-permute-start(f32[32,10240]{1,0:T(8,128)} %get-tuple-element.90), channel_id=1, source_target_pairs={{0,3},{1,0},{2,1},{3,2},{4,7},{5,4},{6,5},{7,6},{8,11},{9,8},{10,9... | collective-permute-start | bytes 3932168 | tf_op jit(solution)/shard_map/ppermute | solution.py:371
  41.2 8.8 %copy-start.16 = (f32[32,10240]{1,0:T(8,128)}, f32[32,10240]{1,0:T(8,128)S(1)}, u32[]{:S(2)}) copy-start(f32[32,10240]{1,0:T(8,128)S(1)} %collective-permute-done.5.refs_11_.refs_14_) | copy-start | bytes 3932164
  41.2 28.9 %collective-permute-start = (f32[32,10240]{1,0:T(8,128)}, f32[32,10240]{1,0:T(8,128)S(1)}, u32[]{:S(2)}, u32[]{:S(2)}) collective-permute-start(f32[32,10240]{1,0:T(8,128)} %get-tuple-element.78), channel_id=1, source_target_pairs={{0,4},{1,5},{2,6},{3,7},{4,8},{5,9},{6,10},{7,11},{8,12},{9,13},{1... | collective-permute-start | bytes 3932168 | tf_op jit(solution)/shard_map/ppermute | solution.py:371
  42.6 28.1 %collective-permute-start.1 = (f32[32,10240]{1,0:T(8,128)}, f32[32,10240]{1,0:T(8,128)S(1)}, u32[]{:S(2)}, u32[]{:S(2)}) collective-permute-start(f32[32,10240]{1,0:T(8,128)} %get-tuple-element.79), channel_id=1, source_target_pairs={{0,12},{1,13},{2,14},{3,15},{4,0},{5,1},{6,2},{7,3},{8,4},{9,5},{1... | collective-permute-start | bytes 3932168 | tf_op jit(solution)/shard_map/ppermute | solution.py:371
  44.1 13.7 %collective-permute-start.10 = (s32[1,8,8192]{2,1,0:T(8,128)S(1)}, s32[1,8,8192]{2,1,0:T(8,128)S(1)}, u32[]{:S(2)}, u32[]{:S(2)}) collective-permute-start(s32[1,8,8192]{2,1,0:T(8,128)S(1)} %copy-done.23), channel_id=1, source_target_pairs={{0,32},{16,48},{32,64},{48,80},{64,96},{80,112},{96,0},{112,16},{1... | collective-permute-start | bytes 786440 | tf_op jit(solution)/shard_map/ppermute | solution.py:375
  53.7 12.8 %copy-start.30 = (f32[32,10240]{1,0:T(8,128)S(1)}, f32[32,10240]{1,0:T(8,128)}, u32[]{:S(2)}) copy-start(f32[32,10240]{1,0:T(8,128)} %copy-done.29) | copy-start | bytes 3932164
  58.5 39.8 %collective-permute-start.6 = (f32[32,10240]{1,0:T(8,128)S(1)}, f32[32,10240]{1,0:T(8,128)}, u32[]{:S(2)}, u32[]{:S(2)}) collective-permute-start(f32[32,10240]{1,0:T(8,128)S(1)} %get-tuple-element.86), channel_id=1, source_target_pairs={{0,4},{1,5},{2,6},{3,7},{4,8},{5,9},{6,10},{7,11},{8,12},{9,13},{1... | collective-permute-start | bytes 3932168 | tf_op jit(solution)/shard_map/ppermute | solution.py:371
  63.4 61.1 %copy-start.4 = (f32[32,10240]{1,0:T(8,128)}, f32[32,10240]{1,0:T(8,128)S(1)}, u32[]{:S(2)}) copy-start(f32[32,10240]{1,0:T(8,128)S(1)} %collective-permute-done.8.refs_7_.refs_5_.refs_6_.refs_8_.refs_9_.refs_30_.refs_31_.refs_32_.refs_33_.refs_34_.refs_1_) | copy-start | bytes 3932164
  63.4 35.5 %collective-permute-start.7 = (f32[32,10240]{1,0:T(8,128)}, f32[32,10240]{1,0:T(8,128)}, u32[]{:S(2)}, u32[]{:S(2)}) collective-permute-start(f32[32,10240]{1,0:T(8,128)} %get-tuple-element.87), channel_id=1, source_target_pairs={{0,12},{1,13},{2,14},{3,15},{4,0},{5,1},{6,2},{7,3},{8,4},{9,5},{1... | collective-permute-start | bytes 3932168 | tf_op jit(solution)/shard_map/ppermute | solution.py:371
  66.4 58.1 %copy-start.6 = (f32[32,10240]{1,0:T(8,128)}, f32[32,10240]{1,0:T(8,128)S(1)}, u32[]{:S(2)}) copy-start(f32[32,10240]{1,0:T(8,128)S(1)} %collective-permute-done.9.refs_8_.refs_10_.refs_11_.refs_12_.refs_13_.refs_14_.refs_35_.refs_36_.refs_37_.refs_38_.refs_39_.refs_2_) | copy-start | bytes 3932164
  66.4 39.9 %collective-permute-start.11 = (f32[32,10240]{1,0:T(8,128)S(1)}, f32[32,10240]{1,0:T(8,128)S(1)}, u32[]{:S(2)}, u32[]{:S(2)}) collective-permute-start(f32[32,10240]{1,0:T(8,128)S(1)} %copy-done.30), channel_id=1, source_target_pairs={{0,1},{1,2},{2,3},{3,0},{4,5},{5,6},{6,7},{7,4},{8,9},{9,10},{10,1... | collective-permute-start | bytes 3932168 | tf_op jit(solution)/shard_map/ppermute | solution.py:371
  70.1 40.9 %copy-start.8 = (f32[32,10240]{1,0:T(8,128)}, f32[32,10240]{1,0:T(8,128)S(1)}, u32[]{:S(2)}) copy-start(f32[32,10240]{1,0:T(8,128)S(1)} %collective-permute-done.refs_9_.refs_5_.refs_6_.refs_7_.refs_8_.refs_30_.refs_31_.refs_32_.refs_33_.refs_34_) | copy-start | bytes 3932164
  70.1 36.7 %collective-permute-start.12 = (f32[32,10240]{1,0:T(8,128)}, f32[32,10240]{1,0:T(8,128)S(1)}, u32[]{:S(2)}, u32[]{:S(2)}) collective-permute-start(f32[32,10240]{1,0:T(8,128)} %get-tuple-element.94), channel_id=1, source_target_pairs={{0,3},{1,0},{2,1},{3,2},{4,7},{5,4},{6,5},{7,6},{8,11},{9,8},{10,9... | collective-permute-start | bytes 3932168 | tf_op jit(solution)/shard_map/ppermute | solution.py:371
  70.7 8.6 %collective-permute-start.13 = (s32[1,8,8192]{2,1,0:T(8,128)S(1)}, s32[1,8,8192]{2,1,0:T(8,128)S(1)}, u32[]{:S(2)}, u32[]{:S(2)}) collective-permute-start(s32[1,8,8192]{2,1,0:T(8,128)S(1)} %copy-done.23), channel_id=1, source_target_pairs={{0,96},{16,112},{32,0},{48,16},{64,32},{80,48},{96,64},{112,80},{1... | collective-permute-start | bytes 786440 | tf_op jit(solution)/shard_map/ppermute | solution.py:375
  79.3 45.2 %copy-start.21 = (s32[1,8,8192]{2,1,0:T(8,128)}, s32[1,8,8192]{2,1,0:T(8,128)S(1)}, u32[]{:S(2)}) copy-start(s32[1,8,8192]{2,1,0:T(8,128)S(1)} %collective-permute-done.13.refs_11_.refs_32_.refs_6_) | copy-start | bytes 786436
  79.3 39.1 %collective-permute-start.16 = (f32[32,6144]{1,0:T(8,128)}, f32[32,6144]{1,0:T(8,128)S(1)}, u32[]{:S(2)}, u32[]{:S(2)}) collective-permute-start(f32[32,6144]{1,0:T(8,128)} %get-tuple-element.100), channel_id=1, source_target_pairs={{0,1},{1,2},{2,3},{3,0},{4,5},{5,6},{6,7},{7,4},{8,9},{9,10},{10,1... | collective-permute-start | bytes 2359304 | tf_op jit(solution)/shard_map/ppermute | solution.py:371
  98.3 30.8 %collective-permute-start.17 = (f32[32,6144]{1,0:T(8,128)}, f32[32,6144]{1,0:T(8,128)}, u32[]{:S(2)}, u32[]{:S(2)}) collective-permute-start(f32[32,6144]{1,0:T(8,128)} %get-tuple-element.101), channel_id=1, source_target_pairs={{0,3},{1,0},{2,1},{3,2},{4,7},{5,4},{6,5},{7,6},{8,11},{9,8},{10,9... | collective-permute-start | bytes 2359304 | tf_op jit(solution)/shard_map/ppermute | solution.py:371
  98.9 17.7 %collective-permute-start.20 = (s32[1,8,8192]{2,1,0:T(8,128)S(1)}, s32[1,8,8192]{2,1,0:T(8,128)S(1)}, u32[]{:S(2)}, u32[]{:S(2)}) collective-permute-start(s32[1,8,8192]{2,1,0:T(8,128)S(1)} %copy-done.23), channel_id=1, source_target_pairs={{0,64},{16,80},{32,96},{48,112},{64,0},{80,16},{96,32},{112,48},{1... | collective-permute-start | bytes 786440 | tf_op jit(solution)/shard_map/ppermute | solution.py:375
  106.4 22.9 %collective-permute-start.18 = (f32[32,6144]{1,0:T(8,128)}, f32[32,6144]{1,0:T(8,128)S(1)}, u32[]{:S(2)}, u32[]{:S(2)}) collective-permute-start(f32[32,6144]{1,0:T(8,128)} %get-tuple-element.107), channel_id=1, source_target_pairs={{0,4},{1,5},{2,6},{3,7},{4,8},{5,9},{6,10},{7,11},{8,12},{9,13},{1... | collective-permute-start | bytes 2359304 | tf_op jit(solution)/shard_map/ppermute | solution.py:371
  111.1 9.6 %copy-start.1 = (f32[32,10240]{1,0:T(8,128)S(1)}, f32[32,10240]{1,0:T(8,128)}, u32[]{:S(2)}) copy-start(f32[32,10240]{1,0:T(8,128)} %copy-done) | copy-start | bytes 3932164
  111.1 9.6 %copy-start.3 = (f32[32,10240]{1,0:T(8,128)S(1)}, f32[32,10240]{1,0:T(8,128)}, u32[]{:S(2)}) copy-start(f32[32,10240]{1,0:T(8,128)} %copy-done.2) | copy-start | bytes 3932164
  115.7 22.5 %collective-permute-start.14 = (f32[32,8704]{1,0:T(8,128)S(1)}, f32[32,8704]{1,0:T(8,128)S(1)}, u32[]{:S(2)}, u32[]{:S(2)}) collective-permute-start(f32[32,8704]{1,0:T(8,128)S(1)} %get-tuple-element.98), channel_id=1, source_target_pairs={{0,1},{1,2},{2,3},{3,0},{4,5},{5,6},{6,7},{7,4},{8,9},{9,10},{10,1... | collective-permute-start | bytes 3342344 | tf_op jit(solution)/shard_map/ppermute | solution.py:371
  116.6 25.8 %collective-permute-start.15 = (f32[32,8704]{1,0:T(8,128)}, f32[32,8704]{1,0:T(8,128)S(1)}, u32[]{:S(2)}, u32[]{:S(2)}) collective-permute-start(f32[32,8704]{1,0:T(8,128)} %get-tuple-element.99), channel_id=1, source_target_pairs={{0,3},{1,0},{2,1},{3,2},{4,7},{5,4},{6,5},{7,6},{8,11},{9,8},{10,9... | collective-permute-start | bytes 3342344 | tf_op jit(solution)/shard_map/ppermute | solution.py:371
  118.4 14.2 %collective-permute-start.19 = (f32[32,6144]{1,0:T(8,128)}, f32[32,6144]{1,0:T(8,128)S(1)}, u32[]{:S(2)}, u32[]{:S(2)}) collective-permute-start(f32[32,6144]{1,0:T(8,128)} %get-tuple-element.108), channel_id=1, source_target_pairs={{0,12},{1,13},{2,14},{3,15},{4,0},{5,1},{6,2},{7,3},{8,4},{9,5},{1... | collective-permute-start | bytes 2359304 | tf_op jit(solution)/shard_map/ppermute | solution.py:371
  129.2 22.0 %collective-permute-start.23 = (f32[32,8704]{1,0:T(8,128)}, f32[32,8704]{1,0:T(8,128)S(1)}, u32[]{:S(2)}, u32[]{:S(2)}) collective-permute-start(f32[32,8704]{1,0:T(8,128)} %get-tuple-element.111), channel_id=1, source_target_pairs={{0,4},{1,5},{2,6},{3,7},{4,8},{5,9},{6,10},{7,11},{8,12},{9,13},{1... | collective-permute-start | bytes 3342344 | tf_op jit(solution)/shard_map/ppermute | solution.py:371
  129.3 27.4 %collective-permute-start.24 = (f32[32,8704]{1,0:T(8,128)}, f32[32,8704]{1,0:T(8,128)S(1)}, u32[]{:S(2)}, u32[]{:S(2)}) collective-permute-start(f32[32,8704]{1,0:T(8,128)} %get-tuple-element.112), channel_id=1, source_target_pairs={{0,12},{1,13},{2,14},{3,15},{4,0},{5,1},{6,2},{7,3},{8,4},{9,5},{1... | collective-permute-start | bytes 3342344 | tf_op jit(solution)/shard_map/ppermute | solution.py:371
  136.9 27.5 %collective-permute-start.21 = (f32[32,6144]{1,0:T(8,128)}, f32[32,6144]{1,0:T(8,128)}, u32[]{:S(2)}, u32[]{:S(2)}) collective-permute-start(f32[32,6144]{1,0:T(8,128)} %get-tuple-element.109), channel_id=1, source_target_pairs={{0,1},{1,2},{2,3},{3,0},{4,5},{5,6},{6,7},{7,4},{8,9},{9,10},{10,1... | collective-permute-start | bytes 2359304 | tf_op jit(solution)/shard_map/ppermute | solution.py:371
  138.2 66.0 %copy-start.11 = (f32[32,8704]{1,0:T(8,128)}, f32[32,8704]{1,0:T(8,128)S(1)}, u32[]{:S(2)}) copy-start(f32[32,8704]{1,0:T(8,128)S(1)} %collective-permute-done.14.refs_61_.refs_50_.refs_51_.refs_52_.refs_53_.refs_54_.refs_3_.refs_4_.refs_5_.refs_18_.refs_19_.refs_20_.refs_1_) | copy-start | bytes 3342340
  138.2 29.1 %collective-permute-start.22 = (f32[32,6144]{1,0:T(8,128)}, f32[32,6144]{1,0:T(8,128)}, u32[]{:S(2)}, u32[]{:S(2)}) collective-permute-start(f32[32,6144]{1,0:T(8,128)} %get-tuple-element.110), channel_id=1, source_target_pairs={{0,3},{1,0},{2,1},{3,2},{4,7},{5,4},{6,5},{7,6},{8,11},{9,8},{10,9... | collective-permute-start | bytes 2359304 | tf_op jit(solution)/shard_map/ppermute | solution.py:371
  142.3 61.9 %copy-start.12 = (f32[32,8704]{1,0:T(8,128)}, f32[32,8704]{1,0:T(8,128)S(1)}, u32[]{:S(2)}) copy-start(f32[32,8704]{1,0:T(8,128)S(1)} %collective-permute-done.15.refs_62_.refs_55_.refs_56_.refs_57_.refs_58_.refs_59_.refs_6_.refs_7_.refs_8_.refs_21_.refs_22_.refs_23_.refs_2_) | copy-start | bytes 3342340
  142.3 25.7 %collective-permute-start.25 = (f32[32,6144]{1,0:T(8,128)S(1)}, f32[32,6144]{1,0:T(8,128)S(1)}, u32[]{:S(2)}, u32[]{:S(2)}) collective-permute-start(f32[32,6144]{1,0:T(8,128)S(1)} %get-tuple-element.117), channel_id=1, source_target_pairs={{0,4},{1,5},{2,6},{3,7},{4,8},{5,9},{6,10},{7,11},{8,12},{9,13},{1... | collective-permute-start | bytes 2359304 | tf_op jit(solution)/shard_map/ppermute | solution.py:371
  151.2 55.1 %copy-start.13 = (f32[32,8704]{1,0:T(8,128)}, f32[32,8704]{1,0:T(8,128)S(1)}, u32[]{:S(2)}) copy-start(f32[32,8704]{1,0:T(8,128)S(1)} %collective-permute-done.23.refs_50_.refs_51_.refs_52_.refs_53_.refs_54_.refs_63_.refs_3_.refs_4_.refs_5_.refs_18_.refs_19_.refs_20_.refs_8_) | copy-start | bytes 3342340
  151.2 22.2 %collective-permute-start.26 = (f32[32,6144]{1,0:T(8,128)S(1)}, f32[32,6144]{1,0:T(8,128)S(1)}, u32[]{:S(2)}, u32[]{:S(2)}) collective-permute-start(f32[32,6144]{1,0:T(8,128)S(1)} %get-tuple-element.118), channel_id=1, source_target_pairs={{0,12},{1,13},{2,14},{3,15},{4,0},{5,1},{6,2},{7,3},{8,4},{9,5},{1... | collective-permute-start | bytes 2359304 | tf_op jit(solution)/shard_map/ppermute | solution.py:371
  156.7 49.6 %copy-start.14 = (f32[32,8704]{1,0:T(8,128)}, f32[32,8704]{1,0:T(8,128)S(1)}, u32[]{:S(2)}) copy-start(f32[32,8704]{1,0:T(8,128)S(1)} %collective-permute-done.24.refs_55_.refs_56_.refs_57_.refs_58_.refs_59_.refs_64_.refs_6_.refs_7_.refs_8_.refs_21_.refs_22_.refs_23_.refs_9_) | copy-start | bytes 3342340
  160.1 22.0 %collective-permute-start.29 = (f32[64,2560]{1,0:T(8,128)S(1)}, f32[64,2560]{1,0:T(8,128)S(1)}, u32[]{:S(2)}, u32[]{:S(2)}) collective-permute-start(f32[64,2560]{1,0:T(8,128)S(1)} %get-tuple-element.121), channel_id=1, source_target_pairs={{0,4},{1,5},{2,6},{3,7},{4,8},{5,9},{6,10},{7,11},{8,12},{9,13},{1... | collective-permute-start | bytes 1966088 | tf_op jit(solution)/shard_map/ppermute | solution.py:371
  164.3 23.3 %collective-permute-start.30 = (f32[64,2560]{1,0:T(8,128)}, f32[64,2560]{1,0:T(8,128)S(1)}, u32[]{:S(2)}, u32[]{:S(2)}) collective-permute-start(f32[64,2560]{1,0:T(8,128)} %get-tuple-element.122), channel_id=1, source_target_pairs={{0,12},{1,13},{2,14},{3,15},{4,0},{5,1},{6,2},{7,3},{8,4},{9,5},{1... | collective-permute-start | bytes 1966088 | tf_op jit(solution)/shard_map/ppermute | solution.py:371
  167.3 20.3 %collective-permute-start.31 = (f32[64,2560]{1,0:T(8,128)S(1)}, f32[64,2560]{1,0:T(8,128)S(1)}, u32[]{:S(2)}, u32[]{:S(2)}) collective-permute-start(f32[64,2560]{1,0:T(8,128)S(1)} %get-tuple-element.123), channel_id=1, source_target_pairs={{0,1},{1,2},{2,3},{3,0},{4,5},{5,6},{6,7},{7,4},{8,9},{9,10},{10,1... | collective-permute-start | bytes 1966088 | tf_op jit(solution)/shard_map/ppermute | solution.py:371
  168.0 22.2 %collective-permute-start.32 = (f32[64,2560]{1,0:T(8,128)}, f32[64,2560]{1,0:T(8,128)S(1)}, u32[]{:S(2)}, u32[]{:S(2)}) collective-permute-start(f32[64,2560]{1,0:T(8,128)} %get-tuple-element.124), channel_id=1, source_target_pairs={{0,3},{1,0},{2,1},{3,2},{4,7},{5,4},{6,5},{7,6},{8,11},{9,8},{10,9... | collective-permute-start | bytes 1966088 | tf_op jit(solution)/shard_map/ppermute | solution.py:371
  175.1 25.9 %collective-permute-start.27 = (f32[32,1536]{1,0:T(8,128)S(1)}, f32[32,1536]{1,0:T(8,128)S(1)}, u32[]{:S(2)}, u32[]{:S(2)}) collective-permute-start(f32[32,1536]{1,0:T(8,128)S(1)} %get-tuple-element.119), channel_id=1, source_target_pairs={{0,4},{1,5},{2,6},{3,7},{4,8},{5,9},{6,10},{7,11},{8,12},{9,13},{1... | collective-permute-start | bytes 589832 | tf_op jit(solution)/shard_map/ppermute | solution.py:371
  182.1 22.1 %collective-permute-start.28 = (f32[32,1536]{1,0:T(8,128)S(1)}, f32[32,1536]{1,0:T(8,128)S(1)}, u32[]{:S(2)}, u32[]{:S(2)}) collective-permute-start(f32[32,1536]{1,0:T(8,128)S(1)} %get-tuple-element.120), channel_id=1, source_target_pairs={{0,12},{1,13},{2,14},{3,15},{4,0},{5,1},{6,2},{7,3},{8,4},{9,5},{1... | collective-permute-start | bytes 589832 | tf_op jit(solution)/shard_map/ppermute | solution.py:371
  182.1 8.2 %copy-start.5 = (f32[32,10240]{1,0:T(8,128)S(1)}, f32[32,10240]{1,0:T(8,128)}, u32[]{:S(2)}) copy-start(f32[32,10240]{1,0:T(8,128)} %copy-done.4) | copy-start | bytes 3932164
  182.1 8.2 %copy-start.7 = (f32[32,10240]{1,0:T(8,128)S(1)}, f32[32,10240]{1,0:T(8,128)}, u32[]{:S(2)}) copy-start(f32[32,10240]{1,0:T(8,128)} %copy-done.6) | copy-start | bytes 3932164
  182.1 8.2 %copy-start.27 = (bf16[64,256]{1,0:T(8,128)(2,1)S(1)}, bf16[64,256]{1,0:T(8,128)(2,1)}, u32[]{:S(2)}) copy-start(bf16[64,256]{1,0:T(8,128)(2,1)} %constant.25.clone.refs_17_.refs_8_) | copy-start | bytes 98308
  182.1 8.2 %copy-start.28 = (bf16[64,256]{1,0:T(8,128)(2,1)S(1)}, bf16[64,256]{1,0:T(8,128)(2,1)}, u32[]{:S(2)}) copy-start(bf16[64,256]{1,0:T(8,128)(2,1)} %constant.24.clone.refs_16_) | copy-start | bytes 98308
  187.6 16.6 %collective-permute-start.33 = (f32[32,1536]{1,0:T(8,128)S(1)}, f32[32,1536]{1,0:T(8,128)S(1)}, u32[]{:S(2)}, u32[]{:S(2)}) collective-permute-start(f32[32,1536]{1,0:T(8,128)S(1)} %get-tuple-element.128), channel_id=1, source_target_pairs={{0,1},{1,2},{2,3},{3,0},{4,5},{5,6},{6,7},{7,4},{8,9},{9,10},{10,1... | collective-permute-start | bytes 589832 | tf_op jit(solution)/shard_map/ppermute | solution.py:371
  187.6 16.6 %collective-permute-start.34 = (f32[32,1536]{1,0:T(8,128)S(1)}, f32[32,1536]{1,0:T(8,128)S(1)}, u32[]{:S(2)}, u32[]{:S(2)}) collective-permute-start(f32[32,1536]{1,0:T(8,128)S(1)} %get-tuple-element.129), channel_id=1, source_target_pairs={{0,3},{1,0},{2,1},{3,2},{4,7},{5,4},{6,5},{7,6},{8,11},{9,8},{10,9... | collective-permute-start | bytes 589832 | tf_op jit(solution)/shard_map/ppermute | solution.py:371
  201.1 7.0 %collective-permute-start.41 = (f32[8,5120]{1,0:T(8,128)S(1)}, f32[8,5120]{1,0:T(8,128)S(1)}, u32[]{:S(2)}, u32[]{:S(2)}) collective-permute-start(f32[8,5120]{1,0:T(8,128)S(1)} %get-tuple-element.136.refs_0_), channel_id=1, source_target_pairs={{0,64},{16,80},{32,96},{48,112},{64,0},{80,16},{96,32},{112,48},{1... | collective-permute-start | bytes 491528 | tf_op jit(solution)/shard_map/ppermute | solution.py:375
  201.1 7.0 %collective-permute-start.40 = (f32[8,5120]{1,0:T(8,128)S(1)}, f32[8,5120]{1,0:T(8,128)S(1)}, u32[]{:S(2)}, u32[]{:S(2)}) collective-permute-start(f32[8,5120]{1,0:T(8,128)S(1)} %get-tuple-element.136.refs_0_), channel_id=1, source_target_pairs={{0,96},{16,112},{32,0},{48,16},{64,32},{80,48},{96,64},{112,80},{1... | collective-permute-start | bytes 491528 | tf_op jit(solution)/shard_map/ppermute | solution.py:375
  204.2 5.4 %collective-permute-start.39 = (f32[8,5120]{1,0:T(8,128)S(1)}, f32[8,5120]{1,0:T(8,128)S(1)}, u32[]{:S(2)}, u32[]{:S(2)}) collective-permute-start(f32[8,5120]{1,0:T(8,128)S(1)} %get-tuple-element.136.refs_0_), channel_id=1, source_target_pairs={{0,32},{16,48},{32,64},{48,80},{64,96},{80,112},{96,0},{112,16},{1... | collective-permute-start | bytes 491528 | tf_op jit(solution)/shard_map/ppermute | solution.py:375
  214.8 34.1 %collective-permute-start.45 = (f32[64,5120]{1,0:T(8,128)S(1)}, f32[64,5120]{1,0:T(8,128)S(1)}, u32[]{:S(2)}, u32[]{:S(2)}) collective-permute-start(f32[64,5120]{1,0:T(8,128)S(1)} %get-tuple-element.140.refs_0_), channel_id=1, source_target_pairs={{0,16},{16,0},{32,48},{48,32},{64,80},{80,64},{96,112},{112,96},{1... | collective-permute-start | bytes 3932168 | tf_op jit(solution)/shard_map/ppermute | solution.py:381
  225.1 11.9 %collective-permute-start.37 = (f32[64,1536]{1,0:T(8,128)S(1)}, f32[64,1536]{1,0:T(8,128)S(1)}, u32[]{:S(2)}, u32[]{:S(2)}) collective-permute-start(f32[64,1536]{1,0:T(8,128)S(1)} %get-tuple-element.133), channel_id=1, source_target_pairs={{0,1},{1,2},{2,3},{3,0},{4,5},{5,6},{6,7},{7,4},{8,9},{9,10},{10,1... | collective-permute-start | bytes 1179656 | tf_op jit(solution)/shard_map/ppermute | solution.py:371
  225.1 11.9 %collective-permute-start.38 = (f32[64,1536]{1,0:T(8,128)S(1)}, f32[64,1536]{1,0:T(8,128)S(1)}, u32[]{:S(2)}, u32[]{:S(2)}) collective-permute-start(f32[64,1536]{1,0:T(8,128)S(1)} %get-tuple-element.134), channel_id=1, source_target_pairs={{0,3},{1,0},{2,1},{3,2},{4,7},{5,4},{6,5},{7,6},{8,11},{9,8},{10,9... | collective-permute-start | bytes 1179656 | tf_op jit(solution)/shard_map/ppermute | solution.py:371
  227.8 12.2 %collective-permute-start.35 = (f32[64,1536]{1,0:T(8,128)S(1)}, f32[64,1536]{1,0:T(8,128)S(1)}, u32[]{:S(2)}, u32[]{:S(2)}) collective-permute-start(f32[64,1536]{1,0:T(8,128)S(1)} %get-tuple-element.130), channel_id=1, source_target_pairs={{0,4},{1,5},{2,6},{3,7},{4,8},{5,9},{6,10},{7,11},{8,12},{9,13},{1... | collective-permute-start | bytes 1179656 | tf_op jit(solution)/shard_map/ppermute | solution.py:371
  228.7 11.3 %collective-permute-start.36 = (f32[64,1536]{1,0:T(8,128)S(1)}, f32[64,1536]{1,0:T(8,128)S(1)}, u32[]{:S(2)}, u32[]{:S(2)}) collective-permute-start(f32[64,1536]{1,0:T(8,128)S(1)} %get-tuple-element.131), channel_id=1, source_target_pairs={{0,12},{1,13},{2,14},{3,15},{4,0},{5,1},{6,2},{7,3},{8,4},{9,5},{1... | collective-permute-start | bytes 1179656 | tf_op jit(solution)/shard_map/ppermute | solution.py:371
  247.4 5.6 %collective-permute-start.44 = (f32[8,3072]{1,0:T(8,128)S(1)}, f32[8,3072]{1,0:T(8,128)S(1)}, u32[]{:S(2)}, u32[]{:S(2)}) collective-permute-start(f32[8,3072]{1,0:T(8,128)S(1)} %get-tuple-element.139.refs_0_), channel_id=1, source_target_pairs={{0,64},{16,80},{32,96},{48,112},{64,0},{80,16},{96,32},{112,48},{1... | collective-permute-start | bytes 294920 | tf_op jit(solution)/shard_map/ppermute | solution.py:375
  247.4 5.6 %collective-permute-start.43 = (f32[8,3072]{1,0:T(8,128)S(1)}, f32[8,3072]{1,0:T(8,128)S(1)}, u32[]{:S(2)}, u32[]{:S(2)}) collective-permute-start(f32[8,3072]{1,0:T(8,128)S(1)} %get-tuple-element.139.refs_0_), channel_id=1, source_target_pairs={{0,96},{16,112},{32,0},{48,16},{64,32},{80,48},{96,64},{112,80},{1... | collective-permute-start | bytes 294920 | tf_op jit(solution)/shard_map/ppermute | solution.py:375
  248.3 5.9 %collective-permute-start.42 = (f32[8,3072]{1,0:T(8,128)S(1)}, f32[8,3072]{1,0:T(8,128)S(1)}, u32[]{:S(2)}, u32[]{:S(2)}) collective-permute-start(f32[8,3072]{1,0:T(8,128)S(1)} %get-tuple-element.139.refs_0_), channel_id=1, source_target_pairs={{0,32},{16,48},{32,64},{48,80},{64,96},{80,112},{96,0},{112,16},{1... | collective-permute-start | bytes 294920 | tf_op jit(solution)/shard_map/ppermute | solution.py:375
  257.5 4.2 %collective-permute-start.46 = (f32[64,3072]{1,0:T(8,128)S(1)}, f32[64,3072]{1,0:T(8,128)S(1)}, u32[]{:S(2)}, u32[]{:S(2)}) collective-permute-start(f32[64,3072]{1,0:T(8,128)S(1)} %get-tuple-element.143.refs_0_), channel_id=1, source_target_pairs={{0,16},{16,0},{32,48},{48,32},{64,80},{80,64},{96,112},{112,96},{1... | collective-permute-start | bytes 2359304 | tf_op jit(solution)/shard_map/ppermute | solution.py:381
  (14 other events, 40.9 us)

commit v3 on v2

--- a/solution.py
+++ b/solution.py
@@ -12,9 +12,10 @@
 KEEP = 8
 SIDE = 4
 TILE = 512
-PIECES = {"a": (0, 2560), "b": (5120, 1536)}
-ORDER = "a1 a2 a3 b1 b2a b3 a5 b4 a6 b5 a7 b6 a8 b7 b8"
-PLACES_WITH = ("a2", "a3", "b1")
+WIDTH = 2048
+CHUNKS = (2048, 2048)
+EARLY = False
+MOVED = 0
 VMEM_LIMIT = 48 * 1024 * 1024
 F32 = jnp.float32
 BF16 = jnp.bfloat16
@@ -116,7 +117,7 @@
             out_shape=(*out_shape, jax.ShapeDtypeStruct((8, 128), F32)),
             input_output_aliases=aliases or {},
             compiler_params=pltpu.CompilerParams(vmem_limit_bytes=VMEM_LIMIT),
-            cost_estimate=pl.CostEstimate(flops=0, bytes_accessed=0, transcendentals=0),
+            cost_estimate=pl.CostEstimate(flops=0, bytes_accessed=MOVED, transcendentals=0),
         )(self.here, *ins)
         return outs
 
@@ -130,7 +131,7 @@
     return [refs[k : k + n] for k in range(0, len(refs), n)]
 
 
-def send_part(line, half, partials, up_from, down_from, extra):
+def send_part(line, half, partials, up_from, down_from):
     w, n = half.width, half.count
 
     def body(here, *refs):
@@ -139,7 +140,7 @@
             up[:, col] = part_up[...].astype(F32)
             down[:, col] = part_down[...].astype(F32)
 
-    shape = jax.ShapeDtypeStruct((HALF, SIDE * w + extra), F32)
+    shape = jax.ShapeDtypeStruct((HALF, SIDE * w), F32)
     spec = pl.BlockSpec((HALF, w), lambda i, here: (0, i))
     return line.call(
         body, SIDE, [partials] * (2 * n), half.grid_blocks(*up_from) + half.grid_blocks(*down_from),
@@ -148,11 +149,11 @@
 
 
 def send_far(line, half, partials):
-    return send_part(line, half, partials, (2, 0), (2, 1), 0)
-
-
-def send_raw(line, half, partials, extra):
-    return send_part(line, half, partials, (1, 1), (-1, 0), extra)
+    return send_part(line, half, partials, (2, 0), (2, 1))
+
+
+def send_raw(line, half, partials):
+    return send_part(line, half, partials, (1, 1), (-1, 0))
 
 
 def send_near(line, half, partials, far_up, far_down):
@@ -183,7 +184,7 @@
     return high, low
 
 
-def send_far2(line, half, partials, got, into=None, first=0):
+def send_far2(line, half, partials, got):
     w, n = half.width, half.count
 
     def body(here, *refs):
@@ -191,29 +192,14 @@
         for col, blocks in tiles(n, *groups(refs[: 5 * n], n)):
             up[:, col], down[:, col] = high_low(*blocks)
 
-    ins = [partials] * n + repeat(got, n)
-    specs = half.one_blocks(2) + half.message_blocks(2) * 4
     shape = jax.ShapeDtypeStruct((HALF, w), F32)
-    if into is None:
-        return line.call(body, 1, ins, specs, (shape, shape), (whole(HALF, w), whole(HALF, w)))
-
-    def by_tile(here, *refs):
-        up, down = refs[-2:]
-        for tile in range(n):
-
-            @pl.when(pl.program_id(0) == tile)
-            def _():
-                up[...], down[...] = high_low(*(group[tile] for group in groups(refs[: 5 * n], n)))
-
-    shape = jax.ShapeDtypeStruct(into[0].shape, F32)
-    spec = pl.BlockSpec((HALF, TILE), lambda i, here: (0, first + i))
-    return line.call(
-        by_tile, n, ins + [*into], specs + [pl.BlockSpec(memory_space=pl.ANY)] * 2,
-        (shape, shape), (spec, spec), aliases={len(ins) + 1: 0, len(ins) + 2: 1},
-    )
-
-
-def send_near2(line, half, partials, got, far, first=0):
+    return line.call(
+        body, 1, [partials] * n + repeat(got, n), half.one_blocks(2) + half.message_blocks(2) * 4,
+        (shape, shape), (whole(HALF, w), whole(HALF, w)),
+    )
+
+
+def send_near2(line, half, partials, got, far):
     w, n = half.width, half.count
 
     def body(here, *refs):
@@ -227,7 +213,7 @@
             down[HALF:, col] = low + blocks[11][...]
 
     def far_spec(tile):
-        return pl.BlockSpec((HALF, TILE), lambda i, here: (0, first + tile))
+        return pl.BlockSpec((HALF, TILE), lambda i, here: (0, tile))
 
     shape = jax.ShapeDtypeStruct((BLOCK, w), F32)
     return line.call(
@@ -245,6 +231,21 @@
     return jnp.dot(
         parts[...], jnp.concatenate([high, low, high, low], axis=0), preferred_element_type=F32
     )
+
+
+def settle(grad, momentum, positions, forward, backward, fresh, values):
+    freq = lax.broadcasted_iota(jnp.int32, grad.shape, 0)
+    moment = 0.9 * momentum[0] + grad
+    coeff = product(forward, moment)
+    chosen = positions[0]
+    own = jnp.zeros_like(coeff)
+    rows = []
+    for place in range(KEEP):
+        hit = jnp.where(chosen[place : place + 1] == freq, coeff, 0.0)
+        rows.append(jnp.sum(hit, axis=0, keepdims=True))
+        own = own + hit
+    values[...] = jnp.concatenate(rows, axis=0)
+    fresh[0] = moment - product(backward, own)
 
 
 def finish(line, pair, partials, momentum, positions, got, tables, so_far):
@@ -280,31 +281,19 @@
 
     def body(here, *refs):
         momentum, positions, forward, backward = refs[14:18]
-        fresh, values = refs[-2:]
-        freq = lax.broadcasted_iota(jnp.int32, (BLOCK, TILE), 0)
-
-        def settle(part, raw_up, raw_down, near_up, near_down, left2, right2):
+
+        def half(part, raw_up, raw_down, near_up, near_down, left2, right2):
             grad = jnp.concatenate(high_low(part, raw_up, raw_down, near_up, near_down), axis=0)
             grad = grad + left2[...] + right2[...]
-            moment = 0.9 * momentum[0] + grad
-            coeff = product(forward, moment)
-            chosen = positions[0]
-            own = jnp.zeros_like(coeff)
-            rows = []
-            for place in range(KEEP):
-                hit = jnp.where(chosen[place : place + 1] == freq, coeff, 0.0)
-                rows.append(jnp.sum(hit, axis=0, keepdims=True))
-                own = own + hit
-            values[...] = jnp.concatenate(rows, axis=0)
-            fresh[0] = moment - product(backward, own)
+            settle(grad, momentum, positions, forward, backward, *refs[-2:])
 
         @pl.when(pl.program_id(0) < n)
         def _():
-            settle(*refs[0:7])
+            half(*refs[0:7])
 
         @pl.when(pl.program_id(0) >= n)
         def _():
-            settle(*refs[7:14])
+            half(*refs[7:14])
 
     spans = 2 * n * TILE
     return line.call(
@@ -315,47 +304,103 @@
     )
 
 
-def spread(line, first, lists, places, table):
-    spans = lists[0].shape[1]
+def widen(line, start, width, spans, partials):
+    n = width // TILE
+
+    def body(here, *refs):
+        for col, (part,) in tiles(n, refs[:n]):
+            refs[n][0, :, col] = part[...].astype(F32)
+
+    def spec(tile):
+        return pl.BlockSpec(
+            (BLOCK, TILE), lambda i, here: (0, i * (spans // TILE) + start // TILE + tile)
+        )
+
+    targets = SIDE * SIDE
+    return line.call(
+        body, targets, [partials] * n, [spec(tile) for tile in range(n)],
+        (jax.ShapeDtypeStruct((targets, BLOCK, width), F32),),
+        (pl.BlockSpec((1, BLOCK, width), lambda i, here: (i, 0, 0)),),
+    )[0]
+
+
+def finish_sum(line, summed, offset, start, width, momentum, positions, tables, so_far):
+    along = lambda rows: pl.BlockSpec((1, rows, TILE), lambda i, here: (0, 0, start // TILE + i))
+
+    def body(here, summed, momentum, positions, forward, backward, so_far, fresh, values):
+        settle(summed[...], momentum, positions, forward, backward, fresh, values)
+
+    return line.call(
+        body, width // TILE, [summed, momentum, positions, *tables, so_far],
+        [pl.BlockSpec((BLOCK, TILE), lambda i, here: (0, offset // TILE + i)), along(BLOCK),
+         along(KEEP), whole(BLOCK, 4 * BLOCK), whole(BLOCK, 4 * BLOCK),
+         pl.BlockSpec(memory_space=pl.ANY)],
+        (jax.ShapeDtypeStruct(momentum.shape, F32), jax.ShapeDtypeStruct((KEEP, width), F32)),
+        (along(BLOCK), pl.BlockSpec((KEEP, TILE), lambda i, here: (0, i))), aliases={6: 0},
+    )
+
+
+def dense(values, chosen):
+    freq = lax.broadcasted_iota(jnp.int32, (BLOCK, values.shape[1]), 0)
+    acc = jnp.zeros((BLOCK, values.shape[1]), F32)
+    for place in range(KEEP):
+        acc = jnp.where(chosen[place : place + 1] == freq, values[place : place + 1], acc)
+    return acc
+
+
+def spread_all(line, start, values, places, table, spans):
+    reps, _, width = values.shape
+
+    def body(here, values, chosen, backward, out):
+        total = dense(values[0], chosen[0])
+        for rep in range(1, reps):
+            total = total + dense(values[rep], chosen[rep])
+        out[...] = product(backward, total)
+
+    return line.call(
+        body, width // TILE, [values, places, table],
+        [pl.BlockSpec((reps, KEEP, TILE), lambda i, here: (0, 0, i)),
+         pl.BlockSpec((reps, KEEP, TILE), lambda i, here: (0, 0, start // TILE + i)),
+         whole(BLOCK, 4 * BLOCK)],
+        (jax.ShapeDtypeStruct((BLOCK, spans), F32),),
+        (pl.BlockSpec((BLOCK, TILE), lambda i, here: (0, start // TILE + i)),),
+    )[0]
+
+
+def spread(line, start, lists, places, table):
+    width = lists[0].shape[1]
 
     def body(here, *refs):
         backward, out = refs[-2:]
-        freq = lax.broadcasted_iota(jnp.int32, (BLOCK, TILE), 0)
-        dense = []
-        for values, chosen in zip(refs[:4], refs[4:8]):
-            acc = jnp.zeros((BLOCK, TILE), F32)
-            for place in range(KEEP):
-                hit = chosen[0, place : place + 1] == freq
-                acc = jnp.where(hit, values[place : place + 1], acc)
-            dense.append(acc)
-        out[...] = product(backward, (dense[0] + dense[3]) + (dense[1] + dense[2]))
-
-    return line.call(
-        body, spans // TILE, [*lists, *places, table],
+        parts = [dense(refs[k][...], refs[4 + k][0]) for k in range(4)]
+        out[...] = product(backward, (parts[0] + parts[3]) + (parts[1] + parts[2]))
+
+    def of(step):
+        return pl.BlockSpec(
+            (1, KEEP, TILE),
+            lambda i, here: (fold(here[2], step) * 2 + here[3], 0, start // TILE + i),
+        )
+
+    return line.call(
+        body, width // TILE, [*lists, *[places] * 4, table],
         [pl.BlockSpec((KEEP, TILE), lambda i, here: (0, i))] * 4
-        + [pl.BlockSpec((1, KEEP, TILE), lambda i, here: (0, 0, first + i))] * 4
-        + [whole(BLOCK, 4 * BLOCK)],
-        (jax.ShapeDtypeStruct((BLOCK, spans), F32),),
+        + [of(step) for step in (0, -1, 1, 2)] + [whole(BLOCK, 4 * BLOCK)],
+        (jax.ShapeDtypeStruct((BLOCK, width), F32),),
         (pl.BlockSpec((BLOCK, TILE), lambda i, here: (0, i)),),
     )[0]
 
 
-def join(line, first, mine, other, spans, so_far):
-    count = mine.shape[1] // TILE
+def join(line, start, mine, other, so_far):
     flat = pl.BlockSpec((BLOCK, TILE), lambda i, here: (0, i))
-    ins, specs, aliases = [mine, other], [flat, flat], {}
-    if so_far is not None:
-        ins.append(so_far)
-        specs.append(pl.BlockSpec(memory_space=pl.ANY))
-        aliases = {3: 0}
-
-    def body(here, *refs):
-        refs[-1][...] = refs[0][...] + refs[1][...]
-
-    return line.call(
-        body, count, ins, specs, (jax.ShapeDtypeStruct((BLOCK, spans), F32),),
-        (pl.BlockSpec((BLOCK, TILE), lambda i, here: (0, first + i)),),
-        aliases=aliases,
+
+    def body(here, mine, other, so_far, out):
+        out[...] = mine[...] + other[...]
+
+    return line.call(
+        body, mine.shape[1] // TILE, [mine, other, so_far],
+        [flat, flat, pl.BlockSpec(memory_space=pl.ANY)],
+        (jax.ShapeDtypeStruct(so_far.shape, F32),),
+        (pl.BlockSpec((BLOCK, TILE), lambda i, here: (0, start // TILE + i)),), aliases={3: 0},
     )[0]
 
 
@@ -388,66 +433,57 @@
 def on_device(partials, momentum, positions):
     spans = momentum.shape[2]
     flat = partials.reshape(partials.shape[2:])
-    me = lax.axis_index("fsdp")
-    here = jnp.stack([me // SIDE, lax.rem(me, SIDE)]).astype(jnp.int32)
+    me, rep = lax.axis_index("fsdp"), lax.axis_index("rep")
+    here = jnp.stack([me // SIDE, lax.rem(me, SIDE), rep // 2, lax.rem(rep, 2)]).astype(jnp.int32)
     tables = tuple(jnp.asarray(part) for part in dct_parts())
     line = Line(here)
-    offset = dict.fromkeys(PIECES, 0)
-    pairs = {
-        name: (Half(True, start, width, spans), Half(False, start + width, width, spans))
-        for name, (start, width) in PIECES.items()
-    }
-    places = [positions] + [along_z(positions, step) for step in (1, -1, 2)]
+    pair = (Half(True, 0, WIDTH, spans), Half(False, WIDTH, WIDTH, spans))
+    start = 2 * WIDTH
     got, sent = {}, []
-    fresh = update = None
-    for index, step in enumerate(ORDER.split()):
-        name, stage, *guest = step
-        pair = pairs[name]
-        line.arrived = sent[index - 2] if index >= 2 else []
-        before = lambda *stages, name=name: [
-            [*sum((got[name, s][h] for s in stages), [])] for h in range(2)
-        ]
-        if stage == "1":
-            out = [both(h.x_first, send_far(line, h, flat)) for h in pair]
-        elif stage == "2" and not guest:
-            out = [both(h.x_first, send_raw(line, h, flat, 0)) for h in pair]
-        elif stage == "2":
-            guests = pairs[guest[0]][::-1]
-            out = []
-            for half, other, g in zip(pair, guests, before(2, 3, name=guest[0])[::-1]):
-                parts = send_raw(line, half, flat, other.width)
-                parts = send_far2(line, other, flat, g, parts, SIDE * half.count)
-                out.append(both(half.x_first, parts))
-            got[guest[0], 4] = out[::-1]
-            offset[guest[0]] = SIDE * pair[0].count
-        elif stage == "3":
-            out = [both(h.x_first, send_near(line, h, flat, *g)) for h, g in zip(pair, before(1))]
-        elif stage == "4":
-            out = [
-                both(not h.x_first, send_far2(line, h, flat, g)) for h, g in zip(pair, before(2, 3))
-            ]
-        elif stage == "5":
-            out = [
-                both(not h.x_first, send_near2(line, h, flat, g, f, offset[name]))
-                for h, g, f in zip(pair, before(2, 3), before(4))
-            ]
-        elif stage == "6":
-            fresh, own = finish(
-                line, pair, flat, momentum, positions, before(2, 3, 5), tables, fresh
-            )
-            lists = [own] + [along_z(own, step) for step in (1, -1, 2)]
-            out = [lists[1:], lists]
-        elif stage == "7":
-            mine = spread(line, pair[0].first, got[name, 6][1], places, tables[1])
-            out = [[other_core(mine)], [mine]]
-        elif stage == "8":
-            (other,), (mine,) = got[name, 7]
-            update = join(line, pair[0].first, mine, other, spans, update)
-            out = []
-        got[name, int(stage)] = out
-        sent.append(sum(out, []) if int(stage) < 6 else (out[0] if out else []))
-        if step in PLACES_WITH:
-            sent[-1] = sent[-1] + [places[1 + PLACES_WITH.index(step)]]
+
+    def each(stage, send):
+        out = [None, None]
+        for axis in range(2):
+            h = axis if stage < 4 else 1 - axis
+            line.arrived = sent[-2][axis] if len(sent) >= 2 else []
+            out[h] = both(axis == 0, send(pair[h], h))
+        line.arrived = []
+        got[stage] = out
+        sent.append(out if stage < 4 else out[::-1])
+
+    def before(h, *stages):
+        return sum((got[stage][h] for stage in stages), [])
+
+    places = lax.all_gather(positions[0], "rep", axis=0, tiled=False)
+    each(1, lambda half, h: send_far(line, half, flat))
+    wide = widen(line, start, spans - start, spans, flat)
+    summed = lax.psum_scatter(wide, "fsdp", scatter_dimension=0, tiled=False)
+    each(2, lambda half, h: send_raw(line, half, flat))
+    each(3, lambda half, h: send_near(line, half, flat, *before(h, 1)))
+    each(4, lambda half, h: send_far2(line, half, flat, before(h, 2, 3)))
+    each(5, lambda half, h: send_near2(line, half, flat, before(h, 2, 3), before(h, 4)))
+    full = [before(h, 2, 3, 5) for h in range(2)]
+    fresh, own = finish(line, pair, flat, momentum, positions, full, tables, None)
+    every = lax.all_gather(own, "rep", axis=0, tiled=False)
+    if EARLY:
+        update = spread_all(line, 0, every, places, tables[1], spans)
+    lists, offset = [], 0
+    for width in CHUNKS:
+        fresh, own = finish_sum(
+            line, summed, offset, start + offset, width, momentum, positions, tables, fresh
+        )
+        lists.append([own] + [along_z(own, step) for step in (1, -1, 2)])
+        offset += width
+    if not EARLY:
+        update = spread_all(line, 0, every, places, tables[1], spans)
+    mine, offset = [], 0
+    for width, four in zip(CHUNKS, lists):
+        mine.append(spread(line, start + offset, four, places, tables[1]))
+        offset += width
+    offset = 0
+    for width, part in zip(CHUNKS, mine):
+        update = join(line, start + offset, part, other_core(part), update)
+        offset += width
     return update, fresh
 
 

time: 268 us -> 280 us (1.045)
  waiting for transfers between devices: 87.2 us -> 140 us
  Pallas kernels: 103 us -> 73.3 us
  starting transfers between devices: 67.8 us -> 40 us
  between operations: 1.07 us -> 15.8 us
    ppermute x36 -> x20, waiting for transfers between devices: 82.6 us -> 123 us  [along(): lax.ppermute(value, 'fsdp', shift(0, step) if x_first else shift(step, 0))]
    pallas_call x26 -> x19, Pallas kernels: 103 us -> 73.3 us  [call(): pl.pallas_call(run, grid_spec=pltpu.PrefetchScalarGridSpec(num_scalar_pre...]
    all_gather x0 -> x2, waiting for transfers between devices: none -> 17 us  [the longest x1 17 us: on_device(): every = lax.all_gather(own, 'rep', axis=0, tiled=False)]
    ppermute x2, starting transfers between devices: 12.6 us -> 0.67 us  [other_core(): return lax.ppermute(value, 'rep', [(r, r ^ 1) for r in range(2 * SIDE)])]
    ppermute x36 -> x20, starting transfers between devices: 41.5 us -> 29.7 us  [along(): lax.ppermute(value, 'fsdp', shift(0, step) if x_first else shift(step, 0))]
    ppermute x9 -> x6, starting transfers between devices: 13.7 us -> 9.56 us  [along_z(): lax.ppermute(value, 'rep', [(z * 2 + c, (z + step) % SIDE * 2 + c) for z...]
    unnamed x62 -> x46, local copies, waits for them, and re-layouts: 5.43 us -> 7.07 us
  transfers between devices with their start and end apart: 47 -> 31, of which waited for: 17 -> 11; matrix products, arithmetic and copies ran while one was open for 0% -> 0% of each run, Pallas kernels for 33% -> 18%
where the time goes in v3:
time: 280 us; the launch traced here: 277 us
  waiting for transfers between devices  140 us (50%)
  Pallas kernels  73.3 us (26%)
  starting transfers between devices  40 us (14%)
  between operations  15.8 us (6%)
  local copies, waits for them, and re-layouts  7.07 us (3%)
    ppermute x20, waiting for transfers between devices, along(): lax.ppermute(value, 'fsdp', shift(0, step) if x_first else shift(step, 0))  123 us
    pallas_call x19, Pallas kernels, call(): pl.pallas_call(run, grid_spec=pltpu.PrefetchScalarGridSpec(num_scalar_pre...  73.3 us
    ppermute x20, starting transfers between devices, along(): lax.ppermute(value, 'fsdp', shift(0, step) if x_first else shift(step, 0))  29.7 us
    all_gather x1, waiting for transfers between devices, on_device(): every = lax.all_gather(own, 'rep', axis=0, tiled=False)  17 us
    ppermute x6, starting transfers between devices, along_z(): lax.ppermute(value, 'rep', [(z * 2 + c, (z + step) % SIDE * 2 + c) for z...  9.56 us
    unnamed x46, local copies, waits for them, and re-layouts  7.07 us
  transfers between devices with their start and end apart: 31, of which 11 were waited for; matrix products, arithmetic and copies ran while one was open for 0% of the time, Pallas kernels for 18%

profile of v3, /device:TPU:1, one launch (start us, length us, event | category | flops | bytes accessed | tf_op | source)
XLA Modules:
  0.0 276.7 jit_solution(11462766069654063646)
XLA Ops:
  8.1 0.1 pad_add_fusion.here
  8.1 3.8 %shard_map.68 = (f32[32,8192]{1,0:T(8,128)}, f32[32,8192]{1,0:T(8,128)S(1)}, f32[8,128]{1,0:T(8,128)S(1)}) custom-call(s32[4]{0:T(128)S(1)} %pad_add_fusion.here, bf16[64,131072]{1,0:T(8,128)(2,1)} %bitcast.11, bf16[64,131072]{1,0:T(8,128)(2,1)} %bitcast.12, bf16[64,131072]{1,0:T(8,128)(2,1)} %bitcast.13, bf16[64,131072]{1,0:T(8,128)(2,1)} %bitcast.14, ...), custom_call_target="tpu_custom_call" | custom-call | tf_op jit(solution)/shard_map/pallas_call | solution.py:109
  12.0 1.0 copy-done.22
  12.9 2.9 %shard_map.69 = (f32[32,8192]{1,0:T(8,128)S(1)}, f32[32,8192]{1,0:T(8,128)S(1)}, f32[8,128]{1,0:T(8,128)S(1)}) custom-call(s32[4]{0:T(128)S(1)} %pad_add_fusion.here, bf16[64,131072]{1,0:T(8,128)(2,1)} %bitcast.19, bf16[64,131072]{1,0:T(8,128)(2,1)} %bitcast.20, bf16[64,131072]{1,0:T(8,128)(2,1)} %bitcast.21, bf16[64,131072]{1,0:T(8,128)(2,1)} %bitcast.22, ...), custom_call_target="tpu_custom_call" | custom-call | tf_op jit(solution)/shard_map/pallas_call | solution.py:109
  15.9 13.8 %shard_map.70 = (f32[16,64,4096]{2,1,0:T(8,128)}, f32[8,128]{1,0:T(8,128)S(1)}) custom-call(s32[4]{0:T(128)S(1)} %pad_add_fusion.here, bf16[64,131072]{1,0:T(8,128)(2,1)} %bitcast.27, bf16[64,131072]{1,0:T(8,128)(2,1)} %bitcast.28, bf16[64,131072]{1,0:T(8,128)(2,1)} %bitcast.29, bf16[64,131072]{1,0:T(8,128)(2,1)} %bitcast.30, bf16[64,131072]{1,0:T(8,128)(2,1)} %bitcast.31, ...), custom_call_target="tpu_custom_call" | custom-call | tf_op jit(solution)/shard_map/pallas_call | solution.py:109
  29.7 0.0 all-gather.4.cloned.1.call-start
  29.8 2.1 collective-permute-start.2
  31.9 1.3 collective-permute-start.3
  33.3 1.5 collective-permute-start.8
  34.8 1.5 collective-permute-start.9
  36.3 2.9 %shard_map.71 = (f32[32,8192]{1,0:T(8,128)S(1)}, f32[32,8192]{1,0:T(8,128)S(1)}, f32[8,128]{1,0:T(8,128)S(1)}) custom-call(s32[4]{0:T(128)S(1)} %pad_add_fusion.here, bf16[64,131072]{1,0:T(8,128)(2,1)} %bitcast.35, bf16[64,131072]{1,0:T(8,128)(2,1)} %bitcast.36, bf16[64,131072]{1,0:T(8,128)(2,1)} %bitcast.37, bf16[64,131072]{1,0:T(8,128)(2,1)} %bitcast.38, ...), custom_call_target="tpu_custom_call" | custom-call | tf_op jit(solution)/shard_map/pallas_call | solution.py:109
  39.2 0.1 collective-permute-start
  39.3 4.2 %shard_map.72 = (f32[32,8192]{1,0:T(8,128)}, f32[32,8192]{1,0:T(8,128)}, f32[8,128]{1,0:T(8,128)S(1)}) custom-call(s32[4]{0:T(128)S(1)} %pad_add_fusion.here, bf16[64,131072]{1,0:T(8,128)(2,1)} %bitcast.43, bf16[64,131072]{1,0:T(8,128)(2,1)} %bitcast.44, bf16[64,131072]{1,0:T(8,128)(2,1)} %bitcast.45, bf16[64,131072]{1,0:T(8,128)(2,1)} %bitcast.46, ...), custom_call_target="tpu_custom_call" | custom-call | tf_op jit(solution)/shard_map/pallas_call | solution.py:109
  43.5 22.4 %collective-permute-done.2.refs_8_.refs_11_ = f32[32,8192]{1,0:T(8,128)S(1)} collective-permute-done((f32[32,8192]{1,0:T(8,128)}, f32[32,8192]{1,0:T(8,128)S(1)}, u32[]{:S(2)}, u32[]{:S(2)}) %collective-permute-start.2) | collective-permute-done | bytes 1048608 | tf_op jit(solution)/shard_map/ppermute | solution.py:416
  65.9 2.6 collective-permute-start.1
  68.5 1.4 collective-permute-start.6
  69.9 3.0 %shard_map.73 = (f32[32,8192]{1,0:T(8,128)S(1)}, f32[32,8192]{1,0:T(8,128)S(1)}, f32[8,128]{1,0:T(8,128)S(1)}) custom-call(s32[4]{0:T(128)S(1)} %pad_add_fusion.here, bf16[64,131072]{1,0:T(8,128)(2,1)} %bitcast.51, bf16[64,131072]{1,0:T(8,128)(2,1)} %bitcast.52, bf16[64,131072]{1,0:T(8,128)(2,1)} %bitcast.53, bf16[64,131072]{1,0:T(8,128)(2,1)} %bitcast.54, ...), custom_call_target="tpu_custom_call" | custom-call | tf_op jit(solution)/shard_map/pallas_call | solution.py:109
  73.0 1.6 collective-permute-start.7
  74.6 3.0 %shard_map.74 = (f32[32,8192]{1,0:T(8,128)S(1)}, f32[32,8192]{1,0:T(8,128)S(1)}, f32[8,128]{1,0:T(8,128)S(1)}) custom-call(s32[4]{0:T(128)S(1)} %pad_add_fusion.here, bf16[64,131072]{1,0:T(8,128)(2,1)} %bitcast.59, bf16[64,131072]{1,0:T(8,128)(2,1)} %bitcast.60, bf16[64,131072]{1,0:T(8,128)(2,1)} %bitcast.61, bf16[64,131072]{1,0:T(8,128)(2,1)} %bitcast.62, ...), custom_call_target="tpu_custom_call" | custom-call | tf_op jit(solution)/shard_map/pallas_call | solution.py:109
  77.6 0.1 collective-permute-start.10
  77.7 33.2 %collective-permute-done.refs_21_.refs_4_.refs_5_.refs_6_.refs_7_.refs_24_.refs_25_.refs_26_.refs_27_.refs_1_ = f32[32,8192]{1,0:T(8,128)S(1)} collective-permute-done((f32[32,8192]{1,0:T(8,128)S(1)}, f32[32,8192]{1,0:T(8,128)S(1)}, u32[]{:S(2)}, u32[]{:S(2)}) %collective-permute-start) | collective-permute-done | bytes 1048608 | tf_op jit(solution)/shard_map/ppermute | solution.py:416
  110.9 3.6 %collective-permute-start.11 = (f32[32,8192]{1,0:T(8,128)S(1)}, f32[32,8192]{1,0:T(8,128)S(1)}, u32[]{:S(2)}, u32[]{:S(2)}) collective-permute-start(f32[32,8192]{1,0:T(8,128)S(1)} %get-tuple-element.70), channel_id=1, source_target_pairs={{0,12},{1,13},{2,14},{3,15},{4,0},{5,1},{6,2},{7,3},{8,4},{9,5},{1... | collective-permute-start | bytes 3145736 | tf_op jit(solution)/shard_map/ppermute | solution.py:416
  114.5 0.9 collective-permute-start.4
  115.5 2.3 collective-permute-done.6.refs_4_.refs_5_.refs_6_.refs_7_.refs_21_.refs_24_.refs_25_.refs_26_.refs_27_.refs_8_
  117.7 1.4 collective-permute-start.5
  119.1 0.7 collective-permute-done.7.refs_8_.refs_9_.refs_10_.refs_11_.refs_22_.refs_28_.refs_29_.refs_30_.refs_31_
  119.9 42.8 %collective-permute-done.10.refs_12_.refs_13_.refs_14_.refs_15_.refs_32_.refs_33_.refs_34_.refs_35_.refs_49_.refs_10_ = f32[32,8192]{1,0:T(8,128)S(1)} collective-permute-done((f32[32,8192]{1,0:T(8,128)S(1)}, f32[32,8192]{1,0:T(8,128)S(1)}, u32[]{:S(2)}, u32[]{:S(2)}) %collective-permute-start.10) | collective-permute-done | bytes 1048608 | tf_op jit(solution)/shard_map/ppermute | solution.py:416
  162.7 2.1 collective-permute-done.11.refs_16_.refs_17_.refs_18_.refs_19_.refs_36_.refs_37_.refs_38_.refs_39_.refs_50_.refs_11_
  164.8 1.6 shard_map.75
  166.4 0.1 collective-permute-start.14
  166.5 2.7 collective-permute-start.15
  169.2 2.0 copy-done.1
  171.1 1.6 shard_map.76
  172.7 1.5 collective-permute-start.12
  174.2 1.7 collective-permute-start.13
  176.0 2.1 shard_map.77
  178.1 1.5 collective-permute-done.12.refs_40_.refs_41_.refs_42_.refs_43_
  179.6 1.9 shard_map.78
  181.5 1.0 collective-permute-start.16
  182.5 1.9 collective-permute-start.17
  184.4 2.7 collective-permute-start.19
  187.1 16.5 %collective-permute-done.16.refs_5_ = f32[64,2048]{1,0:T(8,128)S(1)} collective-permute-done((f32[64,2048]{1,0:T(8,128)S(1)}, f32[64,2048]{1,0:T(8,128)S(1)}, u32[]{:S(2)}, u32[]{:S(2)}) %collective-permute-start.16) | collective-permute-done | bytes 524320 | tf_op jit(solution)/shard_map/ppermute | solution.py:416
  203.6 1.4 collective-permute-done.17.refs_6_
  205.0 0.5 collective-permute-done.18.refs_12_
  205.5 9.1 %shard_map.79 = (f32[1,64,8192]{2,1,0:T(8,128)}, f32[8,4096]{1,0:T(8,128)}, f32[8,128]{1,0:T(8,128)S(1)}) custom-call(s32[4]{0:T(128)S(1)} %pad_add_fusion.here, bf16[64,131072]{1,0:T(8,128)(2,1)} %bitcast.91, f32[32,8192]{1,0:T(8,128)S(1)} %collective-permute-done.refs_21_.refs_4_.refs_5_.refs_6_.refs_7_.refs_24_.refs_25_.refs_26_.refs_27_.refs_1_, ...), custom_call_target="tpu_custom_call" | custom-call | tf_op jit(solution)/shard_map/pallas_call | solution.py:109
  214.7 1.2 copy-done.16
  215.9 3.5 %shard_map.80 = (f32[1,64,8192]{2,1,0:T(8,128)}, f32[8,2048]{1,0:T(8,128)S(1)}, f32[8,128]{1,0:T(8,128)S(1)}) custom-call(s32[4]{0:T(128)S(1)} %pad_add_fusion.here, f32[64,4096]{1,0:T(8,128)S(1)} %bitcast.8, f32[1,64,8192]{2,1,0:T(8,128)S(1)} %copy-done.14, s32[1,8,8192]{2,1,0:T(8,128)S(1)} %copy-done.15, ...), custom_call_target="tpu_custom_call", output_to_operand_aliasing={{0}: (6, {})} | custom-call | tf_op jit(solution)/shard_map/pallas_call | solution.py:109
  219.4 1.7 collective-permute-start.23
  221.1 3.4 %collective-permute-start.24 = (f32[8,2048]{1,0:T(8,128)S(1)}, f32[8,2048]{1,0:T(8,128)S(1)}, u32[]{:S(2)}, u32[]{:S(2)}) collective-permute-start(f32[8,2048]{1,0:T(8,128)S(1)} %get-tuple-element.89.refs_0_), channel_id=1, source_target_pairs={{0,96},{16,112},{32,0},{48,16},{64,32},{80,48},{96,64},{112,80},{1... | collective-permute-start | bytes 196616 | tf_op jit(solution)/shard_map/ppermute | solution.py:420
  224.5 1.2 collective-permute-start.25
  225.7 3.5 %shard_map.81 = (f32[1,64,8192]{2,1,0:T(8,128)}, f32[8,2048]{1,0:T(8,128)S(1)}, f32[8,128]{1,0:T(8,128)S(1)}) custom-call(s32[4]{0:T(128)S(1)} %pad_add_fusion.here, f32[64,4096]{1,0:T(8,128)S(1)} %bitcast.9, f32[1,64,8192]{2,1,0:T(8,128)S(1)} %copy-done.14, s32[1,8,8192]{2,1,0:T(8,128)S(1)} %copy-done.15, ...), custom_call_target="tpu_custom_call", output_to_operand_aliasing={{0}: (6, {})} | custom-call | tf_op jit(solution)/shard_map/pallas_call | solution.py:109
  229.2 0.9 collective-permute-start.20
  230.1 1.8 collective-permute-start.21
  231.9 0.6 collective-permute-start.22
  232.5 17.0 %all-gather.6.cloned.1.call-done = f32[64,4096]{1,0:T(8,128)} async-done(((f32[8,4096]{1,0:T(8,128)}), f32[64,4096]{1,0:T(8,128)}) %all-gather.6.cloned.1.call-update) | async-done | bytes 1048592 | tf_op jit(solution)/shard_map/all_gather | solution.py:467
  249.4 1.6 copy-done.12
  251.0 1.2 copy-done.19
  252.2 7.3 %shard_map.82 = (f32[64,8192]{1,0:T(8,128)}, f32[8,128]{1,0:T(8,128)S(1)}) custom-call(s32[4]{0:T(128)S(1)} %pad_add_fusion.here, f32[8,8,4096]{2,1,0:T(8,128)S(1)} %bitcast.10, s32[8,8,8192]{2,1,0:T(8,128)S(1)} %copy-done.12, bf16[64,256]{1,0:T(8,128)(2,1)S(1)} %copy-done.18, f32[8,128]{1,0:T(8,128)S(1)} %get-tuple-element.91.refs_3_), custom_call_target="tpu_custom_call" | custom-call | tf_op jit(solution)/shard_map/pallas_call | solution.py:109
  259.6 2.5 shard_map.83
  262.1 0.3 collective-permute-start.27
  262.4 2.5 shard_map.84
  264.9 0.3 collective-permute-start.26
  265.3 2.0 shard_map.85
  267.3 2.0 shard_map.86
  (67 shorter events, 0.3 us)
Async XLA Ops:
  8.0 206.6 %reduce-scatter.4.cloned.1.call-start = ((), (), s32[]{:S(2)}) async-start(), calls=%async_computation.3 | async-start | bytes 17825792
  12.0 1.0 copy-start.22
  15.8 13.8 %copy-start.21 = (f32[32,8192]{1,0:T(8,128)}, f32[32,8192]{1,0:T(8,128)S(1)}, u32[]{:S(2)}) copy-start(f32[32,8192]{1,0:T(8,128)S(1)} %get-tuple-element.66) | copy-start | bytes 3145732
  29.7 202.8 %all-gather.4.cloned.1.call-start = ((), (), s32[]{:S(2)}) async-start(), calls=%async_computation.1 | async-start | bytes 2359296 | tf_op jit(solution)/shard_map/all_gather | solution.py:457
  29.8 36.2 %collective-permute-start.2 = (f32[32,8192]{1,0:T(8,128)}, f32[32,8192]{1,0:T(8,128)S(1)}, u32[]{:S(2)}, u32[]{:S(2)}) collective-permute-start(f32[32,8192]{1,0:T(8,128)} %get-tuple-element.58), channel_id=1, source_target_pairs={{0,1},{1,2},{2,3},{3,0},{4,5},{5,6},{6,7},{7,4},{8,9},{9,10},{10,1... | collective-permute-start | bytes 3145736 | tf_op jit(solution)/shard_map/ppermute | solution.py:416
  31.9 36.6 %collective-permute-start.3 = (f32[32,8192]{1,0:T(8,128)}, f32[32,8192]{1,0:T(8,128)S(1)}, u32[]{:S(2)}, u32[]{:S(2)}) collective-permute-start(f32[32,8192]{1,0:T(8,128)} %copy-done.22), channel_id=1, source_target_pairs={{0,3},{1,0},{2,1},{3,2},{4,7},{5,4},{6,5},{7,6},{8,11},{9,8},{10,9... | collective-permute-start | bytes 3145736 | tf_op jit(solution)/shard_map/ppermute | solution.py:416
  33.2 216.2 %all-gather.6.cloned.1.call-start = ((), (), s32[]{:S(2)}) async-start(), calls=%async_computation.2 | async-start | bytes 1179648 | tf_op jit(solution)/shard_map/all_gather | solution.py:467
  33.3 39.7 %collective-permute-start.8 = (f32[32,8192]{1,0:T(8,128)}, f32[32,8192]{1,0:T(8,128)S(1)}, u32[]{:S(2)}, u32[]{:S(2)}) collective-permute-start(f32[32,8192]{1,0:T(8,128)} %copy-done.21), channel_id=1, source_target_pairs={{0,4},{1,5},{2,6},{3,7},{4,8},{5,9},{6,10},{7,11},{8,12},{9,13},{1... | collective-permute-start | bytes 3145736 | tf_op jit(solution)/shard_map/ppermute | solution.py:416
  34.8 39.8 %collective-permute-start.9 = (f32[32,8192]{1,0:T(8,128)S(1)}, f32[32,8192]{1,0:T(8,128)S(1)}, u32[]{:S(2)}, u32[]{:S(2)}) collective-permute-start(f32[32,8192]{1,0:T(8,128)S(1)} %get-tuple-element.67), channel_id=1, source_target_pairs={{0,12},{1,13},{2,14},{3,15},{4,0},{5,1},{6,2},{7,3},{8,4},{9,5},{1... | collective-permute-start | bytes 3145736 | tf_op jit(solution)/shard_map/ppermute | solution.py:416
  39.2 71.6 %collective-permute-start = (f32[32,8192]{1,0:T(8,128)S(1)}, f32[32,8192]{1,0:T(8,128)S(1)}, u32[]{:S(2)}, u32[]{:S(2)}) collective-permute-start(f32[32,8192]{1,0:T(8,128)S(1)} %get-tuple-element.56), channel_id=1, source_target_pairs={{0,1},{1,2},{2,3},{3,0},{4,5},{5,6},{6,7},{7,4},{8,9},{9,10},{10,1... | collective-permute-start | bytes 3145736 | tf_op jit(solution)/shard_map/ppermute | solution.py:416
  65.9 48.6 %collective-permute-start.1 = (f32[32,8192]{1,0:T(8,128)S(1)}, f32[32,8192]{1,0:T(8,128)S(1)}, u32[]{:S(2)}, u32[]{:S(2)}) collective-permute-start(f32[32,8192]{1,0:T(8,128)S(1)} %get-tuple-element.57), channel_id=1, source_target_pairs={{0,3},{1,0},{2,1},{3,2},{4,7},{5,4},{6,5},{7,6},{8,11},{9,8},{10,9... | collective-permute-start | bytes 3145736 | tf_op jit(solution)/shard_map/ppermute | solution.py:416
  68.5 49.2 %collective-permute-start.6 = (f32[32,8192]{1,0:T(8,128)}, f32[32,8192]{1,0:T(8,128)S(1)}, u32[]{:S(2)}, u32[]{:S(2)}) collective-permute-start(f32[32,8192]{1,0:T(8,128)} %get-tuple-element.64), channel_id=1, source_target_pairs={{0,4},{1,5},{2,6},{3,7},{4,8},{5,9},{6,10},{7,11},{8,12},{9,13},{1... | collective-permute-start | bytes 3145736 | tf_op jit(solution)/shard_map/ppermute | solution.py:416
  73.0 46.9 %collective-permute-start.7 = (f32[32,8192]{1,0:T(8,128)}, f32[32,8192]{1,0:T(8,128)S(1)}, u32[]{:S(2)}, u32[]{:S(2)}) collective-permute-start(f32[32,8192]{1,0:T(8,128)} %get-tuple-element.65), channel_id=1, source_target_pairs={{0,12},{1,13},{2,14},{3,15},{4,0},{5,1},{6,2},{7,3},{8,4},{9,5},{1... | collective-permute-start | bytes 3145736 | tf_op jit(solution)/shard_map/ppermute | solution.py:416
  77.6 85.1 %collective-permute-start.10 = (f32[32,8192]{1,0:T(8,128)S(1)}, f32[32,8192]{1,0:T(8,128)S(1)}, u32[]{:S(2)}, u32[]{:S(2)}) collective-permute-start(f32[32,8192]{1,0:T(8,128)S(1)} %get-tuple-element.69), channel_id=1, source_target_pairs={{0,4},{1,5},{2,6},{3,7},{4,8},{5,9},{6,10},{7,11},{8,12},{9,13},{1... | collective-permute-start | bytes 3145736 | tf_op jit(solution)/shard_map/ppermute | solution.py:416
  110.9 53.9 %collective-permute-start.11 = (f32[32,8192]{1,0:T(8,128)S(1)}, f32[32,8192]{1,0:T(8,128)S(1)}, u32[]{:S(2)}, u32[]{:S(2)}) collective-permute-start(f32[32,8192]{1,0:T(8,128)S(1)} %get-tuple-element.70), channel_id=1, source_target_pairs={{0,12},{1,13},{2,14},{3,15},{4,0},{5,1},{6,2},{7,3},{8,4},{9,5},{1... | collective-permute-start | bytes 3145736 | tf_op jit(solution)/shard_map/ppermute | solution.py:416
  114.5 50.3 %copy-start = (f32[32,8192]{1,0:T(8,128)}, f32[32,8192]{1,0:T(8,128)S(1)}, u32[]{:S(2)}) copy-start(f32[32,8192]{1,0:T(8,128)S(1)} %collective-permute-done.1.refs_22_.refs_8_.refs_9_.refs_10_.refs_11_.refs_28_.refs_29_.refs_30_.refs_31_.refs_2_) | copy-start | bytes 3145732
  114.5 54.6 %collective-permute-start.4 = (f32[32,8192]{1,0:T(8,128)S(1)}, f32[32,8192]{1,0:T(8,128)S(1)}, u32[]{:S(2)}, u32[]{:S(2)}) collective-permute-start(f32[32,8192]{1,0:T(8,128)S(1)} %get-tuple-element.62), channel_id=1, source_target_pairs={{0,1},{1,2},{2,3},{3,0},{4,5},{5,6},{6,7},{7,4},{8,9},{9,10},{10,1... | collective-permute-start | bytes 3145736 | tf_op jit(solution)/shard_map/ppermute | solution.py:416
  117.7 58.2 %copy-start.3 = (f32[32,8192]{1,0:T(8,128)}, f32[32,8192]{1,0:T(8,128)S(1)}, u32[]{:S(2)}) copy-start(f32[32,8192]{1,0:T(8,128)S(1)} %collective-permute-done.6.refs_4_.refs_5_.refs_6_.refs_7_.refs_21_.refs_24_.refs_25_.refs_26_.refs_27_.refs_8_) | copy-start | bytes 3145732
  117.7 51.4 %collective-permute-start.5 = (f32[32,8192]{1,0:T(8,128)S(1)}, f32[32,8192]{1,0:T(8,128)S(1)}, u32[]{:S(2)}, u32[]{:S(2)}) collective-permute-start(f32[32,8192]{1,0:T(8,128)S(1)} %get-tuple-element.63), channel_id=1, source_target_pairs={{0,3},{1,0},{2,1},{3,2},{4,7},{5,4},{6,5},{7,6},{8,11},{9,8},{10,9... | collective-permute-start | bytes 3145736 | tf_op jit(solution)/shard_map/ppermute | solution.py:416
  119.9 46.5 %copy-start.4 = (f32[32,8192]{1,0:T(8,128)}, f32[32,8192]{1,0:T(8,128)S(1)}, u32[]{:S(2)}) copy-start(f32[32,8192]{1,0:T(8,128)S(1)} %collective-permute-done.7.refs_8_.refs_9_.refs_10_.refs_11_.refs_22_.refs_28_.refs_29_.refs_30_.refs_31_) | copy-start | bytes 3145732
  162.7 13.2 %copy-start.6 = (f32[32,8192]{1,0:T(8,128)}, f32[32,8192]{1,0:T(8,128)S(1)}, u32[]{:S(2)}) copy-start(f32[32,8192]{1,0:T(8,128)S(1)} %collective-permute-done.10.refs_12_.refs_13_.refs_14_.refs_15_.refs_32_.refs_33_.refs_34_.refs_35_.refs_49_.refs_10_) | copy-start | bytes 3145732
  164.8 11.1 %copy-start.7 = (f32[32,8192]{1,0:T(8,128)}, f32[32,8192]{1,0:T(8,128)S(1)}, u32[]{:S(2)}) copy-start(f32[32,8192]{1,0:T(8,128)S(1)} %collective-permute-done.11.refs_16_.refs_17_.refs_18_.refs_19_.refs_36_.refs_37_.refs_38_.refs_39_.refs_50_.refs_11_) | copy-start | bytes 3145732
  166.4 9.5 %collective-permute-start.14 = (f32[32,2048]{1,0:T(8,128)S(1)}, f32[32,2048]{1,0:T(8,128)S(1)}, u32[]{:S(2)}, u32[]{:S(2)}) collective-permute-start(f32[32,2048]{1,0:T(8,128)S(1)} %get-tuple-element.75), channel_id=1, source_target_pairs={{0,1},{1,2},{2,3},{3,0},{4,5},{5,6},{6,7},{7,4},{8,9},{9,10},{10,1... | collective-permute-start | bytes 786440 | tf_op jit(solution)/shard_map/ppermute | solution.py:416
  166.5 9.4 %collective-permute-start.15 = (f32[32,2048]{1,0:T(8,128)S(1)}, f32[32,2048]{1,0:T(8,128)S(1)}, u32[]{:S(2)}, u32[]{:S(2)}) collective-permute-start(f32[32,2048]{1,0:T(8,128)S(1)} %get-tuple-element.76), channel_id=1, source_target_pairs={{0,3},{1,0},{2,1},{3,2},{4,7},{5,4},{6,5},{7,6},{8,11},{9,8},{10,9... | collective-permute-start | bytes 786440 | tf_op jit(solution)/shard_map/ppermute | solution.py:416
  169.1 3.6 %copy-start.8 = (f32[32,8192]{1,0:T(8,128)}, f32[32,8192]{1,0:T(8,128)S(1)}, u32[]{:S(2)}) copy-start(f32[32,8192]{1,0:T(8,128)S(1)} %collective-permute-done.4.refs_12_.refs_13_.refs_14_.refs_15_.refs_49_.refs_32_.refs_33_.refs_34_.refs_35_.refs_3_) | copy-start | bytes 3145732
  169.1 3.6 %copy-start.10 = (f32[32,8192]{1,0:T(8,128)}, f32[32,8192]{1,0:T(8,128)S(1)}, u32[]{:S(2)}) copy-start(f32[32,8192]{1,0:T(8,128)S(1)} %collective-permute-done.5.refs_16_.refs_17_.refs_18_.refs_19_.refs_50_.refs_36_.refs_37_.refs_38_.refs_39_.refs_4_) | copy-start | bytes 3145732
  169.2 2.0 copy-start.1
  171.1 4.8 %copy-start.5 = (f32[32,8192]{1,0:T(8,128)S(1)}, f32[32,8192]{1,0:T(8,128)}, u32[]{:S(2)}) copy-start(f32[32,8192]{1,0:T(8,128)} %copy-done.4) | copy-start | bytes 3145732
  172.7 6.8 %collective-permute-start.12 = (f32[32,2048]{1,0:T(8,128)S(1)}, f32[32,2048]{1,0:T(8,128)S(1)}, u32[]{:S(2)}, u32[]{:S(2)}) collective-permute-start(f32[32,2048]{1,0:T(8,128)S(1)} %get-tuple-element.73), channel_id=1, source_target_pairs={{0,4},{1,5},{2,6},{3,7},{4,8},{5,9},{6,10},{7,11},{8,12},{9,13},{1... | collective-permute-start | bytes 786440 | tf_op jit(solution)/shard_map/ppermute | solution.py:416
  174.2 5.4 %collective-permute-start.13 = (f32[32,2048]{1,0:T(8,128)S(1)}, f32[32,2048]{1,0:T(8,128)S(1)}, u32[]{:S(2)}, u32[]{:S(2)}) collective-permute-start(f32[32,2048]{1,0:T(8,128)S(1)} %get-tuple-element.74), channel_id=1, source_target_pairs={{0,12},{1,13},{2,14},{3,15},{4,0},{5,1},{6,2},{7,3},{8,4},{9,5},{1... | collective-permute-start | bytes 786440 | tf_op jit(solution)/shard_map/ppermute | solution.py:416
  175.9 3.6 %copy-start.2 = (f32[32,8192]{1,0:T(8,128)S(1)}, f32[32,8192]{1,0:T(8,128)}, u32[]{:S(2)}) copy-start(f32[32,8192]{1,0:T(8,128)} %copy-done) | copy-start | bytes 3145732
  175.9 3.6 %copy-start.9 = (f32[32,8192]{1,0:T(8,128)S(1)}, f32[32,8192]{1,0:T(8,128)}, u32[]{:S(2)}) copy-start(f32[32,8192]{1,0:T(8,128)} %copy-done.8) | copy-start | bytes 3145732
  175.9 3.6 %copy-start.11 = (f32[32,8192]{1,0:T(8,128)S(1)}, f32[32,8192]{1,0:T(8,128)}, u32[]{:S(2)}) copy-start(f32[32,8192]{1,0:T(8,128)} %copy-done.10) | copy-start | bytes 3145732
  179.6 25.9 %copy-start.15 = (s32[1,8,8192]{2,1,0:T(8,128)S(1)}, s32[1,8,8192]{2,1,0:T(8,128)}, u32[]{:S(2)}) copy-start(s32[1,8,8192]{2,1,0:T(8,128)} %refs_2_.4) | copy-start | bytes 786436
  179.6 25.9 %copy-start.18 = (bf16[64,256]{1,0:T(8,128)(2,1)S(1)}, bf16[64,256]{1,0:T(8,128)(2,1)}, u32[]{:S(2)}) copy-start(bf16[64,256]{1,0:T(8,128)(2,1)} %constant.39.clone.refs_17_.refs_4_.refs_2_.refs_8_) | copy-start | bytes 98308
  179.6 25.8 %copy-start.20 = (bf16[64,256]{1,0:T(8,128)(2,1)S(1)}, bf16[64,256]{1,0:T(8,128)(2,1)}, u32[]{:S(2)}) copy-start(bf16[64,256]{1,0:T(8,128)(2,1)} %constant.38.clone.refs_16_.refs_3_) | copy-start | bytes 98308
  181.5 22.1 %collective-permute-start.16 = (f32[64,2048]{1,0:T(8,128)S(1)}, f32[64,2048]{1,0:T(8,128)S(1)}, u32[]{:S(2)}, u32[]{:S(2)}) collective-permute-start(f32[64,2048]{1,0:T(8,128)S(1)} %get-tuple-element.79), channel_id=1, source_target_pairs={{0,4},{1,5},{2,6},{3,7},{4,8},{5,9},{6,10},{7,11},{8,12},{9,13},{1... | collective-permute-start | bytes 1572872 | tf_op jit(solution)/shard_map/ppermute | solution.py:416
  182.5 22.5 %collective-permute-start.17 = (f32[64,2048]{1,0:T(8,128)S(1)}, f32[64,2048]{1,0:T(8,128)S(1)}, u32[]{:S(2)}, u32[]{:S(2)}) collective-permute-start(f32[64,2048]{1,0:T(8,128)S(1)} %get-tuple-element.80), channel_id=1, source_target_pairs={{0,12},{1,13},{2,14},{3,15},{4,0},{5,1},{6,2},{7,3},{8,4},{9,5},{1... | collective-permute-start | bytes 1572872 | tf_op jit(solution)/shard_map/ppermute | solution.py:416
  184.4 21.0 %collective-permute-start.18 = (f32[64,2048]{1,0:T(8,128)S(1)}, f32[64,2048]{1,0:T(8,128)S(1)}, u32[]{:S(2)}, u32[]{:S(2)}) collective-permute-start(f32[64,2048]{1,0:T(8,128)S(1)} %get-tuple-element.81), channel_id=1, source_target_pairs={{0,1},{1,2},{2,3},{3,0},{4,5},{5,6},{6,7},{7,4},{8,9},{9,10},{10,1... | collective-permute-start | bytes 1572872 | tf_op jit(solution)/shard_map/ppermute | solution.py:416
  184.4 21.0 %collective-permute-start.19 = (f32[64,2048]{1,0:T(8,128)S(1)}, f32[64,2048]{1,0:T(8,128)S(1)}, u32[]{:S(2)}, u32[]{:S(2)}) collective-permute-start(f32[64,2048]{1,0:T(8,128)S(1)} %get-tuple-element.82), channel_id=1, source_target_pairs={{0,3},{1,0},{2,1},{3,2},{4,7},{5,4},{6,5},{7,6},{8,11},{9,8},{10,9... | collective-permute-start | bytes 1572872 | tf_op jit(solution)/shard_map/ppermute | solution.py:416
  205.5 9.2 %copy-start.14 = (f32[1,64,8192]{2,1,0:T(8,128)S(1)}, f32[1,64,8192]{2,1,0:T(8,128)}, u32[]{:S(2)}) copy-start(f32[1,64,8192]{2,1,0:T(8,128)} %refs_1_.3) | copy-start | bytes 6291460
  214.7 1.2 copy-start.16
  215.9 9.8 %copy-start.17 = (f32[1,64,4096]{2,1,0:T(8,128)S(1)}, f32[1,64,4096]{2,1,0:T(8,128)}, u32[]{:S(2)}) copy-start(f32[1,64,4096]{2,1,0:T(8,128)} %reduce-scatter.4.cloned.1.call-done) | copy-start | bytes 3145732
  219.4 12.5 %collective-permute-start.23 = (f32[8,2048]{1,0:T(8,128)S(1)}, f32[8,2048]{1,0:T(8,128)S(1)}, u32[]{:S(2)}, u32[]{:S(2)}) collective-permute-start(f32[8,2048]{1,0:T(8,128)S(1)} %get-tuple-element.89.refs_0_), channel_id=1, source_target_pairs={{0,32},{16,48},{32,64},{48,80},{64,96},{80,112},{96,0},{112,16},{1... | collective-permute-start | bytes 196616 | tf_op jit(solution)/shard_map/ppermute | solution.py:420
  221.1 38.5 %collective-permute-start.24 = (f32[8,2048]{1,0:T(8,128)S(1)}, f32[8,2048]{1,0:T(8,128)S(1)}, u32[]{:S(2)}, u32[]{:S(2)}) collective-permute-start(f32[8,2048]{1,0:T(8,128)S(1)} %get-tuple-element.89.refs_0_), channel_id=1, source_target_pairs={{0,96},{16,112},{32,0},{48,16},{64,32},{80,48},{96,64},{112,80},{1... | collective-permute-start | bytes 196616 | tf_op jit(solution)/shard_map/ppermute | solution.py:420
  224.5 35.1 %collective-permute-start.25 = (f32[8,2048]{1,0:T(8,128)S(1)}, f32[8,2048]{1,0:T(8,128)S(1)}, u32[]{:S(2)}, u32[]{:S(2)}) collective-permute-start(f32[8,2048]{1,0:T(8,128)S(1)} %get-tuple-element.89.refs_0_), channel_id=1, source_target_pairs={{0,64},{16,80},{32,96},{48,112},{64,0},{80,16},{96,32},{112,48},{1... | collective-permute-start | bytes 196616 | tf_op jit(solution)/shard_map/ppermute | solution.py:420
  229.2 33.2 %collective-permute-start.20 = (f32[8,2048]{1,0:T(8,128)S(1)}, f32[8,2048]{1,0:T(8,128)S(1)}, u32[]{:S(2)}, u32[]{:S(2)}) collective-permute-start(f32[8,2048]{1,0:T(8,128)S(1)} %get-tuple-element.88.refs_0_), channel_id=1, source_target_pairs={{0,32},{16,48},{32,64},{48,80},{64,96},{80,112},{96,0},{112,16},{1... | collective-permute-start | bytes 196616 | tf_op jit(solution)/shard_map/ppermute | solution.py:420
  230.1 32.4 %collective-permute-start.21 = (f32[8,2048]{1,0:T(8,128)S(1)}, f32[8,2048]{1,0:T(8,128)S(1)}, u32[]{:S(2)}, u32[]{:S(2)}) collective-permute-start(f32[8,2048]{1,0:T(8,128)S(1)} %get-tuple-element.88.refs_0_), channel_id=1, source_target_pairs={{0,96},{16,112},{32,0},{48,16},{64,32},{80,48},{96,64},{112,80},{1... | collective-permute-start | bytes 196616 | tf_op jit(solution)/shard_map/ppermute | solution.py:420
  231.9 30.5 %collective-permute-start.22 = (f32[8,2048]{1,0:T(8,128)S(1)}, f32[8,2048]{1,0:T(8,128)S(1)}, u32[]{:S(2)}, u32[]{:S(2)}) collective-permute-start(f32[8,2048]{1,0:T(8,128)S(1)} %get-tuple-element.88.refs_0_), channel_id=1, source_target_pairs={{0,64},{16,80},{32,96},{48,112},{64,0},{80,16},{96,32},{112,48},{1... | collective-permute-start | bytes 196616 | tf_op jit(solution)/shard_map/ppermute | solution.py:420
  249.4 1.6 copy-start.12
  251.0 1.2 copy-start.19
  252.2 7.3 %copy-start.13 = (s32[8,8,8192]{2,1,0:T(8,128)S(1)}, s32[8,8,8192]{2,1,0:T(8,128)}, u32[]{:S(2)}) copy-start(s32[8,8,8192]{2,1,0:T(8,128)} %all-gather.4.cloned.1.call-done.refs_1_.refs_4_.refs_5_.refs_6_.refs_7_) | copy-start | bytes 6291460
  262.1 3.2 %collective-permute-start.27 = (f32[64,2048]{1,0:T(8,128)S(1)}, f32[64,2048]{1,0:T(8,128)S(1)}, u32[]{:S(2)}, u32[]{:S(2)}) collective-permute-start(f32[64,2048]{1,0:T(8,128)S(1)} %get-tuple-element.95.refs_0_), channel_id=1, source_target_pairs={{0,16},{16,0},{32,48},{48,32},{64,80},{80,64},{96,112},{112,96},{1... | collective-permute-start | bytes 1572872 | tf_op jit(solution)/shard_map/ppermute | solution.py:426
  264.9 2.4 collective-permute-start.26
Sparse Core Ops, SparseCore 0:
  29.8 184.2 reduce-scatter.3
Sparse Core Ops, SparseCore 1:
  33.3 27.8 all-gather.3
  214.7 34.7 all-gather.5

commit v4 on v3

v4 whole, which is shorter than its diff:
```python
import jax
import jax.numpy as jnp
import ml_dtypes
import numpy as np
from jax import lax
from jax.experimental import pallas as pl
from jax.experimental.pallas import tpu as pltpu
from jax.sharding import PartitionSpec as P

BLOCK = 64
HALF = BLOCK // 2
KEEP = 8
SIDE = 4
TILE = 1024
CHUNK = 256
PARTS = (2, 2)
TILE = 1024
CHUNK = 256
WIDTH = 2048
CHUNKS = (2048, 2048)
VMEM_LIMIT = 48 * 1024 * 1024
F32 = jnp.float32
BF16 = jnp.bfloat16


def dct_parts():
    k = np.arange(BLOCK, dtype=np.float64)[:, None]
    n = np.arange(BLOCK, dtype=np.float64)[None, :]
    scale = np.where(k == 0, np.sqrt(1.0 / BLOCK), np.sqrt(2.0 / BLOCK))
    dct = scale * np.cos(np.pi * (2.0 * n + 1.0) * k / (2.0 * BLOCK))

    def wide(mat):
        high = mat.astype(ml_dtypes.bfloat16)
        low = (mat - high.astype(np.float64)).astype(ml_dtypes.bfloat16)
        return np.concatenate([high, high, low, low], axis=1)

    return wide(dct), wide(dct.T.copy())


def fold(coord, step):
    return lax.rem(coord + (step + SIDE), SIDE)


class Half:
    def __init__(self, x_first, start, width, spans):
        self.x_first = x_first
        self.width = width
        self.count = width // TILE
        self.first = start // TILE
        self.per_target = spans // TILE

    def column(self, here, step, other):
        y, x = here[0], here[1]
        if self.x_first:
            target = other * SIDE + fold(x, step)
        else:
            target = fold(y, step) * SIDE + other
        return target * self.per_target + self.first

    def second(self, here, step):
        return fold(here[0] if self.x_first else here[1], step)

    def grid_blocks(self, step, rows):
        def spec(tile):
            return pl.BlockSpec(
                (HALF, TILE), lambda i, here: (rows, self.column(here, step, i) + tile)
            )

        return [spec(tile) for tile in range(self.count)]

    def one_blocks(self, step):
        def spec(tile):
            return pl.BlockSpec(
                (BLOCK, TILE),
                lambda i, here: (0, self.column(here, 0, self.second(here, step)) + tile),
            )

        return [spec(tile) for tile in range(self.count)]

    def message_blocks(self, step):
        def spec(tile):
            return pl.BlockSpec(
                (HALF, TILE), lambda i, here: (0, self.second(here, step) * self.count + tile)
            )

        return [spec(tile) for tile in range(self.count)]


def whole(*shape):
    return pl.BlockSpec(shape, lambda i, here: (0,) * len(shape))


class Line:
    def __init__(self, here):
        self.here = here
        self.token = None
        self.arrived = []

    def call(self, body, grid, ins, in_specs, out_shape, out_specs, aliases=None):
        ins, in_specs = list(ins), list(in_specs)
        count = len(ins)
        order = ([] if self.token is None else [self.token]) + self.arrived
        taken = len(order)
        ins += order
        in_specs += [whole(*(1,) * (array.ndim - 2), 8, 128) for array in order]

        def run(here, *refs):
            refs[-1][...] = jnp.zeros((8, 128), F32)
            body(here, *refs[:count], *refs[count + taken : -1])

        *outs, self.token = pl.pallas_call(
            run,
            grid_spec=pltpu.PrefetchScalarGridSpec(
                num_scalar_prefetch=1,
                grid=(grid,),
                in_specs=in_specs,
                out_specs=(*out_specs, whole(8, 128)),
            ),
            out_shape=(*out_shape, jax.ShapeDtypeStruct((8, 128), F32)),
            input_output_aliases=aliases or {},
            compiler_params=pltpu.CompilerParams(vmem_limit_bytes=VMEM_LIMIT),
            cost_estimate=pl.CostEstimate(flops=0, bytes_accessed=0, transcendentals=0),
        )(self.here, *ins)
        return outs


def tiles(n, *groups):
    for tile in range(n):
        yield slice(tile * TILE, (tile + 1) * TILE), [group[tile] for group in groups]


def groups(refs, n):
    return [refs[k : k + n] for k in range(0, len(refs), n)]


def send_part(line, half, partials, up_from, down_from):
    w, n = half.width, half.count

    def body(here, *refs):
        up, down = refs[2 * n :]
        for col, (part_up, part_down) in tiles(n, *groups(refs[: 2 * n], n)):
            up[:, col] = part_up[...].astype(F32)
            down[:, col] = part_down[...].astype(F32)

    shape = jax.ShapeDtypeStruct((HALF, SIDE * w), F32)
    spec = pl.BlockSpec((HALF, w), lambda i, here: (0, i))
    return line.call(
        body, SIDE, [partials] * (2 * n), half.grid_blocks(*up_from) + half.grid_blocks(*down_from),
        (shape, shape), (spec, spec),
    )


def send_far(line, half, partials):
    return send_part(line, half, partials, (2, 0), (2, 1))


def send_raw(line, half, partials):
    return send_part(line, half, partials, (1, 1), (-1, 0))


def send_near(line, half, partials, far_up, far_down):
    w, n = half.width, half.count

    def body(here, *refs):
        far_up, far_down, up, down = refs[2 * n :]
        for col, (part_up, part_down) in tiles(n, *groups(refs[: 2 * n], n)):
            up[:, col] = part_up[...].astype(F32) + far_up[:, col]
            down[:, col] = part_down[...].astype(F32) + far_down[:, col]

    shape = jax.ShapeDtypeStruct((HALF, SIDE * w), F32)
    spec = pl.BlockSpec((HALF, w), lambda i, here: (0, i))
    return line.call(
        body, SIDE, [partials] * (2 * n) + [far_up, far_down],
        half.grid_blocks(1, 0) + half.grid_blocks(-1, 1) + [spec, spec],
        (shape, shape), (spec, spec),
    )


def repeat(arrays, n):
    return [array for array in arrays for _ in range(n)]


def high_low(part, raw_up, raw_down, near_up, near_down):
    high = part[:HALF].astype(F32) + near_up[...] + raw_down[...]
    low = part[HALF:].astype(F32) + near_down[...] + raw_up[...]
    return high, low


def send_far2(line, half, partials, got):
    w, n = half.width, half.count

    def body(here, *refs):
        up, down = refs[-2:]
        for col, blocks in tiles(n, *groups(refs[: 5 * n], n)):
            up[:, col], down[:, col] = high_low(*blocks)

    shape = jax.ShapeDtypeStruct((HALF, w), F32)
    return line.call(
        body, 1, [partials] * n + repeat(got, n), half.one_blocks(2) + half.message_blocks(2) * 4,
        (shape, shape), (whole(HALF, w), whole(HALF, w)),
    )


def send_near2(line, half, partials, got, far, first, n):
    own = slice(first, first + n)

    def body(here, *refs):
        up, down = refs[-2:]
        for col, blocks in tiles(n, *groups(refs[: 12 * n], n)):
            high, low = high_low(*blocks[:5])
            up[:HALF, col] = high + blocks[10][...]
            up[HALF:, col] = low
            high, low = high_low(*blocks[5:10])
            down[:HALF, col] = high
            down[HALF:, col] = low + blocks[11][...]

    far_specs = [pl.BlockSpec((HALF, TILE), lambda i, here, t=t: (0, t)) for t in range(half.count)]
    w = n * TILE
    shape = jax.ShapeDtypeStruct((BLOCK, w), F32)
    return line.call(
        body, 1, ([partials] * n + repeat(got, n)) * 2 + repeat(far, n),
        half.one_blocks(1)[own] + half.message_blocks(1)[own] * 4 + half.one_blocks(-1)[own]
        + half.message_blocks(-1)[own] * 4 + far_specs[own] * 2,
        (shape, shape), (whole(BLOCK, w), whole(BLOCK, w)),
    )


def product(parts, value):
    high = value.astype(BF16)
    low = (value - high.astype(F32)).astype(BF16)
    return jnp.dot(
        parts[...], jnp.concatenate([high, low, high, low], axis=0), preferred_element_type=F32
    )


def settle(grad_of, momentum, positions, forward, backward, fresh, values):
    for at in range(0, TILE, CHUNK):
        col = slice(at, at + CHUNK)
        moment = 0.9 * momentum[0, :, col] + grad_of(col)
        coeff = product(forward, moment)
        chosen = positions[0, :, col]
        freq = lax.broadcasted_iota(jnp.int32, coeff.shape, 0)
        own = jnp.zeros_like(coeff)
        rows = []
        for place in range(KEEP):
            hit = jnp.where(chosen[place : place + 1] == freq, coeff, 0.0)
            rows.append(jnp.sum(hit, axis=0, keepdims=True))
            own = own + hit
        values[:, col] = jnp.concatenate(rows, axis=0)
        fresh[0, :, col] = moment - product(backward, own)


class Part:
    def __init__(self, pair, first, n):
        self.pair, self.first, self.n = pair, first, n
        self.steps, self.spans = 2 * n, 2 * n * TILE

    def place(self, i):
        return jnp.where(i < self.n, i, i - self.n + self.pair[0].count) + self.first

    def columns(self, rows):
        return pl.BlockSpec((1, rows, TILE), lambda i, here: (0, 0, self.place(i)))

    def result(self):
        return pl.BlockSpec((BLOCK, TILE), lambda i, here: (0, self.place(i)))

    def compact(self, rows):
        return pl.BlockSpec((rows, TILE), lambda i, here: (0, i))


def finish(line, piece, partials, momentum, positions, got, tables, so_far):
    n = piece.n
    ins, specs = [], []
    for number, (half, arrays) in enumerate(zip(piece.pair, got)):
        ins += [partials, *arrays]

        def tile(i, number=number):
            return jnp.minimum(i, n - 1) if number == 0 else jnp.maximum(i - n, 0)

        def part(i, here, half=half, tile=tile):
            return 0, half.column(here, 0, half.second(here, 0)) + piece.first + tile(i)

        def message(i, here, half=half, tile=tile):
            return 0, half.second(here, 0) * half.count + piece.first + tile(i)

        def flat(i, here, tile=tile):
            return 0, tile(i)

        specs += [pl.BlockSpec((BLOCK, TILE), part)]
        specs += [pl.BlockSpec((HALF, TILE), message)] * 4
        specs += [pl.BlockSpec((BLOCK, TILE), flat)] * 2
    ins += [momentum, positions, *tables]
    specs += [piece.columns(BLOCK), piece.columns(KEEP)] + [whole(BLOCK, 4 * BLOCK)] * 2
    aliases = {}
    if so_far is not None:
        ins.append(so_far)
        specs.append(pl.BlockSpec(memory_space=pl.ANY))
        aliases = {len(ins): 0}

    def body(here, *refs):
        momentum, positions, forward, backward = refs[14:18]

        def half(part, raw_up, raw_down, near_up, near_down, left2, right2):
            def grad_of(col):
                first = (raw_up, raw_down, near_up, near_down)
                pair = high_low(part[:, col], *(ref[:, col] for ref in first))
                return jnp.concatenate(pair, axis=0) + left2[:, col] + right2[:, col]

            settle(grad_of, momentum, positions, forward, backward, *refs[-2:])

        @pl.when(pl.program_id(0) < n)
        def _():
            half(*refs[0:7])

        @pl.when(pl.program_id(0) >= n)
        def _():
            half(*refs[7:14])

    return line.call(
        body, piece.steps, ins, specs,
        (jax.ShapeDtypeStruct(momentum.shape, F32), jax.ShapeDtypeStruct((KEEP, piece.spans), F32)),
        (piece.columns(BLOCK), piece.compact(KEEP)), aliases=aliases,
    )


def dense(values, chosen):
    freq = lax.broadcasted_iota(jnp.int32, (BLOCK, values.shape[1]), 0)
    acc = jnp.zeros((BLOCK, values.shape[1]), F32)
    for place in range(KEEP):
        acc = jnp.where(chosen[place : place + 1] == freq, values[place : place + 1], acc)
    return acc


def spread(line, piece, lists, places, table):
    def body(here, *refs):
        backward, out = refs[-2:]
        for at in range(0, TILE, CHUNK):
            col = slice(at, at + CHUNK)
            parts = [dense(refs[k][:, col], refs[4 + k][0, :, col]) for k in range(4)]
            out[:, col] = product(backward, (parts[0] + parts[3]) + (parts[1] + parts[2]))

    return line.call(
        body, piece.steps, [*lists, *places, table],
        [piece.compact(KEEP)] * 4 + [piece.columns(KEEP)] * 4 + [whole(BLOCK, 4 * BLOCK)],
        (jax.ShapeDtypeStruct((BLOCK, piece.spans), F32),), (piece.compact(BLOCK),),
    )[0]


def join(line, piece, mine, other, spans, so_far):
    ins, specs, aliases = [mine, other], [piece.compact(BLOCK)] * 2, {}
    if so_far is not None:
        ins.append(so_far)
        specs.append(pl.BlockSpec(memory_space=pl.ANY))
        aliases = {3: 0}

    def body(here, *refs):
        refs[-1][...] = refs[0][...] + refs[1][...]

    return line.call(
        body, piece.steps, ins, specs, (jax.ShapeDtypeStruct((BLOCK, spans), F32),),
        (piece.result(),), aliases=aliases,
    )[0]


def shift(dy, dx):
    return [
        (y * SIDE + x, (y + dy) % SIDE * SIDE + (x + dx) % SIDE)
        for y in range(SIDE)
        for x in range(SIDE)
    ]


def along(x_first, value, step):
    return lax.ppermute(value, "fsdp", shift(0, step) if x_first else shift(step, 0))


def along_z(value, step):
    return lax.ppermute(
        value, "rep", [(z * 2 + c, (z + step) % SIDE * 2 + c) for z in range(SIDE) for c in range(2)]
    )


def other_core(value):
    return lax.ppermute(value, "rep", [(r, r ^ 1) for r in range(2 * SIDE)])


def both(x_first, sent):
    return [along(x_first, sent[0], 1), along(x_first, sent[1], -1)]


def on_device(partials, momentum, positions):
    spans = momentum.shape[2]
    flat = partials.reshape(partials.shape[2:])
    me = lax.axis_index("fsdp")
    here = jnp.stack([me // SIDE, lax.rem(me, SIDE)]).astype(jnp.int32)
    tables = tuple(jnp.asarray(part) for part in dct_parts())
    line = Line(here)
    width = spans // 2
    pair = (Half(True, 0, width, spans), Half(False, width, width, spans))
    pieces, first = [], 0
    for n in PARTS:
        pieces.append(Part(pair, first, n))
        first += n
    got, sent = {}, []

    def each(stage, second, send):
        out = [None, None]
        for axis in range(2):
            h = 1 - axis if second else axis
            line.arrived = sent[-2][axis] if len(sent) >= 2 else []
            out[h] = both(axis == 0, send(pair[h], h))
        line.arrived = []
        got[stage] = out
        sent.append(out[::-1] if second else out)

    def before(h, *stages):
        return sum((got[stage][h] for stage in stages), [])

    places = [positions] + [along_z(positions, step) for step in (1, -1, 2)]
    each("far", False, lambda half, h: send_far(line, half, flat))
    each("raw", False, lambda half, h: send_raw(line, half, flat))
    sent[0] = [sent[0][0], sent[0][1] + places[1:2]]
    each("near", False, lambda half, h: send_near(line, half, flat, *before(h, "far")))
    sent[1] = [sent[1][0], sent[1][1] + places[2:]]
    each("far2", True, lambda half, h: send_far2(line, half, flat, before(h, "raw", "near")))
    for number, piece in enumerate(pieces):
        each(
            number, True,
            lambda half, h: send_near2(
                line, half, flat, before(h, "raw", "near"), before(h, "far2"), piece.first, piece.n
            ),
        )
    fresh = update = None
    lists, mine = [], []
    for number, piece in enumerate(pieces):
        full = [before(h, "raw", "near", number) for h in range(2)]
        fresh, own = finish(line, piece, flat, momentum, positions, full, tables, fresh)
        lists.append([own] + [along_z(own, step) for step in (1, -1, 2)])
    for piece, four in zip(pieces, lists):
        mine.append(spread(line, piece, four, places, tables[1]))
    for piece, part in zip(pieces, mine):
        update = join(line, piece, part, other_core(part), spans, update)
    return update, fresh


def solution(mesh):
    placed = (P("rep", "fsdp", None, None), P("rep", None, "fsdp"), P("rep", None, "fsdp"))
    return jax.shard_map(
        on_device,
        mesh=mesh,
        in_specs=placed,
        out_specs=(P(None, "fsdp"), P("rep", None, "fsdp")),
        check_vma=False,
    )
```

time: 280 us -> 235 us (0.84)
  waiting for transfers between devices: 140 us -> 108 us
  between operations: 15.8 us -> 0.92 us
  starting transfers between devices: 40 us -> 53.1 us
  Pallas kernels: 73.3 us -> 65.5 us
    all_gather x2 -> x0, waiting for transfers between devices: 17 us -> none  [the longest x1 17 us: on_device(): every = lax.all_gather(own, 'rep', axis=0, tiled=False)]
    ppermute x20 -> x24, waiting for transfers between devices: 123 us -> 108 us  [along(): lax.ppermute(value, 'fsdp', shift(0, step) if x_first else shift(step, 0))]
    ppermute x2, starting transfers between devices: 0.67 us -> 9.89 us  [other_core(): return lax.ppermute(value, 'rep', [(r, r ^ 1) for r in range(2 * SIDE)])]
    pallas_call x19 -> x18, Pallas kernels: 73.3 us -> 65.5 us  [call(): pl.pallas_call(run, grid_spec=pltpu.PrefetchScalarGridSpec(num_scalar_pre...]
    ppermute x6 -> x9, starting transfers between devices: 9.56 us -> 12.4 us  [along_z(): lax.ppermute(value, 'rep', [(z * 2 + c, (z + step) % SIDE * 2 + c) for z...]
    ppermute x20 -> x24, starting transfers between devices: 29.7 us -> 30.9 us  [along(): lax.ppermute(value, 'fsdp', shift(0, step) if x_first else shift(step, 0))]
    unnamed x46 -> x34, local copies, waits for them, and re-layouts: 7.07 us -> 5.88 us
  transfers between devices with their start and end apart: 31 -> 35, of which waited for: 11 -> 9; matrix products, arithmetic and copies ran while one was open for 0% -> 0% of each run, Pallas kernels for 18% -> 26%
where the time goes in v4:
time: 235 us; the launch traced here: 234 us
  waiting for transfers between devices  108 us (46%)
  Pallas kernels  65.5 us (28%)
  starting transfers between devices  53.1 us (23%)
  local copies, waits for them, and re-layouts  5.88 us (3%)
    ppermute x24, waiting for transfers between devices, along(): lax.ppermute(value, 'fsdp', shift(0, step) if x_first else shift(step, 0))  108 us
    pallas_call x18, Pallas kernels, call(): pl.pallas_call(run, grid_spec=pltpu.PrefetchScalarGridSpec(num_scalar_pre...  65.5 us
    ppermute x24, starting transfers between devices, along(): lax.ppermute(value, 'fsdp', shift(0, step) if x_first else shift(step, 0))  30.9 us
    ppermute x9, starting transfers between devices, along_z(): lax.ppermute(value, 'rep', [(z * 2 + c, (z + step) % SIDE * 2 + c) for z...  12.4 us
    ppermute x2, starting transfers between devices, other_core(): return lax.ppermute(value, 'rep', [(r, r ^ 1) for r in range(2 * SIDE)])  9.89 us
    unnamed x34, local copies, waits for them, and re-layouts  5.88 us
  transfers between devices with their start and end apart: 35, of which 9 were waited for; matrix products, arithmetic and copies ran while one was open for 0% of the time, Pallas kernels for 26%

profile of v4, /device:TPU:1, one launch (start us, length us, event | category | flops | bytes accessed | tf_op | source)
XLA Modules:
  0.0 233.9 jit_solution(1379839101641568505)
XLA Ops:
  0.6 0.1 pad_add_fusion.here
  0.7 3.4 %shard_map.68 = (f32[32,16384]{1,0:T(8,128)S(1)}, f32[32,16384]{1,0:T(8,128)S(1)}, f32[8,128]{1,0:T(8,128)S(1)}) custom-call(s32[2]{0:T(128)S(1)} %pad_add_fusion.here, bf16[64,131072]{1,0:T(8,128)(2,1)} %bitcast.3, bf16[64,131072]{1,0:T(8,128)(2,1)} %bitcast.4, bf16[64,131072]{1,0:T(8,128)(2,1)} %bitcast.5, bf16[64,131072]{1,0:T(8,128)(2,1)} %bitcast.6, ...), custom_call_target="tpu_custom_call" | custom-call | tf_op jit(solution)/shard_map/pallas_call | solution.py:111
  4.1 2.1 collective-permute-start.2
  6.3 1.4 collective-permute-start.3
  7.6 1.8 collective-permute-start.10
  9.4 3.4 %shard_map.69 = (f32[32,16384]{1,0:T(8,128)S(1)}, f32[32,16384]{1,0:T(8,128)S(1)}, f32[8,128]{1,0:T(8,128)S(1)}) custom-call(s32[2]{0:T(128)S(1)} %pad_add_fusion.here, bf16[64,131072]{1,0:T(8,128)(2,1)} %bitcast.18, bf16[64,131072]{1,0:T(8,128)(2,1)} %bitcast.12, bf16[64,131072]{1,0:T(8,128)(2,1)} %bitcast.13, bf16[64,131072]{1,0:T(8,128)(2,1)} %bitcast.14, ...), custom_call_target="tpu_custom_call" | custom-call | tf_op jit(solution)/shard_map/pallas_call | solution.py:111
  12.8 1.4 collective-permute-start.8
  14.2 1.5 collective-permute-start.9
  15.7 4.9 %shard_map.70 = (f32[32,16384]{1,0:T(8,128)}, f32[32,16384]{1,0:T(8,128)}, f32[8,128]{1,0:T(8,128)S(1)}) custom-call(s32[2]{0:T(128)S(1)} %pad_add_fusion.here, bf16[64,131072]{1,0:T(8,128)(2,1)} %bitcast.19, bf16[64,131072]{1,0:T(8,128)(2,1)} %bitcast.20, bf16[64,131072]{1,0:T(8,128)(2,1)} %bitcast.21, bf16[64,131072]{1,0:T(8,128)(2,1)} %bitcast.22, ...), custom_call_target="tpu_custom_call" | custom-call | tf_op jit(solution)/shard_map/pallas_call | solution.py:111
  20.5 0.1 collective-permute-start
  20.6 4.9 %shard_map.71 = (f32[32,16384]{1,0:T(8,128)}, f32[32,16384]{1,0:T(8,128)}, f32[8,128]{1,0:T(8,128)S(1)}) custom-call(s32[2]{0:T(128)S(1)} %pad_add_fusion.here, bf16[64,131072]{1,0:T(8,128)(2,1)} %bitcast.27, bf16[64,131072]{1,0:T(8,128)(2,1)} %bitcast.28, bf16[64,131072]{1,0:T(8,128)(2,1)} %bitcast.29, bf16[64,131072]{1,0:T(8,128)(2,1)} %bitcast.30, ...), custom_call_target="tpu_custom_call" | custom-call | tf_op jit(solution)/shard_map/pallas_call | solution.py:111
  25.5 27.0 %collective-permute-done.2.refs_8_.refs_11_ = f32[32,16384]{1,0:T(8,128)} collective-permute-done((f32[32,16384]{1,0:T(8,128)S(1)}, f32[32,16384]{1,0:T(8,128)}, u32[]{:S(2)}, u32[]{:S(2)}) %collective-permute-start.2) | collective-permute-done | bytes 2097184 | tf_op jit(solution)/shard_map/ppermute | solution.py:374
  52.5 1.6 collective-permute-start.1
  54.1 1.3 collective-permute-start.6
  55.4 4.6 %shard_map.72 = (f32[32,16384]{1,0:T(8,128)S(1)}, f32[32,16384]{1,0:T(8,128)S(1)}, f32[8,128]{1,0:T(8,128)S(1)}) custom-call(s32[2]{0:T(128)S(1)} %pad_add_fusion.here, bf16[64,131072]{1,0:T(8,128)(2,1)} %bitcast.40, bf16[64,131072]{1,0:T(8,128)(2,1)} %bitcast.36, bf16[64,131072]{1,0:T(8,128)(2,1)} %bitcast.37, bf16[64,131072]{1,0:T(8,128)(2,1)} %bitcast.38, ...), custom_call_target="tpu_custom_call" | custom-call | tf_op jit(solution)/shard_map/pallas_call | solution.py:111
  60.0 1.3 copy-done.14
  61.3 1.4 collective-permute-start.7
  62.8 4.6 %shard_map.73 = (f32[32,16384]{1,0:T(8,128)S(1)}, f32[32,16384]{1,0:T(8,128)S(1)}, f32[8,128]{1,0:T(8,128)S(1)}) custom-call(s32[2]{0:T(128)S(1)} %pad_add_fusion.here, bf16[64,131072]{1,0:T(8,128)(2,1)} %bitcast.43, bf16[64,131072]{1,0:T(8,128)(2,1)} %bitcast.44, bf16[64,131072]{1,0:T(8,128)(2,1)} %bitcast.45, bf16[64,131072]{1,0:T(8,128)(2,1)} %bitcast.46, ...), custom_call_target="tpu_custom_call" | custom-call | tf_op jit(solution)/shard_map/pallas_call | solution.py:111
  67.4 0.1 collective-permute-start.11
  67.5 29.9 %collective-permute-done.refs_21_.refs_4_.refs_5_.refs_6_.refs_7_.refs_2_.refs_3_.refs_12_.refs_13_.refs_1_ = f32[32,16384]{1,0:T(8,128)S(1)} collective-permute-done((f32[32,16384]{1,0:T(8,128)}, f32[32,16384]{1,0:T(8,128)S(1)}, u32[]{:S(2)}, u32[]{:S(2)}) %collective-permute-start) | collective-permute-done | bytes 2097184 | tf_op jit(solution)/shard_map/ppermute | solution.py:374
  97.4 3.1 %collective-permute-start.12 = (f32[32,16384]{1,0:T(8,128)S(1)}, f32[32,16384]{1,0:T(8,128)S(1)}, u32[]{:S(2)}, u32[]{:S(2)}) collective-permute-start(f32[32,16384]{1,0:T(8,128)S(1)} %get-tuple-element.67), channel_id=1, source_target_pairs={{0,12},{1,13},{2,14},{3,15},{4,0},{5,1},{6,2},{7,3},{8,4},{9,5},{1... | collective-permute-start | bytes 6291464 | tf_op jit(solution)/shard_map/ppermute | solution.py:374
  100.4 4.3 %collective-permute-done.6.refs_4_.refs_5_.refs_6_.refs_7_.refs_21_.refs_2_.refs_3_.refs_12_.refs_13_.refs_8_ = f32[32,16384]{1,0:T(8,128)S(1)} collective-permute-done((f32[32,16384]{1,0:T(8,128)}, f32[32,16384]{1,0:T(8,128)S(1)}, u32[]{:S(2)}, u32[]{:S(2)}) %collective-permute-start.6) | collective-permute-done | bytes 2097184 | tf_op jit(solution)/shard_map/ppermute | solution.py:374
  104.7 1.3 collective-permute-start.5
  106.0 3.4 %collective-permute-start.14 = (s32[1,8,8192]{2,1,0:T(8,128)S(1)}, s32[1,8,8192]{2,1,0:T(8,128)S(1)}, u32[]{:S(2)}, u32[]{:S(2)}) collective-permute-start(s32[1,8,8192]{2,1,0:T(8,128)S(1)} %copy-done.9), channel_id=1, source_target_pairs={{0,64},{16,80},{32,96},{48,112},{64,0},{80,16},{96,32},{112,48},{1... | collective-permute-start | bytes 786440 | tf_op jit(solution)/shard_map/ppermute | solution.py:378
  109.4 40.3 %collective-permute-done.11.refs_12_.refs_13_.refs_14_.refs_15_.refs_6_.refs_7_.refs_16_.refs_17_.refs_25_.refs_10_ = f32[32,16384]{1,0:T(8,128)S(1)} collective-permute-done((f32[32,16384]{1,0:T(8,128)S(1)}, f32[32,16384]{1,0:T(8,128)S(1)}, u32[]{:S(2)}, u32[]{:S(2)}) %collective-permute-start.11) | collective-permute-done | bytes 2097184 | tf_op jit(solution)/shard_map/ppermute | solution.py:374
  149.7 2.5 %collective-permute-start.13 = (s32[1,8,8192]{2,1,0:T(8,128)S(1)}, s32[1,8,8192]{2,1,0:T(8,128)S(1)}, u32[]{:S(2)}, u32[]{:S(2)}) collective-permute-start(s32[1,8,8192]{2,1,0:T(8,128)S(1)} %copy-done.9), channel_id=1, source_target_pairs={{0,96},{16,112},{32,0},{48,16},{64,32},{80,48},{96,64},{112,80},{1... | collective-permute-start | bytes 786440 | tf_op jit(solution)/shard_map/ppermute | solution.py:378
  152.2 1.3 copy-done.16
  153.5 2.1 shard_map.74
  155.7 0.1 collective-permute-start.17
  155.8 2.7 %collective-permute-start.18 = (f32[32,4096]{1,0:T(8,128)S(1)}, f32[32,4096]{1,0:T(8,128)S(1)}, u32[]{:S(2)}, u32[]{:S(2)}) collective-permute-start(f32[32,4096]{1,0:T(8,128)S(1)} %get-tuple-element.73), channel_id=1, source_target_pairs={{0,3},{1,0},{2,1},{3,2},{4,7},{5,4},{6,5},{7,6},{8,11},{9,8},{10,9... | collective-permute-start | bytes 1572872 | tf_op jit(solution)/shard_map/ppermute | solution.py:374
  158.5 1.6 copy-done.1
  160.1 1.6 copy-done.4
  161.6 2.2 shard_map.75
  163.8 0.1 collective-permute-start.15
  163.9 2.7 %collective-permute-start.16 = (f32[32,4096]{1,0:T(8,128)S(1)}, f32[32,4096]{1,0:T(8,128)S(1)}, u32[]{:S(2)}, u32[]{:S(2)}) collective-permute-start(f32[32,4096]{1,0:T(8,128)S(1)} %get-tuple-element.71), channel_id=1, source_target_pairs={{0,12},{1,13},{2,14},{3,15},{4,0},{5,1},{6,2},{7,3},{8,4},{9,5},{1... | collective-permute-start | bytes 1572872 | tf_op jit(solution)/shard_map/ppermute | solution.py:374
  166.6 1.4 collective-permute-done.17.refs_20_.refs_21_.refs_25_
  168.0 2.4 %shard_map.76 = (f32[64,2048]{1,0:T(8,128)S(1)}, f32[64,2048]{1,0:T(8,128)S(1)}, f32[8,128]{1,0:T(8,128)S(1)}) custom-call(s32[2]{0:T(128)S(1)} %pad_add_fusion.here, bf16[64,131072]{1,0:T(8,128)(2,1)} %bitcast.59, bf16[64,131072]{1,0:T(8,128)(2,1)} %bitcast.60, f32[32,16384]{1,0:T(8,128)S(1)} %copy-done.6, f32[32,16384]{1,0:T(8,128)S(1)} %copy-done.6, ...), custom_call_target="tpu_custom_call" | custom-call | tf_op jit(solution)/shard_map/pallas_call | solution.py:111
  170.4 0.1 collective-permute-start.25
  170.5 2.7 %collective-permute-start.26 = (f32[64,2048]{1,0:T(8,128)S(1)}, f32[64,2048]{1,0:T(8,128)S(1)}, u32[]{:S(2)}, u32[]{:S(2)}) collective-permute-start(f32[64,2048]{1,0:T(8,128)S(1)} %get-tuple-element.85), channel_id=1, source_target_pairs={{0,3},{1,0},{2,1},{3,2},{4,7},{5,4},{6,5},{7,6},{8,11},{9,8},{10,9... | collective-permute-start | bytes 1572872 | tf_op jit(solution)/shard_map/ppermute | solution.py:374
  173.2 2.4 %collective-permute-done.15.refs_20_.refs_21_.refs_25_ = f32[32,4096]{1,0:T(8,128)S(1)} collective-permute-done((f32[32,4096]{1,0:T(8,128)S(1)}, f32[32,4096]{1,0:T(8,128)S(1)}, u32[]{:S(2)}, u32[]{:S(2)}) %collective-permute-start.15) | collective-permute-done | bytes 524320 | tf_op jit(solution)/shard_map/ppermute | solution.py:374
  175.6 2.3 shard_map.77
  178.0 0.1 collective-permute-start.23
  178.1 2.7 %collective-permute-start.24 = (f32[64,2048]{1,0:T(8,128)S(1)}, f32[64,2048]{1,0:T(8,128)S(1)}, u32[]{:S(2)}, u32[]{:S(2)}) collective-permute-start(f32[64,2048]{1,0:T(8,128)S(1)} %get-tuple-element.83), channel_id=1, source_target_pairs={{0,12},{1,13},{2,14},{3,15},{4,0},{5,1},{6,2},{7,3},{8,4},{9,5},{1... | collective-permute-start | bytes 1572872 | tf_op jit(solution)/shard_map/ppermute | solution.py:374
  180.7 2.3 shard_map.78
  183.1 2.4 %shard_map.79 = (f32[64,2048]{1,0:T(8,128)S(1)}, f32[64,2048]{1,0:T(8,128)S(1)}, f32[8,128]{1,0:T(8,128)S(1)}) custom-call(s32[2]{0:T(128)S(1)} %pad_add_fusion.here, bf16[64,131072]{1,0:T(8,128)(2,1)} %bitcast.71, bf16[64,131072]{1,0:T(8,128)(2,1)} %bitcast.72, f32[32,16384]{1,0:T(8,128)S(1)} %copy-done.2, f32[32,16384]{1,0:T(8,128)S(1)} %copy-done.2, ...), custom_call_target="tpu_custom_call" | custom-call | tf_op jit(solution)/shard_map/pallas_call | solution.py:111
  185.4 0.1 collective-permute-start.19
  185.5 2.7 %collective-permute-start.20 = (f32[64,2048]{1,0:T(8,128)S(1)}, f32[64,2048]{1,0:T(8,128)S(1)}, u32[]{:S(2)}, u32[]{:S(2)}) collective-permute-start(f32[64,2048]{1,0:T(8,128)S(1)} %get-tuple-element.79), channel_id=1, source_target_pairs={{0,12},{1,13},{2,14},{3,15},{4,0},{5,1},{6,2},{7,3},{8,4},{9,5},{1... | collective-permute-start | bytes 1572872 | tf_op jit(solution)/shard_map/ppermute | solution.py:374
  188.2 0.7 collective-permute-done.23.refs_5_
  188.8 2.0 collective-permute-start.22
  190.9 6.8 %shard_map.80 = (f32[1,64,8192]{2,1,0:T(8,128)}, f32[8,4096]{1,0:T(8,128)S(1)}, f32[8,128]{1,0:T(8,128)S(1)}) custom-call(s32[2]{0:T(128)S(1)} %pad_add_fusion.here, bf16[64,131072]{1,0:T(8,128)(2,1)} %bitcast.75, f32[32,16384]{1,0:T(8,128)S(1)} %copy-done.2, f32[32,16384]{1,0:T(8,128)} %copy-done.3, ...), custom_call_target="tpu_custom_call" | custom-call | tf_op jit(solution)/shard_map/pallas_call | solution.py:111
  197.6 0.9 collective-permute-start.32
  198.5 2.2 collective-permute-done.19.refs_5_
  200.7 0.3 collective-permute-start.31
  201.0 1.1 collective-permute-start.30
  202.2 6.8 %shard_map.81 = (f32[1,64,8192]{2,1,0:T(8,128)}, f32[8,4096]{1,0:T(8,128)S(1)}, f32[8,128]{1,0:T(8,128)S(1)}) custom-call(s32[2]{0:T(128)S(1)} %pad_add_fusion.here, bf16[64,131072]{1,0:T(8,128)(2,1)} %bitcast.77, f32[32,16384]{1,0:T(8,128)S(1)} %copy-done.2, f32[32,16384]{1,0:T(8,128)} %copy-done.3, ...), custom_call_target="tpu_custom_call", output_to_operand_aliasing={{0}: (19, {})} | custom-call | tf_op jit(solution)/shard_map/pallas_call | solution.py:111
  209.0 0.9 collective-permute-start.29
  209.8 1.5 collective-permute-start.28
  211.4 4.0 %shard_map.82 = (f32[64,4096]{1,0:T(8,128)S(1)}, f32[8,128]{1,0:T(8,128)S(1)}) custom-call(s32[2]{0:T(128)S(1)} %pad_add_fusion.here, f32[8,4096]{1,0:T(8,128)S(1)} %get-tuple-element.90.refs_0_, f32[8,4096]{1,0:T(8,128)S(1)} %collective-permute-done.30.refs_1_, f32[8,4096]{1,0:T(8,128)S(1)} %collective-permute-done.31.refs_2_, ...), custom_call_target="tpu_custom_call" | custom-call | tf_op jit(solution)/shard_map/pallas_call | solution.py:111
  215.4 7.8 %collective-permute-start.34 = (f32[64,4096]{1,0:T(8,128)S(1)}, f32[64,4096]{1,0:T(8,128)S(1)}, u32[]{:S(2)}, u32[]{:S(2)}) collective-permute-start(f32[64,4096]{1,0:T(8,128)S(1)} %get-tuple-element.94.refs_0_), channel_id=1, source_target_pairs={{0,16},{16,0},{32,48},{48,32},{64,80},{80,64},{96,112},{112,96},{1... | collective-permute-start | bytes 3145736 | tf_op jit(solution)/shard_map/ppermute | solution.py:384
  223.2 4.0 %shard_map.83 = (f32[64,4096]{1,0:T(8,128)S(1)}, f32[8,128]{1,0:T(8,128)S(1)}) custom-call(s32[2]{0:T(128)S(1)} %pad_add_fusion.here, f32[8,4096]{1,0:T(8,128)S(1)} %get-tuple-element.89.refs_0_, f32[8,4096]{1,0:T(8,128)S(1)} %collective-permute-done.27.refs_1_, f32[8,4096]{1,0:T(8,128)S(1)} %collective-permute-done.28.refs_2_, ...), custom_call_target="tpu_custom_call" | custom-call | tf_op jit(solution)/shard_map/pallas_call | solution.py:111
  227.2 2.1 collective-permute-start.33
  229.4 2.2 shard_map.84
  231.6 0.1 collective-permute-done.33.refs_1_
  231.6 2.2 shard_map.85
  (59 shorter events, 0.1 us)
Async XLA Ops:
  0.7 6.9 %copy-start.8 = (s32[1,8,8192]{2,1,0:T(8,128)S(1)}, s32[1,8,8192]{2,1,0:T(8,128)}, u32[]{:S(2)}) copy-start(s32[1,8,8192]{2,1,0:T(8,128)} %refs_4_.3) | copy-start | bytes 786436
  4.1 48.4 %collective-permute-start.2 = (f32[32,16384]{1,0:T(8,128)S(1)}, f32[32,16384]{1,0:T(8,128)}, u32[]{:S(2)}, u32[]{:S(2)}) collective-permute-start(f32[32,16384]{1,0:T(8,128)S(1)} %get-tuple-element.55), channel_id=1, source_target_pairs={{0,1},{1,2},{2,3},{3,0},{4,5},{5,6},{6,7},{7,4},{8,9},{9,10},{10,1... | collective-permute-start | bytes 6291464 | tf_op jit(solution)/shard_map/ppermute | solution.py:374
  6.3 47.9 %collective-permute-start.3 = (f32[32,16384]{1,0:T(8,128)S(1)}, f32[32,16384]{1,0:T(8,128)}, u32[]{:S(2)}, u32[]{:S(2)}) collective-permute-start(f32[32,16384]{1,0:T(8,128)S(1)} %get-tuple-element.56), channel_id=1, source_target_pairs={{0,3},{1,0},{2,1},{3,2},{4,7},{5,4},{6,5},{7,6},{8,11},{9,8},{10,9... | collective-permute-start | bytes 6291464 | tf_op jit(solution)/shard_map/ppermute | solution.py:374
  7.6 12.9 %collective-permute-start.10 = (s32[1,8,8192]{2,1,0:T(8,128)S(1)}, s32[1,8,8192]{2,1,0:T(8,128)S(1)}, u32[]{:S(2)}, u32[]{:S(2)}) collective-permute-start(s32[1,8,8192]{2,1,0:T(8,128)S(1)} %copy-done.8), channel_id=1, source_target_pairs={{0,32},{16,48},{32,64},{48,80},{64,96},{80,112},{96,0},{112,16},{1... | collective-permute-start | bytes 786440 | tf_op jit(solution)/shard_map/ppermute | solution.py:378
  12.8 48.6 %collective-permute-start.8 = (f32[32,16384]{1,0:T(8,128)S(1)}, f32[32,16384]{1,0:T(8,128)}, u32[]{:S(2)}, u32[]{:S(2)}) collective-permute-start(f32[32,16384]{1,0:T(8,128)S(1)} %get-tuple-element.63), channel_id=1, source_target_pairs={{0,4},{1,5},{2,6},{3,7},{4,8},{5,9},{6,10},{7,11},{8,12},{9,13},{1... | collective-permute-start | bytes 6291464 | tf_op jit(solution)/shard_map/ppermute | solution.py:374
  14.2 48.6 %collective-permute-start.9 = (f32[32,16384]{1,0:T(8,128)S(1)}, f32[32,16384]{1,0:T(8,128)}, u32[]{:S(2)}, u32[]{:S(2)}) collective-permute-start(f32[32,16384]{1,0:T(8,128)S(1)} %get-tuple-element.64), channel_id=1, source_target_pairs={{0,12},{1,13},{2,14},{3,15},{4,0},{5,1},{6,2},{7,3},{8,4},{9,5},{1... | collective-permute-start | bytes 6291464 | tf_op jit(solution)/shard_map/ppermute | solution.py:374
  20.5 42.3 %copy-start.10 = (s32[1,8,8192]{2,1,0:T(8,128)}, s32[1,8,8192]{2,1,0:T(8,128)S(1)}, u32[]{:S(2)}) copy-start(s32[1,8,8192]{2,1,0:T(8,128)S(1)} %collective-permute-done.10.refs_13_.refs_5_) | copy-start | bytes 786436
  20.5 76.8 %collective-permute-start = (f32[32,16384]{1,0:T(8,128)}, f32[32,16384]{1,0:T(8,128)S(1)}, u32[]{:S(2)}, u32[]{:S(2)}) collective-permute-start(f32[32,16384]{1,0:T(8,128)} %get-tuple-element.53), channel_id=1, source_target_pairs={{0,1},{1,2},{2,3},{3,0},{4,5},{5,6},{6,7},{7,4},{8,9},{9,10},{10,1... | collective-permute-start | bytes 6291464 | tf_op jit(solution)/shard_map/ppermute | solution.py:374
  52.5 47.9 %collective-permute-start.1 = (f32[32,16384]{1,0:T(8,128)}, f32[32,16384]{1,0:T(8,128)S(1)}, u32[]{:S(2)}, u32[]{:S(2)}) collective-permute-start(f32[32,16384]{1,0:T(8,128)} %get-tuple-element.54), channel_id=1, source_target_pairs={{0,3},{1,0},{2,1},{3,2},{4,7},{5,4},{6,5},{7,6},{8,11},{9,8},{10,9... | collective-permute-start | bytes 6291464 | tf_op jit(solution)/shard_map/ppermute | solution.py:374
  54.1 50.6 %collective-permute-start.6 = (f32[32,16384]{1,0:T(8,128)}, f32[32,16384]{1,0:T(8,128)S(1)}, u32[]{:S(2)}, u32[]{:S(2)}) collective-permute-start(f32[32,16384]{1,0:T(8,128)} %get-tuple-element.61), channel_id=1, source_target_pairs={{0,4},{1,5},{2,6},{3,7},{4,8},{5,9},{6,10},{7,11},{8,12},{9,13},{1... | collective-permute-start | bytes 6291464 | tf_op jit(solution)/shard_map/ppermute | solution.py:374
  60.0 1.3 copy-start.14
  61.3 44.7 %collective-permute-start.7 = (f32[32,16384]{1,0:T(8,128)}, f32[32,16384]{1,0:T(8,128)S(1)}, u32[]{:S(2)}, u32[]{:S(2)}) collective-permute-start(f32[32,16384]{1,0:T(8,128)} %get-tuple-element.62), channel_id=1, source_target_pairs={{0,12},{1,13},{2,14},{3,15},{4,0},{5,1},{6,2},{7,3},{8,4},{9,5},{1... | collective-permute-start | bytes 6291464 | tf_op jit(solution)/shard_map/ppermute | solution.py:374
  62.8 43.2 %copy-start.9 = (s32[1,8,8192]{2,1,0:T(8,128)S(1)}, s32[1,8,8192]{2,1,0:T(8,128)}, u32[]{:S(2)}) copy-start(s32[1,8,8192]{2,1,0:T(8,128)} %refs_4_.3) | copy-start | bytes 786436
  67.4 82.3 %collective-permute-start.11 = (f32[32,16384]{1,0:T(8,128)S(1)}, f32[32,16384]{1,0:T(8,128)S(1)}, u32[]{:S(2)}, u32[]{:S(2)}) collective-permute-start(f32[32,16384]{1,0:T(8,128)S(1)} %get-tuple-element.66), channel_id=1, source_target_pairs={{0,4},{1,5},{2,6},{3,7},{4,8},{5,9},{6,10},{7,11},{8,12},{9,13},{1... | collective-permute-start | bytes 6291464 | tf_op jit(solution)/shard_map/ppermute | solution.py:374
  97.4 56.1 %copy-start = (f32[32,16384]{1,0:T(8,128)}, f32[32,16384]{1,0:T(8,128)S(1)}, u32[]{:S(2)}) copy-start(f32[32,16384]{1,0:T(8,128)S(1)} %collective-permute-done.refs_21_.refs_4_.refs_5_.refs_6_.refs_7_.refs_2_.refs_3_.refs_12_.refs_13_.refs_1_) | copy-start | bytes 6291460
  97.4 54.8 %collective-permute-start.12 = (f32[32,16384]{1,0:T(8,128)S(1)}, f32[32,16384]{1,0:T(8,128)S(1)}, u32[]{:S(2)}, u32[]{:S(2)}) collective-permute-start(f32[32,16384]{1,0:T(8,128)S(1)} %get-tuple-element.67), channel_id=1, source_target_pairs={{0,12},{1,13},{2,14},{3,15},{4,0},{5,1},{6,2},{7,3},{8,4},{9,5},{1... | collective-permute-start | bytes 6291464 | tf_op jit(solution)/shard_map/ppermute | solution.py:374
  100.4 53.1 %copy-start.3 = (f32[32,16384]{1,0:T(8,128)}, f32[32,16384]{1,0:T(8,128)S(1)}, u32[]{:S(2)}) copy-start(f32[32,16384]{1,0:T(8,128)S(1)} %collective-permute-done.1.refs_22_.refs_8_.refs_9_.refs_10_.refs_11_.refs_4_.refs_5_.refs_14_.refs_15_.refs_2_) | copy-start | bytes 6291460
  100.4 58.0 %collective-permute-start.4 = (f32[32,16384]{1,0:T(8,128)}, f32[32,16384]{1,0:T(8,128)}, u32[]{:S(2)}, u32[]{:S(2)}) collective-permute-start(f32[32,16384]{1,0:T(8,128)} %copy-done.14), channel_id=1, source_target_pairs={{0,1},{1,2},{2,3},{3,0},{4,5},{5,6},{6,7},{7,4},{8,9},{9,10},{10,1... | collective-permute-start | bytes 6291464 | tf_op jit(solution)/shard_map/ppermute | solution.py:374
  104.7 50.9 %copy-start.5 = (f32[32,16384]{1,0:T(8,128)}, f32[32,16384]{1,0:T(8,128)S(1)}, u32[]{:S(2)}) copy-start(f32[32,16384]{1,0:T(8,128)S(1)} %collective-permute-done.6.refs_4_.refs_5_.refs_6_.refs_7_.refs_21_.refs_2_.refs_3_.refs_12_.refs_13_.refs_8_) | copy-start | bytes 6291460
  104.7 53.7 %collective-permute-start.5 = (f32[32,16384]{1,0:T(8,128)S(1)}, f32[32,16384]{1,0:T(8,128)}, u32[]{:S(2)}, u32[]{:S(2)}) collective-permute-start(f32[32,16384]{1,0:T(8,128)S(1)} %get-tuple-element.60), channel_id=1, source_target_pairs={{0,3},{1,0},{2,1},{3,2},{4,7},{5,4},{6,5},{7,6},{8,11},{9,8},{10,9... | collective-permute-start | bytes 6291464 | tf_op jit(solution)/shard_map/ppermute | solution.py:374
  106.0 49.7 %copy-start.7 = (f32[32,16384]{1,0:T(8,128)}, f32[32,16384]{1,0:T(8,128)S(1)}, u32[]{:S(2)}) copy-start(f32[32,16384]{1,0:T(8,128)S(1)} %collective-permute-done.7.refs_8_.refs_9_.refs_10_.refs_11_.refs_22_.refs_4_.refs_5_.refs_14_.refs_15_) | copy-start | bytes 6291460
  106.0 49.8 %collective-permute-start.14 = (s32[1,8,8192]{2,1,0:T(8,128)S(1)}, s32[1,8,8192]{2,1,0:T(8,128)S(1)}, u32[]{:S(2)}, u32[]{:S(2)}) collective-permute-start(s32[1,8,8192]{2,1,0:T(8,128)S(1)} %copy-done.9), channel_id=1, source_target_pairs={{0,64},{16,80},{32,96},{48,112},{64,0},{80,16},{96,32},{112,48},{1... | collective-permute-start | bytes 786440 | tf_op jit(solution)/shard_map/ppermute | solution.py:378
  149.7 2.5 %copy-start.15 = (f32[32,16384]{1,0:T(8,128)}, f32[32,16384]{1,0:T(8,128)S(1)}, u32[]{:S(2)}) copy-start(f32[32,16384]{1,0:T(8,128)S(1)} %collective-permute-done.11.refs_12_.refs_13_.refs_14_.refs_15_.refs_6_.refs_7_.refs_16_.refs_17_.refs_25_.refs_10_) | copy-start | bytes 6291460
  149.7 8.8 %collective-permute-start.13 = (s32[1,8,8192]{2,1,0:T(8,128)S(1)}, s32[1,8,8192]{2,1,0:T(8,128)S(1)}, u32[]{:S(2)}, u32[]{:S(2)}) collective-permute-start(s32[1,8,8192]{2,1,0:T(8,128)S(1)} %copy-done.9), channel_id=1, source_target_pairs={{0,96},{16,112},{32,0},{48,16},{64,32},{80,48},{96,64},{112,80},{1... | collective-permute-start | bytes 786440 | tf_op jit(solution)/shard_map/ppermute | solution.py:378
  152.2 1.3 copy-start.16
  155.7 12.3 %collective-permute-start.17 = (f32[32,4096]{1,0:T(8,128)S(1)}, f32[32,4096]{1,0:T(8,128)S(1)}, u32[]{:S(2)}, u32[]{:S(2)}) collective-permute-start(f32[32,4096]{1,0:T(8,128)S(1)} %get-tuple-element.72), channel_id=1, source_target_pairs={{0,1},{1,2},{2,3},{3,0},{4,5},{5,6},{6,7},{7,4},{8,9},{9,10},{10,1... | collective-permute-start | bytes 1572872 | tf_op jit(solution)/shard_map/ppermute | solution.py:374
  155.8 12.3 %collective-permute-start.18 = (f32[32,4096]{1,0:T(8,128)S(1)}, f32[32,4096]{1,0:T(8,128)S(1)}, u32[]{:S(2)}, u32[]{:S(2)}) collective-permute-start(f32[32,4096]{1,0:T(8,128)S(1)} %get-tuple-element.73), channel_id=1, source_target_pairs={{0,3},{1,0},{2,1},{3,2},{4,7},{5,4},{6,5},{7,6},{8,11},{9,8},{10,9... | collective-permute-start | bytes 1572872 | tf_op jit(solution)/shard_map/ppermute | solution.py:374
  158.5 1.6 copy-start.1
  160.0 1.6 copy-start.4
  161.6 6.4 %copy-start.6 = (f32[32,16384]{1,0:T(8,128)S(1)}, f32[32,16384]{1,0:T(8,128)}, u32[]{:S(2)}) copy-start(f32[32,16384]{1,0:T(8,128)} %copy-done.5) | copy-start | bytes 6291460
  163.8 11.8 %collective-permute-start.15 = (f32[32,4096]{1,0:T(8,128)S(1)}, f32[32,4096]{1,0:T(8,128)S(1)}, u32[]{:S(2)}, u32[]{:S(2)}) collective-permute-start(f32[32,4096]{1,0:T(8,128)S(1)} %get-tuple-element.70), channel_id=1, source_target_pairs={{0,4},{1,5},{2,6},{3,7},{4,8},{5,9},{6,10},{7,11},{8,12},{9,13},{1... | collective-permute-start | bytes 1572872 | tf_op jit(solution)/shard_map/ppermute | solution.py:374
  163.9 11.7 %collective-permute-start.16 = (f32[32,4096]{1,0:T(8,128)S(1)}, f32[32,4096]{1,0:T(8,128)S(1)}, u32[]{:S(2)}, u32[]{:S(2)}) collective-permute-start(f32[32,4096]{1,0:T(8,128)S(1)} %get-tuple-element.71), channel_id=1, source_target_pairs={{0,12},{1,13},{2,14},{3,15},{4,0},{5,1},{6,2},{7,3},{8,4},{9,5},{1... | collective-permute-start | bytes 1572872 | tf_op jit(solution)/shard_map/ppermute | solution.py:374
  168.0 7.6 %copy-start.2 = (f32[32,16384]{1,0:T(8,128)S(1)}, f32[32,16384]{1,0:T(8,128)}, u32[]{:S(2)}) copy-start(f32[32,16384]{1,0:T(8,128)} %copy-done) | copy-start | bytes 6291460
  170.4 15.1 %collective-permute-start.25 = (f32[64,2048]{1,0:T(8,128)S(1)}, f32[64,2048]{1,0:T(8,128)S(1)}, u32[]{:S(2)}, u32[]{:S(2)}) collective-permute-start(f32[64,2048]{1,0:T(8,128)S(1)} %get-tuple-element.84), channel_id=1, source_target_pairs={{0,1},{1,2},{2,3},{3,0},{4,5},{5,6},{6,7},{7,4},{8,9},{9,10},{10,1... | collective-permute-start | bytes 1572872 | tf_op jit(solution)/shard_map/ppermute | solution.py:374
  170.5 17.6 %collective-permute-start.26 = (f32[64,2048]{1,0:T(8,128)S(1)}, f32[64,2048]{1,0:T(8,128)S(1)}, u32[]{:S(2)}, u32[]{:S(2)}) collective-permute-start(f32[64,2048]{1,0:T(8,128)S(1)} %get-tuple-element.85), channel_id=1, source_target_pairs={{0,3},{1,0},{2,1},{3,2},{4,7},{5,4},{6,5},{7,6},{8,11},{9,8},{10,9... | collective-permute-start | bytes 1572872 | tf_op jit(solution)/shard_map/ppermute | solution.py:374
  178.0 10.9 %collective-permute-start.23 = (f32[64,2048]{1,0:T(8,128)S(1)}, f32[64,2048]{1,0:T(8,128)S(1)}, u32[]{:S(2)}, u32[]{:S(2)}) collective-permute-start(f32[64,2048]{1,0:T(8,128)S(1)} %get-tuple-element.82), channel_id=1, source_target_pairs={{0,4},{1,5},{2,6},{3,7},{4,8},{5,9},{6,10},{7,11},{8,12},{9,13},{1... | collective-permute-start | bytes 1572872 | tf_op jit(solution)/shard_map/ppermute | solution.py:374
  178.1 12.8 %collective-permute-start.24 = (f32[64,2048]{1,0:T(8,128)S(1)}, f32[64,2048]{1,0:T(8,128)S(1)}, u32[]{:S(2)}, u32[]{:S(2)}) collective-permute-start(f32[64,2048]{1,0:T(8,128)S(1)} %get-tuple-element.83), channel_id=1, source_target_pairs={{0,12},{1,13},{2,14},{3,15},{4,0},{5,1},{6,2},{7,3},{8,4},{9,5},{1... | collective-permute-start | bytes 1572872 | tf_op jit(solution)/shard_map/ppermute | solution.py:374
  183.0 7.8 %copy-start.12 = (bf16[64,256]{1,0:T(8,128)(2,1)S(1)}, bf16[64,256]{1,0:T(8,128)(2,1)}, u32[]{:S(2)}) copy-start(bf16[64,256]{1,0:T(8,128)(2,1)} %constant.25.clone.refs_17_.refs_8_) | copy-start | bytes 98308
  183.0 7.8 %copy-start.13 = (bf16[64,256]{1,0:T(8,128)(2,1)S(1)}, bf16[64,256]{1,0:T(8,128)(2,1)}, u32[]{:S(2)}) copy-start(bf16[64,256]{1,0:T(8,128)(2,1)} %constant.24.clone.refs_16_) | copy-start | bytes 98308
  185.4 15.3 %collective-permute-start.19 = (f32[64,2048]{1,0:T(8,128)S(1)}, f32[64,2048]{1,0:T(8,128)S(1)}, u32[]{:S(2)}, u32[]{:S(2)}) collective-permute-start(f32[64,2048]{1,0:T(8,128)S(1)} %get-tuple-element.78), channel_id=1, source_target_pairs={{0,4},{1,5},{2,6},{3,7},{4,8},{5,9},{6,10},{7,11},{8,12},{9,13},{1... | collective-permute-start | bytes 1572872 | tf_op jit(solution)/shard_map/ppermute | solution.py:374
  185.5 15.5 %collective-permute-start.20 = (f32[64,2048]{1,0:T(8,128)S(1)}, f32[64,2048]{1,0:T(8,128)S(1)}, u32[]{:S(2)}, u32[]{:S(2)}) collective-permute-start(f32[64,2048]{1,0:T(8,128)S(1)} %get-tuple-element.79), channel_id=1, source_target_pairs={{0,12},{1,13},{2,14},{3,15},{4,0},{5,1},{6,2},{7,3},{8,4},{9,5},{1... | collective-permute-start | bytes 1572872 | tf_op jit(solution)/shard_map/ppermute | solution.py:374
  188.2 14.0 %collective-permute-start.21 = (f32[64,2048]{1,0:T(8,128)S(1)}, f32[64,2048]{1,0:T(8,128)S(1)}, u32[]{:S(2)}, u32[]{:S(2)}) collective-permute-start(f32[64,2048]{1,0:T(8,128)S(1)} %get-tuple-element.80), channel_id=1, source_target_pairs={{0,1},{1,2},{2,3},{3,0},{4,5},{5,6},{6,7},{7,4},{8,9},{9,10},{10,1... | collective-permute-start | bytes 1572872 | tf_op jit(solution)/shard_map/ppermute | solution.py:374
  188.8 13.3 %collective-permute-start.22 = (f32[64,2048]{1,0:T(8,128)S(1)}, f32[64,2048]{1,0:T(8,128)S(1)}, u32[]{:S(2)}, u32[]{:S(2)}) collective-permute-start(f32[64,2048]{1,0:T(8,128)S(1)} %get-tuple-element.81), channel_id=1, source_target_pairs={{0,3},{1,0},{2,1},{3,2},{4,7},{5,4},{6,5},{7,6},{8,11},{9,8},{10,9... | collective-permute-start | bytes 1572872 | tf_op jit(solution)/shard_map/ppermute | solution.py:374
  197.6 13.7 %collective-permute-start.32 = (f32[8,4096]{1,0:T(8,128)S(1)}, f32[8,4096]{1,0:T(8,128)S(1)}, u32[]{:S(2)}, u32[]{:S(2)}) collective-permute-start(f32[8,4096]{1,0:T(8,128)S(1)} %get-tuple-element.90.refs_0_), channel_id=1, source_target_pairs={{0,64},{16,80},{32,96},{48,112},{64,0},{80,16},{96,32},{112,48},{1... | collective-permute-start | bytes 393224 | tf_op jit(solution)/shard_map/ppermute | solution.py:378
  200.7 10.7 %collective-permute-start.31 = (f32[8,4096]{1,0:T(8,128)S(1)}, f32[8,4096]{1,0:T(8,128)S(1)}, u32[]{:S(2)}, u32[]{:S(2)}) collective-permute-start(f32[8,4096]{1,0:T(8,128)S(1)} %get-tuple-element.90.refs_0_), channel_id=1, source_target_pairs={{0,96},{16,112},{32,0},{48,16},{64,32},{80,48},{96,64},{112,80},{1... | collective-permute-start | bytes 393224 | tf_op jit(solution)/shard_map/ppermute | solution.py:378
  201.0 10.4 %collective-permute-start.30 = (f32[8,4096]{1,0:T(8,128)S(1)}, f32[8,4096]{1,0:T(8,128)S(1)}, u32[]{:S(2)}, u32[]{:S(2)}) collective-permute-start(f32[8,4096]{1,0:T(8,128)S(1)} %get-tuple-element.90.refs_0_), channel_id=1, source_target_pairs={{0,32},{16,48},{32,64},{48,80},{64,96},{80,112},{96,0},{112,16},{1... | collective-permute-start | bytes 393224 | tf_op jit(solution)/shard_map/ppermute | solution.py:378
  202.2 9.2 %copy-start.11 = (s32[1,8,8192]{2,1,0:T(8,128)S(1)}, s32[1,8,8192]{2,1,0:T(8,128)}, u32[]{:S(2)}) copy-start(s32[1,8,8192]{2,1,0:T(8,128)} %copy-done.10) | copy-start | bytes 786436
  209.0 14.3 %collective-permute-start.29 = (f32[8,4096]{1,0:T(8,128)S(1)}, f32[8,4096]{1,0:T(8,128)S(1)}, u32[]{:S(2)}, u32[]{:S(2)}) collective-permute-start(f32[8,4096]{1,0:T(8,128)S(1)} %get-tuple-element.89.refs_0_), channel_id=1, source_target_pairs={{0,64},{16,80},{32,96},{48,112},{64,0},{80,16},{96,32},{112,48},{1... | collective-permute-start | bytes 393224 | tf_op jit(solution)/shard_map/ppermute | solution.py:378
  209.8 13.4 %collective-permute-start.28 = (f32[8,4096]{1,0:T(8,128)S(1)}, f32[8,4096]{1,0:T(8,128)S(1)}, u32[]{:S(2)}, u32[]{:S(2)}) collective-permute-start(f32[8,4096]{1,0:T(8,128)S(1)} %get-tuple-element.89.refs_0_), channel_id=1, source_target_pairs={{0,96},{16,112},{32,0},{48,16},{64,32},{80,48},{96,64},{112,80},{1... | collective-permute-start | bytes 393224 | tf_op jit(solution)/shard_map/ppermute | solution.py:378
  211.4 11.8 %collective-permute-start.27 = (f32[8,4096]{1,0:T(8,128)S(1)}, f32[8,4096]{1,0:T(8,128)S(1)}, u32[]{:S(2)}, u32[]{:S(2)}) collective-permute-start(f32[8,4096]{1,0:T(8,128)S(1)} %get-tuple-element.89.refs_0_), channel_id=1, source_target_pairs={{0,32},{16,48},{32,64},{48,80},{64,96},{80,112},{96,0},{112,16},{1... | collective-permute-start | bytes 393224 | tf_op jit(solution)/shard_map/ppermute | solution.py:378
  215.4 13.9 %collective-permute-start.34 = (f32[64,4096]{1,0:T(8,128)S(1)}, f32[64,4096]{1,0:T(8,128)S(1)}, u32[]{:S(2)}, u32[]{:S(2)}) collective-permute-start(f32[64,4096]{1,0:T(8,128)S(1)} %get-tuple-element.94.refs_0_), channel_id=1, source_target_pairs={{0,16},{16,0},{32,48},{48,32},{64,80},{80,64},{96,112},{112,96},{1... | collective-permute-start | bytes 3145736 | tf_op jit(solution)/shard_map/ppermute | solution.py:384
  227.2 4.4 %collective-permute-start.33 = (f32[64,4096]{1,0:T(8,128)S(1)}, f32[64,4096]{1,0:T(8,128)S(1)}, u32[]{:S(2)}, u32[]{:S(2)}) collective-permute-start(f32[64,4096]{1,0:T(8,128)S(1)} %get-tuple-element.93.refs_0_), channel_id=1, source_target_pairs={{0,16},{16,0},{32,48},{48,32},{64,80},{80,64},{96,112},{112,96},{1... | collective-permute-start | bytes 3145736 | tf_op jit(solution)/shard_map/ppermute | solution.py:384

commit v5 on v4

--- a/solution.py
+++ b/solution.py
@@ -13,12 +13,14 @@
 SIDE = 4
 TILE = 1024
 CHUNK = 256
+FINE, BROAD = 512, 1024
 PARTS = (2, 2)
-TILE = 1024
-CHUNK = 256
-WIDTH = 2048
-CHUNKS = (2048, 2048)
-VMEM_LIMIT = 48 * 1024 * 1024
+AXES = (0, 0, 1, 1, 1, 1)
+LAG = (2, 2, 2, 2, 2, 2)
+PLACES_WITH = ((1, 0), (1, 0), (1, 1))
+STEPS = (1, -1, 2)
+TAIL = ("f0", "f1", "s0", "j0", "s1", "j1")
+VMEM_LIMIT = 40 * 1024 * 1024
 F32 = jnp.float32
 BF16 = jnp.bfloat16
 
@@ -234,7 +236,7 @@
 
 
 def settle(grad_of, momentum, positions, forward, backward, fresh, values):
-    for at in range(0, TILE, CHUNK):
+    for at in range(0, fresh.shape[2], CHUNK):
         col = slice(at, at + CHUNK)
         moment = 0.9 * momentum[0, :, col] + grad_of(col)
         coeff = product(forward, moment)
@@ -251,21 +253,22 @@
 
 
 class Part:
-    def __init__(self, pair, first, n):
-        self.pair, self.first, self.n = pair, first, n
-        self.steps, self.spans = 2 * n, 2 * n * TILE
+    def __init__(self, pair, first, width, tile):
+        self.pair, self.tile = pair, tile
+        self.first, self.n, self.count = first // tile, width // tile, pair[0].width // tile
+        self.steps, self.spans = 2 * self.n, 2 * width
 
     def place(self, i):
-        return jnp.where(i < self.n, i, i - self.n + self.pair[0].count) + self.first
+        return jnp.where(i < self.n, i, i - self.n + self.count) + self.first
 
     def columns(self, rows):
-        return pl.BlockSpec((1, rows, TILE), lambda i, here: (0, 0, self.place(i)))
+        return pl.BlockSpec((1, rows, self.tile), lambda i, here: (0, 0, self.place(i)))
 
     def result(self):
-        return pl.BlockSpec((BLOCK, TILE), lambda i, here: (0, self.place(i)))
+        return pl.BlockSpec((BLOCK, self.tile), lambda i, here: (0, self.place(i)))
 
     def compact(self, rows):
-        return pl.BlockSpec((rows, TILE), lambda i, here: (0, i))
+        return pl.BlockSpec((rows, self.tile), lambda i, here: (0, i))
 
 
 def finish(line, piece, partials, momentum, positions, got, tables, so_far):
@@ -278,17 +281,18 @@
             return jnp.minimum(i, n - 1) if number == 0 else jnp.maximum(i - n, 0)
 
         def part(i, here, half=half, tile=tile):
-            return 0, half.column(here, 0, half.second(here, 0)) + piece.first + tile(i)
+            target = half.column(here, 0, half.second(here, 0)) * (TILE // piece.tile)
+            return 0, target + piece.first + tile(i)
 
         def message(i, here, half=half, tile=tile):
-            return 0, half.second(here, 0) * half.count + piece.first + tile(i)
+            return 0, half.second(here, 0) * piece.count + piece.first + tile(i)
 
         def flat(i, here, tile=tile):
             return 0, tile(i)
 
-        specs += [pl.BlockSpec((BLOCK, TILE), part)]
-        specs += [pl.BlockSpec((HALF, TILE), message)] * 4
-        specs += [pl.BlockSpec((BLOCK, TILE), flat)] * 2
+        specs += [pl.BlockSpec((BLOCK, piece.tile), part)]
+        specs += [pl.BlockSpec((HALF, piece.tile), message)] * 4
+        specs += [pl.BlockSpec((BLOCK, piece.tile), flat)] * 2
     ins += [momentum, positions, *tables]
     specs += [piece.columns(BLOCK), piece.columns(KEEP)] + [whole(BLOCK, 4 * BLOCK)] * 2
     aliases = {}
@@ -334,10 +338,10 @@
 def spread(line, piece, lists, places, table):
     def body(here, *refs):
         backward, out = refs[-2:]
-        for at in range(0, TILE, CHUNK):
+        for at in range(0, piece.tile, CHUNK):
             col = slice(at, at + CHUNK)
             parts = [dense(refs[k][:, col], refs[4 + k][0, :, col]) for k in range(4)]
-            out[:, col] = product(backward, (parts[0] + parts[3]) + (parts[1] + parts[2]))
+            out[:, col] = product(backward, (parts[0] + parts[1 + STEPS.index(2)]) + (parts[1 + STEPS.index(1)] + parts[1 + STEPS.index(-1)]))
 
     return line.call(
         body, piece.steps, [*lists, *places, table],
@@ -395,51 +399,57 @@
     here = jnp.stack([me // SIDE, lax.rem(me, SIDE)]).astype(jnp.int32)
     tables = tuple(jnp.asarray(part) for part in dct_parts())
     line = Line(here)
+    places = [positions] + [along_z(positions, step) for step in STEPS]
     width = spans // 2
     pair = (Half(True, 0, width, spans), Half(False, width, width, spans))
-    pieces, first = [], 0
-    for n in PARTS:
-        pieces.append(Part(pair, first, n))
-        first += n
+    ends = [TILE * sum(PARTS[:number]) for number in range(len(PARTS) + 1)]
+    spaces = list(zip(ends, ends[1:]))
     got, sent = {}, []
 
     def each(stage, second, send):
+        number = len(sent)
         out = [None, None]
-        for axis in range(2):
+        for axis in (AXES[number], 1 - AXES[number]):
             h = 1 - axis if second else axis
-            line.arrived = sent[-2][axis] if len(sent) >= 2 else []
+            line.arrived = sent[number - LAG[number]][axis] if number >= LAG[number] else []
             out[h] = both(axis == 0, send(pair[h], h))
         line.arrived = []
         got[stage] = out
-        sent.append(out[::-1] if second else out)
+        messages = out[::-1] if second else out
+        sent.append([
+            messages[axis] + [p for p, w in zip(places[1:], PLACES_WITH) if w == (number, axis)]
+            for axis in range(2)
+        ])
 
     def before(h, *stages):
         return sum((got[stage][h] for stage in stages), [])
 
-    places = [positions] + [along_z(positions, step) for step in (1, -1, 2)]
     each("far", False, lambda half, h: send_far(line, half, flat))
     each("raw", False, lambda half, h: send_raw(line, half, flat))
-    sent[0] = [sent[0][0], sent[0][1] + places[1:2]]
     each("near", False, lambda half, h: send_near(line, half, flat, *before(h, "far")))
-    sent[1] = [sent[1][0], sent[1][1] + places[2:]]
     each("far2", True, lambda half, h: send_far2(line, half, flat, before(h, "raw", "near")))
-    for number, piece in enumerate(pieces):
+    for number, (first, end) in enumerate(spaces):
         each(
             number, True,
             lambda half, h: send_near2(
-                line, half, flat, before(h, "raw", "near"), before(h, "far2"), piece.first, piece.n
+                line, half, flat, before(h, "raw", "near"), before(h, "far2"), first // TILE, (end - first) // TILE
             ),
         )
     fresh = update = None
-    lists, mine = [], []
-    for number, piece in enumerate(pieces):
-        full = [before(h, "raw", "near", number) for h in range(2)]
-        fresh, own = finish(line, piece, flat, momentum, positions, full, tables, fresh)
-        lists.append([own] + [along_z(own, step) for step in (1, -1, 2)])
-    for piece, four in zip(pieces, lists):
-        mine.append(spread(line, piece, four, places, tables[1]))
-    for piece, part in zip(pieces, mine):
-        update = join(line, piece, part, other_core(part), spans, update)
+    lists, mine = {}, {}
+    for what, number in TAIL:
+        number = int(number)
+        first, end = spaces[number]
+        piece = Part(pair, first, end - first, dict(f=FINE, s=TILE, j=BROAD)[what])
+        if what == "f":
+            full = [before(h, "raw", "near", number) for h in range(2)]
+            fresh, own = finish(line, piece, flat, momentum, positions, full, tables, fresh)
+            lists[number] = [own] + [along_z(own, step) for step in STEPS]
+        elif what == "s":
+            part = spread(line, piece, lists[number], places, tables[1])
+            mine[number] = part, other_core(part)
+        else:
+            update = join(line, piece, *mine[number], spans, update)
     return update, fresh
 
 

time: 235 us -> 242 us (1.030)
  starting transfers between devices: 53.1 us -> 58 us
  Pallas kernels: 65.5 us -> 69.4 us
    ppermute x24, waiting for transfers between devices: 108 us -> 98.8 us  [along(): lax.ppermute(value, 'fsdp', shift(0, step) if x_first else shift(step, 0))]
    ppermute x9, waiting for transfers between devices: 0.02 us -> 5.97 us  [along_z(): lax.ppermute(value, 'rep', [(z * 2 + c, (z + step) % SIDE * 2 + c) for z...]
    ppermute x9, starting transfers between devices: 12.4 us -> 17.1 us  [along_z(): lax.ppermute(value, 'rep', [(z * 2 + c, (z + step) % SIDE * 2 + c) for z...]
    pallas_call x18, Pallas kernels: 65.5 us -> 69.4 us  [call(): pl.pallas_call(run, grid_spec=pltpu.PrefetchScalarGridSpec(num_scalar_pre...]
    unnamed x34 -> x46, local copies, waits for them, and re-layouts: 5.88 us -> 4.34 us
  transfers between devices with their start and end apart: 35 -> 35, of which waited for: 9 -> 14; matrix products, arithmetic and copies ran while one was open for 0% -> 0% of each run, Pallas kernels for 26% -> 23%
where the time goes in v5:
time: 242 us; the launch traced here: 240 us
  waiting for transfers between devices  107 us (44%)
  Pallas kernels  69.4 us (29%)
  starting transfers between devices  58 us (24%)
  local copies, waits for them, and re-layouts  4.34 us (2%)
    ppermute x24, waiting for transfers between devices, along(): lax.ppermute(value, 'fsdp', shift(0, step) if x_first else shift(step, 0))  98.8 us
    pallas_call x18, Pallas kernels, call(): pl.pallas_call(run, grid_spec=pltpu.PrefetchScalarGridSpec(num_scalar_pre...  69.4 us
    ppermute x24, starting transfers between devices, along(): lax.ppermute(value, 'fsdp', shift(0, step) if x_first else shift(step, 0))  31.1 us
    ppermute x9, starting transfers between devices, along_z(): lax.ppermute(value, 'rep', [(z * 2 + c, (z + step) % SIDE * 2 + c) for z...  17.1 us
    ppermute x2, starting transfers between devices, other_core(): return lax.ppermute(value, 'rep', [(r, r ^ 1) for r in range(2 * SIDE)])  9.87 us
    ppermute x9, waiting for transfers between devices, along_z(): lax.ppermute(value, 'rep', [(z * 2 + c, (z + step) % SIDE * 2 + c) for z...  5.97 us
  transfers between devices with their start and end apart: 35, of which 14 were waited for; matrix products, arithmetic and copies ran while one was open for 0% of the time, Pallas kernels for 23%

profile of v5, /device:TPU:1, one launch (start us, length us, event | category | flops | bytes accessed | tf_op | source)
XLA Modules:
  0.0 239.9 jit_solution(12640013908367192558)
XLA Ops:
  0.6 0.1 pad_add_fusion.here
  0.7 3.4 %shard_map.68 = (f32[32,16384]{1,0:T(8,128)S(1)}, f32[32,16384]{1,0:T(8,128)S(1)}, f32[8,128]{1,0:T(8,128)S(1)}) custom-call(s32[2]{0:T(128)S(1)} %pad_add_fusion.here, bf16[64,131072]{1,0:T(8,128)(2,1)} %bitcast.3, bf16[64,131072]{1,0:T(8,128)(2,1)} %bitcast.4, bf16[64,131072]{1,0:T(8,128)(2,1)} %bitcast.5, bf16[64,131072]{1,0:T(8,128)(2,1)} %bitcast.6, ...), custom_call_target="tpu_custom_call" | custom-call | tf_op jit(solution)/shard_map/pallas_call | solution.py:113
  4.1 2.1 collective-permute-start.2
  6.3 1.3 collective-permute-start.3
  7.6 4.4 %shard_map.69 = (f32[32,16384]{1,0:T(8,128)}, f32[32,16384]{1,0:T(8,128)S(1)}, f32[8,128]{1,0:T(8,128)S(1)}) custom-call(s32[2]{0:T(128)S(1)} %pad_add_fusion.here, bf16[64,131072]{1,0:T(8,128)(2,1)} %bitcast.18, bf16[64,131072]{1,0:T(8,128)(2,1)} %bitcast.12, bf16[64,131072]{1,0:T(8,128)(2,1)} %bitcast.13, bf16[64,131072]{1,0:T(8,128)(2,1)} %bitcast.14, ...), custom_call_target="tpu_custom_call" | custom-call | tf_op jit(solution)/shard_map/pallas_call | solution.py:113
  12.0 1.4 collective-permute-start.4
  13.4 1.5 collective-permute-start.5
  14.9 4.9 %shard_map.70 = (f32[32,16384]{1,0:T(8,128)}, f32[32,16384]{1,0:T(8,128)}, f32[8,128]{1,0:T(8,128)S(1)}) custom-call(s32[2]{0:T(128)S(1)} %pad_add_fusion.here, bf16[64,131072]{1,0:T(8,128)(2,1)} %bitcast.19, bf16[64,131072]{1,0:T(8,128)(2,1)} %bitcast.20, bf16[64,131072]{1,0:T(8,128)(2,1)} %bitcast.21, bf16[64,131072]{1,0:T(8,128)(2,1)} %bitcast.22, ...), custom_call_target="tpu_custom_call" | custom-call | tf_op jit(solution)/shard_map/pallas_call | solution.py:113
  19.8 4.9 %shard_map.71 = (f32[32,16384]{1,0:T(8,128)}, f32[32,16384]{1,0:T(8,128)}, f32[8,128]{1,0:T(8,128)S(1)}) custom-call(s32[2]{0:T(128)S(1)} %pad_add_fusion.here, bf16[64,131072]{1,0:T(8,128)(2,1)} %bitcast.27, bf16[64,131072]{1,0:T(8,128)(2,1)} %bitcast.28, bf16[64,131072]{1,0:T(8,128)(2,1)} %bitcast.29, bf16[64,131072]{1,0:T(8,128)(2,1)} %bitcast.30, ...), custom_call_target="tpu_custom_call" | custom-call | tf_op jit(solution)/shard_map/pallas_call | solution.py:113
  24.7 27.8 %collective-permute-done.2.refs_8_.refs_11_ = f32[32,16384]{1,0:T(8,128)S(1)} collective-permute-done((f32[32,16384]{1,0:T(8,128)S(1)}, f32[32,16384]{1,0:T(8,128)S(1)}, u32[]{:S(2)}, u32[]{:S(2)}) %collective-permute-start.2) | collective-permute-done | bytes 2097184 | tf_op jit(solution)/shard_map/ppermute | solution.py:378
  52.4 1.6 collective-permute-start.1
  54.0 1.3 collective-permute-start.8
  55.3 4.3 %collective-permute-done.4.refs_8_.refs_11_ = f32[32,16384]{1,0:T(8,128)S(1)} collective-permute-done((f32[32,16384]{1,0:T(8,128)}, f32[32,16384]{1,0:T(8,128)S(1)}, u32[]{:S(2)}, u32[]{:S(2)}) %collective-permute-start.4) | collective-permute-done | bytes 2097184 | tf_op jit(solution)/shard_map/ppermute | solution.py:378
  59.6 3.5 %collective-permute-start.10 = (s32[1,8,8192]{2,1,0:T(8,128)S(1)}, s32[1,8,8192]{2,1,0:T(8,128)S(1)}, u32[]{:S(2)}, u32[]{:S(2)}) collective-permute-start(s32[1,8,8192]{2,1,0:T(8,128)S(1)} %copy-done.12), channel_id=1, source_target_pairs={{0,64},{16,80},{32,96},{48,112},{64,0},{80,16},{96,32},{112,48},{1... | collective-permute-start | bytes 786440 | tf_op jit(solution)/shard_map/ppermute | solution.py:382
  63.1 1.3 copy-done.10
  64.5 1.4 collective-permute-start.9
  65.9 1.6 copy-done.11
  67.5 3.6 %shard_map.72 = (f32[32,16384]{1,0:T(8,128)S(1)}, f32[32,16384]{1,0:T(8,128)S(1)}, f32[8,128]{1,0:T(8,128)S(1)}) custom-call(s32[2]{0:T(128)S(1)} %pad_add_fusion.here, bf16[64,131072]{1,0:T(8,128)(2,1)} %bitcast.40, bf16[64,131072]{1,0:T(8,128)(2,1)} %bitcast.36, bf16[64,131072]{1,0:T(8,128)(2,1)} %bitcast.37, bf16[64,131072]{1,0:T(8,128)(2,1)} %bitcast.38, ...), custom_call_target="tpu_custom_call" | custom-call | tf_op jit(solution)/shard_map/pallas_call | solution.py:113
  71.0 1.3 copy-done.22
  72.4 5.1 %shard_map.73 = (f32[32,16384]{1,0:T(8,128)}, f32[32,16384]{1,0:T(8,128)}, f32[8,128]{1,0:T(8,128)S(1)}) custom-call(s32[2]{0:T(128)S(1)} %pad_add_fusion.here, bf16[64,131072]{1,0:T(8,128)(2,1)} %bitcast.43, bf16[64,131072]{1,0:T(8,128)(2,1)} %bitcast.44, bf16[64,131072]{1,0:T(8,128)(2,1)} %bitcast.45, bf16[64,131072]{1,0:T(8,128)(2,1)} %bitcast.46, ...), custom_call_target="tpu_custom_call" | custom-call | tf_op jit(solution)/shard_map/pallas_call | solution.py:113
  77.5 19.8 %collective-permute-done.refs_4_.refs_5_.refs_6_.refs_7_.refs_21_.refs_2_.refs_3_.refs_12_.refs_13_.refs_1_ = f32[32,16384]{1,0:T(8,128)S(1)} collective-permute-done((f32[32,16384]{1,0:T(8,128)}, f32[32,16384]{1,0:T(8,128)S(1)}, u32[]{:S(2)}, u32[]{:S(2)}) %collective-permute-start) | collective-permute-done | bytes 2097184 | tf_op jit(solution)/shard_map/ppermute | solution.py:378
  97.4 1.6 collective-permute-start.7
  99.0 1.3 collective-permute-start.13
  100.3 4.3 %collective-permute-done.8.refs_21_.refs_4_.refs_5_.refs_6_.refs_7_.refs_2_.refs_3_.refs_12_.refs_13_.refs_8_ = f32[32,16384]{1,0:T(8,128)S(1)} collective-permute-done((f32[32,16384]{1,0:T(8,128)}, f32[32,16384]{1,0:T(8,128)S(1)}, u32[]{:S(2)}, u32[]{:S(2)}) %collective-permute-start.8) | collective-permute-done | bytes 2097184 | tf_op jit(solution)/shard_map/ppermute | solution.py:378
  104.6 1.3 collective-permute-start.14
  105.9 1.8 collective-permute-done.9.refs_22_.refs_8_.refs_9_.refs_10_.refs_11_.refs_4_.refs_5_.refs_14_.refs_15_
  107.7 1.9 collective-permute-start.16
  109.6 32.7 %collective-permute-done.6.refs_12_.refs_13_.refs_14_.refs_15_.refs_6_.refs_7_.refs_16_.refs_17_.refs_25_.refs_3_ = f32[32,16384]{1,0:T(8,128)S(1)} collective-permute-done((f32[32,16384]{1,0:T(8,128)}, f32[32,16384]{1,0:T(8,128)S(1)}, u32[]{:S(2)}, u32[]{:S(2)}) %collective-permute-start.6) | collective-permute-done | bytes 2097184 | tf_op jit(solution)/shard_map/ppermute | solution.py:378
  142.3 2.0 collective-permute-start.15
  144.3 1.9 shard_map.74
  146.2 1.4 collective-permute-start.11
  147.6 1.5 collective-permute-start.12
  149.1 2.3 collective-permute-done.15.refs_23_.refs_5_
  151.5 1.2 collective-permute-done.14.refs_16_.refs_17_.refs_18_.refs_19_.refs_26_.refs_8_.refs_9_.refs_11_
  152.7 1.9 shard_map.75
  154.7 2.7 %collective-permute-start.18 = (f32[32,4096]{1,0:T(8,128)S(1)}, f32[32,4096]{1,0:T(8,128)S(1)}, u32[]{:S(2)}, u32[]{:S(2)}) collective-permute-start(f32[32,4096]{1,0:T(8,128)S(1)} %get-tuple-element.73), channel_id=1, source_target_pairs={{0,3},{1,0},{2,1},{3,2},{4,7},{5,4},{6,5},{7,6},{8,11},{9,8},{10,9... | collective-permute-start | bytes 1572872 | tf_op jit(solution)/shard_map/ppermute | solution.py:378
  157.4 3.5 %collective-permute-done.11.refs_20_.refs_21_.refs_25_ = f32[32,4096]{1,0:T(8,128)S(1)} collective-permute-done((f32[32,4096]{1,0:T(8,128)S(1)}, f32[32,4096]{1,0:T(8,128)S(1)}, u32[]{:S(2)}, u32[]{:S(2)}) %collective-permute-start.11) | collective-permute-done | bytes 524320 | tf_op jit(solution)/shard_map/ppermute | solution.py:378
  160.9 3.0 %collective-permute-done.12.refs_22_.refs_23_.refs_26_ = f32[32,4096]{1,0:T(8,128)S(1)} collective-permute-done((f32[32,4096]{1,0:T(8,128)S(1)}, f32[32,4096]{1,0:T(8,128)S(1)}, u32[]{:S(2)}, u32[]{:S(2)}) %collective-permute-start.12) | collective-permute-done | bytes 524320 | tf_op jit(solution)/shard_map/ppermute | solution.py:378
  163.9 3.1 %shard_map.76 = (f32[64,2048]{1,0:T(8,128)}, f32[64,2048]{1,0:T(8,128)}, f32[8,128]{1,0:T(8,128)S(1)}) custom-call(s32[2]{0:T(128)S(1)} %pad_add_fusion.here, bf16[64,131072]{1,0:T(8,128)(2,1)} %bitcast.59, bf16[64,131072]{1,0:T(8,128)(2,1)} %bitcast.60, ...), custom_call_target="tpu_custom_call" | custom-call | tf_op jit(solution)/shard_map/pallas_call | solution.py:113
  167.0 2.7 %collective-permute-start.24 = (f32[64,2048]{1,0:T(8,128)}, f32[64,2048]{1,0:T(8,128)S(1)}, u32[]{:S(2)}, u32[]{:S(2)}) collective-permute-start(f32[64,2048]{1,0:T(8,128)} %get-tuple-element.83), channel_id=1, source_target_pairs={{0,12},{1,13},{2,14},{3,15},{4,0},{5,1},{6,2},{7,3},{8,4},{9,5},{1... | collective-permute-start | bytes 1572872 | tf_op jit(solution)/shard_map/ppermute | solution.py:378
  169.7 2.2 shard_map.77
  172.0 2.7 %collective-permute-start.26 = (f32[64,2048]{1,0:T(8,128)S(1)}, f32[64,2048]{1,0:T(8,128)S(1)}, u32[]{:S(2)}, u32[]{:S(2)}) collective-permute-start(f32[64,2048]{1,0:T(8,128)S(1)} %get-tuple-element.85), channel_id=1, source_target_pairs={{0,3},{1,0},{2,1},{3,2},{4,7},{5,4},{6,5},{7,6},{8,11},{9,8},{10,9... | collective-permute-start | bytes 1572872 | tf_op jit(solution)/shard_map/ppermute | solution.py:378
  174.7 1.8 shard_map.78
  176.5 1.9 shard_map.79
  178.5 2.7 %collective-permute-start.22 = (f32[64,2048]{1,0:T(8,128)S(1)}, f32[64,2048]{1,0:T(8,128)S(1)}, u32[]{:S(2)}, u32[]{:S(2)}) collective-permute-start(f32[64,2048]{1,0:T(8,128)S(1)} %get-tuple-element.81), channel_id=1, source_target_pairs={{0,3},{1,0},{2,1},{3,2},{4,7},{5,4},{6,5},{7,6},{8,11},{9,8},{10,9... | collective-permute-start | bytes 1572872 | tf_op jit(solution)/shard_map/ppermute | solution.py:378
  181.2 0.3 collective-permute-done.25.refs_12_
  181.5 2.3 collective-permute-start.20
  183.8 8.9 %shard_map.80 = (f32[1,64,8192]{2,1,0:T(8,128)}, f32[8,4096]{1,0:T(8,128)S(1)}, f32[8,128]{1,0:T(8,128)S(1)}) custom-call(s32[2]{0:T(128)S(1)} %pad_add_fusion.here, bf16[64,131072]{1,0:T(8,128)(2,1)} %bitcast.75, f32[32,16384]{1,0:T(8,128)S(1)} %collective-permute-done.refs_4_.refs_5_.refs_6_.refs_7_.refs_21_.refs_2_.refs_3_.refs_12_.refs_13_.refs_1_, ...), custom_call_target="tpu_custom_call" | custom-call | tf_op jit(solution)/shard_map/pallas_call | solution.py:113
  192.8 4.4 %collective-permute-start.32 = (f32[8,4096]{1,0:T(8,128)S(1)}, f32[8,4096]{1,0:T(8,128)S(1)}, u32[]{:S(2)}, u32[]{:S(2)}) collective-permute-start(f32[8,4096]{1,0:T(8,128)S(1)} %get-tuple-element.90.refs_0_), channel_id=1, source_target_pairs={{0,64},{16,80},{32,96},{48,112},{64,0},{80,16},{96,32},{112,48},{1... | collective-permute-start | bytes 393224 | tf_op jit(solution)/shard_map/ppermute | solution.py:382
  197.2 1.3 collective-permute-start.31
  198.5 0.1 collective-permute-start.30
  198.7 9.0 %shard_map.81 = (f32[1,64,8192]{2,1,0:T(8,128)}, f32[8,4096]{1,0:T(8,128)S(1)}, f32[8,128]{1,0:T(8,128)S(1)}) custom-call(s32[2]{0:T(128)S(1)} %pad_add_fusion.here, bf16[64,131072]{1,0:T(8,128)(2,1)} %bitcast.77, ...), custom_call_target="tpu_custom_call", output_to_operand_aliasing={{0}: (19, {})} | custom-call | tf_op jit(solution)/shard_map/pallas_call | solution.py:113
  207.7 4.0 %shard_map.82 = (f32[64,4096]{1,0:T(8,128)S(1)}, f32[8,128]{1,0:T(8,128)S(1)}) custom-call(s32[2]{0:T(128)S(1)} %pad_add_fusion.here, f32[8,4096]{1,0:T(8,128)S(1)} %get-tuple-element.90.refs_0_, f32[8,4096]{1,0:T(8,128)S(1)} %collective-permute-done.30.refs_1_, f32[8,4096]{1,0:T(8,128)S(1)} %collective-permute-done.31.refs_2_, ...), custom_call_target="tpu_custom_call" | custom-call | tf_op jit(solution)/shard_map/pallas_call | solution.py:113
  211.7 8.9 %collective-permute-start.33 = (f32[64,4096]{1,0:T(8,128)S(1)}, f32[64,4096]{1,0:T(8,128)S(1)}, u32[]{:S(2)}, u32[]{:S(2)}) collective-permute-start(f32[64,4096]{1,0:T(8,128)S(1)} %get-tuple-element.92.refs_0_), channel_id=1, source_target_pairs={{0,16},{16,0},{32,48},{48,32},{64,80},{80,64},{96,112},{112,96},{1... | collective-permute-start | bytes 3145736 | tf_op jit(solution)/shard_map/ppermute | solution.py:388
  220.6 2.4 collective-permute-start.29
  223.0 0.8 collective-permute-start.28
  223.8 0.7 collective-permute-start.27
  224.5 2.2 shard_map.83
  226.7 0.5 collective-permute-done.29.refs_3_
  227.2 3.2 %collective-permute-done.28.refs_2_ = f32[8,4096]{1,0:T(8,128)S(1)} collective-permute-done((f32[8,4096]{1,0:T(8,128)S(1)}, f32[8,4096]{1,0:T(8,128)S(1)}, u32[]{:S(2)}, u32[]{:S(2)}) %collective-permute-start.28) | collective-permute-done | bytes 131104 | tf_op jit(solution)/shard_map/ppermute | solution.py:382
  230.3 4.0 %shard_map.84 = (f32[64,4096]{1,0:T(8,128)S(1)}, f32[8,128]{1,0:T(8,128)S(1)}) custom-call(s32[2]{0:T(128)S(1)} %pad_add_fusion.here, f32[8,4096]{1,0:T(8,128)S(1)} %get-tuple-element.89.refs_0_, f32[8,4096]{1,0:T(8,128)S(1)} %collective-permute-done.27.refs_1_, f32[8,4096]{1,0:T(8,128)S(1)} %collective-permute-done.28.refs_2_, ...), custom_call_target="tpu_custom_call" | custom-call | tf_op jit(solution)/shard_map/pallas_call | solution.py:113
  234.4 1.0 collective-permute-start.34
  235.3 2.3 collective-permute-done.34.refs_1_
  237.6 2.2 shard_map.85
  (71 shorter events, 0.5 us)
Async XLA Ops:
  4.1 48.3 %collective-permute-start.2 = (f32[32,16384]{1,0:T(8,128)S(1)}, f32[32,16384]{1,0:T(8,128)S(1)}, u32[]{:S(2)}, u32[]{:S(2)}) collective-permute-start(f32[32,16384]{1,0:T(8,128)S(1)} %get-tuple-element.55), channel_id=1, source_target_pairs={{0,1},{1,2},{2,3},{3,0},{4,5},{5,6},{6,7},{7,4},{8,9},{9,10},{10,1... | collective-permute-start | bytes 6291464 | tf_op jit(solution)/shard_map/ppermute | solution.py:378
  6.3 47.8 %collective-permute-start.3 = (f32[32,16384]{1,0:T(8,128)S(1)}, f32[32,16384]{1,0:T(8,128)S(1)}, u32[]{:S(2)}, u32[]{:S(2)}) collective-permute-start(f32[32,16384]{1,0:T(8,128)S(1)} %get-tuple-element.56), channel_id=1, source_target_pairs={{0,3},{1,0},{2,1},{3,2},{4,7},{5,4},{6,5},{7,6},{8,11},{9,8},{10,9... | collective-permute-start | bytes 6291464 | tf_op jit(solution)/shard_map/ppermute | solution.py:378
  12.0 47.6 %collective-permute-start.4 = (f32[32,16384]{1,0:T(8,128)}, f32[32,16384]{1,0:T(8,128)S(1)}, u32[]{:S(2)}, u32[]{:S(2)}) collective-permute-start(f32[32,16384]{1,0:T(8,128)} %get-tuple-element.57), channel_id=1, source_target_pairs={{0,4},{1,5},{2,6},{3,7},{4,8},{5,9},{6,10},{7,11},{8,12},{9,13},{1... | collective-permute-start | bytes 6291464 | tf_op jit(solution)/shard_map/ppermute | solution.py:378
  13.4 49.7 %collective-permute-start.5 = (f32[32,16384]{1,0:T(8,128)S(1)}, f32[32,16384]{1,0:T(8,128)S(1)}, u32[]{:S(2)}, u32[]{:S(2)}) collective-permute-start(f32[32,16384]{1,0:T(8,128)S(1)} %get-tuple-element.58), channel_id=1, source_target_pairs={{0,12},{1,13},{2,14},{3,15},{4,0},{5,1},{6,2},{7,3},{8,4},{9,5},{1... | collective-permute-start | bytes 6291464 | tf_op jit(solution)/shard_map/ppermute | solution.py:378
  19.8 77.6 %collective-permute-start = (f32[32,16384]{1,0:T(8,128)}, f32[32,16384]{1,0:T(8,128)S(1)}, u32[]{:S(2)}, u32[]{:S(2)}) collective-permute-start(f32[32,16384]{1,0:T(8,128)} %get-tuple-element.53), channel_id=1, source_target_pairs={{0,1},{1,2},{2,3},{3,0},{4,5},{5,6},{6,7},{7,4},{8,9},{9,10},{10,1... | collective-permute-start | bytes 6291464 | tf_op jit(solution)/shard_map/ppermute | solution.py:378
  19.8 39.8 %copy-start.12 = (s32[1,8,8192]{2,1,0:T(8,128)S(1)}, s32[1,8,8192]{2,1,0:T(8,128)}, u32[]{:S(2)}) copy-start(s32[1,8,8192]{2,1,0:T(8,128)} %refs_4_.3) | copy-start | bytes 786436
  52.4 46.5 %collective-permute-start.1 = (f32[32,16384]{1,0:T(8,128)}, f32[32,16384]{1,0:T(8,128)S(1)}, u32[]{:S(2)}, u32[]{:S(2)}) collective-permute-start(f32[32,16384]{1,0:T(8,128)} %get-tuple-element.54), channel_id=1, source_target_pairs={{0,3},{1,0},{2,1},{3,2},{4,7},{5,4},{6,5},{7,6},{8,11},{9,8},{10,9... | collective-permute-start | bytes 6291464 | tf_op jit(solution)/shard_map/ppermute | solution.py:378
  54.0 50.5 %collective-permute-start.8 = (f32[32,16384]{1,0:T(8,128)}, f32[32,16384]{1,0:T(8,128)S(1)}, u32[]{:S(2)}, u32[]{:S(2)}) collective-permute-start(f32[32,16384]{1,0:T(8,128)} %get-tuple-element.65), channel_id=1, source_target_pairs={{0,4},{1,5},{2,6},{3,7},{4,8},{5,9},{6,10},{7,11},{8,12},{9,13},{1... | collective-permute-start | bytes 6291464 | tf_op jit(solution)/shard_map/ppermute | solution.py:378
  59.6 17.8 %collective-permute-start.10 = (s32[1,8,8192]{2,1,0:T(8,128)S(1)}, s32[1,8,8192]{2,1,0:T(8,128)S(1)}, u32[]{:S(2)}, u32[]{:S(2)}) collective-permute-start(s32[1,8,8192]{2,1,0:T(8,128)S(1)} %copy-done.12), channel_id=1, source_target_pairs={{0,64},{16,80},{32,96},{48,112},{64,0},{80,16},{96,32},{112,48},{1... | collective-permute-start | bytes 786440 | tf_op jit(solution)/shard_map/ppermute | solution.py:382
  63.1 1.3 copy-start.10
  64.5 43.3 %collective-permute-start.9 = (f32[32,16384]{1,0:T(8,128)}, f32[32,16384]{1,0:T(8,128)S(1)}, u32[]{:S(2)}, u32[]{:S(2)}) collective-permute-start(f32[32,16384]{1,0:T(8,128)} %get-tuple-element.66), channel_id=1, source_target_pairs={{0,12},{1,13},{2,14},{3,15},{4,0},{5,1},{6,2},{7,3},{8,4},{9,5},{1... | collective-permute-start | bytes 6291464 | tf_op jit(solution)/shard_map/ppermute | solution.py:378
  65.9 1.6 copy-start.11
  71.0 1.3 copy-start.22
  72.4 5.1 %copy-start.21 = (f32[32,16384]{1,0:T(8,128)}, f32[32,16384]{1,0:T(8,128)S(1)}, u32[]{:S(2)}) copy-start(f32[32,16384]{1,0:T(8,128)S(1)} %get-tuple-element.70) | copy-start | bytes 6291460
  77.5 68.8 %copy-start.13 = (s32[1,8,8192]{2,1,0:T(8,128)}, s32[1,8,8192]{2,1,0:T(8,128)S(1)}, u32[]{:S(2)}) copy-start(s32[1,8,8192]{2,1,0:T(8,128)S(1)} %collective-permute-done.10.refs_23_.refs_7_) | copy-start | bytes 786436
  77.5 64.8 %collective-permute-start.6 = (f32[32,16384]{1,0:T(8,128)}, f32[32,16384]{1,0:T(8,128)S(1)}, u32[]{:S(2)}, u32[]{:S(2)}) collective-permute-start(f32[32,16384]{1,0:T(8,128)} %get-tuple-element.62), channel_id=1, source_target_pairs={{0,1},{1,2},{2,3},{3,0},{4,5},{5,6},{6,7},{7,4},{8,9},{9,10},{10,1... | collective-permute-start | bytes 6291464 | tf_op jit(solution)/shard_map/ppermute | solution.py:378
  97.4 46.9 %collective-permute-start.7 = (f32[32,16384]{1,0:T(8,128)}, f32[32,16384]{1,0:T(8,128)S(1)}, u32[]{:S(2)}, u32[]{:S(2)}) collective-permute-start(f32[32,16384]{1,0:T(8,128)} %get-tuple-element.63), channel_id=1, source_target_pairs={{0,3},{1,0},{2,1},{3,2},{4,7},{5,4},{6,5},{7,6},{8,11},{9,8},{10,9... | collective-permute-start | bytes 6291464 | tf_op jit(solution)/shard_map/ppermute | solution.py:378
  99.0 52.5 %collective-permute-start.13 = (f32[32,16384]{1,0:T(8,128)}, f32[32,16384]{1,0:T(8,128)S(1)}, u32[]{:S(2)}, u32[]{:S(2)}) collective-permute-start(f32[32,16384]{1,0:T(8,128)} %copy-done.22), channel_id=1, source_target_pairs={{0,4},{1,5},{2,6},{3,7},{4,8},{5,9},{6,10},{7,11},{8,12},{9,13},{1... | collective-permute-start | bytes 6291464 | tf_op jit(solution)/shard_map/ppermute | solution.py:378
  104.6 48.1 %collective-permute-start.14 = (f32[32,16384]{1,0:T(8,128)}, f32[32,16384]{1,0:T(8,128)S(1)}, u32[]{:S(2)}, u32[]{:S(2)}) collective-permute-start(f32[32,16384]{1,0:T(8,128)} %copy-done.21), channel_id=1, source_target_pairs={{0,12},{1,13},{2,14},{3,15},{4,0},{5,1},{6,2},{7,3},{8,4},{9,5},{1... | collective-permute-start | bytes 6291464 | tf_op jit(solution)/shard_map/ppermute | solution.py:378
  107.7 68.8 %copy-start = (f32[32,16384]{1,0:T(8,128)}, f32[32,16384]{1,0:T(8,128)S(1)}, u32[]{:S(2)}) copy-start(f32[32,16384]{1,0:T(8,128)S(1)} %collective-permute-done.9.refs_22_.refs_8_.refs_9_.refs_10_.refs_11_.refs_4_.refs_5_.refs_14_.refs_15_) | copy-start | bytes 6291460
  107.7 39.9 %collective-permute-start.16 = (s32[1,8,8192]{2,1,0:T(8,128)S(1)}, s32[1,8,8192]{2,1,0:T(8,128)S(1)}, u32[]{:S(2)}, u32[]{:S(2)}) collective-permute-start(s32[1,8,8192]{2,1,0:T(8,128)S(1)} %copy-done.12), channel_id=1, source_target_pairs={{0,96},{16,112},{32,0},{48,16},{64,32},{80,48},{96,64},{112,80},{1... | collective-permute-start | bytes 786440 | tf_op jit(solution)/shard_map/ppermute | solution.py:382
  142.3 9.1 %collective-permute-start.15 = (s32[1,8,8192]{2,1,0:T(8,128)S(1)}, s32[1,8,8192]{2,1,0:T(8,128)S(1)}, u32[]{:S(2)}, u32[]{:S(2)}) collective-permute-start(s32[1,8,8192]{2,1,0:T(8,128)S(1)} %copy-done.12), channel_id=1, source_target_pairs={{0,32},{16,48},{32,64},{48,80},{64,96},{80,112},{96,0},{112,16},{1... | collective-permute-start | bytes 786440 | tf_op jit(solution)/shard_map/ppermute | solution.py:382
  144.3 19.6 %copy-start.1 = (f32[32,16384]{1,0:T(8,128)}, f32[32,16384]{1,0:T(8,128)S(1)}, u32[]{:S(2)}) copy-start(f32[32,16384]{1,0:T(8,128)S(1)} %collective-permute-done.7.refs_16_.refs_17_.refs_18_.refs_19_.refs_8_.refs_9_.refs_26_.refs_4_) | copy-start | bytes 6291460
  146.2 14.7 %collective-permute-start.11 = (f32[32,4096]{1,0:T(8,128)S(1)}, f32[32,4096]{1,0:T(8,128)S(1)}, u32[]{:S(2)}, u32[]{:S(2)}) collective-permute-start(f32[32,4096]{1,0:T(8,128)S(1)} %get-tuple-element.67), channel_id=1, source_target_pairs={{0,4},{1,5},{2,6},{3,7},{4,8},{5,9},{6,10},{7,11},{8,12},{9,13},{1... | collective-permute-start | bytes 1572872 | tf_op jit(solution)/shard_map/ppermute | solution.py:378
  147.6 7.0 %copy-start.15 = (s32[1,8,8192]{2,1,0:T(8,128)}, s32[1,8,8192]{2,1,0:T(8,128)S(1)}, u32[]{:S(2)}) copy-start(s32[1,8,8192]{2,1,0:T(8,128)S(1)} %collective-permute-done.16.refs_24_.refs_6_) | copy-start | bytes 786436
  147.6 16.3 %collective-permute-start.12 = (f32[32,4096]{1,0:T(8,128)S(1)}, f32[32,4096]{1,0:T(8,128)S(1)}, u32[]{:S(2)}, u32[]{:S(2)}) collective-permute-start(f32[32,4096]{1,0:T(8,128)S(1)} %get-tuple-element.68), channel_id=1, source_target_pairs={{0,12},{1,13},{2,14},{3,15},{4,0},{5,1},{6,2},{7,3},{8,4},{9,5},{1... | collective-permute-start | bytes 1572872 | tf_op jit(solution)/shard_map/ppermute | solution.py:378
  151.5 3.2 %copy-start.17 = (s32[1,8,8192]{2,1,0:T(8,128)}, s32[1,8,8192]{2,1,0:T(8,128)S(1)}, u32[]{:S(2)}) copy-start(s32[1,8,8192]{2,1,0:T(8,128)S(1)} %collective-permute-done.15.refs_23_.refs_5_) | copy-start | bytes 786436
  151.5 25.0 %copy-start.3 = (f32[32,16384]{1,0:T(8,128)}, f32[32,16384]{1,0:T(8,128)S(1)}, u32[]{:S(2)}) copy-start(f32[32,16384]{1,0:T(8,128)S(1)} %collective-permute-done.13.refs_12_.refs_13_.refs_14_.refs_15_.refs_25_.refs_6_.refs_7_.refs_16_.refs_17_.refs_10_) | copy-start | bytes 6291460
  152.7 2.0 copy-start.4
  154.6 15.1 %collective-permute-start.17 = (f32[32,4096]{1,0:T(8,128)S(1)}, f32[32,4096]{1,0:T(8,128)S(1)}, u32[]{:S(2)}, u32[]{:S(2)}) collective-permute-start(f32[32,4096]{1,0:T(8,128)S(1)} %get-tuple-element.72), channel_id=1, source_target_pairs={{0,1},{1,2},{2,3},{3,0},{4,5},{5,6},{6,7},{7,4},{8,9},{9,10},{10,1... | collective-permute-start | bytes 1572872 | tf_op jit(solution)/shard_map/ppermute | solution.py:378
  154.7 15.0 %collective-permute-start.18 = (f32[32,4096]{1,0:T(8,128)S(1)}, f32[32,4096]{1,0:T(8,128)S(1)}, u32[]{:S(2)}, u32[]{:S(2)}) collective-permute-start(f32[32,4096]{1,0:T(8,128)S(1)} %get-tuple-element.73), channel_id=1, source_target_pairs={{0,3},{1,0},{2,1},{3,2},{4,7},{5,4},{6,5},{7,6},{8,11},{9,8},{10,9... | collective-permute-start | bytes 1572872 | tf_op jit(solution)/shard_map/ppermute | solution.py:378
  160.9 6.1 %copy-start.6 = (f32[32,4096]{1,0:T(8,128)}, f32[32,4096]{1,0:T(8,128)S(1)}, u32[]{:S(2)}) copy-start(f32[32,4096]{1,0:T(8,128)S(1)} %collective-permute-done.11.refs_20_.refs_21_.refs_25_) | copy-start | bytes 1572868
  163.9 3.1 %copy-start.8 = (f32[32,4096]{1,0:T(8,128)}, f32[32,4096]{1,0:T(8,128)S(1)}, u32[]{:S(2)}) copy-start(f32[32,4096]{1,0:T(8,128)S(1)} %collective-permute-done.12.refs_22_.refs_23_.refs_26_) | copy-start | bytes 1572868
  163.9 5.8 %copy-start.5 = (f32[32,16384]{1,0:T(8,128)S(1)}, f32[32,16384]{1,0:T(8,128)}, u32[]{:S(2)}) copy-start(f32[32,16384]{1,0:T(8,128)} %copy-done.4) | copy-start | bytes 6291460
  167.0 11.5 %collective-permute-start.23 = (f32[64,2048]{1,0:T(8,128)}, f32[64,2048]{1,0:T(8,128)S(1)}, u32[]{:S(2)}, u32[]{:S(2)}) collective-permute-start(f32[64,2048]{1,0:T(8,128)} %get-tuple-element.82), channel_id=1, source_target_pairs={{0,4},{1,5},{2,6},{3,7},{4,8},{5,9},{6,10},{7,11},{8,12},{9,13},{1... | collective-permute-start | bytes 1572872 | tf_op jit(solution)/shard_map/ppermute | solution.py:378
  167.0 14.1 %collective-permute-start.24 = (f32[64,2048]{1,0:T(8,128)}, f32[64,2048]{1,0:T(8,128)S(1)}, u32[]{:S(2)}, u32[]{:S(2)}) collective-permute-start(f32[64,2048]{1,0:T(8,128)} %get-tuple-element.83), channel_id=1, source_target_pairs={{0,12},{1,13},{2,14},{3,15},{4,0},{5,1},{6,2},{7,3},{8,4},{9,5},{1... | collective-permute-start | bytes 1572872 | tf_op jit(solution)/shard_map/ppermute | solution.py:378
  169.7 4.9 %copy-start.2 = (f32[32,16384]{1,0:T(8,128)S(1)}, f32[32,16384]{1,0:T(8,128)}, u32[]{:S(2)}) copy-start(f32[32,16384]{1,0:T(8,128)} %copy-done.1) | copy-start | bytes 6291460
  169.7 4.9 %copy-start.7 = (f32[32,4096]{1,0:T(8,128)S(1)}, f32[32,4096]{1,0:T(8,128)}, u32[]{:S(2)}) copy-start(f32[32,4096]{1,0:T(8,128)} %copy-done.6) | copy-start | bytes 1572868
  169.7 4.9 %copy-start.9 = (f32[32,4096]{1,0:T(8,128)S(1)}, f32[32,4096]{1,0:T(8,128)}, u32[]{:S(2)}) copy-start(f32[32,4096]{1,0:T(8,128)} %copy-done.8) | copy-start | bytes 1572868
  171.9 9.6 %collective-permute-start.25 = (f32[64,2048]{1,0:T(8,128)S(1)}, f32[64,2048]{1,0:T(8,128)S(1)}, u32[]{:S(2)}, u32[]{:S(2)}) collective-permute-start(f32[64,2048]{1,0:T(8,128)S(1)} %get-tuple-element.84), channel_id=1, source_target_pairs={{0,1},{1,2},{2,3},{3,0},{4,5},{5,6},{6,7},{7,4},{8,9},{9,10},{10,1... | collective-permute-start | bytes 1572872 | tf_op jit(solution)/shard_map/ppermute | solution.py:378
  172.0 11.9 %collective-permute-start.26 = (f32[64,2048]{1,0:T(8,128)S(1)}, f32[64,2048]{1,0:T(8,128)S(1)}, u32[]{:S(2)}, u32[]{:S(2)}) collective-permute-start(f32[64,2048]{1,0:T(8,128)S(1)} %get-tuple-element.85), channel_id=1, source_target_pairs={{0,3},{1,0},{2,1},{3,2},{4,7},{5,4},{6,5},{7,6},{8,11},{9,8},{10,9... | collective-permute-start | bytes 1572872 | tf_op jit(solution)/shard_map/ppermute | solution.py:378
  176.5 7.3 %copy-start.19 = (bf16[64,256]{1,0:T(8,128)(2,1)S(1)}, bf16[64,256]{1,0:T(8,128)(2,1)}, u32[]{:S(2)}) copy-start(bf16[64,256]{1,0:T(8,128)(2,1)} %constant.25.clone.refs_17_.refs_8_) | copy-start | bytes 98308
  176.5 7.3 %copy-start.20 = (bf16[64,256]{1,0:T(8,128)(2,1)S(1)}, bf16[64,256]{1,0:T(8,128)(2,1)}, u32[]{:S(2)}) copy-start(bf16[64,256]{1,0:T(8,128)(2,1)} %constant.24.clone.refs_16_) | copy-start | bytes 98308
  178.4 18.7 %collective-permute-start.21 = (f32[64,2048]{1,0:T(8,128)S(1)}, f32[64,2048]{1,0:T(8,128)S(1)}, u32[]{:S(2)}, u32[]{:S(2)}) collective-permute-start(f32[64,2048]{1,0:T(8,128)S(1)} %get-tuple-element.80), channel_id=1, source_target_pairs={{0,1},{1,2},{2,3},{3,0},{4,5},{5,6},{6,7},{7,4},{8,9},{9,10},{10,1... | collective-permute-start | bytes 1572872 | tf_op jit(solution)/shard_map/ppermute | solution.py:378
  178.5 20.0 %collective-permute-start.22 = (f32[64,2048]{1,0:T(8,128)S(1)}, f32[64,2048]{1,0:T(8,128)S(1)}, u32[]{:S(2)}, u32[]{:S(2)}) collective-permute-start(f32[64,2048]{1,0:T(8,128)S(1)} %get-tuple-element.81), channel_id=1, source_target_pairs={{0,3},{1,0},{2,1},{3,2},{4,7},{5,4},{6,5},{7,6},{8,11},{9,8},{10,9... | collective-permute-start | bytes 1572872 | tf_op jit(solution)/shard_map/ppermute | solution.py:378
  181.2 17.5 %collective-permute-start.19 = (f32[64,2048]{1,0:T(8,128)S(1)}, f32[64,2048]{1,0:T(8,128)S(1)}, u32[]{:S(2)}, u32[]{:S(2)}) collective-permute-start(f32[64,2048]{1,0:T(8,128)S(1)} %get-tuple-element.77), channel_id=1, source_target_pairs={{0,4},{1,5},{2,6},{3,7},{4,8},{5,9},{6,10},{7,11},{8,12},{9,13},{1... | collective-permute-start | bytes 1572872 | tf_op jit(solution)/shard_map/ppermute | solution.py:378
  181.5 17.1 %collective-permute-start.20 = (f32[64,2048]{1,0:T(8,128)S(1)}, f32[64,2048]{1,0:T(8,128)S(1)}, u32[]{:S(2)}, u32[]{:S(2)}) collective-permute-start(f32[64,2048]{1,0:T(8,128)S(1)} %get-tuple-element.78), channel_id=1, source_target_pairs={{0,12},{1,13},{2,14},{3,15},{4,0},{5,1},{6,2},{7,3},{8,4},{9,5},{1... | collective-permute-start | bytes 1572872 | tf_op jit(solution)/shard_map/ppermute | solution.py:378
  192.8 14.8 %collective-permute-start.32 = (f32[8,4096]{1,0:T(8,128)S(1)}, f32[8,4096]{1,0:T(8,128)S(1)}, u32[]{:S(2)}, u32[]{:S(2)}) collective-permute-start(f32[8,4096]{1,0:T(8,128)S(1)} %get-tuple-element.90.refs_0_), channel_id=1, source_target_pairs={{0,64},{16,80},{32,96},{48,112},{64,0},{80,16},{96,32},{112,48},{1... | collective-permute-start | bytes 393224 | tf_op jit(solution)/shard_map/ppermute | solution.py:382
  197.2 10.5 %collective-permute-start.31 = (f32[8,4096]{1,0:T(8,128)S(1)}, f32[8,4096]{1,0:T(8,128)S(1)}, u32[]{:S(2)}, u32[]{:S(2)}) collective-permute-start(f32[8,4096]{1,0:T(8,128)S(1)} %get-tuple-element.90.refs_0_), channel_id=1, source_target_pairs={{0,96},{16,112},{32,0},{48,16},{64,32},{80,48},{96,64},{112,80},{1... | collective-permute-start | bytes 393224 | tf_op jit(solution)/shard_map/ppermute | solution.py:382
  198.5 9.1 %collective-permute-start.30 = (f32[8,4096]{1,0:T(8,128)S(1)}, f32[8,4096]{1,0:T(8,128)S(1)}, u32[]{:S(2)}, u32[]{:S(2)}) collective-permute-start(f32[8,4096]{1,0:T(8,128)S(1)} %get-tuple-element.90.refs_0_), channel_id=1, source_target_pairs={{0,32},{16,48},{32,64},{48,80},{64,96},{80,112},{96,0},{112,16},{1... | collective-permute-start | bytes 393224 | tf_op jit(solution)/shard_map/ppermute | solution.py:382
  198.6 9.0 %copy-start.14 = (s32[1,8,8192]{2,1,0:T(8,128)S(1)}, s32[1,8,8192]{2,1,0:T(8,128)}, u32[]{:S(2)}) copy-start(s32[1,8,8192]{2,1,0:T(8,128)} %copy-done.13) | copy-start | bytes 786436
  198.6 9.0 %copy-start.16 = (s32[1,8,8192]{2,1,0:T(8,128)S(1)}, s32[1,8,8192]{2,1,0:T(8,128)}, u32[]{:S(2)}) copy-start(s32[1,8,8192]{2,1,0:T(8,128)} %copy-done.15) | copy-start | bytes 786436
  198.6 9.0 %copy-start.18 = (s32[1,8,8192]{2,1,0:T(8,128)S(1)}, s32[1,8,8192]{2,1,0:T(8,128)}, u32[]{:S(2)}) copy-start(s32[1,8,8192]{2,1,0:T(8,128)} %copy-done.17) | copy-start | bytes 786436
  211.7 12.8 %collective-permute-start.33 = (f32[64,4096]{1,0:T(8,128)S(1)}, f32[64,4096]{1,0:T(8,128)S(1)}, u32[]{:S(2)}, u32[]{:S(2)}) collective-permute-start(f32[64,4096]{1,0:T(8,128)S(1)} %get-tuple-element.92.refs_0_), channel_id=1, source_target_pairs={{0,16},{16,0},{32,48},{48,32},{64,80},{80,64},{96,112},{112,96},{1... | collective-permute-start | bytes 3145736 | tf_op jit(solution)/shard_map/ppermute | solution.py:388
  220.6 6.6 %collective-permute-start.29 = (f32[8,4096]{1,0:T(8,128)S(1)}, f32[8,4096]{1,0:T(8,128)S(1)}, u32[]{:S(2)}, u32[]{:S(2)}) collective-permute-start(f32[8,4096]{1,0:T(8,128)S(1)} %get-tuple-element.89.refs_0_), channel_id=1, source_target_pairs={{0,64},{16,80},{32,96},{48,112},{64,0},{80,16},{96,32},{112,48},{1... | collective-permute-start | bytes 393224 | tf_op jit(solution)/shard_map/ppermute | solution.py:382
  223.0 7.3 %collective-permute-start.28 = (f32[8,4096]{1,0:T(8,128)S(1)}, f32[8,4096]{1,0:T(8,128)S(1)}, u32[]{:S(2)}, u32[]{:S(2)}) collective-permute-start(f32[8,4096]{1,0:T(8,128)S(1)} %get-tuple-element.89.refs_0_), channel_id=1, source_target_pairs={{0,96},{16,112},{32,0},{48,16},{64,32},{80,48},{96,64},{112,80},{1... | collective-permute-start | bytes 393224 | tf_op jit(solution)/shard_map/ppermute | solution.py:382
  223.8 6.6 %collective-permute-start.27 = (f32[8,4096]{1,0:T(8,128)S(1)}, f32[8,4096]{1,0:T(8,128)S(1)}, u32[]{:S(2)}, u32[]{:S(2)}) collective-permute-start(f32[8,4096]{1,0:T(8,128)S(1)} %get-tuple-element.89.refs_0_), channel_id=1, source_target_pairs={{0,32},{16,48},{32,64},{48,80},{64,96},{80,112},{96,0},{112,16},{1... | collective-permute-start | bytes 393224 | tf_op jit(solution)/shard_map/ppermute | solution.py:382
  234.4 3.2 %collective-permute-start.34 = (f32[64,4096]{1,0:T(8,128)S(1)}, f32[64,4096]{1,0:T(8,128)S(1)}, u32[]{:S(2)}, u32[]{:S(2)}) collective-permute-start(f32[64,4096]{1,0:T(8,128)S(1)} %get-tuple-element.95.refs_0_), channel_id=1, source_target_pairs={{0,16},{16,0},{32,48},{48,32},{64,80},{80,64},{96,112},{112,96},{1... | collective-permute-start | bytes 3145736 | tf_op jit(solution)/shard_map/ppermute | solution.py:388

commit v6 on v5

--- a/solution.py
+++ b/solution.py
@@ -13,14 +13,14 @@
 SIDE = 4
 TILE = 1024
 CHUNK = 256
-FINE, BROAD = 512, 1024
+FINE, BROAD = 1024, 1024
 PARTS = (2, 2)
-AXES = (0, 0, 1, 1, 1, 1)
+AXES = (0, 0, 0, 1, 1, 0)
 LAG = (2, 2, 2, 2, 2, 2)
-PLACES_WITH = ((1, 0), (1, 0), (1, 1))
+PLACES_WITH = ((0, 1), (1, 0), (1, 0))
 STEPS = (1, -1, 2)
-TAIL = ("f0", "f1", "s0", "j0", "s1", "j1")
-VMEM_LIMIT = 40 * 1024 * 1024
+TAIL = ("f0", "f1", "s0", "s1", "j0", "j1")
+VMEM_LIMIT = 48 * 1024 * 1024
 F32 = jnp.float32
 BF16 = jnp.bfloat16
 

time: 242 us -> 232 us (0.959)
  waiting for transfers between devices: 107 us -> 98.2 us
    ppermute x9, waiting for transfers between devices: 5.97 us -> 0.02 us  [along_z(): lax.ppermute(value, 'rep', [(z * 2 + c, (z + step) % SIDE * 2 + c) for z...]
    ppermute x2, starting transfers between devices: 9.87 us -> 13.5 us  [other_core(): return lax.ppermute(value, 'rep', [(r, r ^ 1) for r in range(2 * SIDE)])]
  transfers between devices with their start and end apart: 35 -> 35, of which waited for: 14 -> 9; matrix products, arithmetic and copies ran while one was open for 0% -> 0% of each run, Pallas kernels for 23% -> 27%
where the time goes in v6:
time: 232 us; the launch traced here: 230 us
  waiting for transfers between devices  98.2 us (42%)
  Pallas kernels  68.2 us (29%)
  starting transfers between devices  60 us (26%)
  local copies, waits for them, and re-layouts  3.23 us (1%)
    ppermute x24, waiting for transfers between devices, along(): lax.ppermute(value, 'fsdp', shift(0, step) if x_first else shift(step, 0))  98.1 us
    pallas_call x18, Pallas kernels, call(): pl.pallas_call(run, grid_spec=pltpu.PrefetchScalarGridSpec(num_scalar_pre...  68.2 us
    ppermute x24, starting transfers between devices, along(): lax.ppermute(value, 'fsdp', shift(0, step) if x_first else shift(step, 0))  30.7 us
    ppermute x9, starting transfers between devices, along_z(): lax.ppermute(value, 'rep', [(z * 2 + c, (z + step) % SIDE * 2 + c) for z...  15.9 us
    ppermute x2, starting transfers between devices, other_core(): return lax.ppermute(value, 'rep', [(r, r ^ 1) for r in range(2 * SIDE)])  13.5 us
  transfers between devices with their start and end apart: 35, of which 9 were waited for; matrix products, arithmetic and copies ran while one was open for 0% of the time, Pallas kernels for 27%

profile of v6, /device:TPU:1, one launch (start us, length us, event | category | flops | bytes accessed | tf_op | source)
XLA Modules:
  0.0 230.5 jit_solution(7211063307941082609)
XLA Ops:
  0.6 0.1 pad_add_fusion.here
  0.7 3.4 %shard_map.68 = (f32[32,16384]{1,0:T(8,128)S(1)}, f32[32,16384]{1,0:T(8,128)S(1)}, f32[8,128]{1,0:T(8,128)S(1)}) custom-call(s32[2]{0:T(128)S(1)} %pad_add_fusion.here, bf16[64,131072]{1,0:T(8,128)(2,1)} %bitcast.3, bf16[64,131072]{1,0:T(8,128)(2,1)} %bitcast.4, bf16[64,131072]{1,0:T(8,128)(2,1)} %bitcast.5, bf16[64,131072]{1,0:T(8,128)(2,1)} %bitcast.6, ...), custom_call_target="tpu_custom_call" | custom-call | tf_op jit(solution)/shard_map/pallas_call | solution.py:113
  4.1 2.1 collective-permute-start.2
  6.3 1.3 collective-permute-start.3
  7.6 1.8 collective-permute-start.8
  9.4 4.4 %shard_map.69 = (f32[32,16384]{1,0:T(8,128)}, f32[32,16384]{1,0:T(8,128)S(1)}, f32[8,128]{1,0:T(8,128)S(1)}) custom-call(s32[2]{0:T(128)S(1)} %pad_add_fusion.here, bf16[64,131072]{1,0:T(8,128)(2,1)} %bitcast.18, bf16[64,131072]{1,0:T(8,128)(2,1)} %bitcast.12, bf16[64,131072]{1,0:T(8,128)(2,1)} %bitcast.13, bf16[64,131072]{1,0:T(8,128)(2,1)} %bitcast.14, ...), custom_call_target="tpu_custom_call" | custom-call | tf_op jit(solution)/shard_map/pallas_call | solution.py:113
  13.8 1.3 collective-permute-start.6
  15.0 1.5 collective-permute-start.7
  16.6 4.9 %shard_map.70 = (f32[32,16384]{1,0:T(8,128)}, f32[32,16384]{1,0:T(8,128)}, f32[8,128]{1,0:T(8,128)S(1)}) custom-call(s32[2]{0:T(128)S(1)} %pad_add_fusion.here, bf16[64,131072]{1,0:T(8,128)(2,1)} %bitcast.19, bf16[64,131072]{1,0:T(8,128)(2,1)} %bitcast.20, bf16[64,131072]{1,0:T(8,128)(2,1)} %bitcast.21, bf16[64,131072]{1,0:T(8,128)(2,1)} %bitcast.22, ...), custom_call_target="tpu_custom_call" | custom-call | tf_op jit(solution)/shard_map/pallas_call | solution.py:113
  21.5 0.1 collective-permute-start
  21.5 4.4 %shard_map.71 = (f32[32,16384]{1,0:T(8,128)}, f32[32,16384]{1,0:T(8,128)S(1)}, f32[8,128]{1,0:T(8,128)S(1)}) custom-call(s32[2]{0:T(128)S(1)} %pad_add_fusion.here, bf16[64,131072]{1,0:T(8,128)(2,1)} %bitcast.27, bf16[64,131072]{1,0:T(8,128)(2,1)} %bitcast.28, bf16[64,131072]{1,0:T(8,128)(2,1)} %bitcast.29, bf16[64,131072]{1,0:T(8,128)(2,1)} %bitcast.30, ...), custom_call_target="tpu_custom_call" | custom-call | tf_op jit(solution)/shard_map/pallas_call | solution.py:113
  26.0 26.6 %collective-permute-done.2.refs_8_.refs_11_ = f32[32,16384]{1,0:T(8,128)S(1)} collective-permute-done((f32[32,16384]{1,0:T(8,128)S(1)}, f32[32,16384]{1,0:T(8,128)S(1)}, u32[]{:S(2)}, u32[]{:S(2)}) %collective-permute-start.2) | collective-permute-done | bytes 2097184 | tf_op jit(solution)/shard_map/ppermute | solution.py:378
  52.5 1.6 collective-permute-start.1
  54.1 1.3 collective-permute-start.9
  55.4 5.9 %shard_map.72 = (f32[32,16384]{1,0:T(8,128)}, f32[32,16384]{1,0:T(8,128)}, f32[8,128]{1,0:T(8,128)S(1)}) custom-call(s32[2]{0:T(128)S(1)} %pad_add_fusion.here, bf16[64,131072]{1,0:T(8,128)(2,1)} %bitcast.40, bf16[64,131072]{1,0:T(8,128)(2,1)} %bitcast.36, bf16[64,131072]{1,0:T(8,128)(2,1)} %bitcast.37, bf16[64,131072]{1,0:T(8,128)(2,1)} %bitcast.38, ...), custom_call_target="tpu_custom_call" | custom-call | tf_op jit(solution)/shard_map/pallas_call | solution.py:113
  61.4 1.6 collective-permute-start.10
  62.9 0.2 collective-permute-start.4
  63.1 34.3 %collective-permute-done.refs_4_.refs_5_.refs_6_.refs_7_.refs_21_.refs_2_.refs_3_.refs_12_.refs_13_.refs_1_ = f32[32,16384]{1,0:T(8,128)S(1)} collective-permute-done((f32[32,16384]{1,0:T(8,128)}, f32[32,16384]{1,0:T(8,128)S(1)}, u32[]{:S(2)}, u32[]{:S(2)}) %collective-permute-start) | collective-permute-done | bytes 2097184 | tf_op jit(solution)/shard_map/ppermute | solution.py:378
  97.4 1.6 collective-permute-start.5
  99.0 5.4 %shard_map.73 = (f32[32,16384]{1,0:T(8,128)}, f32[32,16384]{1,0:T(8,128)S(1)}, f32[8,128]{1,0:T(8,128)S(1)}) custom-call(s32[2]{0:T(128)S(1)} %pad_add_fusion.here, bf16[64,131072]{1,0:T(8,128)(2,1)} %bitcast.43, bf16[64,131072]{1,0:T(8,128)(2,1)} %bitcast.44, bf16[64,131072]{1,0:T(8,128)(2,1)} %bitcast.45, bf16[64,131072]{1,0:T(8,128)(2,1)} %bitcast.46, ...), custom_call_target="tpu_custom_call" | custom-call | tf_op jit(solution)/shard_map/pallas_call | solution.py:113
  104.4 1.4 collective-permute-start.13
  105.7 0.2 collective-permute-done.9.refs_21_.refs_4_.refs_5_.refs_6_.refs_7_.refs_2_.refs_3_.refs_12_.refs_13_.refs_8_
  105.9 1.4 collective-permute-start.14
  107.4 3.6 %collective-permute-start.16 = (s32[1,8,8192]{2,1,0:T(8,128)S(1)}, s32[1,8,8192]{2,1,0:T(8,128)S(1)}, u32[]{:S(2)}, u32[]{:S(2)}) collective-permute-start(s32[1,8,8192]{2,1,0:T(8,128)S(1)} %copy-done.8), channel_id=1, source_target_pairs={{0,64},{16,80},{32,96},{48,112},{64,0},{80,16},{96,32},{112,48},{1... | collective-permute-start | bytes 786440 | tf_op jit(solution)/shard_map/ppermute | solution.py:382
  111.0 31.5 %collective-permute-done.4.refs_12_.refs_13_.refs_14_.refs_15_.refs_6_.refs_7_.refs_16_.refs_17_.refs_25_.refs_3_ = f32[32,16384]{1,0:T(8,128)} collective-permute-done((f32[32,16384]{1,0:T(8,128)}, f32[32,16384]{1,0:T(8,128)}, u32[]{:S(2)}, u32[]{:S(2)}) %collective-permute-start.4) | collective-permute-done | bytes 2097184 | tf_op jit(solution)/shard_map/ppermute | solution.py:378
  142.4 4.1 %collective-permute-start.15 = (s32[1,8,8192]{2,1,0:T(8,128)S(1)}, s32[1,8,8192]{2,1,0:T(8,128)S(1)}, u32[]{:S(2)}, u32[]{:S(2)}) collective-permute-start(s32[1,8,8192]{2,1,0:T(8,128)S(1)} %copy-done.8), channel_id=1, source_target_pairs={{0,96},{16,112},{32,0},{48,16},{64,32},{80,48},{96,64},{112,80},{1... | collective-permute-start | bytes 786440 | tf_op jit(solution)/shard_map/ppermute | solution.py:382
  146.5 2.2 shard_map.74
  148.7 1.4 collective-permute-start.11
  150.1 1.5 collective-permute-start.12
  151.6 1.6 copy-done.4
  153.2 1.6 copy-done.6
  154.8 2.2 shard_map.75
  157.0 0.1 collective-permute-start.17
  157.1 2.7 %collective-permute-start.18 = (f32[32,4096]{1,0:T(8,128)S(1)}, f32[32,4096]{1,0:T(8,128)S(1)}, u32[]{:S(2)}, u32[]{:S(2)}) collective-permute-start(f32[32,4096]{1,0:T(8,128)S(1)} %get-tuple-element.73), channel_id=1, source_target_pairs={{0,3},{1,0},{2,1},{3,2},{4,7},{5,4},{6,5},{7,6},{8,11},{9,8},{10,9... | collective-permute-start | bytes 1572872 | tf_op jit(solution)/shard_map/ppermute | solution.py:378
  159.7 3.6 %collective-permute-done.11.refs_20_.refs_21_.refs_25_ = f32[32,4096]{1,0:T(8,128)S(1)} collective-permute-done((f32[32,4096]{1,0:T(8,128)S(1)}, f32[32,4096]{1,0:T(8,128)S(1)}, u32[]{:S(2)}, u32[]{:S(2)}) %collective-permute-start.11) | collective-permute-done | bytes 524320 | tf_op jit(solution)/shard_map/ppermute | solution.py:378
  163.3 0.5 collective-permute-done.12.refs_22_.refs_23_.refs_26_
  163.9 2.3 %shard_map.76 = (f32[64,2048]{1,0:T(8,128)S(1)}, f32[64,2048]{1,0:T(8,128)S(1)}, f32[8,128]{1,0:T(8,128)S(1)}) custom-call(s32[2]{0:T(128)S(1)} %pad_add_fusion.here, bf16[64,131072]{1,0:T(8,128)(2,1)} %bitcast.59, bf16[64,131072]{1,0:T(8,128)(2,1)} %bitcast.60, f32[32,16384]{1,0:T(8,128)S(1)} %copy-done.1, f32[32,16384]{1,0:T(8,128)S(1)} %copy-done.1, ...), custom_call_target="tpu_custom_call" | custom-call | tf_op jit(solution)/shard_map/pallas_call | solution.py:113
  166.2 1.4 collective-permute-start.23
  167.6 1.6 collective-permute-start.24
  169.2 2.3 %shard_map.77 = (f32[64,2048]{1,0:T(8,128)S(1)}, f32[64,2048]{1,0:T(8,128)S(1)}, f32[8,128]{1,0:T(8,128)S(1)}) custom-call(s32[2]{0:T(128)S(1)} %pad_add_fusion.here, bf16[64,131072]{1,0:T(8,128)(2,1)} %bitcast.63, bf16[64,131072]{1,0:T(8,128)(2,1)} %bitcast.64, f32[32,16384]{1,0:T(8,128)S(1)} %copy-done.4, f32[32,16384]{1,0:T(8,128)S(1)} %copy-done.4, ...), custom_call_target="tpu_custom_call" | custom-call | tf_op jit(solution)/shard_map/pallas_call | solution.py:113
  171.5 0.2 collective-permute-start.25
  171.7 2.5 %collective-permute-start.26 = (f32[64,2048]{1,0:T(8,128)S(1)}, f32[64,2048]{1,0:T(8,128)S(1)}, u32[]{:S(2)}, u32[]{:S(2)}) collective-permute-start(f32[64,2048]{1,0:T(8,128)S(1)} %get-tuple-element.85), channel_id=1, source_target_pairs={{0,3},{1,0},{2,1},{3,2},{4,7},{5,4},{6,5},{7,6},{8,11},{9,8},{10,9... | collective-permute-start | bytes 1572872 | tf_op jit(solution)/shard_map/ppermute | solution.py:378
  174.3 2.3 %shard_map.78 = (f32[64,2048]{1,0:T(8,128)S(1)}, f32[64,2048]{1,0:T(8,128)S(1)}, f32[8,128]{1,0:T(8,128)S(1)}) custom-call(s32[2]{0:T(128)S(1)} %pad_add_fusion.here, bf16[64,131072]{1,0:T(8,128)(2,1)} %bitcast.67, bf16[64,131072]{1,0:T(8,128)(2,1)} %bitcast.68, f32[32,16384]{1,0:T(8,128)S(1)} %copy-done.4, f32[32,16384]{1,0:T(8,128)S(1)} %copy-done.4, ...), custom_call_target="tpu_custom_call" | custom-call | tf_op jit(solution)/shard_map/pallas_call | solution.py:113
  176.6 0.0 copy-start.12
  176.6 2.4 %shard_map.79 = (f32[64,2048]{1,0:T(8,128)S(1)}, f32[64,2048]{1,0:T(8,128)S(1)}, f32[8,128]{1,0:T(8,128)S(1)}) custom-call(s32[2]{0:T(128)S(1)} %pad_add_fusion.here, bf16[64,131072]{1,0:T(8,128)(2,1)} %bitcast.71, bf16[64,131072]{1,0:T(8,128)(2,1)} %bitcast.72, f32[32,16384]{1,0:T(8,128)S(1)} %copy-done.1, f32[32,16384]{1,0:T(8,128)S(1)} %copy-done.1, ...), custom_call_target="tpu_custom_call" | custom-call | tf_op jit(solution)/shard_map/pallas_call | solution.py:113
  179.0 0.1 collective-permute-start.19
  179.0 0.4 collective-permute-done.23.refs_5_
  179.4 2.3 %collective-permute-start.20 = (f32[64,2048]{1,0:T(8,128)S(1)}, f32[64,2048]{1,0:T(8,128)S(1)}, u32[]{:S(2)}, u32[]{:S(2)}) collective-permute-start(f32[64,2048]{1,0:T(8,128)S(1)} %get-tuple-element.79), channel_id=1, source_target_pairs={{0,12},{1,13},{2,14},{3,15},{4,0},{5,1},{6,2},{7,3},{8,4},{9,5},{1... | collective-permute-start | bytes 1572872 | tf_op jit(solution)/shard_map/ppermute | solution.py:378
  181.7 1.0 collective-permute-done.25.refs_12_
  182.8 1.6 collective-permute-start.22
  184.4 6.8 %shard_map.80 = (f32[1,64,8192]{2,1,0:T(8,128)}, f32[8,4096]{1,0:T(8,128)S(1)}, f32[8,128]{1,0:T(8,128)S(1)}) custom-call(s32[2]{0:T(128)S(1)} %pad_add_fusion.here, bf16[64,131072]{1,0:T(8,128)(2,1)} %bitcast.75, f32[32,16384]{1,0:T(8,128)S(1)} %copy-done.1, f32[32,16384]{1,0:T(8,128)} %copy-done.2, ...), custom_call_target="tpu_custom_call" | custom-call | tf_op jit(solution)/shard_map/pallas_call | solution.py:113
  191.2 1.8 collective-permute-start.32
  193.0 0.4 collective-permute-start.31
  193.4 1.0 collective-permute-start.30
  194.5 6.8 %shard_map.81 = (f32[1,64,8192]{2,1,0:T(8,128)}, f32[8,4096]{1,0:T(8,128)S(1)}, f32[8,128]{1,0:T(8,128)S(1)}) custom-call(s32[2]{0:T(128)S(1)} %pad_add_fusion.here, bf16[64,131072]{1,0:T(8,128)(2,1)} %bitcast.77, f32[32,16384]{1,0:T(8,128)S(1)} %copy-done.1, f32[32,16384]{1,0:T(8,128)} %copy-done.2, ...), custom_call_target="tpu_custom_call", output_to_operand_aliasing={{0}: (19, {})} | custom-call | tf_op jit(solution)/shard_map/pallas_call | solution.py:113
  201.2 1.1 collective-permute-start.29
  202.4 2.0 collective-permute-start.28
  204.4 4.0 %shard_map.82 = (f32[64,4096]{1,0:T(8,128)S(1)}, f32[8,128]{1,0:T(8,128)S(1)}) custom-call(s32[2]{0:T(128)S(1)} %pad_add_fusion.here, f32[8,4096]{1,0:T(8,128)S(1)} %get-tuple-element.90.refs_0_, f32[8,4096]{1,0:T(8,128)S(1)} %collective-permute-done.30.refs_1_, f32[8,4096]{1,0:T(8,128)S(1)} %collective-permute-done.31.refs_2_, ...), custom_call_target="tpu_custom_call" | custom-call | tf_op jit(solution)/shard_map/pallas_call | solution.py:113
  208.4 11.4 %collective-permute-start.34 = (f32[64,4096]{1,0:T(8,128)S(1)}, f32[64,4096]{1,0:T(8,128)S(1)}, u32[]{:S(2)}, u32[]{:S(2)}) collective-permute-start(f32[64,4096]{1,0:T(8,128)S(1)} %get-tuple-element.94.refs_0_), channel_id=1, source_target_pairs={{0,16},{16,0},{32,48},{48,32},{64,80},{80,64},{96,112},{112,96},{1... | collective-permute-start | bytes 3145736 | tf_op jit(solution)/shard_map/ppermute | solution.py:388
  219.8 4.0 %shard_map.83 = (f32[64,4096]{1,0:T(8,128)S(1)}, f32[8,128]{1,0:T(8,128)S(1)}) custom-call(s32[2]{0:T(128)S(1)} %pad_add_fusion.here, f32[8,4096]{1,0:T(8,128)S(1)} %get-tuple-element.89.refs_0_, f32[8,4096]{1,0:T(8,128)S(1)} %collective-permute-done.27.refs_1_, f32[8,4096]{1,0:T(8,128)S(1)} %collective-permute-done.28.refs_2_, ...), custom_call_target="tpu_custom_call" | custom-call | tf_op jit(solution)/shard_map/pallas_call | solution.py:113
  223.9 2.1 collective-permute-start.33
  226.0 2.2 shard_map.84
  228.2 0.1 collective-permute-done.33.refs_1_
  228.2 2.2 shard_map.85
  (53 shorter events, 0.1 us)
Async XLA Ops:
  0.7 6.9 %copy-start.7 = (s32[1,8,8192]{2,1,0:T(8,128)S(1)}, s32[1,8,8192]{2,1,0:T(8,128)}, u32[]{:S(2)}) copy-start(s32[1,8,8192]{2,1,0:T(8,128)} %refs_4_.3) | copy-start | bytes 786436
  4.1 48.4 %collective-permute-start.2 = (f32[32,16384]{1,0:T(8,128)S(1)}, f32[32,16384]{1,0:T(8,128)S(1)}, u32[]{:S(2)}, u32[]{:S(2)}) collective-permute-start(f32[32,16384]{1,0:T(8,128)S(1)} %get-tuple-element.55), channel_id=1, source_target_pairs={{0,1},{1,2},{2,3},{3,0},{4,5},{5,6},{6,7},{7,4},{8,9},{9,10},{10,1... | collective-permute-start | bytes 6291464 | tf_op jit(solution)/shard_map/ppermute | solution.py:378
  6.3 47.9 %collective-permute-start.3 = (f32[32,16384]{1,0:T(8,128)S(1)}, f32[32,16384]{1,0:T(8,128)}, u32[]{:S(2)}, u32[]{:S(2)}) collective-permute-start(f32[32,16384]{1,0:T(8,128)S(1)} %get-tuple-element.56), channel_id=1, source_target_pairs={{0,3},{1,0},{2,1},{3,2},{4,7},{5,4},{6,5},{7,6},{8,11},{9,8},{10,9... | collective-permute-start | bytes 6291464 | tf_op jit(solution)/shard_map/ppermute | solution.py:378
  7.6 13.8 %collective-permute-start.8 = (s32[1,8,8192]{2,1,0:T(8,128)S(1)}, s32[1,8,8192]{2,1,0:T(8,128)S(1)}, u32[]{:S(2)}, u32[]{:S(2)}) collective-permute-start(s32[1,8,8192]{2,1,0:T(8,128)S(1)} %copy-done.7), channel_id=1, source_target_pairs={{0,32},{16,48},{32,64},{48,80},{64,96},{80,112},{96,0},{112,16},{1... | collective-permute-start | bytes 786440 | tf_op jit(solution)/shard_map/ppermute | solution.py:382
  13.8 47.6 %collective-permute-start.6 = (f32[32,16384]{1,0:T(8,128)}, f32[32,16384]{1,0:T(8,128)}, u32[]{:S(2)}, u32[]{:S(2)}) collective-permute-start(f32[32,16384]{1,0:T(8,128)} %get-tuple-element.61), channel_id=1, source_target_pairs={{0,4},{1,5},{2,6},{3,7},{4,8},{5,9},{6,10},{7,11},{8,12},{9,13},{1... | collective-permute-start | bytes 6291464 | tf_op jit(solution)/shard_map/ppermute | solution.py:378
  15.0 47.9 %collective-permute-start.7 = (f32[32,16384]{1,0:T(8,128)S(1)}, f32[32,16384]{1,0:T(8,128)}, u32[]{:S(2)}, u32[]{:S(2)}) collective-permute-start(f32[32,16384]{1,0:T(8,128)S(1)} %get-tuple-element.62), channel_id=1, source_target_pairs={{0,12},{1,13},{2,14},{3,15},{4,0},{5,1},{6,2},{7,3},{8,4},{9,5},{1... | collective-permute-start | bytes 6291464 | tf_op jit(solution)/shard_map/ppermute | solution.py:378
  21.4 77.5 %copy-start.9 = (s32[1,8,8192]{2,1,0:T(8,128)}, s32[1,8,8192]{2,1,0:T(8,128)S(1)}, u32[]{:S(2)}) copy-start(s32[1,8,8192]{2,1,0:T(8,128)S(1)} %collective-permute-done.8.refs_13_.refs_5_) | copy-start | bytes 786436
  21.5 75.9 %collective-permute-start = (f32[32,16384]{1,0:T(8,128)}, f32[32,16384]{1,0:T(8,128)S(1)}, u32[]{:S(2)}, u32[]{:S(2)}) collective-permute-start(f32[32,16384]{1,0:T(8,128)} %get-tuple-element.53), channel_id=1, source_target_pairs={{0,1},{1,2},{2,3},{3,0},{4,5},{5,6},{6,7},{7,4},{8,9},{9,10},{10,1... | collective-permute-start | bytes 6291464 | tf_op jit(solution)/shard_map/ppermute | solution.py:378
  52.5 2.9 %copy-start.13 = (f32[32,16384]{1,0:T(8,128)}, f32[32,16384]{1,0:T(8,128)S(1)}, u32[]{:S(2)}) copy-start(f32[32,16384]{1,0:T(8,128)S(1)} %collective-permute-done.2.refs_8_.refs_11_) | copy-start | bytes 6291460
  52.5 51.8 %collective-permute-start.1 = (f32[32,16384]{1,0:T(8,128)}, f32[32,16384]{1,0:T(8,128)S(1)}, u32[]{:S(2)}, u32[]{:S(2)}) collective-permute-start(f32[32,16384]{1,0:T(8,128)} %get-tuple-element.54), channel_id=1, source_target_pairs={{0,3},{1,0},{2,1},{3,2},{4,7},{5,4},{6,5},{7,6},{8,11},{9,8},{10,9... | collective-permute-start | bytes 6291464 | tf_op jit(solution)/shard_map/ppermute | solution.py:378
  54.1 51.8 %collective-permute-start.9 = (f32[32,16384]{1,0:T(8,128)}, f32[32,16384]{1,0:T(8,128)S(1)}, u32[]{:S(2)}, u32[]{:S(2)}) collective-permute-start(f32[32,16384]{1,0:T(8,128)} %get-tuple-element.65), channel_id=1, source_target_pairs={{0,4},{1,5},{2,6},{3,7},{4,8},{5,9},{6,10},{7,11},{8,12},{9,13},{1... | collective-permute-start | bytes 6291464 | tf_op jit(solution)/shard_map/ppermute | solution.py:378
  61.4 46.0 %collective-permute-start.10 = (f32[32,16384]{1,0:T(8,128)S(1)}, f32[32,16384]{1,0:T(8,128)S(1)}, u32[]{:S(2)}, u32[]{:S(2)}) collective-permute-start(f32[32,16384]{1,0:T(8,128)S(1)} %get-tuple-element.66), channel_id=1, source_target_pairs={{0,12},{1,13},{2,14},{3,15},{4,0},{5,1},{6,2},{7,3},{8,4},{9,5},{1... | collective-permute-start | bytes 6291464 | tf_op jit(solution)/shard_map/ppermute | solution.py:378
  62.9 79.5 %collective-permute-start.4 = (f32[32,16384]{1,0:T(8,128)}, f32[32,16384]{1,0:T(8,128)}, u32[]{:S(2)}, u32[]{:S(2)}) collective-permute-start(f32[32,16384]{1,0:T(8,128)} %get-tuple-element.59), channel_id=1, source_target_pairs={{0,1},{1,2},{2,3},{3,0},{4,5},{5,6},{6,7},{7,4},{8,9},{9,10},{10,1... | collective-permute-start | bytes 6291464 | tf_op jit(solution)/shard_map/ppermute | solution.py:378
  97.4 49.1 %copy-start = (f32[32,16384]{1,0:T(8,128)}, f32[32,16384]{1,0:T(8,128)S(1)}, u32[]{:S(2)}) copy-start(f32[32,16384]{1,0:T(8,128)S(1)} %collective-permute-done.refs_4_.refs_5_.refs_6_.refs_7_.refs_21_.refs_2_.refs_3_.refs_12_.refs_13_.refs_1_) | copy-start | bytes 6291460
  97.4 49.1 %collective-permute-start.5 = (f32[32,16384]{1,0:T(8,128)}, f32[32,16384]{1,0:T(8,128)}, u32[]{:S(2)}, u32[]{:S(2)}) collective-permute-start(f32[32,16384]{1,0:T(8,128)} %get-tuple-element.60), channel_id=1, source_target_pairs={{0,3},{1,0},{2,1},{3,2},{4,7},{5,4},{6,5},{7,6},{8,11},{9,8},{10,9... | collective-permute-start | bytes 6291464 | tf_op jit(solution)/shard_map/ppermute | solution.py:378
  99.0 8.4 %copy-start.8 = (s32[1,8,8192]{2,1,0:T(8,128)S(1)}, s32[1,8,8192]{2,1,0:T(8,128)}, u32[]{:S(2)}) copy-start(s32[1,8,8192]{2,1,0:T(8,128)} %refs_4_.3) | copy-start | bytes 786436
  104.4 44.3 %copy-start.2 = (f32[32,16384]{1,0:T(8,128)}, f32[32,16384]{1,0:T(8,128)S(1)}, u32[]{:S(2)}) copy-start(f32[32,16384]{1,0:T(8,128)S(1)} %collective-permute-done.1.refs_8_.refs_9_.refs_10_.refs_11_.refs_22_.refs_4_.refs_5_.refs_14_.refs_15_.refs_2_) | copy-start | bytes 6291460
  104.4 47.2 %collective-permute-start.13 = (f32[32,16384]{1,0:T(8,128)}, f32[32,16384]{1,0:T(8,128)}, u32[]{:S(2)}, u32[]{:S(2)}) collective-permute-start(f32[32,16384]{1,0:T(8,128)} %get-tuple-element.69), channel_id=1, source_target_pairs={{0,4},{1,5},{2,6},{3,7},{4,8},{5,9},{6,10},{7,11},{8,12},{9,13},{1... | collective-permute-start | bytes 6291464 | tf_op jit(solution)/shard_map/ppermute | solution.py:378
  105.9 40.6 %copy-start.3 = (f32[32,16384]{1,0:T(8,128)}, f32[32,16384]{1,0:T(8,128)S(1)}, u32[]{:S(2)}) copy-start(f32[32,16384]{1,0:T(8,128)S(1)} %collective-permute-done.9.refs_21_.refs_4_.refs_5_.refs_6_.refs_7_.refs_2_.refs_3_.refs_12_.refs_13_.refs_8_) | copy-start | bytes 6291460
  105.9 45.7 %collective-permute-start.14 = (f32[32,16384]{1,0:T(8,128)S(1)}, f32[32,16384]{1,0:T(8,128)}, u32[]{:S(2)}, u32[]{:S(2)}) collective-permute-start(f32[32,16384]{1,0:T(8,128)S(1)} %get-tuple-element.70), channel_id=1, source_target_pairs={{0,12},{1,13},{2,14},{3,15},{4,0},{5,1},{6,2},{7,3},{8,4},{9,5},{1... | collective-permute-start | bytes 6291464 | tf_op jit(solution)/shard_map/ppermute | solution.py:378
  107.4 39.2 %copy-start.5 = (f32[32,16384]{1,0:T(8,128)}, f32[32,16384]{1,0:T(8,128)S(1)}, u32[]{:S(2)}) copy-start(f32[32,16384]{1,0:T(8,128)S(1)} %collective-permute-done.10.refs_22_.refs_8_.refs_9_.refs_10_.refs_11_.refs_4_.refs_5_.refs_14_.refs_15_) | copy-start | bytes 6291460
  107.4 42.7 %collective-permute-start.16 = (s32[1,8,8192]{2,1,0:T(8,128)S(1)}, s32[1,8,8192]{2,1,0:T(8,128)S(1)}, u32[]{:S(2)}, u32[]{:S(2)}) collective-permute-start(s32[1,8,8192]{2,1,0:T(8,128)S(1)} %copy-done.8), channel_id=1, source_target_pairs={{0,64},{16,80},{32,96},{48,112},{64,0},{80,16},{96,32},{112,48},{1... | collective-permute-start | bytes 786440 | tf_op jit(solution)/shard_map/ppermute | solution.py:382
  142.4 9.2 %collective-permute-start.15 = (s32[1,8,8192]{2,1,0:T(8,128)S(1)}, s32[1,8,8192]{2,1,0:T(8,128)S(1)}, u32[]{:S(2)}, u32[]{:S(2)}) collective-permute-start(s32[1,8,8192]{2,1,0:T(8,128)S(1)} %copy-done.8), channel_id=1, source_target_pairs={{0,96},{16,112},{32,0},{48,16},{64,32},{80,48},{96,64},{112,80},{1... | collective-permute-start | bytes 786440 | tf_op jit(solution)/shard_map/ppermute | solution.py:382
  148.7 14.6 %collective-permute-start.11 = (f32[32,4096]{1,0:T(8,128)S(1)}, f32[32,4096]{1,0:T(8,128)S(1)}, u32[]{:S(2)}, u32[]{:S(2)}) collective-permute-start(f32[32,4096]{1,0:T(8,128)S(1)} %get-tuple-element.67), channel_id=1, source_target_pairs={{0,4},{1,5},{2,6},{3,7},{4,8},{5,9},{6,10},{7,11},{8,12},{9,13},{1... | collective-permute-start | bytes 1572872 | tf_op jit(solution)/shard_map/ppermute | solution.py:378
  150.1 13.8 %collective-permute-start.12 = (f32[32,4096]{1,0:T(8,128)S(1)}, f32[32,4096]{1,0:T(8,128)S(1)}, u32[]{:S(2)}, u32[]{:S(2)}) collective-permute-start(f32[32,4096]{1,0:T(8,128)S(1)} %get-tuple-element.68), channel_id=1, source_target_pairs={{0,12},{1,13},{2,14},{3,15},{4,0},{5,1},{6,2},{7,3},{8,4},{9,5},{1... | collective-permute-start | bytes 1572872 | tf_op jit(solution)/shard_map/ppermute | solution.py:378
  151.6 1.6 copy-start.4
  153.2 1.6 copy-start.6
  154.8 9.1 %copy-start.1 = (f32[32,16384]{1,0:T(8,128)S(1)}, f32[32,16384]{1,0:T(8,128)}, u32[]{:S(2)}) copy-start(f32[32,16384]{1,0:T(8,128)} %copy-done) | copy-start | bytes 6291460
  157.0 12.2 %collective-permute-start.17 = (f32[32,4096]{1,0:T(8,128)S(1)}, f32[32,4096]{1,0:T(8,128)S(1)}, u32[]{:S(2)}, u32[]{:S(2)}) collective-permute-start(f32[32,4096]{1,0:T(8,128)S(1)} %get-tuple-element.72), channel_id=1, source_target_pairs={{0,1},{1,2},{2,3},{3,0},{4,5},{5,6},{6,7},{7,4},{8,9},{9,10},{10,1... | collective-permute-start | bytes 1572872 | tf_op jit(solution)/shard_map/ppermute | solution.py:378
  157.1 12.1 %collective-permute-start.18 = (f32[32,4096]{1,0:T(8,128)S(1)}, f32[32,4096]{1,0:T(8,128)S(1)}, u32[]{:S(2)}, u32[]{:S(2)}) collective-permute-start(f32[32,4096]{1,0:T(8,128)S(1)} %get-tuple-element.73), channel_id=1, source_target_pairs={{0,3},{1,0},{2,1},{3,2},{4,7},{5,4},{6,5},{7,6},{8,11},{9,8},{10,9... | collective-permute-start | bytes 1572872 | tf_op jit(solution)/shard_map/ppermute | solution.py:378
  166.2 13.2 %collective-permute-start.23 = (f32[64,2048]{1,0:T(8,128)S(1)}, f32[64,2048]{1,0:T(8,128)S(1)}, u32[]{:S(2)}, u32[]{:S(2)}) collective-permute-start(f32[64,2048]{1,0:T(8,128)S(1)} %get-tuple-element.82), channel_id=1, source_target_pairs={{0,4},{1,5},{2,6},{3,7},{4,8},{5,9},{6,10},{7,11},{8,12},{9,13},{1... | collective-permute-start | bytes 1572872 | tf_op jit(solution)/shard_map/ppermute | solution.py:378
  167.6 14.1 %collective-permute-start.24 = (f32[64,2048]{1,0:T(8,128)S(1)}, f32[64,2048]{1,0:T(8,128)S(1)}, u32[]{:S(2)}, u32[]{:S(2)}) collective-permute-start(f32[64,2048]{1,0:T(8,128)S(1)} %get-tuple-element.83), channel_id=1, source_target_pairs={{0,12},{1,13},{2,14},{3,15},{4,0},{5,1},{6,2},{7,3},{8,4},{9,5},{1... | collective-permute-start | bytes 1572872 | tf_op jit(solution)/shard_map/ppermute | solution.py:378
  171.5 11.2 %collective-permute-start.25 = (f32[64,2048]{1,0:T(8,128)S(1)}, f32[64,2048]{1,0:T(8,128)S(1)}, u32[]{:S(2)}, u32[]{:S(2)}) collective-permute-start(f32[64,2048]{1,0:T(8,128)S(1)} %get-tuple-element.84), channel_id=1, source_target_pairs={{0,1},{1,2},{2,3},{3,0},{4,5},{5,6},{6,7},{7,4},{8,9},{9,10},{10,1... | collective-permute-start | bytes 1572872 | tf_op jit(solution)/shard_map/ppermute | solution.py:378
  171.7 12.7 %collective-permute-start.26 = (f32[64,2048]{1,0:T(8,128)S(1)}, f32[64,2048]{1,0:T(8,128)S(1)}, u32[]{:S(2)}, u32[]{:S(2)}) collective-permute-start(f32[64,2048]{1,0:T(8,128)S(1)} %get-tuple-element.85), channel_id=1, source_target_pairs={{0,3},{1,0},{2,1},{3,2},{4,7},{5,4},{6,5},{7,6},{8,11},{9,8},{10,9... | collective-permute-start | bytes 1572872 | tf_op jit(solution)/shard_map/ppermute | solution.py:378
  176.6 7.8 %copy-start.11 = (bf16[64,256]{1,0:T(8,128)(2,1)S(1)}, bf16[64,256]{1,0:T(8,128)(2,1)}, u32[]{:S(2)}) copy-start(bf16[64,256]{1,0:T(8,128)(2,1)} %constant.25.clone.refs_17_.refs_8_) | copy-start | bytes 98308
  176.6 7.8 %copy-start.12 = (bf16[64,256]{1,0:T(8,128)(2,1)S(1)}, bf16[64,256]{1,0:T(8,128)(2,1)}, u32[]{:S(2)}) copy-start(bf16[64,256]{1,0:T(8,128)(2,1)} %constant.24.clone.refs_16_) | copy-start | bytes 98308
  179.0 14.0 %collective-permute-start.19 = (f32[64,2048]{1,0:T(8,128)S(1)}, f32[64,2048]{1,0:T(8,128)S(1)}, u32[]{:S(2)}, u32[]{:S(2)}) collective-permute-start(f32[64,2048]{1,0:T(8,128)S(1)} %get-tuple-element.78), channel_id=1, source_target_pairs={{0,4},{1,5},{2,6},{3,7},{4,8},{5,9},{6,10},{7,11},{8,12},{9,13},{1... | collective-permute-start | bytes 1572872 | tf_op jit(solution)/shard_map/ppermute | solution.py:378
  179.4 14.0 %collective-permute-start.20 = (f32[64,2048]{1,0:T(8,128)S(1)}, f32[64,2048]{1,0:T(8,128)S(1)}, u32[]{:S(2)}, u32[]{:S(2)}) collective-permute-start(f32[64,2048]{1,0:T(8,128)S(1)} %get-tuple-element.79), channel_id=1, source_target_pairs={{0,12},{1,13},{2,14},{3,15},{4,0},{5,1},{6,2},{7,3},{8,4},{9,5},{1... | collective-permute-start | bytes 1572872 | tf_op jit(solution)/shard_map/ppermute | solution.py:378
  181.7 12.8 %collective-permute-start.21 = (f32[64,2048]{1,0:T(8,128)S(1)}, f32[64,2048]{1,0:T(8,128)S(1)}, u32[]{:S(2)}, u32[]{:S(2)}) collective-permute-start(f32[64,2048]{1,0:T(8,128)S(1)} %get-tuple-element.80), channel_id=1, source_target_pairs={{0,1},{1,2},{2,3},{3,0},{4,5},{5,6},{6,7},{7,4},{8,9},{9,10},{10,1... | collective-permute-start | bytes 1572872 | tf_op jit(solution)/shard_map/ppermute | solution.py:378
  182.8 11.7 %collective-permute-start.22 = (f32[64,2048]{1,0:T(8,128)S(1)}, f32[64,2048]{1,0:T(8,128)S(1)}, u32[]{:S(2)}, u32[]{:S(2)}) collective-permute-start(f32[64,2048]{1,0:T(8,128)S(1)} %get-tuple-element.81), channel_id=1, source_target_pairs={{0,3},{1,0},{2,1},{3,2},{4,7},{5,4},{6,5},{7,6},{8,11},{9,8},{10,9... | collective-permute-start | bytes 1572872 | tf_op jit(solution)/shard_map/ppermute | solution.py:378
  191.2 13.2 %collective-permute-start.32 = (f32[8,4096]{1,0:T(8,128)S(1)}, f32[8,4096]{1,0:T(8,128)S(1)}, u32[]{:S(2)}, u32[]{:S(2)}) collective-permute-start(f32[8,4096]{1,0:T(8,128)S(1)} %get-tuple-element.90.refs_0_), channel_id=1, source_target_pairs={{0,64},{16,80},{32,96},{48,112},{64,0},{80,16},{96,32},{112,48},{1... | collective-permute-start | bytes 393224 | tf_op jit(solution)/shard_map/ppermute | solution.py:382
  193.0 11.4 %collective-permute-start.31 = (f32[8,4096]{1,0:T(8,128)S(1)}, f32[8,4096]{1,0:T(8,128)S(1)}, u32[]{:S(2)}, u32[]{:S(2)}) collective-permute-start(f32[8,4096]{1,0:T(8,128)S(1)} %get-tuple-element.90.refs_0_), channel_id=1, source_target_pairs={{0,96},{16,112},{32,0},{48,16},{64,32},{80,48},{96,64},{112,80},{1... | collective-permute-start | bytes 393224 | tf_op jit(solution)/shard_map/ppermute | solution.py:382
  193.4 11.0 %collective-permute-start.30 = (f32[8,4096]{1,0:T(8,128)S(1)}, f32[8,4096]{1,0:T(8,128)S(1)}, u32[]{:S(2)}, u32[]{:S(2)}) collective-permute-start(f32[8,4096]{1,0:T(8,128)S(1)} %get-tuple-element.90.refs_0_), channel_id=1, source_target_pairs={{0,32},{16,48},{32,64},{48,80},{64,96},{80,112},{96,0},{112,16},{1... | collective-permute-start | bytes 393224 | tf_op jit(solution)/shard_map/ppermute | solution.py:382
  194.5 9.9 %copy-start.10 = (s32[1,8,8192]{2,1,0:T(8,128)S(1)}, s32[1,8,8192]{2,1,0:T(8,128)}, u32[]{:S(2)}) copy-start(s32[1,8,8192]{2,1,0:T(8,128)} %copy-done.9) | copy-start | bytes 786436
  201.2 18.6 %collective-permute-start.29 = (f32[8,4096]{1,0:T(8,128)S(1)}, f32[8,4096]{1,0:T(8,128)S(1)}, u32[]{:S(2)}, u32[]{:S(2)}) collective-permute-start(f32[8,4096]{1,0:T(8,128)S(1)} %get-tuple-element.89.refs_0_), channel_id=1, source_target_pairs={{0,64},{16,80},{32,96},{48,112},{64,0},{80,16},{96,32},{112,48},{1... | collective-permute-start | bytes 393224 | tf_op jit(solution)/shard_map/ppermute | solution.py:382
  202.4 17.4 %collective-permute-start.28 = (f32[8,4096]{1,0:T(8,128)S(1)}, f32[8,4096]{1,0:T(8,128)S(1)}, u32[]{:S(2)}, u32[]{:S(2)}) collective-permute-start(f32[8,4096]{1,0:T(8,128)S(1)} %get-tuple-element.89.refs_0_), channel_id=1, source_target_pairs={{0,96},{16,112},{32,0},{48,16},{64,32},{80,48},{96,64},{112,80},{1... | collective-permute-start | bytes 393224 | tf_op jit(solution)/shard_map/ppermute | solution.py:382
  204.4 15.4 %collective-permute-start.27 = (f32[8,4096]{1,0:T(8,128)S(1)}, f32[8,4096]{1,0:T(8,128)S(1)}, u32[]{:S(2)}, u32[]{:S(2)}) collective-permute-start(f32[8,4096]{1,0:T(8,128)S(1)} %get-tuple-element.89.refs_0_), channel_id=1, source_target_pairs={{0,32},{16,48},{32,64},{48,80},{64,96},{80,112},{96,0},{112,16},{1... | collective-permute-start | bytes 393224 | tf_op jit(solution)/shard_map/ppermute | solution.py:382
  208.4 17.5 %collective-permute-start.34 = (f32[64,4096]{1,0:T(8,128)S(1)}, f32[64,4096]{1,0:T(8,128)S(1)}, u32[]{:S(2)}, u32[]{:S(2)}) collective-permute-start(f32[64,4096]{1,0:T(8,128)S(1)} %get-tuple-element.94.refs_0_), channel_id=1, source_target_pairs={{0,16},{16,0},{32,48},{48,32},{64,80},{80,64},{96,112},{112,96},{1... | collective-permute-start | bytes 3145736 | tf_op jit(solution)/shard_map/ppermute | solution.py:388
  223.9 4.4 %collective-permute-start.33 = (f32[64,4096]{1,0:T(8,128)S(1)}, f32[64,4096]{1,0:T(8,128)S(1)}, u32[]{:S(2)}, u32[]{:S(2)}) collective-permute-start(f32[64,4096]{1,0:T(8,128)S(1)} %get-tuple-element.93.refs_0_), channel_id=1, source_target_pairs={{0,16},{16,0},{32,48},{48,32},{64,80},{80,64},{96,112},{112,96},{1... | collective-permute-start | bytes 3145736 | tf_op jit(solution)/shard_map/ppermute | solution.py:388

commit v7 on v6

--- a/solution.py
+++ b/solution.py
@@ -13,13 +13,14 @@
 SIDE = 4
 TILE = 1024
 CHUNK = 256
-FINE, BROAD = 1024, 1024
+FINE, BROAD = 1024, 2048
 PARTS = (2, 2)
-AXES = (0, 0, 0, 1, 1, 0)
+AXES = (0, 0, 0, 1, 1, 1)
 LAG = (2, 2, 2, 2, 2, 2)
 PLACES_WITH = ((0, 1), (1, 0), (1, 0))
 STEPS = (1, -1, 2)
-TAIL = ("f0", "f1", "s0", "s1", "j0", "j1")
+TAIL = ('f0', 'f1', 's0', 's1', 'j0', 'j1')
+TOGETHER = 2
 VMEM_LIMIT = 48 * 1024 * 1024
 F32 = jnp.float32
 BF16 = jnp.bfloat16
@@ -63,12 +64,13 @@
         return fold(here[0] if self.x_first else here[1], step)
 
     def grid_blocks(self, step, rows):
-        def spec(tile):
+        def spec(other, tile):
             return pl.BlockSpec(
-                (HALF, TILE), lambda i, here: (rows, self.column(here, step, i) + tile)
+                (HALF, TILE),
+                lambda i, here: (rows, self.column(here, step, i * TOGETHER + other) + tile),
             )
 
-        return [spec(tile) for tile in range(self.count)]
+        return [spec(other, tile) for other in range(TOGETHER) for tile in range(self.count)]
 
     def one_blocks(self, step):
         def spec(tile):
@@ -136,7 +138,7 @@
 
 
 def send_part(line, half, partials, up_from, down_from):
-    w, n = half.width, half.count
+    n = half.count * TOGETHER
 
     def body(here, *refs):
         up, down = refs[2 * n :]
@@ -144,11 +146,11 @@
             up[:, col] = part_up[...].astype(F32)
             down[:, col] = part_down[...].astype(F32)
 
-    shape = jax.ShapeDtypeStruct((HALF, SIDE * w), F32)
-    spec = pl.BlockSpec((HALF, w), lambda i, here: (0, i))
-    return line.call(
-        body, SIDE, [partials] * (2 * n), half.grid_blocks(*up_from) + half.grid_blocks(*down_from),
-        (shape, shape), (spec, spec),
+    shape = jax.ShapeDtypeStruct((HALF, SIDE * half.width), F32)
+    spec = pl.BlockSpec((HALF, n * TILE), lambda i, here: (0, i))
+    return line.call(
+        body, SIDE // TOGETHER, [partials] * (2 * n),
+        half.grid_blocks(*up_from) + half.grid_blocks(*down_from), (shape, shape), (spec, spec),
     )
 
 
@@ -161,7 +163,7 @@
 
 
 def send_near(line, half, partials, far_up, far_down):
-    w, n = half.width, half.count
+    n = half.count * TOGETHER
 
     def body(here, *refs):
         far_up, far_down, up, down = refs[2 * n :]
@@ -169,10 +171,10 @@
             up[:, col] = part_up[...].astype(F32) + far_up[:, col]
             down[:, col] = part_down[...].astype(F32) + far_down[:, col]
 
-    shape = jax.ShapeDtypeStruct((HALF, SIDE * w), F32)
-    spec = pl.BlockSpec((HALF, w), lambda i, here: (0, i))
-    return line.call(
-        body, SIDE, [partials] * (2 * n) + [far_up, far_down],
+    shape = jax.ShapeDtypeStruct((HALF, SIDE * half.width), F32)
+    spec = pl.BlockSpec((HALF, n * TILE), lambda i, here: (0, i))
+    return line.call(
+        body, SIDE // TOGETHER, [partials] * (2 * n) + [far_up, far_down],
         half.grid_blocks(1, 0) + half.grid_blocks(-1, 1) + [spec, spec],
         (shape, shape), (spec, spec),
     )

time: 232 us -> 233 us (level)
  waiting for transfers between devices: 98.2 us -> 105 us
    ppermute x24, waiting for transfers between devices: 98.1 us -> 104 us  [along(): lax.ppermute(value, 'fsdp', shift(0, step) if x_first else shift(step, 0))]
  transfers between devices with their start and end apart: 35 -> 35, of which waited for: 9 -> 10; matrix products, arithmetic and copies ran while one was open for 0% -> 0% of each run, Pallas kernels for 27% -> 26%
where the time goes in v7:
time: 233 us; the launch traced here: 232 us
  waiting for transfers between devices  105 us (45%)
  Pallas kernels  66.4 us (28%)
  starting transfers between devices  57.9 us (25%)
    ppermute x24, waiting for transfers between devices, along(): lax.ppermute(value, 'fsdp', shift(0, step) if x_first else shift(step, 0))  104 us
    pallas_call x18, Pallas kernels, call(): pl.pallas_call(run, grid_spec=pltpu.PrefetchScalarGridSpec(num_scalar_pre...  66.4 us
    ppermute x24, starting transfers between devices, along(): lax.ppermute(value, 'fsdp', shift(0, step) if x_first else shift(step, 0))  30.5 us
    ppermute x9, starting transfers between devices, along_z(): lax.ppermute(value, 'rep', [(z * 2 + c, (z + step) % SIDE * 2 + c) for z...  16 us
    ppermute x2, starting transfers between devices, other_core(): return lax.ppermute(value, 'rep', [(r, r ^ 1) for r in range(2 * SIDE)])  11.3 us
  transfers between devices with their start and end apart: 35, of which 10 were waited for; matrix products, arithmetic and copies ran while one was open for 0% of the time, Pallas kernels for 26%

profile of v7, /device:TPU:1, one launch (start us, length us, event | category | flops | bytes accessed | tf_op | source)
XLA Modules:
  0.0 231.7 jit_solution(9203715070608872300)
XLA Ops:
  0.6 0.1 pad_add_fusion.here
  0.7 4.1 %shard_map.68 = (f32[32,16384]{1,0:T(8,128)}, f32[32,16384]{1,0:T(8,128)}, f32[8,128]{1,0:T(8,128)S(1)}) custom-call(s32[2]{0:T(128)S(1)} %pad_add_fusion.here, bf16[64,131072]{1,0:T(8,128)(2,1)} %bitcast.3, bf16[64,131072]{1,0:T(8,128)(2,1)} %bitcast.4, bf16[64,131072]{1,0:T(8,128)(2,1)} %bitcast.5, bf16[64,131072]{1,0:T(8,128)(2,1)} %bitcast.6, ...), custom_call_target="tpu_custom_call" | custom-call | tf_op jit(solution)/shard_map/pallas_call | solution.py:115
  4.8 2.1 collective-permute-start.2
  6.9 1.4 collective-permute-start.3
  8.3 1.8 collective-permute-start.8
  10.0 4.1 %shard_map.69 = (f32[32,16384]{1,0:T(8,128)}, f32[32,16384]{1,0:T(8,128)}, f32[8,128]{1,0:T(8,128)S(1)}) custom-call(s32[2]{0:T(128)S(1)} %pad_add_fusion.here, bf16[64,131072]{1,0:T(8,128)(2,1)} %bitcast.26, bf16[64,131072]{1,0:T(8,128)(2,1)} %bitcast.20, bf16[64,131072]{1,0:T(8,128)(2,1)} %bitcast.21, bf16[64,131072]{1,0:T(8,128)(2,1)} %bitcast.22, ...), custom_call_target="tpu_custom_call" | custom-call | tf_op jit(solution)/shard_map/pallas_call | solution.py:115
  14.2 1.4 collective-permute-start.6
  15.5 1.5 collective-permute-start.7
  17.0 4.0 %shard_map.70 = (f32[32,16384]{1,0:T(8,128)}, f32[32,16384]{1,0:T(8,128)}, f32[8,128]{1,0:T(8,128)S(1)}) custom-call(s32[2]{0:T(128)S(1)} %pad_add_fusion.here, bf16[64,131072]{1,0:T(8,128)(2,1)} %bitcast.35, bf16[64,131072]{1,0:T(8,128)(2,1)} %bitcast.36, bf16[64,131072]{1,0:T(8,128)(2,1)} %bitcast.37, bf16[64,131072]{1,0:T(8,128)(2,1)} %bitcast.38, ...), custom_call_target="tpu_custom_call" | custom-call | tf_op jit(solution)/shard_map/pallas_call | solution.py:115
  21.1 0.1 collective-permute-start
  21.2 3.5 %shard_map.71 = (f32[32,16384]{1,0:T(8,128)}, f32[32,16384]{1,0:T(8,128)S(1)}, f32[8,128]{1,0:T(8,128)S(1)}) custom-call(s32[2]{0:T(128)S(1)} %pad_add_fusion.here, bf16[64,131072]{1,0:T(8,128)(2,1)} %bitcast.64, bf16[64,131072]{1,0:T(8,128)(2,1)} %bitcast.52, bf16[64,131072]{1,0:T(8,128)(2,1)} %bitcast.53, bf16[64,131072]{1,0:T(8,128)(2,1)} %bitcast.54, ...), custom_call_target="tpu_custom_call" | custom-call | tf_op jit(solution)/shard_map/pallas_call | solution.py:115
  24.7 28.7 %collective-permute-done.2.refs_16_.refs_19_ = f32[32,16384]{1,0:T(8,128)} collective-permute-done((f32[32,16384]{1,0:T(8,128)}, f32[32,16384]{1,0:T(8,128)}, u32[]{:S(2)}, u32[]{:S(2)}) %collective-permute-start.2) | collective-permute-done | bytes 2097184 | tf_op jit(solution)/shard_map/ppermute | solution.py:380
  53.4 1.6 collective-permute-start.1
  55.0 1.3 collective-permute-start.9
  56.3 4.2 %shard_map.72 = (f32[32,16384]{1,0:T(8,128)S(1)}, f32[32,16384]{1,0:T(8,128)S(1)}, f32[8,128]{1,0:T(8,128)S(1)}) custom-call(s32[2]{0:T(128)S(1)} %pad_add_fusion.here, bf16[64,131072]{1,0:T(8,128)(2,1)} %bitcast.67, bf16[64,131072]{1,0:T(8,128)(2,1)} %bitcast.68, bf16[64,131072]{1,0:T(8,128)(2,1)} %bitcast.69, bf16[64,131072]{1,0:T(8,128)(2,1)} %bitcast.70, ...), custom_call_target="tpu_custom_call" | custom-call | tf_op jit(solution)/shard_map/pallas_call | solution.py:115
  60.5 1.0 collective-permute-done.6.refs_16_.refs_19_
  61.5 1.4 collective-permute-start.10
  62.9 35.5 %collective-permute-done.refs_4_.refs_5_.refs_6_.refs_7_.refs_21_.refs_2_.refs_3_.refs_12_.refs_13_.refs_1_ = f32[32,16384]{1,0:T(8,128)} collective-permute-done((f32[32,16384]{1,0:T(8,128)}, f32[32,16384]{1,0:T(8,128)}, u32[]{:S(2)}, u32[]{:S(2)}) %collective-permute-start) | collective-permute-done | bytes 2097184 | tf_op jit(solution)/shard_map/ppermute | solution.py:380
  98.4 1.6 collective-permute-start.5
  99.9 4.9 %shard_map.73 = (f32[32,16384]{1,0:T(8,128)}, f32[32,16384]{1,0:T(8,128)S(1)}, f32[8,128]{1,0:T(8,128)S(1)}) custom-call(s32[2]{0:T(128)S(1)} %pad_add_fusion.here, bf16[64,131072]{1,0:T(8,128)(2,1)} %bitcast.89, bf16[64,131072]{1,0:T(8,128)(2,1)} %bitcast.84, bf16[64,131072]{1,0:T(8,128)(2,1)} %bitcast.85, bf16[64,131072]{1,0:T(8,128)(2,1)} %bitcast.86, ...), custom_call_target="tpu_custom_call" | custom-call | tf_op jit(solution)/shard_map/pallas_call | solution.py:115
  104.8 1.4 collective-permute-start.13
  106.2 0.2 collective-permute-done.9.refs_21_.refs_4_.refs_5_.refs_6_.refs_7_.refs_2_.refs_3_.refs_12_.refs_13_.refs_8_
  106.4 1.4 collective-permute-start.14
  107.8 3.5 %collective-permute-start.16 = (s32[1,8,8192]{2,1,0:T(8,128)}, s32[1,8,8192]{2,1,0:T(8,128)S(1)}, u32[]{:S(2)}, u32[]{:S(2)}) collective-permute-start(s32[1,8,8192]{2,1,0:T(8,128)} %refs_4_.3), channel_id=1, source_target_pairs={{0,64},{16,80},{32,96},{48,112},{64,0},{80,16},{96,32},{112,48},{1... | collective-permute-start | bytes 786440 | tf_op jit(solution)/shard_map/ppermute | solution.py:384
  111.3 32.0 %collective-permute-done.4.refs_12_.refs_13_.refs_14_.refs_15_.refs_6_.refs_7_.refs_16_.refs_17_.refs_25_.refs_3_ = f32[32,16384]{1,0:T(8,128)} collective-permute-done((f32[32,16384]{1,0:T(8,128)S(1)}, f32[32,16384]{1,0:T(8,128)}, u32[]{:S(2)}, u32[]{:S(2)}) %collective-permute-start.4) | collective-permute-done | bytes 2097184 | tf_op jit(solution)/shard_map/ppermute | solution.py:380
  143.3 4.1 %collective-permute-start.15 = (s32[1,8,8192]{2,1,0:T(8,128)}, s32[1,8,8192]{2,1,0:T(8,128)S(1)}, u32[]{:S(2)}, u32[]{:S(2)}) collective-permute-start(s32[1,8,8192]{2,1,0:T(8,128)} %refs_4_.3), channel_id=1, source_target_pairs={{0,96},{16,112},{32,0},{48,16},{64,32},{80,48},{96,64},{112,80},{1... | collective-permute-start | bytes 786440 | tf_op jit(solution)/shard_map/ppermute | solution.py:384
  147.4 2.5 %shard_map.74 = (f32[32,4096]{1,0:T(8,128)S(1)}, f32[32,4096]{1,0:T(8,128)S(1)}, f32[8,128]{1,0:T(8,128)S(1)}) custom-call(s32[2]{0:T(128)S(1)} %pad_add_fusion.here, bf16[64,131072]{1,0:T(8,128)(2,1)} %bitcast.99, bf16[64,131072]{1,0:T(8,128)(2,1)} %bitcast.100, bf16[64,131072]{1,0:T(8,128)(2,1)} %bitcast.101, bf16[64,131072]{1,0:T(8,128)(2,1)} %bitcast.102, ...), custom_call_target="tpu_custom_call" | custom-call | tf_op jit(solution)/shard_map/pallas_call | solution.py:115
  149.8 1.4 collective-permute-start.11
  151.2 1.5 collective-permute-start.12
  152.8 1.6 copy-done.1
  154.3 2.3 shard_map.75
  156.6 0.1 collective-permute-start.17
  156.7 2.7 %collective-permute-start.18 = (f32[32,4096]{1,0:T(8,128)S(1)}, f32[32,4096]{1,0:T(8,128)S(1)}, u32[]{:S(2)}, u32[]{:S(2)}) collective-permute-start(f32[32,4096]{1,0:T(8,128)S(1)} %get-tuple-element.73), channel_id=1, source_target_pairs={{0,3},{1,0},{2,1},{3,2},{4,7},{5,4},{6,5},{7,6},{8,11},{9,8},{10,9... | collective-permute-start | bytes 1572872 | tf_op jit(solution)/shard_map/ppermute | solution.py:380
  159.4 3.7 %collective-permute-done.11.refs_20_.refs_21_.refs_25_ = f32[32,4096]{1,0:T(8,128)S(1)} collective-permute-done((f32[32,4096]{1,0:T(8,128)S(1)}, f32[32,4096]{1,0:T(8,128)S(1)}, u32[]{:S(2)}, u32[]{:S(2)}) %collective-permute-start.11) | collective-permute-done | bytes 524320 | tf_op jit(solution)/shard_map/ppermute | solution.py:380
  163.1 2.5 %shard_map.76 = (f32[64,2048]{1,0:T(8,128)S(1)}, f32[64,2048]{1,0:T(8,128)S(1)}, f32[8,128]{1,0:T(8,128)S(1)}) custom-call(s32[2]{0:T(128)S(1)} %pad_add_fusion.here, bf16[64,131072]{1,0:T(8,128)(2,1)} %bitcast.107, bf16[64,131072]{1,0:T(8,128)(2,1)} %bitcast.108, ...), custom_call_target="tpu_custom_call" | custom-call | tf_op jit(solution)/shard_map/pallas_call | solution.py:115
  165.6 0.8 collective-permute-start.23
  166.4 2.0 collective-permute-start.24
  168.3 0.8 collective-permute-done.17.refs_20_.refs_21_.refs_25_
  169.1 2.5 %shard_map.77 = (f32[64,2048]{1,0:T(8,128)S(1)}, f32[64,2048]{1,0:T(8,128)S(1)}, f32[8,128]{1,0:T(8,128)S(1)}) custom-call(s32[2]{0:T(128)S(1)} %pad_add_fusion.here, bf16[64,131072]{1,0:T(8,128)(2,1)} %bitcast.111, bf16[64,131072]{1,0:T(8,128)(2,1)} %bitcast.112, ...), custom_call_target="tpu_custom_call" | custom-call | tf_op jit(solution)/shard_map/pallas_call | solution.py:115
  171.6 0.1 collective-permute-start.25
  171.7 2.7 %collective-permute-start.26 = (f32[64,2048]{1,0:T(8,128)S(1)}, f32[64,2048]{1,0:T(8,128)S(1)}, u32[]{:S(2)}, u32[]{:S(2)}) collective-permute-start(f32[64,2048]{1,0:T(8,128)S(1)} %get-tuple-element.85), channel_id=1, source_target_pairs={{0,3},{1,0},{2,1},{3,2},{4,7},{5,4},{6,5},{7,6},{8,11},{9,8},{10,9... | collective-permute-start | bytes 1572872 | tf_op jit(solution)/shard_map/ppermute | solution.py:380
  174.3 2.5 %shard_map.78 = (f32[64,2048]{1,0:T(8,128)S(1)}, f32[64,2048]{1,0:T(8,128)S(1)}, f32[8,128]{1,0:T(8,128)S(1)}) custom-call(s32[2]{0:T(128)S(1)} %pad_add_fusion.here, bf16[64,131072]{1,0:T(8,128)(2,1)} %bitcast.115, bf16[64,131072]{1,0:T(8,128)(2,1)} %bitcast.116, ...), custom_call_target="tpu_custom_call" | custom-call | tf_op jit(solution)/shard_map/pallas_call | solution.py:115
  176.8 0.0 copy-start.2
  176.8 0.0 copy-start.3
  176.8 2.5 %shard_map.79 = (f32[64,2048]{1,0:T(8,128)S(1)}, f32[64,2048]{1,0:T(8,128)S(1)}, f32[8,128]{1,0:T(8,128)S(1)}) custom-call(s32[2]{0:T(128)S(1)} %pad_add_fusion.here, bf16[64,131072]{1,0:T(8,128)(2,1)} %bitcast.119, bf16[64,131072]{1,0:T(8,128)(2,1)} %bitcast.120, ...), custom_call_target="tpu_custom_call" | custom-call | tf_op jit(solution)/shard_map/pallas_call | solution.py:115
  179.3 0.1 collective-permute-start.21
  179.4 2.7 %collective-permute-start.22 = (f32[64,2048]{1,0:T(8,128)S(1)}, f32[64,2048]{1,0:T(8,128)S(1)}, u32[]{:S(2)}, u32[]{:S(2)}) collective-permute-start(f32[64,2048]{1,0:T(8,128)S(1)} %get-tuple-element.81), channel_id=1, source_target_pairs={{0,3},{1,0},{2,1},{3,2},{4,7},{5,4},{6,5},{7,6},{8,11},{9,8},{10,9... | collective-permute-start | bytes 1572872 | tf_op jit(solution)/shard_map/ppermute | solution.py:380
  182.1 1.0 collective-permute-done.25.refs_12_
  183.1 1.7 collective-permute-start.20
  184.8 6.8 %shard_map.80 = (f32[1,64,8192]{2,1,0:T(8,128)}, f32[8,4096]{1,0:T(8,128)S(1)}, f32[8,128]{1,0:T(8,128)S(1)}) custom-call(s32[2]{0:T(128)S(1)} %pad_add_fusion.here, bf16[64,131072]{1,0:T(8,128)(2,1)} %bitcast.123, f32[32,16384]{1,0:T(8,128)} %collective-permute-done.refs_4_.refs_5_.refs_6_.refs_7_.refs_21_.refs_2_.refs_3_.refs_12_.refs_13_.refs_1_, ...), custom_call_target="tpu_custom_call" | custom-call | tf_op jit(solution)/shard_map/pallas_call | solution.py:115
  191.6 1.6 collective-permute-start.32
  193.2 1.4 collective-permute-done.21.refs_12_
  194.6 1.8 collective-permute-start.31
  196.4 6.8 %shard_map.81 = (f32[1,64,8192]{2,1,0:T(8,128)}, f32[8,4096]{1,0:T(8,128)S(1)}, f32[8,128]{1,0:T(8,128)S(1)}) custom-call(s32[2]{0:T(128)S(1)} %pad_add_fusion.here, bf16[64,131072]{1,0:T(8,128)(2,1)} %bitcast.125, ...), custom_call_target="tpu_custom_call", output_to_operand_aliasing={{0}: (19, {})} | custom-call | tf_op jit(solution)/shard_map/pallas_call | solution.py:115
  203.3 1.3 collective-permute-start.29
  204.5 1.5 collective-permute-start.28
  206.1 0.5 collective-permute-start.27
  206.6 4.8 %shard_map.82 = (f32[64,4096]{1,0:T(8,128)S(1)}, f32[8,128]{1,0:T(8,128)S(1)}) custom-call(s32[2]{0:T(128)S(1)} %pad_add_fusion.here, f32[8,4096]{1,0:T(8,128)S(1)} %get-tuple-element.90.refs_0_, f32[8,4096]{1,0:T(8,128)S(1)} %collective-permute-done.30.refs_1_, f32[8,4096]{1,0:T(8,128)S(1)} %collective-permute-done.31.refs_2_, ...), custom_call_target="tpu_custom_call" | custom-call | tf_op jit(solution)/shard_map/pallas_call | solution.py:115
  211.4 10.1 %collective-permute-start.34 = (f32[64,4096]{1,0:T(8,128)S(1)}, f32[64,4096]{1,0:T(8,128)S(1)}, u32[]{:S(2)}, u32[]{:S(2)}) collective-permute-start(f32[64,4096]{1,0:T(8,128)S(1)} %get-tuple-element.94.refs_0_), channel_id=1, source_target_pairs={{0,16},{16,0},{32,48},{48,32},{64,80},{80,64},{96,112},{112,96},{1... | collective-permute-start | bytes 3145736 | tf_op jit(solution)/shard_map/ppermute | solution.py:390
  221.5 4.8 %shard_map.83 = (f32[64,4096]{1,0:T(8,128)S(1)}, f32[8,128]{1,0:T(8,128)S(1)}) custom-call(s32[2]{0:T(128)S(1)} %pad_add_fusion.here, f32[8,4096]{1,0:T(8,128)S(1)} %get-tuple-element.89.refs_0_, f32[8,4096]{1,0:T(8,128)S(1)} %collective-permute-done.27.refs_1_, f32[8,4096]{1,0:T(8,128)S(1)} %collective-permute-done.28.refs_2_, ...), custom_call_target="tpu_custom_call" | custom-call | tf_op jit(solution)/shard_map/pallas_call | solution.py:115
  226.3 1.3 collective-permute-start.33
  227.6 1.7 shard_map.84
  229.4 0.5 collective-permute-done.33.refs_1_
  229.9 1.7 shard_map.85
  (33 shorter events, 0.1 us)
Async XLA Ops:
  4.8 48.6 %collective-permute-start.2 = (f32[32,16384]{1,0:T(8,128)}, f32[32,16384]{1,0:T(8,128)}, u32[]{:S(2)}, u32[]{:S(2)}) collective-permute-start(f32[32,16384]{1,0:T(8,128)} %get-tuple-element.55), channel_id=1, source_target_pairs={{0,1},{1,2},{2,3},{3,0},{4,5},{5,6},{6,7},{7,4},{8,9},{9,10},{10,1... | collective-permute-start | bytes 6291464 | tf_op jit(solution)/shard_map/ppermute | solution.py:380
  6.9 48.1 %collective-permute-start.3 = (f32[32,16384]{1,0:T(8,128)}, f32[32,16384]{1,0:T(8,128)}, u32[]{:S(2)}, u32[]{:S(2)}) collective-permute-start(f32[32,16384]{1,0:T(8,128)} %get-tuple-element.56), channel_id=1, source_target_pairs={{0,3},{1,0},{2,1},{3,2},{4,7},{5,4},{6,5},{7,6},{8,11},{9,8},{10,9... | collective-permute-start | bytes 6291464 | tf_op jit(solution)/shard_map/ppermute | solution.py:380
  8.3 12.8 %collective-permute-start.8 = (s32[1,8,8192]{2,1,0:T(8,128)}, s32[1,8,8192]{2,1,0:T(8,128)}, u32[]{:S(2)}, u32[]{:S(2)}) collective-permute-start(s32[1,8,8192]{2,1,0:T(8,128)} %refs_4_.3), channel_id=1, source_target_pairs={{0,32},{16,48},{32,64},{48,80},{64,96},{80,112},{96,0},{112,16},{1... | collective-permute-start | bytes 786440 | tf_op jit(solution)/shard_map/ppermute | solution.py:384
  14.2 47.3 %collective-permute-start.6 = (f32[32,16384]{1,0:T(8,128)}, f32[32,16384]{1,0:T(8,128)}, u32[]{:S(2)}, u32[]{:S(2)}) collective-permute-start(f32[32,16384]{1,0:T(8,128)} %get-tuple-element.61), channel_id=1, source_target_pairs={{0,4},{1,5},{2,6},{3,7},{4,8},{5,9},{6,10},{7,11},{8,12},{9,13},{1... | collective-permute-start | bytes 6291464 | tf_op jit(solution)/shard_map/ppermute | solution.py:380
  15.5 47.4 %collective-permute-start.7 = (f32[32,16384]{1,0:T(8,128)}, f32[32,16384]{1,0:T(8,128)}, u32[]{:S(2)}, u32[]{:S(2)}) collective-permute-start(f32[32,16384]{1,0:T(8,128)} %get-tuple-element.62), channel_id=1, source_target_pairs={{0,12},{1,13},{2,14},{3,15},{4,0},{5,1},{6,2},{7,3},{8,4},{9,5},{1... | collective-permute-start | bytes 6291464 | tf_op jit(solution)/shard_map/ppermute | solution.py:380
  21.1 77.2 %collective-permute-start = (f32[32,16384]{1,0:T(8,128)}, f32[32,16384]{1,0:T(8,128)}, u32[]{:S(2)}, u32[]{:S(2)}) collective-permute-start(f32[32,16384]{1,0:T(8,128)} %get-tuple-element.53), channel_id=1, source_target_pairs={{0,1},{1,2},{2,3},{3,0},{4,5},{5,6},{6,7},{7,4},{8,9},{9,10},{10,1... | collective-permute-start | bytes 6291464 | tf_op jit(solution)/shard_map/ppermute | solution.py:380
  53.4 51.4 %collective-permute-start.1 = (f32[32,16384]{1,0:T(8,128)}, f32[32,16384]{1,0:T(8,128)}, u32[]{:S(2)}, u32[]{:S(2)}) collective-permute-start(f32[32,16384]{1,0:T(8,128)} %get-tuple-element.54), channel_id=1, source_target_pairs={{0,3},{1,0},{2,1},{3,2},{4,7},{5,4},{6,5},{7,6},{8,11},{9,8},{10,9... | collective-permute-start | bytes 6291464 | tf_op jit(solution)/shard_map/ppermute | solution.py:380
  55.0 51.4 %collective-permute-start.9 = (f32[32,16384]{1,0:T(8,128)}, f32[32,16384]{1,0:T(8,128)}, u32[]{:S(2)}, u32[]{:S(2)}) collective-permute-start(f32[32,16384]{1,0:T(8,128)} %get-tuple-element.65), channel_id=1, source_target_pairs={{0,4},{1,5},{2,6},{3,7},{4,8},{5,9},{6,10},{7,11},{8,12},{9,13},{1... | collective-permute-start | bytes 6291464 | tf_op jit(solution)/shard_map/ppermute | solution.py:380
  61.5 46.3 %collective-permute-start.10 = (f32[32,16384]{1,0:T(8,128)S(1)}, f32[32,16384]{1,0:T(8,128)S(1)}, u32[]{:S(2)}, u32[]{:S(2)}) collective-permute-start(f32[32,16384]{1,0:T(8,128)S(1)} %get-tuple-element.66), channel_id=1, source_target_pairs={{0,12},{1,13},{2,14},{3,15},{4,0},{5,1},{6,2},{7,3},{8,4},{9,5},{1... | collective-permute-start | bytes 6291464 | tf_op jit(solution)/shard_map/ppermute | solution.py:380
  62.9 80.4 %collective-permute-start.4 = (f32[32,16384]{1,0:T(8,128)S(1)}, f32[32,16384]{1,0:T(8,128)}, u32[]{:S(2)}, u32[]{:S(2)}) collective-permute-start(f32[32,16384]{1,0:T(8,128)S(1)} %get-tuple-element.59), channel_id=1, source_target_pairs={{0,1},{1,2},{2,3},{3,0},{4,5},{5,6},{6,7},{7,4},{8,9},{9,10},{10,1... | collective-permute-start | bytes 6291464 | tf_op jit(solution)/shard_map/ppermute | solution.py:380
  98.4 49.0 %collective-permute-start.5 = (f32[32,16384]{1,0:T(8,128)S(1)}, f32[32,16384]{1,0:T(8,128)}, u32[]{:S(2)}, u32[]{:S(2)}) collective-permute-start(f32[32,16384]{1,0:T(8,128)S(1)} %get-tuple-element.60), channel_id=1, source_target_pairs={{0,3},{1,0},{2,1},{3,2},{4,7},{5,4},{6,5},{7,6},{8,11},{9,8},{10,9... | collective-permute-start | bytes 6291464 | tf_op jit(solution)/shard_map/ppermute | solution.py:380
  104.8 47.9 %collective-permute-start.13 = (f32[32,16384]{1,0:T(8,128)}, f32[32,16384]{1,0:T(8,128)}, u32[]{:S(2)}, u32[]{:S(2)}) collective-permute-start(f32[32,16384]{1,0:T(8,128)} %get-tuple-element.69), channel_id=1, source_target_pairs={{0,4},{1,5},{2,6},{3,7},{4,8},{5,9},{6,10},{7,11},{8,12},{9,13},{1... | collective-permute-start | bytes 6291464 | tf_op jit(solution)/shard_map/ppermute | solution.py:380
  106.4 46.3 %collective-permute-start.14 = (f32[32,16384]{1,0:T(8,128)S(1)}, f32[32,16384]{1,0:T(8,128)}, u32[]{:S(2)}, u32[]{:S(2)}) collective-permute-start(f32[32,16384]{1,0:T(8,128)S(1)} %get-tuple-element.70), channel_id=1, source_target_pairs={{0,12},{1,13},{2,14},{3,15},{4,0},{5,1},{6,2},{7,3},{8,4},{9,5},{1... | collective-permute-start | bytes 6291464 | tf_op jit(solution)/shard_map/ppermute | solution.py:380
  107.8 39.5 %copy-start = (f32[32,16384]{1,0:T(8,128)}, f32[32,16384]{1,0:T(8,128)S(1)}, u32[]{:S(2)}) copy-start(f32[32,16384]{1,0:T(8,128)S(1)} %collective-permute-done.10.refs_22_.refs_8_.refs_9_.refs_10_.refs_11_.refs_4_.refs_5_.refs_14_.refs_15_) | copy-start | bytes 6291460
  107.8 43.4 %collective-permute-start.16 = (s32[1,8,8192]{2,1,0:T(8,128)}, s32[1,8,8192]{2,1,0:T(8,128)S(1)}, u32[]{:S(2)}, u32[]{:S(2)}) collective-permute-start(s32[1,8,8192]{2,1,0:T(8,128)} %refs_4_.3), channel_id=1, source_target_pairs={{0,64},{16,80},{32,96},{48,112},{64,0},{80,16},{96,32},{112,48},{1... | collective-permute-start | bytes 786440 | tf_op jit(solution)/shard_map/ppermute | solution.py:384
  143.3 9.4 %collective-permute-start.15 = (s32[1,8,8192]{2,1,0:T(8,128)}, s32[1,8,8192]{2,1,0:T(8,128)S(1)}, u32[]{:S(2)}, u32[]{:S(2)}) collective-permute-start(s32[1,8,8192]{2,1,0:T(8,128)} %refs_4_.3), channel_id=1, source_target_pairs={{0,96},{16,112},{32,0},{48,16},{64,32},{80,48},{96,64},{112,80},{1... | collective-permute-start | bytes 786440 | tf_op jit(solution)/shard_map/ppermute | solution.py:384
  149.8 13.3 %collective-permute-start.11 = (f32[32,4096]{1,0:T(8,128)S(1)}, f32[32,4096]{1,0:T(8,128)S(1)}, u32[]{:S(2)}, u32[]{:S(2)}) collective-permute-start(f32[32,4096]{1,0:T(8,128)S(1)} %get-tuple-element.67), channel_id=1, source_target_pairs={{0,4},{1,5},{2,6},{3,7},{4,8},{5,9},{6,10},{7,11},{8,12},{9,13},{1... | collective-permute-start | bytes 1572872 | tf_op jit(solution)/shard_map/ppermute | solution.py:380
  151.2 11.9 %collective-permute-start.12 = (f32[32,4096]{1,0:T(8,128)S(1)}, f32[32,4096]{1,0:T(8,128)S(1)}, u32[]{:S(2)}, u32[]{:S(2)}) collective-permute-start(f32[32,4096]{1,0:T(8,128)S(1)} %get-tuple-element.68), channel_id=1, source_target_pairs={{0,12},{1,13},{2,14},{3,15},{4,0},{5,1},{6,2},{7,3},{8,4},{9,5},{1... | collective-permute-start | bytes 1572872 | tf_op jit(solution)/shard_map/ppermute | solution.py:380
  152.7 1.6 copy-start.1
  156.6 12.5 %collective-permute-start.17 = (f32[32,4096]{1,0:T(8,128)S(1)}, f32[32,4096]{1,0:T(8,128)S(1)}, u32[]{:S(2)}, u32[]{:S(2)}) collective-permute-start(f32[32,4096]{1,0:T(8,128)S(1)} %get-tuple-element.72), channel_id=1, source_target_pairs={{0,1},{1,2},{2,3},{3,0},{4,5},{5,6},{6,7},{7,4},{8,9},{9,10},{10,1... | collective-permute-start | bytes 1572872 | tf_op jit(solution)/shard_map/ppermute | solution.py:380
  156.7 12.4 %collective-permute-start.18 = (f32[32,4096]{1,0:T(8,128)S(1)}, f32[32,4096]{1,0:T(8,128)S(1)}, u32[]{:S(2)}, u32[]{:S(2)}) collective-permute-start(f32[32,4096]{1,0:T(8,128)S(1)} %get-tuple-element.73), channel_id=1, source_target_pairs={{0,3},{1,0},{2,1},{3,2},{4,7},{5,4},{6,5},{7,6},{8,11},{9,8},{10,9... | collective-permute-start | bytes 1572872 | tf_op jit(solution)/shard_map/ppermute | solution.py:380
  165.6 13.8 %collective-permute-start.23 = (f32[64,2048]{1,0:T(8,128)S(1)}, f32[64,2048]{1,0:T(8,128)S(1)}, u32[]{:S(2)}, u32[]{:S(2)}) collective-permute-start(f32[64,2048]{1,0:T(8,128)S(1)} %get-tuple-element.82), channel_id=1, source_target_pairs={{0,4},{1,5},{2,6},{3,7},{4,8},{5,9},{6,10},{7,11},{8,12},{9,13},{1... | collective-permute-start | bytes 1572872 | tf_op jit(solution)/shard_map/ppermute | solution.py:380
  166.4 15.7 %collective-permute-start.24 = (f32[64,2048]{1,0:T(8,128)S(1)}, f32[64,2048]{1,0:T(8,128)S(1)}, u32[]{:S(2)}, u32[]{:S(2)}) collective-permute-start(f32[64,2048]{1,0:T(8,128)S(1)} %get-tuple-element.83), channel_id=1, source_target_pairs={{0,12},{1,13},{2,14},{3,15},{4,0},{5,1},{6,2},{7,3},{8,4},{9,5},{1... | collective-permute-start | bytes 1572872 | tf_op jit(solution)/shard_map/ppermute | solution.py:380
  171.6 11.5 %collective-permute-start.25 = (f32[64,2048]{1,0:T(8,128)S(1)}, f32[64,2048]{1,0:T(8,128)S(1)}, u32[]{:S(2)}, u32[]{:S(2)}) collective-permute-start(f32[64,2048]{1,0:T(8,128)S(1)} %get-tuple-element.84), channel_id=1, source_target_pairs={{0,1},{1,2},{2,3},{3,0},{4,5},{5,6},{6,7},{7,4},{8,9},{9,10},{10,1... | collective-permute-start | bytes 1572872 | tf_op jit(solution)/shard_map/ppermute | solution.py:380
  171.7 13.1 %collective-permute-start.26 = (f32[64,2048]{1,0:T(8,128)S(1)}, f32[64,2048]{1,0:T(8,128)S(1)}, u32[]{:S(2)}, u32[]{:S(2)}) collective-permute-start(f32[64,2048]{1,0:T(8,128)S(1)} %get-tuple-element.85), channel_id=1, source_target_pairs={{0,3},{1,0},{2,1},{3,2},{4,7},{5,4},{6,5},{7,6},{8,11},{9,8},{10,9... | collective-permute-start | bytes 1572872 | tf_op jit(solution)/shard_map/ppermute | solution.py:380
  176.8 8.0 %copy-start.2 = (bf16[64,256]{1,0:T(8,128)(2,1)S(1)}, bf16[64,256]{1,0:T(8,128)(2,1)}, u32[]{:S(2)}) copy-start(bf16[64,256]{1,0:T(8,128)(2,1)} %constant.25.clone.refs_17_.refs_8_) | copy-start | bytes 98308
  176.8 8.0 %copy-start.3 = (bf16[64,256]{1,0:T(8,128)(2,1)S(1)}, bf16[64,256]{1,0:T(8,128)(2,1)}, u32[]{:S(2)}) copy-start(bf16[64,256]{1,0:T(8,128)(2,1)} %constant.24.clone.refs_16_) | copy-start | bytes 98308
  179.3 15.3 %collective-permute-start.21 = (f32[64,2048]{1,0:T(8,128)S(1)}, f32[64,2048]{1,0:T(8,128)S(1)}, u32[]{:S(2)}, u32[]{:S(2)}) collective-permute-start(f32[64,2048]{1,0:T(8,128)S(1)} %get-tuple-element.80), channel_id=1, source_target_pairs={{0,1},{1,2},{2,3},{3,0},{4,5},{5,6},{6,7},{7,4},{8,9},{9,10},{10,1... | collective-permute-start | bytes 1572872 | tf_op jit(solution)/shard_map/ppermute | solution.py:380
  179.4 17.0 %collective-permute-start.22 = (f32[64,2048]{1,0:T(8,128)S(1)}, f32[64,2048]{1,0:T(8,128)S(1)}, u32[]{:S(2)}, u32[]{:S(2)}) collective-permute-start(f32[64,2048]{1,0:T(8,128)S(1)} %get-tuple-element.81), channel_id=1, source_target_pairs={{0,3},{1,0},{2,1},{3,2},{4,7},{5,4},{6,5},{7,6},{8,11},{9,8},{10,9... | collective-permute-start | bytes 1572872 | tf_op jit(solution)/shard_map/ppermute | solution.py:380
  182.1 14.3 %collective-permute-start.19 = (f32[64,2048]{1,0:T(8,128)S(1)}, f32[64,2048]{1,0:T(8,128)S(1)}, u32[]{:S(2)}, u32[]{:S(2)}) collective-permute-start(f32[64,2048]{1,0:T(8,128)S(1)} %get-tuple-element.77), channel_id=1, source_target_pairs={{0,4},{1,5},{2,6},{3,7},{4,8},{5,9},{6,10},{7,11},{8,12},{9,13},{1... | collective-permute-start | bytes 1572872 | tf_op jit(solution)/shard_map/ppermute | solution.py:380
  183.1 13.3 %collective-permute-start.20 = (f32[64,2048]{1,0:T(8,128)S(1)}, f32[64,2048]{1,0:T(8,128)S(1)}, u32[]{:S(2)}, u32[]{:S(2)}) collective-permute-start(f32[64,2048]{1,0:T(8,128)S(1)} %get-tuple-element.78), channel_id=1, source_target_pairs={{0,12},{1,13},{2,14},{3,15},{4,0},{5,1},{6,2},{7,3},{8,4},{9,5},{1... | collective-permute-start | bytes 1572872 | tf_op jit(solution)/shard_map/ppermute | solution.py:380
  191.6 14.5 %collective-permute-start.32 = (f32[8,4096]{1,0:T(8,128)S(1)}, f32[8,4096]{1,0:T(8,128)S(1)}, u32[]{:S(2)}, u32[]{:S(2)}) collective-permute-start(f32[8,4096]{1,0:T(8,128)S(1)} %get-tuple-element.90.refs_0_), channel_id=1, source_target_pairs={{0,64},{16,80},{32,96},{48,112},{64,0},{80,16},{96,32},{112,48},{1... | collective-permute-start | bytes 393224 | tf_op jit(solution)/shard_map/ppermute | solution.py:384
  194.6 12.0 %collective-permute-start.31 = (f32[8,4096]{1,0:T(8,128)S(1)}, f32[8,4096]{1,0:T(8,128)S(1)}, u32[]{:S(2)}, u32[]{:S(2)}) collective-permute-start(f32[8,4096]{1,0:T(8,128)S(1)} %get-tuple-element.90.refs_0_), channel_id=1, source_target_pairs={{0,96},{16,112},{32,0},{48,16},{64,32},{80,48},{96,64},{112,80},{1... | collective-permute-start | bytes 393224 | tf_op jit(solution)/shard_map/ppermute | solution.py:384
  196.4 10.2 %collective-permute-start.30 = (f32[8,4096]{1,0:T(8,128)S(1)}, f32[8,4096]{1,0:T(8,128)S(1)}, u32[]{:S(2)}, u32[]{:S(2)}) collective-permute-start(f32[8,4096]{1,0:T(8,128)S(1)} %get-tuple-element.90.refs_0_), channel_id=1, source_target_pairs={{0,32},{16,48},{32,64},{48,80},{64,96},{80,112},{96,0},{112,16},{1... | collective-permute-start | bytes 393224 | tf_op jit(solution)/shard_map/ppermute | solution.py:384
  203.3 18.2 %collective-permute-start.29 = (f32[8,4096]{1,0:T(8,128)S(1)}, f32[8,4096]{1,0:T(8,128)S(1)}, u32[]{:S(2)}, u32[]{:S(2)}) collective-permute-start(f32[8,4096]{1,0:T(8,128)S(1)} %get-tuple-element.89.refs_0_), channel_id=1, source_target_pairs={{0,64},{16,80},{32,96},{48,112},{64,0},{80,16},{96,32},{112,48},{1... | collective-permute-start | bytes 393224 | tf_op jit(solution)/shard_map/ppermute | solution.py:384
  204.5 16.9 %collective-permute-start.28 = (f32[8,4096]{1,0:T(8,128)S(1)}, f32[8,4096]{1,0:T(8,128)S(1)}, u32[]{:S(2)}, u32[]{:S(2)}) collective-permute-start(f32[8,4096]{1,0:T(8,128)S(1)} %get-tuple-element.89.refs_0_), channel_id=1, source_target_pairs={{0,96},{16,112},{32,0},{48,16},{64,32},{80,48},{96,64},{112,80},{1... | collective-permute-start | bytes 393224 | tf_op jit(solution)/shard_map/ppermute | solution.py:384
  206.1 15.4 %collective-permute-start.27 = (f32[8,4096]{1,0:T(8,128)S(1)}, f32[8,4096]{1,0:T(8,128)S(1)}, u32[]{:S(2)}, u32[]{:S(2)}) collective-permute-start(f32[8,4096]{1,0:T(8,128)S(1)} %get-tuple-element.89.refs_0_), channel_id=1, source_target_pairs={{0,32},{16,48},{32,64},{48,80},{64,96},{80,112},{96,0},{112,16},{1... | collective-permute-start | bytes 393224 | tf_op jit(solution)/shard_map/ppermute | solution.py:384
  211.4 16.2 %collective-permute-start.34 = (f32[64,4096]{1,0:T(8,128)S(1)}, f32[64,4096]{1,0:T(8,128)S(1)}, u32[]{:S(2)}, u32[]{:S(2)}) collective-permute-start(f32[64,4096]{1,0:T(8,128)S(1)} %get-tuple-element.94.refs_0_), channel_id=1, source_target_pairs={{0,16},{16,0},{32,48},{48,32},{64,80},{80,64},{96,112},{112,96},{1... | collective-permute-start | bytes 3145736 | tf_op jit(solution)/shard_map/ppermute | solution.py:390
  226.3 3.6 %collective-permute-start.33 = (f32[64,4096]{1,0:T(8,128)S(1)}, f32[64,4096]{1,0:T(8,128)S(1)}, u32[]{:S(2)}, u32[]{:S(2)}) collective-permute-start(f32[64,4096]{1,0:T(8,128)S(1)} %get-tuple-element.93.refs_0_), channel_id=1, source_target_pairs={{0,16},{16,0},{32,48},{48,32},{64,80},{80,64},{96,112},{112,96},{1... | collective-permute-start | bytes 3145736 | tf_op jit(solution)/shard_map/ppermute | solution.py:390

commit v8 on v7

--- a/solution.py
+++ b/solution.py
@@ -15,12 +15,11 @@
 CHUNK = 256
 FINE, BROAD = 1024, 2048
 PARTS = (2, 2)
-AXES = (0, 0, 0, 1, 1, 1)
+AXES = (0, 0, 0, 1, 1, 0)
 LAG = (2, 2, 2, 2, 2, 2)
-PLACES_WITH = ((0, 1), (1, 0), (1, 0))
-STEPS = (1, -1, 2)
+PLACES_WITH = ((0, 1), (1, 0))
 TAIL = ('f0', 'f1', 's0', 's1', 'j0', 'j1')
-TOGETHER = 2
+TOGETHER = 1
 VMEM_LIMIT = 48 * 1024 * 1024
 F32 = jnp.float32
 BF16 = jnp.bfloat16
@@ -263,8 +262,8 @@
     def place(self, i):
         return jnp.where(i < self.n, i, i - self.n + self.count) + self.first
 
-    def columns(self, rows):
-        return pl.BlockSpec((1, rows, self.tile), lambda i, here: (0, 0, self.place(i)))
+    def columns(self, rows, block=0):
+        return pl.BlockSpec((1, rows, self.tile), lambda i, here: (0, block, self.place(i)))
 
     def result(self):
         return pl.BlockSpec((BLOCK, self.tile), lambda i, here: (0, self.place(i)))
@@ -343,11 +342,12 @@
         for at in range(0, piece.tile, CHUNK):
             col = slice(at, at + CHUNK)
             parts = [dense(refs[k][:, col], refs[4 + k][0, :, col]) for k in range(4)]
-            out[:, col] = product(backward, (parts[0] + parts[1 + STEPS.index(2)]) + (parts[1 + STEPS.index(1)] + parts[1 + STEPS.index(-1)]))
-
-    return line.call(
-        body, piece.steps, [*lists, *places, table],
-        [piece.compact(KEEP)] * 4 + [piece.columns(KEEP)] * 4 + [whole(BLOCK, 4 * BLOCK)],
+            out[:, col] = product(backward, (parts[0] + parts[3]) + (parts[1] + parts[2]))
+
+    return line.call(
+        body, piece.steps, [*lists, *(array for array, _ in places), table],
+        [piece.compact(KEEP)] * 4 + [piece.columns(KEEP, block) for _, block in places]
+        + [whole(BLOCK, 4 * BLOCK)],
         (jax.ShapeDtypeStruct((BLOCK, piece.spans), F32),), (piece.compact(BLOCK),),
     )[0]
 
@@ -401,7 +401,9 @@
     here = jnp.stack([me // SIDE, lax.rem(me, SIDE)]).astype(jnp.int32)
     tables = tuple(jnp.asarray(part) for part in dct_parts())
     line = Line(here)
-    places = [positions] + [along_z(positions, step) for step in STEPS]
+    one_back = along_z(positions, 1)
+    two_back = along_z(jnp.concatenate([positions, one_back], axis=1), 2)
+    places = [(positions, 0), (one_back, 0), (two_back, 1), (two_back, 0)]
     width = spans // 2
     pair = (Half(True, 0, width, spans), Half(False, width, width, spans))
     ends = [TILE * sum(PARTS[:number]) for number in range(len(PARTS) + 1)]
@@ -419,7 +421,7 @@
         got[stage] = out
         messages = out[::-1] if second else out
         sent.append([
-            messages[axis] + [p for p, w in zip(places[1:], PLACES_WITH) if w == (number, axis)]
+            messages[axis] + [p for p, w in zip((one_back, two_back), PLACES_WITH) if w == (number, axis)]
             for axis in range(2)
         ])
 
@@ -446,7 +448,7 @@
         if what == "f":
             full = [before(h, "raw", "near", number) for h in range(2)]
             fresh, own = finish(line, piece, flat, momentum, positions, full, tables, fresh)
-            lists[number] = [own] + [along_z(own, step) for step in STEPS]
+            lists[number] = [own] + [along_z(own, step) for step in (1, -1, 2)]
         elif what == "s":
             part = spread(line, piece, lists[number], places, tables[1])
             mine[number] = part, other_core(part)

time: 233 us -> 233 us (level)
  waiting for transfers between devices: 105 us -> 97.9 us
  starting transfers between devices: 57.9 us -> 61.6 us
    ppermute x24, waiting for transfers between devices: 104 us -> 96.4 us  [along(): lax.ppermute(value, 'fsdp', shift(0, step) if x_first else shift(step, 0))]
    ppermute x2, starting transfers between devices: 11.3 us -> 15 us  [other_core(): return lax.ppermute(value, 'rep', [(r, r ^ 1) for r in range(2 * SIDE)])]
    ppermute x9 -> x8, starting transfers between devices: 16 us -> 14.2 us  [along_z(): lax.ppermute(value, 'rep', [(z * 2 + c, (z + step) % SIDE * 2 + c) for z...]
  transfers between devices with their start and end apart: 35 -> 34, of which waited for: 10 -> 8; matrix products, arithmetic and copies ran while one was open for 0% -> 0% of each run, Pallas kernels for 26% -> 27%
where the time goes in v8:
time: 233 us; the launch traced here: 232 us
  waiting for transfers between devices  97.9 us (42%)
  Pallas kernels  67.8 us (29%)
  starting transfers between devices  61.6 us (26%)
  local copies, waits for them, and re-layouts  3.24 us (1%)
    ppermute x24, waiting for transfers between devices, along(): lax.ppermute(value, 'fsdp', shift(0, step) if x_first else shift(step, 0))  96.4 us
    pallas_call x18, Pallas kernels, call(): pl.pallas_call(run, grid_spec=pltpu.PrefetchScalarGridSpec(num_scalar_pre...  67.8 us
    ppermute x24, starting transfers between devices, along(): lax.ppermute(value, 'fsdp', shift(0, step) if x_first else shift(step, 0))  32.4 us
    ppermute x2, starting transfers between devices, other_core(): return lax.ppermute(value, 'rep', [(r, r ^ 1) for r in range(2 * SIDE)])  15 us
    ppermute x8, starting transfers between devices, along_z(): lax.ppermute(value, 'rep', [(z * 2 + c, (z + step) % SIDE * 2 + c) for z...  14.2 us
  transfers between devices with their start and end apart: 34, of which 8 were waited for; matrix products, arithmetic and copies ran while one was open for 0% of the time, Pallas kernels for 27%

profile of v8, /device:TPU:1, one launch (start us, length us, event | category | flops | bytes accessed | tf_op | source)
XLA Modules:
  0.0 231.5 jit_solution(15169160364613929742)
XLA Ops:
  0.6 0.1 pad_add_fusion.1.here
  0.7 3.4 %shard_map.68 = (f32[32,16384]{1,0:T(8,128)S(1)}, f32[32,16384]{1,0:T(8,128)S(1)}, f32[8,128]{1,0:T(8,128)S(1)}) custom-call(s32[2]{0:T(128)S(1)} %pad_add_fusion.1.here, bf16[64,131072]{1,0:T(8,128)(2,1)} %bitcast.3, bf16[64,131072]{1,0:T(8,128)(2,1)} %bitcast.4, bf16[64,131072]{1,0:T(8,128)(2,1)} %bitcast.5, bf16[64,131072]{1,0:T(8,128)(2,1)} %bitcast.6, ...), custom_call_target="tpu_custom_call" | custom-call | tf_op jit(solution)/shard_map/pallas_call | solution.py:114
  4.1 2.1 collective-permute-start.2
  6.3 1.4 collective-permute-start.3
  7.6 4.5 %shard_map.69 = (f32[32,16384]{1,0:T(8,128)S(1)}, f32[32,16384]{1,0:T(8,128)}, f32[8,128]{1,0:T(8,128)S(1)}) custom-call(s32[2]{0:T(128)S(1)} %pad_add_fusion.1.here, bf16[64,131072]{1,0:T(8,128)(2,1)} %bitcast.18, bf16[64,131072]{1,0:T(8,128)(2,1)} %bitcast.12, bf16[64,131072]{1,0:T(8,128)(2,1)} %bitcast.13, bf16[64,131072]{1,0:T(8,128)(2,1)} %bitcast.14, ...), custom_call_target="tpu_custom_call" | custom-call | tf_op jit(solution)/shard_map/pallas_call | solution.py:114
  12.1 1.4 collective-permute-start.6
  13.5 1.6 collective-permute-start.8
  15.2 1.5 collective-permute-start.7
  16.7 4.9 %shard_map.70 = (f32[32,16384]{1,0:T(8,128)}, f32[32,16384]{1,0:T(8,128)}, f32[8,128]{1,0:T(8,128)S(1)}) custom-call(s32[2]{0:T(128)S(1)} %pad_add_fusion.1.here, bf16[64,131072]{1,0:T(8,128)(2,1)} %bitcast.19, bf16[64,131072]{1,0:T(8,128)(2,1)} %bitcast.20, bf16[64,131072]{1,0:T(8,128)(2,1)} %bitcast.21, bf16[64,131072]{1,0:T(8,128)(2,1)} %bitcast.22, ...), custom_call_target="tpu_custom_call" | custom-call | tf_op jit(solution)/shard_map/pallas_call | solution.py:114
  21.6 0.9 collective-permute-done.8.refs_13_.refs_5_
  22.5 4.9 %shard_map.71 = (f32[32,16384]{1,0:T(8,128)}, f32[32,16384]{1,0:T(8,128)}, f32[8,128]{1,0:T(8,128)S(1)}) custom-call(s32[2]{0:T(128)S(1)} %pad_add_fusion.1.here, bf16[64,131072]{1,0:T(8,128)(2,1)} %bitcast.27, bf16[64,131072]{1,0:T(8,128)(2,1)} %bitcast.28, bf16[64,131072]{1,0:T(8,128)(2,1)} %bitcast.29, bf16[64,131072]{1,0:T(8,128)(2,1)} %bitcast.30, ...), custom_call_target="tpu_custom_call" | custom-call | tf_op jit(solution)/shard_map/pallas_call | solution.py:114
  27.4 25.1 %collective-permute-done.2.refs_8_.refs_11_ = f32[32,16384]{1,0:T(8,128)} collective-permute-done((f32[32,16384]{1,0:T(8,128)S(1)}, f32[32,16384]{1,0:T(8,128)}, u32[]{:S(2)}, u32[]{:S(2)}) %collective-permute-start.2) | collective-permute-done | bytes 2097184 | tf_op jit(solution)/shard_map/ppermute | solution.py:380
  52.5 1.6 collective-permute-start.1
  54.1 1.3 collective-permute-start.9
  55.4 4.2 %collective-permute-done.6.refs_8_.refs_11_ = f32[32,16384]{1,0:T(8,128)} collective-permute-done((f32[32,16384]{1,0:T(8,128)S(1)}, f32[32,16384]{1,0:T(8,128)}, u32[]{:S(2)}, u32[]{:S(2)}) %collective-permute-start.6) | collective-permute-done | bytes 2097184 | tf_op jit(solution)/shard_map/ppermute | solution.py:380
  59.6 1.3 collective-permute-start.10
  61.0 5.9 %shard_map.72 = (f32[32,16384]{1,0:T(8,128)}, f32[32,16384]{1,0:T(8,128)}, f32[8,128]{1,0:T(8,128)S(1)}) custom-call(s32[2]{0:T(128)S(1)} %pad_add_fusion.1.here, bf16[64,131072]{1,0:T(8,128)(2,1)} %bitcast.40, bf16[64,131072]{1,0:T(8,128)(2,1)} %bitcast.36, bf16[64,131072]{1,0:T(8,128)(2,1)} %bitcast.37, bf16[64,131072]{1,0:T(8,128)(2,1)} %bitcast.38, ...), custom_call_target="tpu_custom_call" | custom-call | tf_op jit(solution)/shard_map/pallas_call | solution.py:114
  66.9 0.1 collective-permute-start.4
  66.9 30.4 %collective-permute-done.refs_4_.refs_5_.refs_6_.refs_7_.refs_21_.refs_2_.refs_3_.refs_12_.refs_13_.refs_1_ = f32[32,16384]{1,0:T(8,128)S(1)} collective-permute-done((f32[32,16384]{1,0:T(8,128)}, f32[32,16384]{1,0:T(8,128)S(1)}, u32[]{:S(2)}, u32[]{:S(2)}) %collective-permute-start) | collective-permute-done | bytes 2097184 | tf_op jit(solution)/shard_map/ppermute | solution.py:380
  97.4 1.6 collective-permute-start.5
  99.0 5.5 %shard_map.73 = (f32[32,16384]{1,0:T(8,128)S(1)}, f32[32,16384]{1,0:T(8,128)}, f32[8,128]{1,0:T(8,128)S(1)}) custom-call(s32[2]{0:T(128)S(1)} %pad_add_fusion.1.here, bf16[64,131072]{1,0:T(8,128)(2,1)} %bitcast.43, bf16[64,131072]{1,0:T(8,128)(2,1)} %bitcast.44, bf16[64,131072]{1,0:T(8,128)(2,1)} %bitcast.45, bf16[64,131072]{1,0:T(8,128)(2,1)} %bitcast.46, ...), custom_call_target="tpu_custom_call" | custom-call | tf_op jit(solution)/shard_map/pallas_call | solution.py:114
  104.4 1.4 collective-permute-start.13
  105.8 1.5 collective-permute-start.14
  107.4 3.7 %collective-permute-start.15 = (s32[1,16,8192]{2,1,0:T(8,128)S(1)}, s32[1,16,8192]{2,1,0:T(8,128)S(1)}, u32[]{:S(2)}, u32[]{:S(2)}) collective-permute-start(s32[1,16,8192]{2,1,0:T(8,128)S(1)} %pad_add_fusion), channel_id=1, source_target_pairs={{0,64},{16,80},{32,96},{48,112},{64,0},{80,16},{96,32},{112,48},{1... | collective-permute-start | bytes 1572872 | tf_op jit(solution)/shard_map/ppermute | solution.py:384
  111.1 31.3 %collective-permute-done.4.refs_12_.refs_13_.refs_14_.refs_15_.refs_6_.refs_7_.refs_16_.refs_17_.refs_25_.refs_3_ = f32[32,16384]{1,0:T(8,128)} collective-permute-done((f32[32,16384]{1,0:T(8,128)}, f32[32,16384]{1,0:T(8,128)}, u32[]{:S(2)}, u32[]{:S(2)}) %collective-permute-start.4) | collective-permute-done | bytes 2097184 | tf_op jit(solution)/shard_map/ppermute | solution.py:380
  142.4 2.2 shard_map.74
  144.6 1.7 collective-permute-start.11
  146.3 1.5 collective-permute-start.12
  147.8 2.3 collective-permute-done.13.refs_12_.refs_13_.refs_14_.refs_15_.refs_25_.refs_6_.refs_7_.refs_16_.refs_17_.refs_10_
  150.1 1.6 copy-done.4
  151.7 1.6 copy-done.6
  153.3 2.2 shard_map.75
  155.5 0.3 collective-permute-start.16
  155.8 2.4 %collective-permute-start.17 = (f32[32,4096]{1,0:T(8,128)S(1)}, f32[32,4096]{1,0:T(8,128)S(1)}, u32[]{:S(2)}, u32[]{:S(2)}) collective-permute-start(f32[32,4096]{1,0:T(8,128)S(1)} %get-tuple-element.73), channel_id=1, source_target_pairs={{0,3},{1,0},{2,1},{3,2},{4,7},{5,4},{6,5},{7,6},{8,11},{9,8},{10,9... | collective-permute-start | bytes 1572872 | tf_op jit(solution)/shard_map/ppermute | solution.py:380
  158.2 3.0 %collective-permute-done.11.refs_20_.refs_21_.refs_25_ = f32[32,4096]{1,0:T(8,128)S(1)} collective-permute-done((f32[32,4096]{1,0:T(8,128)S(1)}, f32[32,4096]{1,0:T(8,128)S(1)}, u32[]{:S(2)}, u32[]{:S(2)}) %collective-permute-start.11) | collective-permute-done | bytes 524320 | tf_op jit(solution)/shard_map/ppermute | solution.py:380
  161.2 2.3 %shard_map.76 = (f32[64,2048]{1,0:T(8,128)S(1)}, f32[64,2048]{1,0:T(8,128)S(1)}, f32[8,128]{1,0:T(8,128)S(1)}) custom-call(s32[2]{0:T(128)S(1)} %pad_add_fusion.1.here, bf16[64,131072]{1,0:T(8,128)(2,1)} %bitcast.59, bf16[64,131072]{1,0:T(8,128)(2,1)} %bitcast.60, f32[32,16384]{1,0:T(8,128)S(1)} %copy-done.1, f32[32,16384]{1,0:T(8,128)S(1)} %copy-done.1, ...), custom_call_target="tpu_custom_call" | custom-call | tf_op jit(solution)/shard_map/pallas_call | solution.py:114
  163.6 1.3 collective-permute-start.22
  164.8 1.7 collective-permute-start.23
  166.5 2.3 %shard_map.77 = (f32[64,2048]{1,0:T(8,128)S(1)}, f32[64,2048]{1,0:T(8,128)S(1)}, f32[8,128]{1,0:T(8,128)S(1)}) custom-call(s32[2]{0:T(128)S(1)} %pad_add_fusion.1.here, bf16[64,131072]{1,0:T(8,128)(2,1)} %bitcast.63, bf16[64,131072]{1,0:T(8,128)(2,1)} %bitcast.64, f32[32,16384]{1,0:T(8,128)S(1)} %copy-done.4, f32[32,16384]{1,0:T(8,128)S(1)} %copy-done.4, ...), custom_call_target="tpu_custom_call" | custom-call | tf_op jit(solution)/shard_map/pallas_call | solution.py:114
  168.8 0.3 collective-permute-start.24
  169.2 2.4 %collective-permute-start.25 = (f32[64,2048]{1,0:T(8,128)S(1)}, f32[64,2048]{1,0:T(8,128)S(1)}, u32[]{:S(2)}, u32[]{:S(2)}) collective-permute-start(f32[64,2048]{1,0:T(8,128)S(1)} %get-tuple-element.85), channel_id=1, source_target_pairs={{0,3},{1,0},{2,1},{3,2},{4,7},{5,4},{6,5},{7,6},{8,11},{9,8},{10,9... | collective-permute-start | bytes 1572872 | tf_op jit(solution)/shard_map/ppermute | solution.py:380
  171.6 2.3 shard_map.78
  173.9 0.0 copy-start.9
  173.9 0.0 copy-start.12
  173.9 0.0 copy-start.13
  173.9 2.4 %shard_map.79 = (f32[64,2048]{1,0:T(8,128)S(1)}, f32[64,2048]{1,0:T(8,128)S(1)}, f32[8,128]{1,0:T(8,128)S(1)}) custom-call(s32[2]{0:T(128)S(1)} %pad_add_fusion.1.here, bf16[64,131072]{1,0:T(8,128)(2,1)} %bitcast.71, bf16[64,131072]{1,0:T(8,128)(2,1)} %bitcast.72, f32[32,16384]{1,0:T(8,128)S(1)} %copy-done.1, f32[32,16384]{1,0:T(8,128)S(1)} %copy-done.1, ...), custom_call_target="tpu_custom_call" | custom-call | tf_op jit(solution)/shard_map/pallas_call | solution.py:114
  176.3 0.3 collective-permute-start.18
  176.6 2.7 %collective-permute-start.19 = (f32[64,2048]{1,0:T(8,128)S(1)}, f32[64,2048]{1,0:T(8,128)S(1)}, u32[]{:S(2)}, u32[]{:S(2)}) collective-permute-start(f32[64,2048]{1,0:T(8,128)S(1)} %get-tuple-element.79), channel_id=1, source_target_pairs={{0,12},{1,13},{2,14},{3,15},{4,0},{5,1},{6,2},{7,3},{8,4},{9,5},{1... | collective-permute-start | bytes 1572872 | tf_op jit(solution)/shard_map/ppermute | solution.py:380
  179.2 2.7 %collective-permute-start.21 = (f32[64,2048]{1,0:T(8,128)S(1)}, f32[64,2048]{1,0:T(8,128)S(1)}, u32[]{:S(2)}, u32[]{:S(2)}) collective-permute-start(f32[64,2048]{1,0:T(8,128)S(1)} %get-tuple-element.81), channel_id=1, source_target_pairs={{0,3},{1,0},{2,1},{3,2},{4,7},{5,4},{6,5},{7,6},{8,11},{9,8},{10,9... | collective-permute-start | bytes 1572872 | tf_op jit(solution)/shard_map/ppermute | solution.py:380
  181.9 6.8 %shard_map.80 = (f32[1,64,8192]{2,1,0:T(8,128)}, f32[8,4096]{1,0:T(8,128)S(1)}, f32[8,128]{1,0:T(8,128)S(1)}) custom-call(s32[2]{0:T(128)S(1)} %pad_add_fusion.1.here, bf16[64,131072]{1,0:T(8,128)(2,1)} %bitcast.75, f32[32,16384]{1,0:T(8,128)S(1)} %copy-done.1, f32[32,16384]{1,0:T(8,128)} %copy-done.2, ...), custom_call_target="tpu_custom_call" | custom-call | tf_op jit(solution)/shard_map/pallas_call | solution.py:114
  188.7 3.6 %collective-permute-start.31 = (f32[8,4096]{1,0:T(8,128)S(1)}, f32[8,4096]{1,0:T(8,128)S(1)}, u32[]{:S(2)}, u32[]{:S(2)}) collective-permute-start(f32[8,4096]{1,0:T(8,128)S(1)} %get-tuple-element.90.refs_0_), channel_id=1, source_target_pairs={{0,64},{16,80},{32,96},{48,112},{64,0},{80,16},{96,32},{112,48},{1... | collective-permute-start | bytes 393224 | tf_op jit(solution)/shard_map/ppermute | solution.py:384
  192.3 0.4 collective-permute-start.30
  192.7 1.0 collective-permute-start.29
  193.8 6.8 %shard_map.81 = (f32[1,64,8192]{2,1,0:T(8,128)}, f32[8,4096]{1,0:T(8,128)S(1)}, f32[8,128]{1,0:T(8,128)S(1)}) custom-call(s32[2]{0:T(128)S(1)} %pad_add_fusion.1.here, bf16[64,131072]{1,0:T(8,128)(2,1)} %bitcast.77, f32[32,16384]{1,0:T(8,128)S(1)} %copy-done.1, f32[32,16384]{1,0:T(8,128)} %copy-done.2, ...), custom_call_target="tpu_custom_call", output_to_operand_aliasing={{0}: (19, {})} | custom-call | tf_op jit(solution)/shard_map/pallas_call | solution.py:114
  200.5 2.4 %collective-permute-start.28 = (f32[8,4096]{1,0:T(8,128)S(1)}, f32[8,4096]{1,0:T(8,128)S(1)}, u32[]{:S(2)}, u32[]{:S(2)}) collective-permute-start(f32[8,4096]{1,0:T(8,128)S(1)} %get-tuple-element.89.refs_0_), channel_id=1, source_target_pairs={{0,64},{16,80},{32,96},{48,112},{64,0},{80,16},{96,32},{112,48},{1... | collective-permute-start | bytes 393224 | tf_op jit(solution)/shard_map/ppermute | solution.py:384
  202.9 0.7 collective-permute-start.27
  203.7 0.7 collective-permute-start.26
  204.4 4.0 %shard_map.82 = (f32[64,4096]{1,0:T(8,128)S(1)}, f32[8,128]{1,0:T(8,128)S(1)}) custom-call(s32[2]{0:T(128)S(1)} %pad_add_fusion.1.here, f32[8,4096]{1,0:T(8,128)S(1)} %get-tuple-element.90.refs_0_, f32[8,4096]{1,0:T(8,128)S(1)} %collective-permute-done.29.refs_1_, f32[8,4096]{1,0:T(8,128)S(1)} %collective-permute-done.30.refs_2_, ...), custom_call_target="tpu_custom_call" | custom-call | tf_op jit(solution)/shard_map/pallas_call | solution.py:114
  208.4 12.9 %collective-permute-start.33 = (f32[64,4096]{1,0:T(8,128)S(1)}, f32[64,4096]{1,0:T(8,128)S(1)}, u32[]{:S(2)}, u32[]{:S(2)}) collective-permute-start(f32[64,4096]{1,0:T(8,128)S(1)} %get-tuple-element.94.refs_0_), channel_id=1, source_target_pairs={{0,16},{16,0},{32,48},{48,32},{64,80},{80,64},{96,112},{112,96},{1... | collective-permute-start | bytes 3145736 | tf_op jit(solution)/shard_map/ppermute | solution.py:390
  221.3 4.0 %shard_map.83 = (f32[64,4096]{1,0:T(8,128)S(1)}, f32[8,128]{1,0:T(8,128)S(1)}) custom-call(s32[2]{0:T(128)S(1)} %pad_add_fusion.1.here, f32[8,4096]{1,0:T(8,128)S(1)} %get-tuple-element.89.refs_0_, f32[8,4096]{1,0:T(8,128)S(1)} %collective-permute-done.26.refs_1_, f32[8,4096]{1,0:T(8,128)S(1)} %collective-permute-done.27.refs_2_, ...), custom_call_target="tpu_custom_call" | custom-call | tf_op jit(solution)/shard_map/pallas_call | solution.py:114
  225.4 2.1 collective-permute-start.32
  227.5 1.7 shard_map.84
  229.2 0.5 collective-permute-done.32.refs_1_
  229.8 1.7 shard_map.85
  (52 shorter events, 0.2 us)
Async XLA Ops:
  4.1 48.4 %collective-permute-start.2 = (f32[32,16384]{1,0:T(8,128)S(1)}, f32[32,16384]{1,0:T(8,128)}, u32[]{:S(2)}, u32[]{:S(2)}) collective-permute-start(f32[32,16384]{1,0:T(8,128)S(1)} %get-tuple-element.55), channel_id=1, source_target_pairs={{0,1},{1,2},{2,3},{3,0},{4,5},{5,6},{6,7},{7,4},{8,9},{9,10},{10,1... | collective-permute-start | bytes 6291464 | tf_op jit(solution)/shard_map/ppermute | solution.py:380
  6.3 47.9 %collective-permute-start.3 = (f32[32,16384]{1,0:T(8,128)S(1)}, f32[32,16384]{1,0:T(8,128)}, u32[]{:S(2)}, u32[]{:S(2)}) collective-permute-start(f32[32,16384]{1,0:T(8,128)S(1)} %get-tuple-element.56), channel_id=1, source_target_pairs={{0,3},{1,0},{2,1},{3,2},{4,7},{5,4},{6,5},{7,6},{8,11},{9,8},{10,9... | collective-permute-start | bytes 6291464 | tf_op jit(solution)/shard_map/ppermute | solution.py:380
  7.6 5.9 %copy-start.7 = (s32[1,8,8192]{2,1,0:T(8,128)S(1)}, s32[1,8,8192]{2,1,0:T(8,128)}, u32[]{:S(2)}) copy-start(s32[1,8,8192]{2,1,0:T(8,128)} %refs_4_.3) | copy-start | bytes 786436
  12.1 47.5 %collective-permute-start.6 = (f32[32,16384]{1,0:T(8,128)S(1)}, f32[32,16384]{1,0:T(8,128)}, u32[]{:S(2)}, u32[]{:S(2)}) collective-permute-start(f32[32,16384]{1,0:T(8,128)S(1)} %get-tuple-element.61), channel_id=1, source_target_pairs={{0,4},{1,5},{2,6},{3,7},{4,8},{5,9},{6,10},{7,11},{8,12},{9,13},{1... | collective-permute-start | bytes 6291464 | tf_op jit(solution)/shard_map/ppermute | solution.py:380
  13.5 9.0 %collective-permute-start.8 = (s32[1,8,8192]{2,1,0:T(8,128)S(1)}, s32[1,8,8192]{2,1,0:T(8,128)S(1)}, u32[]{:S(2)}, u32[]{:S(2)}) collective-permute-start(s32[1,8,8192]{2,1,0:T(8,128)S(1)} %copy-done.7), channel_id=1, source_target_pairs={{0,32},{16,48},{32,64},{48,80},{64,96},{80,112},{96,0},{112,16},{1... | collective-permute-start | bytes 786440 | tf_op jit(solution)/shard_map/ppermute | solution.py:384
  15.2 51.7 %collective-permute-start.7 = (f32[32,16384]{1,0:T(8,128)}, f32[32,16384]{1,0:T(8,128)}, u32[]{:S(2)}, u32[]{:S(2)}) collective-permute-start(f32[32,16384]{1,0:T(8,128)} %get-tuple-element.62), channel_id=1, source_target_pairs={{0,12},{1,13},{2,14},{3,15},{4,0},{5,1},{6,2},{7,3},{8,4},{9,5},{1... | collective-permute-start | bytes 6291464 | tf_op jit(solution)/shard_map/ppermute | solution.py:380
  22.5 84.9 %copy-start.10 = (s32[1,8,8192]{2,1,0:T(8,128)}, s32[1,8,8192]{2,1,0:T(8,128)S(1)}, u32[]{:S(2)}) copy-start(s32[1,8,8192]{2,1,0:T(8,128)S(1)} %collective-permute-done.8.refs_13_.refs_5_) | copy-start | bytes 786436
  22.5 74.9 %collective-permute-start = (f32[32,16384]{1,0:T(8,128)}, f32[32,16384]{1,0:T(8,128)S(1)}, u32[]{:S(2)}, u32[]{:S(2)}) collective-permute-start(f32[32,16384]{1,0:T(8,128)} %get-tuple-element.53), channel_id=1, source_target_pairs={{0,1},{1,2},{2,3},{3,0},{4,5},{5,6},{6,7},{7,4},{8,9},{9,10},{10,1... | collective-permute-start | bytes 6291464 | tf_op jit(solution)/shard_map/ppermute | solution.py:380
  52.5 51.9 %collective-permute-start.1 = (f32[32,16384]{1,0:T(8,128)}, f32[32,16384]{1,0:T(8,128)S(1)}, u32[]{:S(2)}, u32[]{:S(2)}) collective-permute-start(f32[32,16384]{1,0:T(8,128)} %get-tuple-element.54), channel_id=1, source_target_pairs={{0,3},{1,0},{2,1},{3,2},{4,7},{5,4},{6,5},{7,6},{8,11},{9,8},{10,9... | collective-permute-start | bytes 6291464 | tf_op jit(solution)/shard_map/ppermute | solution.py:380
  54.1 51.7 %collective-permute-start.9 = (f32[32,16384]{1,0:T(8,128)}, f32[32,16384]{1,0:T(8,128)S(1)}, u32[]{:S(2)}, u32[]{:S(2)}) collective-permute-start(f32[32,16384]{1,0:T(8,128)} %get-tuple-element.65), channel_id=1, source_target_pairs={{0,4},{1,5},{2,6},{3,7},{4,8},{5,9},{6,10},{7,11},{8,12},{9,13},{1... | collective-permute-start | bytes 6291464 | tf_op jit(solution)/shard_map/ppermute | solution.py:380
  59.6 47.7 %collective-permute-start.10 = (f32[32,16384]{1,0:T(8,128)}, f32[32,16384]{1,0:T(8,128)S(1)}, u32[]{:S(2)}, u32[]{:S(2)}) collective-permute-start(f32[32,16384]{1,0:T(8,128)} %get-tuple-element.66), channel_id=1, source_target_pairs={{0,12},{1,13},{2,14},{3,15},{4,0},{5,1},{6,2},{7,3},{8,4},{9,5},{1... | collective-permute-start | bytes 6291464 | tf_op jit(solution)/shard_map/ppermute | solution.py:380
  66.9 75.6 %collective-permute-start.4 = (f32[32,16384]{1,0:T(8,128)}, f32[32,16384]{1,0:T(8,128)}, u32[]{:S(2)}, u32[]{:S(2)}) collective-permute-start(f32[32,16384]{1,0:T(8,128)} %get-tuple-element.59), channel_id=1, source_target_pairs={{0,1},{1,2},{2,3},{3,0},{4,5},{5,6},{6,7},{7,4},{8,9},{9,10},{10,1... | collective-permute-start | bytes 6291464 | tf_op jit(solution)/shard_map/ppermute | solution.py:380
  97.4 45.1 %copy-start = (f32[32,16384]{1,0:T(8,128)}, f32[32,16384]{1,0:T(8,128)S(1)}, u32[]{:S(2)}) copy-start(f32[32,16384]{1,0:T(8,128)S(1)} %collective-permute-done.refs_4_.refs_5_.refs_6_.refs_7_.refs_21_.refs_2_.refs_3_.refs_12_.refs_13_.refs_1_) | copy-start | bytes 6291460
  97.4 45.0 %collective-permute-start.5 = (f32[32,16384]{1,0:T(8,128)}, f32[32,16384]{1,0:T(8,128)}, u32[]{:S(2)}, u32[]{:S(2)}) collective-permute-start(f32[32,16384]{1,0:T(8,128)} %get-tuple-element.60), channel_id=1, source_target_pairs={{0,3},{1,0},{2,1},{3,2},{4,7},{5,4},{6,5},{7,6},{8,11},{9,8},{10,9... | collective-permute-start | bytes 6291464 | tf_op jit(solution)/shard_map/ppermute | solution.py:380
  99.0 8.4 %copy-start.8 = (s32[1,8,8192]{2,1,0:T(8,128)S(1)}, s32[1,8,8192]{2,1,0:T(8,128)}, u32[]{:S(2)}) copy-start(s32[1,8,8192]{2,1,0:T(8,128)} %refs_4_.3) | copy-start | bytes 786436
  104.4 40.2 %copy-start.2 = (f32[32,16384]{1,0:T(8,128)}, f32[32,16384]{1,0:T(8,128)S(1)}, u32[]{:S(2)}) copy-start(f32[32,16384]{1,0:T(8,128)S(1)} %collective-permute-done.1.refs_8_.refs_9_.refs_10_.refs_11_.refs_22_.refs_4_.refs_5_.refs_14_.refs_15_.refs_2_) | copy-start | bytes 6291460
  104.4 45.7 %collective-permute-start.13 = (f32[32,16384]{1,0:T(8,128)S(1)}, f32[32,16384]{1,0:T(8,128)}, u32[]{:S(2)}, u32[]{:S(2)}) collective-permute-start(f32[32,16384]{1,0:T(8,128)S(1)} %get-tuple-element.69), channel_id=1, source_target_pairs={{0,4},{1,5},{2,6},{3,7},{4,8},{5,9},{6,10},{7,11},{8,12},{9,13},{1... | collective-permute-start | bytes 6291464 | tf_op jit(solution)/shard_map/ppermute | solution.py:380
  105.8 36.6 %copy-start.3 = (f32[32,16384]{1,0:T(8,128)}, f32[32,16384]{1,0:T(8,128)S(1)}, u32[]{:S(2)}) copy-start(f32[32,16384]{1,0:T(8,128)S(1)} %collective-permute-done.9.refs_21_.refs_4_.refs_5_.refs_6_.refs_7_.refs_2_.refs_3_.refs_12_.refs_13_.refs_8_) | copy-start | bytes 6291460
  105.8 44.3 %collective-permute-start.14 = (f32[32,16384]{1,0:T(8,128)}, f32[32,16384]{1,0:T(8,128)}, u32[]{:S(2)}, u32[]{:S(2)}) collective-permute-start(f32[32,16384]{1,0:T(8,128)} %get-tuple-element.70), channel_id=1, source_target_pairs={{0,12},{1,13},{2,14},{3,15},{4,0},{5,1},{6,2},{7,3},{8,4},{9,5},{1... | collective-permute-start | bytes 6291464 | tf_op jit(solution)/shard_map/ppermute | solution.py:380
  107.4 35.0 %copy-start.5 = (f32[32,16384]{1,0:T(8,128)}, f32[32,16384]{1,0:T(8,128)S(1)}, u32[]{:S(2)}) copy-start(f32[32,16384]{1,0:T(8,128)S(1)} %collective-permute-done.10.refs_22_.refs_8_.refs_9_.refs_10_.refs_11_.refs_4_.refs_5_.refs_14_.refs_15_) | copy-start | bytes 6291460
  107.4 40.4 %collective-permute-start.15 = (s32[1,16,8192]{2,1,0:T(8,128)S(1)}, s32[1,16,8192]{2,1,0:T(8,128)S(1)}, u32[]{:S(2)}, u32[]{:S(2)}) collective-permute-start(s32[1,16,8192]{2,1,0:T(8,128)S(1)} %pad_add_fusion), channel_id=1, source_target_pairs={{0,64},{16,80},{32,96},{48,112},{64,0},{80,16},{96,32},{112,48},{1... | collective-permute-start | bytes 1572872 | tf_op jit(solution)/shard_map/ppermute | solution.py:384
  144.6 16.6 %collective-permute-start.11 = (f32[32,4096]{1,0:T(8,128)S(1)}, f32[32,4096]{1,0:T(8,128)S(1)}, u32[]{:S(2)}, u32[]{:S(2)}) collective-permute-start(f32[32,4096]{1,0:T(8,128)S(1)} %get-tuple-element.67), channel_id=1, source_target_pairs={{0,4},{1,5},{2,6},{3,7},{4,8},{5,9},{6,10},{7,11},{8,12},{9,13},{1... | collective-permute-start | bytes 1572872 | tf_op jit(solution)/shard_map/ppermute | solution.py:380
  146.3 14.9 %collective-permute-start.12 = (f32[32,4096]{1,0:T(8,128)S(1)}, f32[32,4096]{1,0:T(8,128)S(1)}, u32[]{:S(2)}, u32[]{:S(2)}) collective-permute-start(f32[32,4096]{1,0:T(8,128)S(1)} %get-tuple-element.68), channel_id=1, source_target_pairs={{0,12},{1,13},{2,14},{3,15},{4,0},{5,1},{6,2},{7,3},{8,4},{9,5},{1... | collective-permute-start | bytes 1572872 | tf_op jit(solution)/shard_map/ppermute | solution.py:380
  150.1 1.6 copy-start.4
  151.7 1.6 copy-start.6
  153.3 7.9 %copy-start.1 = (f32[32,16384]{1,0:T(8,128)S(1)}, f32[32,16384]{1,0:T(8,128)}, u32[]{:S(2)}) copy-start(f32[32,16384]{1,0:T(8,128)} %copy-done) | copy-start | bytes 6291460
  155.5 11.0 %collective-permute-start.16 = (f32[32,4096]{1,0:T(8,128)S(1)}, f32[32,4096]{1,0:T(8,128)S(1)}, u32[]{:S(2)}, u32[]{:S(2)}) collective-permute-start(f32[32,4096]{1,0:T(8,128)S(1)} %get-tuple-element.72), channel_id=1, source_target_pairs={{0,1},{1,2},{2,3},{3,0},{4,5},{5,6},{6,7},{7,4},{8,9},{9,10},{10,1... | collective-permute-start | bytes 1572872 | tf_op jit(solution)/shard_map/ppermute | solution.py:380
  155.8 10.7 %collective-permute-start.17 = (f32[32,4096]{1,0:T(8,128)S(1)}, f32[32,4096]{1,0:T(8,128)S(1)}, u32[]{:S(2)}, u32[]{:S(2)}) collective-permute-start(f32[32,4096]{1,0:T(8,128)S(1)} %get-tuple-element.73), channel_id=1, source_target_pairs={{0,3},{1,0},{2,1},{3,2},{4,7},{5,4},{6,5},{7,6},{8,11},{9,8},{10,9... | collective-permute-start | bytes 1572872 | tf_op jit(solution)/shard_map/ppermute | solution.py:380
  163.6 13.0 %collective-permute-start.22 = (f32[64,2048]{1,0:T(8,128)S(1)}, f32[64,2048]{1,0:T(8,128)S(1)}, u32[]{:S(2)}, u32[]{:S(2)}) collective-permute-start(f32[64,2048]{1,0:T(8,128)S(1)} %get-tuple-element.82), channel_id=1, source_target_pairs={{0,4},{1,5},{2,6},{3,7},{4,8},{5,9},{6,10},{7,11},{8,12},{9,13},{1... | collective-permute-start | bytes 1572872 | tf_op jit(solution)/shard_map/ppermute | solution.py:380
  164.8 14.4 %collective-permute-start.23 = (f32[64,2048]{1,0:T(8,128)S(1)}, f32[64,2048]{1,0:T(8,128)S(1)}, u32[]{:S(2)}, u32[]{:S(2)}) collective-permute-start(f32[64,2048]{1,0:T(8,128)S(1)} %get-tuple-element.83), channel_id=1, source_target_pairs={{0,12},{1,13},{2,14},{3,15},{4,0},{5,1},{6,2},{7,3},{8,4},{9,5},{1... | collective-permute-start | bytes 1572872 | tf_op jit(solution)/shard_map/ppermute | solution.py:380
  168.8 10.4 %collective-permute-start.24 = (f32[64,2048]{1,0:T(8,128)S(1)}, f32[64,2048]{1,0:T(8,128)S(1)}, u32[]{:S(2)}, u32[]{:S(2)}) collective-permute-start(f32[64,2048]{1,0:T(8,128)S(1)} %get-tuple-element.84), channel_id=1, source_target_pairs={{0,1},{1,2},{2,3},{3,0},{4,5},{5,6},{6,7},{7,4},{8,9},{9,10},{10,1... | collective-permute-start | bytes 1572872 | tf_op jit(solution)/shard_map/ppermute | solution.py:380
  169.2 12.7 %collective-permute-start.25 = (f32[64,2048]{1,0:T(8,128)S(1)}, f32[64,2048]{1,0:T(8,128)S(1)}, u32[]{:S(2)}, u32[]{:S(2)}) collective-permute-start(f32[64,2048]{1,0:T(8,128)S(1)} %get-tuple-element.85), channel_id=1, source_target_pairs={{0,3},{1,0},{2,1},{3,2},{4,7},{5,4},{6,5},{7,6},{8,11},{9,8},{10,9... | collective-permute-start | bytes 1572872 | tf_op jit(solution)/shard_map/ppermute | solution.py:380
  173.9 8.0 %copy-start.9 = (s32[1,8,8192]{2,1,0:T(8,128)S(1)}, s32[1,8,8192]{2,1,0:T(8,128)}, u32[]{:S(2)}) copy-start(s32[1,8,8192]{2,1,0:T(8,128)} %refs_4_.3) | copy-start | bytes 786436
  173.9 8.0 %copy-start.12 = (bf16[64,256]{1,0:T(8,128)(2,1)S(1)}, bf16[64,256]{1,0:T(8,128)(2,1)}, u32[]{:S(2)}) copy-start(bf16[64,256]{1,0:T(8,128)(2,1)} %constant.25.clone.refs_17_.refs_8_) | copy-start | bytes 98308
  173.9 8.0 %copy-start.13 = (bf16[64,256]{1,0:T(8,128)(2,1)S(1)}, bf16[64,256]{1,0:T(8,128)(2,1)}, u32[]{:S(2)}) copy-start(bf16[64,256]{1,0:T(8,128)(2,1)} %constant.24.clone.refs_16_) | copy-start | bytes 98308
  176.3 16.0 %collective-permute-start.18 = (f32[64,2048]{1,0:T(8,128)S(1)}, f32[64,2048]{1,0:T(8,128)S(1)}, u32[]{:S(2)}, u32[]{:S(2)}) collective-permute-start(f32[64,2048]{1,0:T(8,128)S(1)} %get-tuple-element.78), channel_id=1, source_target_pairs={{0,4},{1,5},{2,6},{3,7},{4,8},{5,9},{6,10},{7,11},{8,12},{9,13},{1... | collective-permute-start | bytes 1572872 | tf_op jit(solution)/shard_map/ppermute | solution.py:380
  176.6 16.1 %collective-permute-start.19 = (f32[64,2048]{1,0:T(8,128)S(1)}, f32[64,2048]{1,0:T(8,128)S(1)}, u32[]{:S(2)}, u32[]{:S(2)}) collective-permute-start(f32[64,2048]{1,0:T(8,128)S(1)} %get-tuple-element.79), channel_id=1, source_target_pairs={{0,12},{1,13},{2,14},{3,15},{4,0},{5,1},{6,2},{7,3},{8,4},{9,5},{1... | collective-permute-start | bytes 1572872 | tf_op jit(solution)/shard_map/ppermute | solution.py:380
  179.2 14.5 %collective-permute-start.20 = (f32[64,2048]{1,0:T(8,128)S(1)}, f32[64,2048]{1,0:T(8,128)S(1)}, u32[]{:S(2)}, u32[]{:S(2)}) collective-permute-start(f32[64,2048]{1,0:T(8,128)S(1)} %get-tuple-element.80), channel_id=1, source_target_pairs={{0,1},{1,2},{2,3},{3,0},{4,5},{5,6},{6,7},{7,4},{8,9},{9,10},{10,1... | collective-permute-start | bytes 1572872 | tf_op jit(solution)/shard_map/ppermute | solution.py:380
  179.2 14.5 %collective-permute-start.21 = (f32[64,2048]{1,0:T(8,128)S(1)}, f32[64,2048]{1,0:T(8,128)S(1)}, u32[]{:S(2)}, u32[]{:S(2)}) collective-permute-start(f32[64,2048]{1,0:T(8,128)S(1)} %get-tuple-element.81), channel_id=1, source_target_pairs={{0,3},{1,0},{2,1},{3,2},{4,7},{5,4},{6,5},{7,6},{8,11},{9,8},{10,9... | collective-permute-start | bytes 1572872 | tf_op jit(solution)/shard_map/ppermute | solution.py:380
  188.7 15.0 %collective-permute-start.31 = (f32[8,4096]{1,0:T(8,128)S(1)}, f32[8,4096]{1,0:T(8,128)S(1)}, u32[]{:S(2)}, u32[]{:S(2)}) collective-permute-start(f32[8,4096]{1,0:T(8,128)S(1)} %get-tuple-element.90.refs_0_), channel_id=1, source_target_pairs={{0,64},{16,80},{32,96},{48,112},{64,0},{80,16},{96,32},{112,48},{1... | collective-permute-start | bytes 393224 | tf_op jit(solution)/shard_map/ppermute | solution.py:384
  192.3 12.1 %collective-permute-start.30 = (f32[8,4096]{1,0:T(8,128)S(1)}, f32[8,4096]{1,0:T(8,128)S(1)}, u32[]{:S(2)}, u32[]{:S(2)}) collective-permute-start(f32[8,4096]{1,0:T(8,128)S(1)} %get-tuple-element.90.refs_0_), channel_id=1, source_target_pairs={{0,96},{16,112},{32,0},{48,16},{64,32},{80,48},{96,64},{112,80},{1... | collective-permute-start | bytes 393224 | tf_op jit(solution)/shard_map/ppermute | solution.py:384
  192.7 11.7 %collective-permute-start.29 = (f32[8,4096]{1,0:T(8,128)S(1)}, f32[8,4096]{1,0:T(8,128)S(1)}, u32[]{:S(2)}, u32[]{:S(2)}) collective-permute-start(f32[8,4096]{1,0:T(8,128)S(1)} %get-tuple-element.90.refs_0_), channel_id=1, source_target_pairs={{0,32},{16,48},{32,64},{48,80},{64,96},{80,112},{96,0},{112,16},{1... | collective-permute-start | bytes 393224 | tf_op jit(solution)/shard_map/ppermute | solution.py:384
  193.8 10.6 %copy-start.11 = (s32[1,8,8192]{2,1,0:T(8,128)S(1)}, s32[1,8,8192]{2,1,0:T(8,128)}, u32[]{:S(2)}) copy-start(s32[1,8,8192]{2,1,0:T(8,128)} %copy-done.10) | copy-start | bytes 786436
  200.5 20.8 %collective-permute-start.28 = (f32[8,4096]{1,0:T(8,128)S(1)}, f32[8,4096]{1,0:T(8,128)S(1)}, u32[]{:S(2)}, u32[]{:S(2)}) collective-permute-start(f32[8,4096]{1,0:T(8,128)S(1)} %get-tuple-element.89.refs_0_), channel_id=1, source_target_pairs={{0,64},{16,80},{32,96},{48,112},{64,0},{80,16},{96,32},{112,48},{1... | collective-permute-start | bytes 393224 | tf_op jit(solution)/shard_map/ppermute | solution.py:384
  202.9 18.4 %collective-permute-start.27 = (f32[8,4096]{1,0:T(8,128)S(1)}, f32[8,4096]{1,0:T(8,128)S(1)}, u32[]{:S(2)}, u32[]{:S(2)}) collective-permute-start(f32[8,4096]{1,0:T(8,128)S(1)} %get-tuple-element.89.refs_0_), channel_id=1, source_target_pairs={{0,96},{16,112},{32,0},{48,16},{64,32},{80,48},{96,64},{112,80},{1... | collective-permute-start | bytes 393224 | tf_op jit(solution)/shard_map/ppermute | solution.py:384
  203.7 17.7 %collective-permute-start.26 = (f32[8,4096]{1,0:T(8,128)S(1)}, f32[8,4096]{1,0:T(8,128)S(1)}, u32[]{:S(2)}, u32[]{:S(2)}) collective-permute-start(f32[8,4096]{1,0:T(8,128)S(1)} %get-tuple-element.89.refs_0_), channel_id=1, source_target_pairs={{0,32},{16,48},{32,64},{48,80},{64,96},{80,112},{96,0},{112,16},{1... | collective-permute-start | bytes 393224 | tf_op jit(solution)/shard_map/ppermute | solution.py:384
  208.4 19.1 %collective-permute-start.33 = (f32[64,4096]{1,0:T(8,128)S(1)}, f32[64,4096]{1,0:T(8,128)S(1)}, u32[]{:S(2)}, u32[]{:S(2)}) collective-permute-start(f32[64,4096]{1,0:T(8,128)S(1)} %get-tuple-element.94.refs_0_), channel_id=1, source_target_pairs={{0,16},{16,0},{32,48},{48,32},{64,80},{80,64},{96,112},{112,96},{1... | collective-permute-start | bytes 3145736 | tf_op jit(solution)/shard_map/ppermute | solution.py:390
  225.4 4.4 %collective-permute-start.32 = (f32[64,4096]{1,0:T(8,128)S(1)}, f32[64,4096]{1,0:T(8,128)S(1)}, u32[]{:S(2)}, u32[]{:S(2)}) collective-permute-start(f32[64,4096]{1,0:T(8,128)S(1)} %get-tuple-element.93.refs_0_), channel_id=1, source_target_pairs={{0,16},{16,0},{32,48},{48,32},{64,80},{80,64},{96,112},{112,96},{1... | collective-permute-start | bytes 3145736 | tf_op jit(solution)/shard_map/ppermute | solution.py:390

commit v9 on v8

--- a/solution.py
+++ b/solution.py
@@ -15,12 +15,12 @@
 CHUNK = 256
 FINE, BROAD = 1024, 2048
 PARTS = (2, 2)
-AXES = (0, 0, 0, 1, 1, 0)
+AXES = (0, 0, 1, 1, 1, 0)
 LAG = (2, 2, 2, 2, 2, 2)
-PLACES_WITH = ((0, 1), (1, 0))
+PLACES_WITH = ((1, 0), (1, 0))
 TAIL = ('f0', 'f1', 's0', 's1', 'j0', 'j1')
-TOGETHER = 1
-VMEM_LIMIT = 48 * 1024 * 1024
+TOGETHER = 2
+VMEM_LIMIT = 62 * 1024 * 1024
 F32 = jnp.float32
 BF16 = jnp.bfloat16
 

time: 233 us -> 242 us (1.039)
  Pallas kernels: 67.8 us -> 82.1 us
  starting transfers between devices: 61.6 us -> 52.2 us
    pallas_call x18, Pallas kernels: 67.8 us -> 82.1 us  [call(): pl.pallas_call(run, grid_spec=pltpu.PrefetchScalarGridSpec(num_scalar_pre...]
    ppermute x2, starting transfers between devices: 15 us -> 6.61 us  [other_core(): return lax.ppermute(value, 'rep', [(r, r ^ 1) for r in range(2 * SIDE)])]
  transfers between devices with their start and end apart: 34 -> 34, of which waited for: 8 -> 8; matrix products, arithmetic and copies ran while one was open for 0% -> 1% of each run, Pallas kernels for 27% -> 31%
where the time goes in v9:
time: 242 us; the launch traced here: 240 us
  waiting for transfers between devices  98 us (40%)
  Pallas kernels  82.1 us (34%)
  starting transfers between devices  52.2 us (22%)
  local copies, waits for them, and re-layouts  4.6 us (2%)
  other arithmetic  2.46 us (1%)
    ppermute x24, waiting for transfers between devices, along(): lax.ppermute(value, 'fsdp', shift(0, step) if x_first else shift(step, 0))  98 us
    pallas_call x18, Pallas kernels, call(): pl.pallas_call(run, grid_spec=pltpu.PrefetchScalarGridSpec(num_scalar_pre...  82.1 us
    ppermute x24, starting transfers between devices, along(): lax.ppermute(value, 'fsdp', shift(0, step) if x_first else shift(step, 0))  32 us
    ppermute x8, starting transfers between devices, along_z(): lax.ppermute(value, 'rep', [(z * 2 + c, (z + step) % SIDE * 2 + c) for z...  13.6 us
    ppermute x2, starting transfers between devices, other_core(): return lax.ppermute(value, 'rep', [(r, r ^ 1) for r in range(2 * SIDE)])  6.61 us
  transfers between devices with their start and end apart: 34, of which 8 were waited for; matrix products, arithmetic and copies ran while one was open for 1% of the time, Pallas kernels for 31%

profile of v9, /device:TPU:1, one launch (start us, length us, event | category | flops | bytes accessed | tf_op | source)
XLA Modules:
  0.0 240.2 jit_solution(8380616729156983463)
XLA Ops:
  0.6 0.6 pad_add_fusion.1.here
  1.3 4.2 %shard_map.68 = (f32[32,16384]{1,0:T(8,128)}, f32[32,16384]{1,0:T(8,128)}, f32[8,128]{1,0:T(8,128)}) custom-call(s32[2]{0:T(128)} %pad_add_fusion.1.here, bf16[64,131072]{1,0:T(8,128)(2,1)} %bitcast.3, bf16[64,131072]{1,0:T(8,128)(2,1)} %bitcast.4, bf16[64,131072]{1,0:T(8,128)(2,1)} %bitcast.5, bf16[64,131072]{1,0:T(8,128)(2,1)} %bitcast.6, ...), custom_call_target="tpu_custom_call" | custom-call | tf_op jit(solution)/shard_map/pallas_call | solution.py:114
  5.5 2.1 collective-permute-start.2
  7.6 1.4 collective-permute-start.3
  8.9 4.3 %shard_map.69 = (f32[32,16384]{1,0:T(8,128)}, f32[32,16384]{1,0:T(8,128)}, f32[8,128]{1,0:T(8,128)}) custom-call(s32[2]{0:T(128)} %pad_add_fusion.1.here, bf16[64,131072]{1,0:T(8,128)(2,1)} %bitcast.26, bf16[64,131072]{1,0:T(8,128)(2,1)} %bitcast.20, bf16[64,131072]{1,0:T(8,128)(2,1)} %bitcast.21, bf16[64,131072]{1,0:T(8,128)(2,1)} %bitcast.22, ...), custom_call_target="tpu_custom_call" | custom-call | tf_op jit(solution)/shard_map/pallas_call | solution.py:114
  13.2 1.5 collective-permute-start.4
  14.7 1.5 collective-permute-start.5
  16.2 4.2 %shard_map.70 = (f32[32,16384]{1,0:T(8,128)}, f32[32,16384]{1,0:T(8,128)}, f32[8,128]{1,0:T(8,128)}) custom-call(s32[2]{0:T(128)} %pad_add_fusion.1.here, bf16[64,131072]{1,0:T(8,128)(2,1)} %bitcast.35, bf16[64,131072]{1,0:T(8,128)(2,1)} %bitcast.36, bf16[64,131072]{1,0:T(8,128)(2,1)} %bitcast.37, bf16[64,131072]{1,0:T(8,128)(2,1)} %bitcast.38, ...), custom_call_target="tpu_custom_call" | custom-call | tf_op jit(solution)/shard_map/pallas_call | solution.py:114
  20.4 0.1 collective-permute-start
  20.5 4.3 %shard_map.71 = (f32[32,16384]{1,0:T(8,128)}, f32[32,16384]{1,0:T(8,128)}, f32[8,128]{1,0:T(8,128)}) custom-call(s32[2]{0:T(128)} %pad_add_fusion.1.here, bf16[64,131072]{1,0:T(8,128)(2,1)} %bitcast.64, bf16[64,131072]{1,0:T(8,128)(2,1)} %bitcast.52, bf16[64,131072]{1,0:T(8,128)(2,1)} %bitcast.53, bf16[64,131072]{1,0:T(8,128)(2,1)} %bitcast.54, ...), custom_call_target="tpu_custom_call" | custom-call | tf_op jit(solution)/shard_map/pallas_call | solution.py:114
  24.8 29.3 %collective-permute-done.2.refs_16_.refs_19_ = f32[32,16384]{1,0:T(8,128)} collective-permute-done((f32[32,16384]{1,0:T(8,128)}, f32[32,16384]{1,0:T(8,128)}, u32[]{:S(2)}, u32[]{:S(2)}) %collective-permute-start.2) | collective-permute-done | bytes 2097184 | tf_op jit(solution)/shard_map/ppermute | solution.py:380
  54.1 1.6 collective-permute-start.1
  55.7 1.3 collective-permute-start.8
  57.0 4.1 %collective-permute-done.4.refs_16_.refs_19_ = f32[32,16384]{1,0:T(8,128)} collective-permute-done((f32[32,16384]{1,0:T(8,128)}, f32[32,16384]{1,0:T(8,128)}, u32[]{:S(2)}, u32[]{:S(2)}) %collective-permute-start.4) | collective-permute-done | bytes 2097184 | tf_op jit(solution)/shard_map/ppermute | solution.py:380
  61.0 1.3 collective-permute-start.9
  62.3 1.6 collective-permute-start.14
  64.0 5.3 %shard_map.72 = (f32[32,16384]{1,0:T(8,128)}, f32[32,16384]{1,0:T(8,128)}, f32[8,128]{1,0:T(8,128)}) custom-call(s32[2]{0:T(128)} %pad_add_fusion.1.here, bf16[64,131072]{1,0:T(8,128)(2,1)} %bitcast.67, bf16[64,131072]{1,0:T(8,128)(2,1)} %bitcast.68, bf16[64,131072]{1,0:T(8,128)(2,1)} %bitcast.69, bf16[64,131072]{1,0:T(8,128)(2,1)} %bitcast.70, ...), custom_call_target="tpu_custom_call" | custom-call | tf_op jit(solution)/shard_map/pallas_call | solution.py:114
  69.3 5.4 %shard_map.73 = (f32[32,16384]{1,0:T(8,128)}, f32[32,16384]{1,0:T(8,128)}, f32[8,128]{1,0:T(8,128)}) custom-call(s32[2]{0:T(128)} %pad_add_fusion.1.here, bf16[64,131072]{1,0:T(8,128)(2,1)} %bitcast.89, bf16[64,131072]{1,0:T(8,128)(2,1)} %bitcast.84, bf16[64,131072]{1,0:T(8,128)(2,1)} %bitcast.85, bf16[64,131072]{1,0:T(8,128)(2,1)} %bitcast.86, ...), custom_call_target="tpu_custom_call" | custom-call | tf_op jit(solution)/shard_map/pallas_call | solution.py:114
  74.7 0.1 collective-permute-start.6
  74.8 24.2 %collective-permute-done.refs_4_.refs_5_.refs_6_.refs_7_.refs_21_.refs_2_.refs_3_.refs_12_.refs_13_.refs_1_ = f32[32,16384]{1,0:T(8,128)} collective-permute-done((f32[32,16384]{1,0:T(8,128)}, f32[32,16384]{1,0:T(8,128)}, u32[]{:S(2)}, u32[]{:S(2)}) %collective-permute-start) | collective-permute-done | bytes 2097184 | tf_op jit(solution)/shard_map/ppermute | solution.py:380
  99.0 1.6 collective-permute-start.7
  100.6 1.3 collective-permute-start.12
  101.9 4.1 %collective-permute-done.8.refs_21_.refs_4_.refs_5_.refs_6_.refs_7_.refs_2_.refs_3_.refs_12_.refs_13_.refs_8_ = f32[32,16384]{1,0:T(8,128)} collective-permute-done((f32[32,16384]{1,0:T(8,128)}, f32[32,16384]{1,0:T(8,128)}, u32[]{:S(2)}, u32[]{:S(2)}) %collective-permute-start.8) | collective-permute-done | bytes 2097184 | tf_op jit(solution)/shard_map/ppermute | solution.py:380
  106.0 1.3 collective-permute-start.13
  107.3 1.8 pad_add_fusion
  109.1 3.6 %collective-permute-start.15 = (s32[1,16,8192]{2,1,0:T(8,128)}, s32[1,16,8192]{2,1,0:T(8,128)S(1)}, u32[]{:S(2)}, u32[]{:S(2)}) collective-permute-start(s32[1,16,8192]{2,1,0:T(8,128)} %pad_add_fusion), channel_id=1, source_target_pairs={{0,64},{16,80},{32,96},{48,112},{64,0},{80,16},{96,32},{112,48},{1... | collective-permute-start | bytes 1572872 | tf_op jit(solution)/shard_map/ppermute | solution.py:384
  112.7 31.2 %collective-permute-done.6.refs_12_.refs_13_.refs_14_.refs_15_.refs_6_.refs_7_.refs_16_.refs_17_.refs_25_.refs_3_ = f32[32,16384]{1,0:T(8,128)} collective-permute-done((f32[32,16384]{1,0:T(8,128)}, f32[32,16384]{1,0:T(8,128)}, u32[]{:S(2)}, u32[]{:S(2)}) %collective-permute-start.6) | collective-permute-done | bytes 2097184 | tf_op jit(solution)/shard_map/ppermute | solution.py:380
  144.0 3.5 %shard_map.74 = (f32[32,4096]{1,0:T(8,128)}, f32[32,4096]{1,0:T(8,128)}, f32[8,128]{1,0:T(8,128)}) custom-call(s32[2]{0:T(128)} %pad_add_fusion.1.here, bf16[64,131072]{1,0:T(8,128)(2,1)} %bitcast.99, bf16[64,131072]{1,0:T(8,128)(2,1)} %bitcast.100, bf16[64,131072]{1,0:T(8,128)(2,1)} %bitcast.101, bf16[64,131072]{1,0:T(8,128)(2,1)} %bitcast.102, ...), custom_call_target="tpu_custom_call" | custom-call | tf_op jit(solution)/shard_map/pallas_call | solution.py:114
  147.5 1.7 collective-permute-start.10
  149.1 1.5 collective-permute-start.11
  150.7 0.2 collective-permute-done.12.refs_12_.refs_13_.refs_14_.refs_15_.refs_25_.refs_6_.refs_7_.refs_16_.refs_17_.refs_10_
  150.9 0.6 copy-done.3
  151.5 3.5 %shard_map.75 = (f32[32,4096]{1,0:T(8,128)}, f32[32,4096]{1,0:T(8,128)}, f32[8,128]{1,0:T(8,128)}) custom-call(s32[2]{0:T(128)} %pad_add_fusion.1.here, bf16[64,131072]{1,0:T(8,128)(2,1)} %bitcast.105, bf16[64,131072]{1,0:T(8,128)(2,1)} %bitcast.104, bf16[64,131072]{1,0:T(8,128)(2,1)} %bitcast.103, bf16[64,131072]{1,0:T(8,128)(2,1)} %bitcast.106, ...), custom_call_target="tpu_custom_call" | custom-call | tf_op jit(solution)/shard_map/pallas_call | solution.py:114
  155.1 2.7 %collective-permute-start.17 = (f32[32,4096]{1,0:T(8,128)}, f32[32,4096]{1,0:T(8,128)}, u32[]{:S(2)}, u32[]{:S(2)}) collective-permute-start(f32[32,4096]{1,0:T(8,128)} %get-tuple-element.73), channel_id=1, source_target_pairs={{0,3},{1,0},{2,1},{3,2},{4,7},{5,4},{6,5},{7,6},{8,11},{9,8},{10,9... | collective-permute-start | bytes 1572872 | tf_op jit(solution)/shard_map/ppermute | solution.py:380
  157.7 2.6 %collective-permute-done.10.refs_20_.refs_21_.refs_25_ = f32[32,4096]{1,0:T(8,128)S(1)} collective-permute-done((f32[32,4096]{1,0:T(8,128)}, f32[32,4096]{1,0:T(8,128)S(1)}, u32[]{:S(2)}, u32[]{:S(2)}) %collective-permute-start.10) | collective-permute-done | bytes 524320 | tf_op jit(solution)/shard_map/ppermute | solution.py:380
  160.4 2.2 collective-permute-done.11.refs_22_.refs_23_.refs_26_
  162.6 0.8 copy-done.1
  163.4 3.7 %shard_map.76 = (f32[64,2048]{1,0:T(8,128)}, f32[64,2048]{1,0:T(8,128)}, f32[8,128]{1,0:T(8,128)}) custom-call(s32[2]{0:T(128)} %pad_add_fusion.1.here, bf16[64,131072]{1,0:T(8,128)(2,1)} %bitcast.107, bf16[64,131072]{1,0:T(8,128)(2,1)} %bitcast.108, ...), custom_call_target="tpu_custom_call" | custom-call | tf_op jit(solution)/shard_map/pallas_call | solution.py:114
  167.1 2.7 %collective-permute-start.23 = (f32[64,2048]{1,0:T(8,128)}, f32[64,2048]{1,0:T(8,128)}, u32[]{:S(2)}, u32[]{:S(2)}) collective-permute-start(f32[64,2048]{1,0:T(8,128)} %get-tuple-element.83), channel_id=1, source_target_pairs={{0,12},{1,13},{2,14},{3,15},{4,0},{5,1},{6,2},{7,3},{8,4},{9,5},{1... | collective-permute-start | bytes 1572872 | tf_op jit(solution)/shard_map/ppermute | solution.py:380
  169.8 0.8 copy-done.2
  170.6 3.7 %shard_map.77 = (f32[64,2048]{1,0:T(8,128)}, f32[64,2048]{1,0:T(8,128)}, f32[8,128]{1,0:T(8,128)}) custom-call(s32[2]{0:T(128)} %pad_add_fusion.1.here, bf16[64,131072]{1,0:T(8,128)(2,1)} %bitcast.111, bf16[64,131072]{1,0:T(8,128)(2,1)} %bitcast.112, ...), custom_call_target="tpu_custom_call" | custom-call | tf_op jit(solution)/shard_map/pallas_call | solution.py:114
  174.3 0.3 collective-permute-start.24
  174.6 2.7 %collective-permute-start.25 = (f32[64,2048]{1,0:T(8,128)}, f32[64,2048]{1,0:T(8,128)}, u32[]{:S(2)}, u32[]{:S(2)}) collective-permute-start(f32[64,2048]{1,0:T(8,128)} %get-tuple-element.85), channel_id=1, source_target_pairs={{0,3},{1,0},{2,1},{3,2},{4,7},{5,4},{6,5},{7,6},{8,11},{9,8},{10,9... | collective-permute-start | bytes 1572872 | tf_op jit(solution)/shard_map/ppermute | solution.py:380
  177.2 3.7 %shard_map.78 = (f32[64,2048]{1,0:T(8,128)}, f32[64,2048]{1,0:T(8,128)}, f32[8,128]{1,0:T(8,128)}) custom-call(s32[2]{0:T(128)} %pad_add_fusion.1.here, bf16[64,131072]{1,0:T(8,128)(2,1)} %bitcast.115, bf16[64,131072]{1,0:T(8,128)(2,1)} %bitcast.116, ...), custom_call_target="tpu_custom_call" | custom-call | tf_op jit(solution)/shard_map/pallas_call | solution.py:114
  180.9 3.7 %shard_map.79 = (f32[64,2048]{1,0:T(8,128)}, f32[64,2048]{1,0:T(8,128)}, f32[8,128]{1,0:T(8,128)}) custom-call(s32[2]{0:T(128)} %pad_add_fusion.1.here, bf16[64,131072]{1,0:T(8,128)(2,1)} %bitcast.119, bf16[64,131072]{1,0:T(8,128)(2,1)} %bitcast.120, ...), custom_call_target="tpu_custom_call" | custom-call | tf_op jit(solution)/shard_map/pallas_call | solution.py:114
  184.7 2.6 %collective-permute-start.19 = (f32[64,2048]{1,0:T(8,128)}, f32[64,2048]{1,0:T(8,128)S(1)}, u32[]{:S(2)}, u32[]{:S(2)}) collective-permute-start(f32[64,2048]{1,0:T(8,128)} %get-tuple-element.79), channel_id=1, source_target_pairs={{0,12},{1,13},{2,14},{3,15},{4,0},{5,1},{6,2},{7,3},{8,4},{9,5},{1... | collective-permute-start | bytes 1572872 | tf_op jit(solution)/shard_map/ppermute | solution.py:380
  187.4 2.7 %collective-permute-start.21 = (f32[64,2048]{1,0:T(8,128)}, f32[64,2048]{1,0:T(8,128)}, u32[]{:S(2)}, u32[]{:S(2)}) collective-permute-start(f32[64,2048]{1,0:T(8,128)} %get-tuple-element.81), channel_id=1, source_target_pairs={{0,3},{1,0},{2,1},{3,2},{4,7},{5,4},{6,5},{7,6},{8,11},{9,8},{10,9... | collective-permute-start | bytes 1572872 | tf_op jit(solution)/shard_map/ppermute | solution.py:380
  190.1 7.3 %shard_map.80 = (f32[1,64,8192]{2,1,0:T(8,128)}, f32[8,4096]{1,0:T(8,128)}, f32[8,128]{1,0:T(8,128)}) custom-call(s32[2]{0:T(128)} %pad_add_fusion.1.here, bf16[64,131072]{1,0:T(8,128)(2,1)} %bitcast.123, f32[32,16384]{1,0:T(8,128)} %collective-permute-done.refs_4_.refs_5_.refs_6_.refs_7_.refs_21_.refs_2_.refs_3_.refs_12_.refs_13_.refs_1_, ...), custom_call_target="tpu_custom_call" | custom-call | tf_op jit(solution)/shard_map/pallas_call | solution.py:114
  197.4 3.5 %collective-permute-start.31 = (f32[8,4096]{1,0:T(8,128)}, f32[8,4096]{1,0:T(8,128)S(1)}, u32[]{:S(2)}, u32[]{:S(2)}) collective-permute-start(f32[8,4096]{1,0:T(8,128)} %get-tuple-element.90.refs_0_), channel_id=1, source_target_pairs={{0,64},{16,80},{32,96},{48,112},{64,0},{80,16},{96,32},{112,48},{1... | collective-permute-start | bytes 393224 | tf_op jit(solution)/shard_map/ppermute | solution.py:384
  200.9 0.4 collective-permute-start.30
  201.4 1.0 collective-permute-start.29
  202.4 7.4 %shard_map.81 = (f32[1,64,8192]{2,1,0:T(8,128)}, f32[8,4096]{1,0:T(8,128)}, f32[8,128]{1,0:T(8,128)}) custom-call(s32[2]{0:T(128)} %pad_add_fusion.1.here, bf16[64,131072]{1,0:T(8,128)(2,1)} %bitcast.125, ...), custom_call_target="tpu_custom_call", output_to_operand_aliasing={{0}: (19, {})} | custom-call | tf_op jit(solution)/shard_map/pallas_call | solution.py:114
  209.8 1.9 collective-permute-start.28
  211.7 1.3 collective-permute-start.27
  213.1 0.1 collective-permute-start.26
  213.2 0.5 copy-done.8
  213.7 0.1 copy-done.9
  213.9 5.9 %shard_map.82 = (f32[64,4096]{1,0:T(8,128)}, f32[8,128]{1,0:T(8,128)}) custom-call(s32[2]{0:T(128)} %pad_add_fusion.1.here, f32[8,4096]{1,0:T(8,128)} %get-tuple-element.90.refs_0_, f32[8,4096]{1,0:T(8,128)} %copy-done.10, f32[8,4096]{1,0:T(8,128)} %copy-done.9, f32[8,4096]{1,0:T(8,128)} %copy-done.8, s32[1,8,8192]{2,1,0:T(8,128)} %refs_4_.3, ...), custom_call_target="tpu_custom_call" | custom-call | tf_op jit(solution)/shard_map/pallas_call | solution.py:114
  219.8 6.6 %collective-permute-start.33 = (f32[64,4096]{1,0:T(8,128)}, f32[64,4096]{1,0:T(8,128)}, u32[]{:S(2)}, u32[]{:S(2)}) collective-permute-start(f32[64,4096]{1,0:T(8,128)} %get-tuple-element.94.refs_0_), channel_id=1, source_target_pairs={{0,16},{16,0},{32,48},{48,32},{64,80},{80,64},{96,112},{112,96},{1... | collective-permute-start | bytes 3145736 | tf_op jit(solution)/shard_map/ppermute | solution.py:390
  226.4 0.6 copy-done.11
  227.1 5.9 %shard_map.83 = (f32[64,4096]{1,0:T(8,128)}, f32[8,128]{1,0:T(8,128)}) custom-call(s32[2]{0:T(128)} %pad_add_fusion.1.here, f32[8,4096]{1,0:T(8,128)} %get-tuple-element.89.refs_0_, f32[8,4096]{1,0:T(8,128)} %copy-done.13, f32[8,4096]{1,0:T(8,128)} %copy-done.12, f32[8,4096]{1,0:T(8,128)} %copy-done.11, s32[1,8,8192]{2,1,0:T(8,128)} %refs_4_.3, ...), custom_call_target="tpu_custom_call" | custom-call | tf_op jit(solution)/shard_map/pallas_call | solution.py:114
  233.0 3.1 %shard_map.84 = (f32[64,8192]{1,0:T(8,128)}, f32[8,128]{1,0:T(8,128)}) custom-call(s32[2]{0:T(128)} %pad_add_fusion.1.here, f32[64,4096]{1,0:T(8,128)} %get-tuple-element.94.refs_0_, f32[64,4096]{1,0:T(8,128)} %collective-permute-done.33.refs_1_, f32[8,128]{1,0:T(8,128)} %get-tuple-element.95.refs_2_), custom_call_target="tpu_custom_call" | custom-call | tf_op jit(solution)/shard_map/pallas_call | solution.py:114
  236.1 1.0 copy-done.4
  237.1 3.1 %shard_map.85 = (f32[64,8192]{1,0:T(8,128)}, f32[8,128]{1,0:T(8,128)}) custom-call(s32[2]{0:T(128)} %pad_add_fusion.1.here, f32[64,4096]{1,0:T(8,128)} %get-tuple-element.93.refs_0_, f32[64,4096]{1,0:T(8,128)} %copy-done.4, f32[64,8192]{1,0:T(8,128)} %get-tuple-element.96.refs_2_, f32[8,128]{1,0:T(8,128)} %get-tuple-element.97.refs_3_), custom_call_target="tpu_custom_call", output_to_operand_aliasing={{0}: (3, {})} | custom-call | tf_op jit(solution)/shard_map/pallas_call | solution.py:114
  (52 shorter events, 0.5 us)
Async XLA Ops:
  5.5 48.6 %collective-permute-start.2 = (f32[32,16384]{1,0:T(8,128)}, f32[32,16384]{1,0:T(8,128)}, u32[]{:S(2)}, u32[]{:S(2)}) collective-permute-start(f32[32,16384]{1,0:T(8,128)} %get-tuple-element.55), channel_id=1, source_target_pairs={{0,1},{1,2},{2,3},{3,0},{4,5},{5,6},{6,7},{7,4},{8,9},{9,10},{10,1... | collective-permute-start | bytes 6291464 | tf_op jit(solution)/shard_map/ppermute | solution.py:380
  7.6 48.1 %collective-permute-start.3 = (f32[32,16384]{1,0:T(8,128)}, f32[32,16384]{1,0:T(8,128)}, u32[]{:S(2)}, u32[]{:S(2)}) collective-permute-start(f32[32,16384]{1,0:T(8,128)} %get-tuple-element.56), channel_id=1, source_target_pairs={{0,3},{1,0},{2,1},{3,2},{4,7},{5,4},{6,5},{7,6},{8,11},{9,8},{10,9... | collective-permute-start | bytes 6291464 | tf_op jit(solution)/shard_map/ppermute | solution.py:380
  13.2 47.8 %collective-permute-start.4 = (f32[32,16384]{1,0:T(8,128)}, f32[32,16384]{1,0:T(8,128)}, u32[]{:S(2)}, u32[]{:S(2)}) collective-permute-start(f32[32,16384]{1,0:T(8,128)} %get-tuple-element.57), channel_id=1, source_target_pairs={{0,4},{1,5},{2,6},{3,7},{4,8},{5,9},{6,10},{7,11},{8,12},{9,13},{1... | collective-permute-start | bytes 6291464 | tf_op jit(solution)/shard_map/ppermute | solution.py:380
  14.7 47.6 %collective-permute-start.5 = (f32[32,16384]{1,0:T(8,128)}, f32[32,16384]{1,0:T(8,128)}, u32[]{:S(2)}, u32[]{:S(2)}) collective-permute-start(f32[32,16384]{1,0:T(8,128)} %get-tuple-element.58), channel_id=1, source_target_pairs={{0,12},{1,13},{2,14},{3,15},{4,0},{5,1},{6,2},{7,3},{8,4},{9,5},{1... | collective-permute-start | bytes 6291464 | tf_op jit(solution)/shard_map/ppermute | solution.py:380
  20.4 78.6 %collective-permute-start = (f32[32,16384]{1,0:T(8,128)}, f32[32,16384]{1,0:T(8,128)}, u32[]{:S(2)}, u32[]{:S(2)}) collective-permute-start(f32[32,16384]{1,0:T(8,128)} %get-tuple-element.53), channel_id=1, source_target_pairs={{0,1},{1,2},{2,3},{3,0},{4,5},{5,6},{6,7},{7,4},{8,9},{9,10},{10,1... | collective-permute-start | bytes 6291464 | tf_op jit(solution)/shard_map/ppermute | solution.py:380
  54.1 46.5 %collective-permute-start.1 = (f32[32,16384]{1,0:T(8,128)}, f32[32,16384]{1,0:T(8,128)}, u32[]{:S(2)}, u32[]{:S(2)}) collective-permute-start(f32[32,16384]{1,0:T(8,128)} %get-tuple-element.54), channel_id=1, source_target_pairs={{0,3},{1,0},{2,1},{3,2},{4,7},{5,4},{6,5},{7,6},{8,11},{9,8},{10,9... | collective-permute-start | bytes 6291464 | tf_op jit(solution)/shard_map/ppermute | solution.py:380
  55.7 50.3 %collective-permute-start.8 = (f32[32,16384]{1,0:T(8,128)}, f32[32,16384]{1,0:T(8,128)}, u32[]{:S(2)}, u32[]{:S(2)}) collective-permute-start(f32[32,16384]{1,0:T(8,128)} %get-tuple-element.65), channel_id=1, source_target_pairs={{0,4},{1,5},{2,6},{3,7},{4,8},{5,9},{6,10},{7,11},{8,12},{9,13},{1... | collective-permute-start | bytes 6291464 | tf_op jit(solution)/shard_map/ppermute | solution.py:380
  61.0 48.1 %collective-permute-start.9 = (f32[32,16384]{1,0:T(8,128)}, f32[32,16384]{1,0:T(8,128)}, u32[]{:S(2)}, u32[]{:S(2)}) collective-permute-start(f32[32,16384]{1,0:T(8,128)} %get-tuple-element.66), channel_id=1, source_target_pairs={{0,12},{1,13},{2,14},{3,15},{4,0},{5,1},{6,2},{7,3},{8,4},{9,5},{1... | collective-permute-start | bytes 6291464 | tf_op jit(solution)/shard_map/ppermute | solution.py:380
  62.3 12.4 %collective-permute-start.14 = (s32[1,8,8192]{2,1,0:T(8,128)}, s32[1,8,8192]{2,1,0:T(8,128)}, u32[]{:S(2)}, u32[]{:S(2)}) collective-permute-start(s32[1,8,8192]{2,1,0:T(8,128)} %refs_4_.3), channel_id=1, source_target_pairs={{0,32},{16,48},{32,64},{48,80},{64,96},{80,112},{96,0},{112,16},{1... | collective-permute-start | bytes 786440 | tf_op jit(solution)/shard_map/ppermute | solution.py:384
  74.7 69.3 %collective-permute-start.6 = (f32[32,16384]{1,0:T(8,128)}, f32[32,16384]{1,0:T(8,128)}, u32[]{:S(2)}, u32[]{:S(2)}) collective-permute-start(f32[32,16384]{1,0:T(8,128)} %get-tuple-element.62), channel_id=1, source_target_pairs={{0,1},{1,2},{2,3},{3,0},{4,5},{5,6},{6,7},{7,4},{8,9},{9,10},{10,1... | collective-permute-start | bytes 6291464 | tf_op jit(solution)/shard_map/ppermute | solution.py:380
  99.0 44.9 %collective-permute-start.7 = (f32[32,16384]{1,0:T(8,128)}, f32[32,16384]{1,0:T(8,128)}, u32[]{:S(2)}, u32[]{:S(2)}) collective-permute-start(f32[32,16384]{1,0:T(8,128)} %get-tuple-element.63), channel_id=1, source_target_pairs={{0,3},{1,0},{2,1},{3,2},{4,7},{5,4},{6,5},{7,6},{8,11},{9,8},{10,9... | collective-permute-start | bytes 6291464 | tf_op jit(solution)/shard_map/ppermute | solution.py:380
  100.6 50.3 %collective-permute-start.12 = (f32[32,16384]{1,0:T(8,128)}, f32[32,16384]{1,0:T(8,128)}, u32[]{:S(2)}, u32[]{:S(2)}) collective-permute-start(f32[32,16384]{1,0:T(8,128)} %get-tuple-element.69), channel_id=1, source_target_pairs={{0,4},{1,5},{2,6},{3,7},{4,8},{5,9},{6,10},{7,11},{8,12},{9,13},{1... | collective-permute-start | bytes 6291464 | tf_op jit(solution)/shard_map/ppermute | solution.py:380
  106.0 44.9 %collective-permute-start.13 = (f32[32,16384]{1,0:T(8,128)}, f32[32,16384]{1,0:T(8,128)}, u32[]{:S(2)}, u32[]{:S(2)}) collective-permute-start(f32[32,16384]{1,0:T(8,128)} %get-tuple-element.70), channel_id=1, source_target_pairs={{0,12},{1,13},{2,14},{3,15},{4,0},{5,1},{6,2},{7,3},{8,4},{9,5},{1... | collective-permute-start | bytes 6291464 | tf_op jit(solution)/shard_map/ppermute | solution.py:380
  109.1 41.6 %collective-permute-start.15 = (s32[1,16,8192]{2,1,0:T(8,128)}, s32[1,16,8192]{2,1,0:T(8,128)S(1)}, u32[]{:S(2)}, u32[]{:S(2)}) collective-permute-start(s32[1,16,8192]{2,1,0:T(8,128)} %pad_add_fusion), channel_id=1, source_target_pairs={{0,64},{16,80},{32,96},{48,112},{64,0},{80,16},{96,32},{112,48},{1... | collective-permute-start | bytes 1572872 | tf_op jit(solution)/shard_map/ppermute | solution.py:384
  147.5 12.9 %collective-permute-start.10 = (f32[32,4096]{1,0:T(8,128)}, f32[32,4096]{1,0:T(8,128)S(1)}, u32[]{:S(2)}, u32[]{:S(2)}) collective-permute-start(f32[32,4096]{1,0:T(8,128)} %get-tuple-element.67), channel_id=1, source_target_pairs={{0,4},{1,5},{2,6},{3,7},{4,8},{5,9},{6,10},{7,11},{8,12},{9,13},{1... | collective-permute-start | bytes 1572872 | tf_op jit(solution)/shard_map/ppermute | solution.py:380
  149.1 13.4 %collective-permute-start.11 = (f32[32,4096]{1,0:T(8,128)}, f32[32,4096]{1,0:T(8,128)S(1)}, u32[]{:S(2)}, u32[]{:S(2)}) collective-permute-start(f32[32,4096]{1,0:T(8,128)} %get-tuple-element.68), channel_id=1, source_target_pairs={{0,12},{1,13},{2,14},{3,15},{4,0},{5,1},{6,2},{7,3},{8,4},{9,5},{1... | collective-permute-start | bytes 1572872 | tf_op jit(solution)/shard_map/ppermute | solution.py:380
  150.7 0.8 copy-start.3
  155.0 14.8 %collective-permute-start.16 = (f32[32,4096]{1,0:T(8,128)}, f32[32,4096]{1,0:T(8,128)S(1)}, u32[]{:S(2)}, u32[]{:S(2)}) collective-permute-start(f32[32,4096]{1,0:T(8,128)} %get-tuple-element.72), channel_id=1, source_target_pairs={{0,1},{1,2},{2,3},{3,0},{4,5},{5,6},{6,7},{7,4},{8,9},{9,10},{10,1... | collective-permute-start | bytes 1572872 | tf_op jit(solution)/shard_map/ppermute | solution.py:380
  155.1 14.7 %collective-permute-start.17 = (f32[32,4096]{1,0:T(8,128)}, f32[32,4096]{1,0:T(8,128)}, u32[]{:S(2)}, u32[]{:S(2)}) collective-permute-start(f32[32,4096]{1,0:T(8,128)} %get-tuple-element.73), channel_id=1, source_target_pairs={{0,3},{1,0},{2,1},{3,2},{4,7},{5,4},{6,5},{7,6},{8,11},{9,8},{10,9... | collective-permute-start | bytes 1572872 | tf_op jit(solution)/shard_map/ppermute | solution.py:380
  160.3 2.2 copy-start
  162.6 0.8 copy-start.1
  167.1 17.7 %collective-permute-start.22 = (f32[64,2048]{1,0:T(8,128)}, f32[64,2048]{1,0:T(8,128)S(1)}, u32[]{:S(2)}, u32[]{:S(2)}) collective-permute-start(f32[64,2048]{1,0:T(8,128)} %get-tuple-element.82), channel_id=1, source_target_pairs={{0,4},{1,5},{2,6},{3,7},{4,8},{5,9},{6,10},{7,11},{8,12},{9,13},{1... | collective-permute-start | bytes 1572872 | tf_op jit(solution)/shard_map/ppermute | solution.py:380
  167.1 20.3 %collective-permute-start.23 = (f32[64,2048]{1,0:T(8,128)}, f32[64,2048]{1,0:T(8,128)}, u32[]{:S(2)}, u32[]{:S(2)}) collective-permute-start(f32[64,2048]{1,0:T(8,128)} %get-tuple-element.83), channel_id=1, source_target_pairs={{0,12},{1,13},{2,14},{3,15},{4,0},{5,1},{6,2},{7,3},{8,4},{9,5},{1... | collective-permute-start | bytes 1572872 | tf_op jit(solution)/shard_map/ppermute | solution.py:380
  169.8 0.8 copy-start.2
  174.3 13.1 %collective-permute-start.24 = (f32[64,2048]{1,0:T(8,128)}, f32[64,2048]{1,0:T(8,128)}, u32[]{:S(2)}, u32[]{:S(2)}) collective-permute-start(f32[64,2048]{1,0:T(8,128)} %get-tuple-element.84), channel_id=1, source_target_pairs={{0,1},{1,2},{2,3},{3,0},{4,5},{5,6},{6,7},{7,4},{8,9},{9,10},{10,1... | collective-permute-start | bytes 1572872 | tf_op jit(solution)/shard_map/ppermute | solution.py:380
  174.6 15.5 %collective-permute-start.25 = (f32[64,2048]{1,0:T(8,128)}, f32[64,2048]{1,0:T(8,128)}, u32[]{:S(2)}, u32[]{:S(2)}) collective-permute-start(f32[64,2048]{1,0:T(8,128)} %get-tuple-element.85), channel_id=1, source_target_pairs={{0,3},{1,0},{2,1},{3,2},{4,7},{5,4},{6,5},{7,6},{8,11},{9,8},{10,9... | collective-permute-start | bytes 1572872 | tf_op jit(solution)/shard_map/ppermute | solution.py:380
  184.6 16.3 %collective-permute-start.18 = (f32[64,2048]{1,0:T(8,128)}, f32[64,2048]{1,0:T(8,128)S(1)}, u32[]{:S(2)}, u32[]{:S(2)}) collective-permute-start(f32[64,2048]{1,0:T(8,128)} %get-tuple-element.78), channel_id=1, source_target_pairs={{0,4},{1,5},{2,6},{3,7},{4,8},{5,9},{6,10},{7,11},{8,12},{9,13},{1... | collective-permute-start | bytes 1572872 | tf_op jit(solution)/shard_map/ppermute | solution.py:380
  184.7 5.3 %copy-start.6 = (f32[64,2048]{1,0:T(8,128)}, f32[64,2048]{1,0:T(8,128)S(1)}, u32[]{:S(2)}) copy-start(f32[64,2048]{1,0:T(8,128)S(1)} %collective-permute-done.22.refs_5_) | copy-start | bytes 1572868
  184.7 16.6 %collective-permute-start.19 = (f32[64,2048]{1,0:T(8,128)}, f32[64,2048]{1,0:T(8,128)S(1)}, u32[]{:S(2)}, u32[]{:S(2)}) collective-permute-start(f32[64,2048]{1,0:T(8,128)} %get-tuple-element.79), channel_id=1, source_target_pairs={{0,12},{1,13},{2,14},{3,15},{4,0},{5,1},{6,2},{7,3},{8,4},{9,5},{1... | collective-permute-start | bytes 1572872 | tf_op jit(solution)/shard_map/ppermute | solution.py:380
  187.4 15.0 %collective-permute-start.20 = (f32[64,2048]{1,0:T(8,128)}, f32[64,2048]{1,0:T(8,128)}, u32[]{:S(2)}, u32[]{:S(2)}) collective-permute-start(f32[64,2048]{1,0:T(8,128)} %get-tuple-element.80), channel_id=1, source_target_pairs={{0,1},{1,2},{2,3},{3,0},{4,5},{5,6},{6,7},{7,4},{8,9},{9,10},{10,1... | collective-permute-start | bytes 1572872 | tf_op jit(solution)/shard_map/ppermute | solution.py:380
  187.4 15.0 %collective-permute-start.21 = (f32[64,2048]{1,0:T(8,128)}, f32[64,2048]{1,0:T(8,128)}, u32[]{:S(2)}, u32[]{:S(2)}) collective-permute-start(f32[64,2048]{1,0:T(8,128)} %get-tuple-element.81), channel_id=1, source_target_pairs={{0,3},{1,0},{2,1},{3,2},{4,7},{5,4},{6,5},{7,6},{8,11},{9,8},{10,9... | collective-permute-start | bytes 1572872 | tf_op jit(solution)/shard_map/ppermute | solution.py:380
  197.4 15.6 %collective-permute-start.31 = (f32[8,4096]{1,0:T(8,128)}, f32[8,4096]{1,0:T(8,128)S(1)}, u32[]{:S(2)}, u32[]{:S(2)}) collective-permute-start(f32[8,4096]{1,0:T(8,128)} %get-tuple-element.90.refs_0_), channel_id=1, source_target_pairs={{0,64},{16,80},{32,96},{48,112},{64,0},{80,16},{96,32},{112,48},{1... | collective-permute-start | bytes 393224 | tf_op jit(solution)/shard_map/ppermute | solution.py:384
  200.9 1.5 copy-start.5
  200.9 12.2 %collective-permute-start.30 = (f32[8,4096]{1,0:T(8,128)}, f32[8,4096]{1,0:T(8,128)S(1)}, u32[]{:S(2)}, u32[]{:S(2)}) collective-permute-start(f32[8,4096]{1,0:T(8,128)} %get-tuple-element.90.refs_0_), channel_id=1, source_target_pairs={{0,96},{16,112},{32,0},{48,16},{64,32},{80,48},{96,64},{112,80},{1... | collective-permute-start | bytes 393224 | tf_op jit(solution)/shard_map/ppermute | solution.py:384
  201.4 1.1 copy-start.7
  201.4 11.8 %collective-permute-start.29 = (f32[8,4096]{1,0:T(8,128)}, f32[8,4096]{1,0:T(8,128)S(1)}, u32[]{:S(2)}, u32[]{:S(2)}) collective-permute-start(f32[8,4096]{1,0:T(8,128)} %get-tuple-element.90.refs_0_), channel_id=1, source_target_pairs={{0,32},{16,48},{32,64},{48,80},{64,96},{80,112},{96,0},{112,16},{1... | collective-permute-start | bytes 393224 | tf_op jit(solution)/shard_map/ppermute | solution.py:384
  209.8 16.6 %collective-permute-start.28 = (f32[8,4096]{1,0:T(8,128)}, f32[8,4096]{1,0:T(8,128)S(1)}, u32[]{:S(2)}, u32[]{:S(2)}) collective-permute-start(f32[8,4096]{1,0:T(8,128)} %get-tuple-element.89.refs_0_), channel_id=1, source_target_pairs={{0,64},{16,80},{32,96},{48,112},{64,0},{80,16},{96,32},{112,48},{1... | collective-permute-start | bytes 393224 | tf_op jit(solution)/shard_map/ppermute | solution.py:384
  211.7 14.7 %collective-permute-start.27 = (f32[8,4096]{1,0:T(8,128)}, f32[8,4096]{1,0:T(8,128)S(1)}, u32[]{:S(2)}, u32[]{:S(2)}) collective-permute-start(f32[8,4096]{1,0:T(8,128)} %get-tuple-element.89.refs_0_), channel_id=1, source_target_pairs={{0,96},{16,112},{32,0},{48,16},{64,32},{80,48},{96,64},{112,80},{1... | collective-permute-start | bytes 393224 | tf_op jit(solution)/shard_map/ppermute | solution.py:384
  213.1 0.7 copy-start.8
  213.1 13.3 %collective-permute-start.26 = (f32[8,4096]{1,0:T(8,128)}, f32[8,4096]{1,0:T(8,128)S(1)}, u32[]{:S(2)}, u32[]{:S(2)}) collective-permute-start(f32[8,4096]{1,0:T(8,128)} %get-tuple-element.89.refs_0_), channel_id=1, source_target_pairs={{0,32},{16,48},{32,64},{48,80},{64,96},{80,112},{96,0},{112,16},{1... | collective-permute-start | bytes 393224 | tf_op jit(solution)/shard_map/ppermute | solution.py:384
  213.2 0.6 copy-start.9
  213.2 0.7 copy-start.10
  219.8 13.2 %collective-permute-start.33 = (f32[64,4096]{1,0:T(8,128)}, f32[64,4096]{1,0:T(8,128)}, u32[]{:S(2)}, u32[]{:S(2)}) collective-permute-start(f32[64,4096]{1,0:T(8,128)} %get-tuple-element.94.refs_0_), channel_id=1, source_target_pairs={{0,16},{16,0},{32,48},{48,32},{64,80},{80,64},{96,112},{112,96},{1... | collective-permute-start | bytes 3145736 | tf_op jit(solution)/shard_map/ppermute | solution.py:390
  226.4 0.7 copy-start.11
  226.4 0.7 copy-start.12
  226.4 0.7 copy-start.13
  233.0 3.1 %collective-permute-start.32 = (f32[64,4096]{1,0:T(8,128)}, f32[64,4096]{1,0:T(8,128)S(1)}, u32[]{:S(2)}, u32[]{:S(2)}) collective-permute-start(f32[64,4096]{1,0:T(8,128)} %get-tuple-element.93.refs_0_), channel_id=1, source_target_pairs={{0,16},{16,0},{32,48},{48,32},{64,80},{80,64},{96,112},{112,96},{1... | collective-permute-start | bytes 3145736 | tf_op jit(solution)/shard_map/ppermute | solution.py:390
  236.1 1.0 copy-start.4

commit v10 on v9

--- a/solution.py
+++ b/solution.py
@@ -20,7 +20,7 @@
 PLACES_WITH = ((1, 0), (1, 0))
 TAIL = ('f0', 'f1', 's0', 's1', 'j0', 'j1')
 TOGETHER = 2
-VMEM_LIMIT = 62 * 1024 * 1024
+VMEM_LIMIT = 48 * 1024 * 1024
 F32 = jnp.float32
 BF16 = jnp.bfloat16
 

time: 242 us -> 227 us (0.938)
  Pallas kernels: 82.1 us -> 66.4 us
  waiting for transfers between devices: 98 us -> 103 us
  local copies, waits for them, and re-layouts: 4.6 us -> 2 us
    pallas_call x18, Pallas kernels: 82.1 us -> 66.4 us  [call(): pl.pallas_call(run, grid_spec=pltpu.PrefetchScalarGridSpec(num_scalar_pre...]
    ppermute x24, waiting for transfers between devices: 98 us -> 103 us  [along(): lax.ppermute(value, 'fsdp', shift(0, step) if x_first else shift(step, 0))]
    unnamed x28 -> x8, local copies, waits for them, and re-layouts: 4.6 us -> 2 us
  transfers between devices with their start and end apart: 34 -> 34, of which waited for: 8 -> 9; matrix products, arithmetic and copies ran while one was open for 1% -> 0% of each run, Pallas kernels for 31% -> 27%
where the time goes in v10:
time: 227 us; the launch traced here: 226 us
  waiting for transfers between devices  103 us (45%)
  Pallas kernels  66.4 us (29%)
  starting transfers between devices  52.6 us (23%)
    ppermute x24, waiting for transfers between devices, along(): lax.ppermute(value, 'fsdp', shift(0, step) if x_first else shift(step, 0))  103 us
    pallas_call x18, Pallas kernels, call(): pl.pallas_call(run, grid_spec=pltpu.PrefetchScalarGridSpec(num_scalar_pre...  66.4 us
    ppermute x24, starting transfers between devices, along(): lax.ppermute(value, 'fsdp', shift(0, step) if x_first else shift(step, 0))  31.2 us
    ppermute x8, starting transfers between devices, along_z(): lax.ppermute(value, 'rep', [(z * 2 + c, (z + step) % SIDE * 2 + c) for z...  13.5 us
    ppermute x2, starting transfers between devices, other_core(): return lax.ppermute(value, 'rep', [(r, r ^ 1) for r in range(2 * SIDE)])  7.91 us
  transfers between devices with their start and end apart: 34, of which 9 were waited for; matrix products, arithmetic and copies ran while one was open for 0% of the time, Pallas kernels for 27%

profile of v10, /device:TPU:1, one launch (start us, length us, event | category | flops | bytes accessed | tf_op | source)
XLA Modules:
  0.0 226.2 jit_solution(14916020438925142861)
XLA Ops:
  0.6 0.1 pad_add_fusion.1.here
  0.7 4.1 %shard_map.68 = (f32[32,16384]{1,0:T(8,128)}, f32[32,16384]{1,0:T(8,128)}, f32[8,128]{1,0:T(8,128)S(1)}) custom-call(s32[2]{0:T(128)S(1)} %pad_add_fusion.1.here, bf16[64,131072]{1,0:T(8,128)(2,1)} %bitcast.3, bf16[64,131072]{1,0:T(8,128)(2,1)} %bitcast.4, bf16[64,131072]{1,0:T(8,128)(2,1)} %bitcast.5, bf16[64,131072]{1,0:T(8,128)(2,1)} %bitcast.6, ...), custom_call_target="tpu_custom_call" | custom-call | tf_op jit(solution)/shard_map/pallas_call | solution.py:114
  4.8 2.1 collective-permute-start.2
  6.9 1.4 collective-permute-start.3
  8.3 4.1 %shard_map.69 = (f32[32,16384]{1,0:T(8,128)}, f32[32,16384]{1,0:T(8,128)}, f32[8,128]{1,0:T(8,128)S(1)}) custom-call(s32[2]{0:T(128)S(1)} %pad_add_fusion.1.here, bf16[64,131072]{1,0:T(8,128)(2,1)} %bitcast.26, bf16[64,131072]{1,0:T(8,128)(2,1)} %bitcast.20, bf16[64,131072]{1,0:T(8,128)(2,1)} %bitcast.21, bf16[64,131072]{1,0:T(8,128)(2,1)} %bitcast.22, ...), custom_call_target="tpu_custom_call" | custom-call | tf_op jit(solution)/shard_map/pallas_call | solution.py:114
  12.3 1.5 collective-permute-start.4
  13.8 1.5 collective-permute-start.5
  15.3 4.1 %shard_map.70 = (f32[32,16384]{1,0:T(8,128)}, f32[32,16384]{1,0:T(8,128)}, f32[8,128]{1,0:T(8,128)S(1)}) custom-call(s32[2]{0:T(128)S(1)} %pad_add_fusion.1.here, bf16[64,131072]{1,0:T(8,128)(2,1)} %bitcast.35, bf16[64,131072]{1,0:T(8,128)(2,1)} %bitcast.36, bf16[64,131072]{1,0:T(8,128)(2,1)} %bitcast.37, bf16[64,131072]{1,0:T(8,128)(2,1)} %bitcast.38, ...), custom_call_target="tpu_custom_call" | custom-call | tf_op jit(solution)/shard_map/pallas_call | solution.py:114
  19.4 0.1 collective-permute-start
  19.5 4.1 %shard_map.71 = (f32[32,16384]{1,0:T(8,128)}, f32[32,16384]{1,0:T(8,128)}, f32[8,128]{1,0:T(8,128)S(1)}) custom-call(s32[2]{0:T(128)S(1)} %pad_add_fusion.1.here, bf16[64,131072]{1,0:T(8,128)(2,1)} %bitcast.64, bf16[64,131072]{1,0:T(8,128)(2,1)} %bitcast.52, bf16[64,131072]{1,0:T(8,128)(2,1)} %bitcast.53, bf16[64,131072]{1,0:T(8,128)(2,1)} %bitcast.54, ...), custom_call_target="tpu_custom_call" | custom-call | tf_op jit(solution)/shard_map/pallas_call | solution.py:114
  23.6 29.9 %collective-permute-done.2.refs_16_.refs_19_ = f32[32,16384]{1,0:T(8,128)} collective-permute-done((f32[32,16384]{1,0:T(8,128)}, f32[32,16384]{1,0:T(8,128)}, u32[]{:S(2)}, u32[]{:S(2)}) %collective-permute-start.2) | collective-permute-done | bytes 2097184 | tf_op jit(solution)/shard_map/ppermute | solution.py:380
  53.4 1.6 collective-permute-start.1
  55.0 1.3 collective-permute-start.8
  56.3 3.8 %collective-permute-done.4.refs_16_.refs_19_ = f32[32,16384]{1,0:T(8,128)} collective-permute-done((f32[32,16384]{1,0:T(8,128)}, f32[32,16384]{1,0:T(8,128)}, u32[]{:S(2)}, u32[]{:S(2)}) %collective-permute-start.4) | collective-permute-done | bytes 2097184 | tf_op jit(solution)/shard_map/ppermute | solution.py:380
  60.1 1.3 collective-permute-start.9
  61.5 1.6 collective-permute-start.14
  63.1 4.2 %shard_map.72 = (f32[32,16384]{1,0:T(8,128)S(1)}, f32[32,16384]{1,0:T(8,128)S(1)}, f32[8,128]{1,0:T(8,128)S(1)}) custom-call(s32[2]{0:T(128)S(1)} %pad_add_fusion.1.here, bf16[64,131072]{1,0:T(8,128)(2,1)} %bitcast.67, bf16[64,131072]{1,0:T(8,128)(2,1)} %bitcast.68, bf16[64,131072]{1,0:T(8,128)(2,1)} %bitcast.69, bf16[64,131072]{1,0:T(8,128)(2,1)} %bitcast.70, ...), custom_call_target="tpu_custom_call" | custom-call | tf_op jit(solution)/shard_map/pallas_call | solution.py:114
  67.3 4.2 %shard_map.73 = (f32[32,16384]{1,0:T(8,128)S(1)}, f32[32,16384]{1,0:T(8,128)S(1)}, f32[8,128]{1,0:T(8,128)S(1)}) custom-call(s32[2]{0:T(128)S(1)} %pad_add_fusion.1.here, bf16[64,131072]{1,0:T(8,128)(2,1)} %bitcast.89, bf16[64,131072]{1,0:T(8,128)(2,1)} %bitcast.84, bf16[64,131072]{1,0:T(8,128)(2,1)} %bitcast.85, bf16[64,131072]{1,0:T(8,128)(2,1)} %bitcast.86, ...), custom_call_target="tpu_custom_call" | custom-call | tf_op jit(solution)/shard_map/pallas_call | solution.py:114
  71.6 0.1 collective-permute-start.6
  71.6 26.7 %collective-permute-done.refs_4_.refs_5_.refs_6_.refs_7_.refs_21_.refs_2_.refs_3_.refs_12_.refs_13_.refs_1_ = f32[32,16384]{1,0:T(8,128)} collective-permute-done((f32[32,16384]{1,0:T(8,128)}, f32[32,16384]{1,0:T(8,128)}, u32[]{:S(2)}, u32[]{:S(2)}) %collective-permute-start) | collective-permute-done | bytes 2097184 | tf_op jit(solution)/shard_map/ppermute | solution.py:380
  98.4 1.6 collective-permute-start.7
  99.9 1.3 collective-permute-start.12
  101.2 3.8 %collective-permute-done.8.refs_21_.refs_4_.refs_5_.refs_6_.refs_7_.refs_2_.refs_3_.refs_12_.refs_13_.refs_8_ = f32[32,16384]{1,0:T(8,128)} collective-permute-done((f32[32,16384]{1,0:T(8,128)}, f32[32,16384]{1,0:T(8,128)}, u32[]{:S(2)}, u32[]{:S(2)}) %collective-permute-start.8) | collective-permute-done | bytes 2097184 | tf_op jit(solution)/shard_map/ppermute | solution.py:380
  105.1 1.3 collective-permute-start.13
  106.4 1.1 pad_add_fusion
  107.5 3.7 %collective-permute-start.15 = (s32[1,16,8192]{2,1,0:T(8,128)S(1)}, s32[1,16,8192]{2,1,0:T(8,128)S(1)}, u32[]{:S(2)}, u32[]{:S(2)}) collective-permute-start(s32[1,16,8192]{2,1,0:T(8,128)S(1)} %pad_add_fusion), channel_id=1, source_target_pairs={{0,64},{16,80},{32,96},{48,112},{64,0},{80,16},{96,32},{112,48},{1... | collective-permute-start | bytes 1572872 | tf_op jit(solution)/shard_map/ppermute | solution.py:384
  111.1 32.2 %collective-permute-done.6.refs_12_.refs_13_.refs_14_.refs_15_.refs_6_.refs_7_.refs_16_.refs_17_.refs_25_.refs_3_ = f32[32,16384]{1,0:T(8,128)S(1)} collective-permute-done((f32[32,16384]{1,0:T(8,128)S(1)}, f32[32,16384]{1,0:T(8,128)S(1)}, u32[]{:S(2)}, u32[]{:S(2)}) %collective-permute-start.6) | collective-permute-done | bytes 2097184 | tf_op jit(solution)/shard_map/ppermute | solution.py:380
  143.3 1.3 copy-done.2
  144.6 0.7 copy-done.3
  145.3 2.5 %shard_map.74 = (f32[32,4096]{1,0:T(8,128)S(1)}, f32[32,4096]{1,0:T(8,128)S(1)}, f32[8,128]{1,0:T(8,128)S(1)}) custom-call(s32[2]{0:T(128)S(1)} %pad_add_fusion.1.here, bf16[64,131072]{1,0:T(8,128)(2,1)} %bitcast.99, bf16[64,131072]{1,0:T(8,128)(2,1)} %bitcast.100, bf16[64,131072]{1,0:T(8,128)(2,1)} %bitcast.101, bf16[64,131072]{1,0:T(8,128)(2,1)} %bitcast.102, ...), custom_call_target="tpu_custom_call" | custom-call | tf_op jit(solution)/shard_map/pallas_call | solution.py:114
  147.7 1.6 collective-permute-start.10
  149.3 1.6 collective-permute-start.11
  151.0 2.5 %shard_map.75 = (f32[32,4096]{1,0:T(8,128)S(1)}, f32[32,4096]{1,0:T(8,128)S(1)}, f32[8,128]{1,0:T(8,128)S(1)}) custom-call(s32[2]{0:T(128)S(1)} %pad_add_fusion.1.here, bf16[64,131072]{1,0:T(8,128)(2,1)} %bitcast.105, bf16[64,131072]{1,0:T(8,128)(2,1)} %bitcast.104, bf16[64,131072]{1,0:T(8,128)(2,1)} %bitcast.103, bf16[64,131072]{1,0:T(8,128)(2,1)} %bitcast.106, ...), custom_call_target="tpu_custom_call" | custom-call | tf_op jit(solution)/shard_map/pallas_call | solution.py:114
  153.4 0.1 collective-permute-start.16
  153.5 2.7 %collective-permute-start.17 = (f32[32,4096]{1,0:T(8,128)S(1)}, f32[32,4096]{1,0:T(8,128)S(1)}, u32[]{:S(2)}, u32[]{:S(2)}) collective-permute-start(f32[32,4096]{1,0:T(8,128)S(1)} %get-tuple-element.73), channel_id=1, source_target_pairs={{0,3},{1,0},{2,1},{3,2},{4,7},{5,4},{6,5},{7,6},{8,11},{9,8},{10,9... | collective-permute-start | bytes 1572872 | tf_op jit(solution)/shard_map/ppermute | solution.py:380
  156.2 4.3 %collective-permute-done.10.refs_20_.refs_21_.refs_25_ = f32[32,4096]{1,0:T(8,128)S(1)} collective-permute-done((f32[32,4096]{1,0:T(8,128)S(1)}, f32[32,4096]{1,0:T(8,128)S(1)}, u32[]{:S(2)}, u32[]{:S(2)}) %collective-permute-start.10) | collective-permute-done | bytes 524320 | tf_op jit(solution)/shard_map/ppermute | solution.py:380
  160.5 1.1 collective-permute-done.11.refs_22_.refs_23_.refs_26_
  161.6 2.5 %shard_map.76 = (f32[64,2048]{1,0:T(8,128)S(1)}, f32[64,2048]{1,0:T(8,128)S(1)}, f32[8,128]{1,0:T(8,128)S(1)}) custom-call(s32[2]{0:T(128)S(1)} %pad_add_fusion.1.here, bf16[64,131072]{1,0:T(8,128)(2,1)} %bitcast.107, bf16[64,131072]{1,0:T(8,128)(2,1)} %bitcast.108, ...), custom_call_target="tpu_custom_call" | custom-call | tf_op jit(solution)/shard_map/pallas_call | solution.py:114
  164.0 0.1 collective-permute-start.22
  164.1 2.8 %collective-permute-start.23 = (f32[64,2048]{1,0:T(8,128)S(1)}, f32[64,2048]{1,0:T(8,128)S(1)}, u32[]{:S(2)}, u32[]{:S(2)}) collective-permute-start(f32[64,2048]{1,0:T(8,128)S(1)} %get-tuple-element.83), channel_id=1, source_target_pairs={{0,12},{1,13},{2,14},{3,15},{4,0},{5,1},{6,2},{7,3},{8,4},{9,5},{1... | collective-permute-start | bytes 1572872 | tf_op jit(solution)/shard_map/ppermute | solution.py:380
  167.0 2.5 %shard_map.77 = (f32[64,2048]{1,0:T(8,128)S(1)}, f32[64,2048]{1,0:T(8,128)S(1)}, f32[8,128]{1,0:T(8,128)S(1)}) custom-call(s32[2]{0:T(128)S(1)} %pad_add_fusion.1.here, bf16[64,131072]{1,0:T(8,128)(2,1)} %bitcast.111, bf16[64,131072]{1,0:T(8,128)(2,1)} %bitcast.112, ...), custom_call_target="tpu_custom_call" | custom-call | tf_op jit(solution)/shard_map/pallas_call | solution.py:114
  169.4 0.1 collective-permute-start.24
  169.5 2.7 %collective-permute-start.25 = (f32[64,2048]{1,0:T(8,128)S(1)}, f32[64,2048]{1,0:T(8,128)S(1)}, u32[]{:S(2)}, u32[]{:S(2)}) collective-permute-start(f32[64,2048]{1,0:T(8,128)S(1)} %get-tuple-element.85), channel_id=1, source_target_pairs={{0,3},{1,0},{2,1},{3,2},{4,7},{5,4},{6,5},{7,6},{8,11},{9,8},{10,9... | collective-permute-start | bytes 1572872 | tf_op jit(solution)/shard_map/ppermute | solution.py:380
  172.2 2.5 %shard_map.78 = (f32[64,2048]{1,0:T(8,128)S(1)}, f32[64,2048]{1,0:T(8,128)S(1)}, f32[8,128]{1,0:T(8,128)S(1)}) custom-call(s32[2]{0:T(128)S(1)} %pad_add_fusion.1.here, bf16[64,131072]{1,0:T(8,128)(2,1)} %bitcast.115, bf16[64,131072]{1,0:T(8,128)(2,1)} %bitcast.116, ...), custom_call_target="tpu_custom_call" | custom-call | tf_op jit(solution)/shard_map/pallas_call | solution.py:114
  174.7 0.0 copy-start.1
  174.7 2.5 %shard_map.79 = (f32[64,2048]{1,0:T(8,128)S(1)}, f32[64,2048]{1,0:T(8,128)S(1)}, f32[8,128]{1,0:T(8,128)S(1)}) custom-call(s32[2]{0:T(128)S(1)} %pad_add_fusion.1.here, bf16[64,131072]{1,0:T(8,128)(2,1)} %bitcast.119, bf16[64,131072]{1,0:T(8,128)(2,1)} %bitcast.120, ...), custom_call_target="tpu_custom_call" | custom-call | tf_op jit(solution)/shard_map/pallas_call | solution.py:114
  177.2 0.1 collective-permute-start.18
  177.3 2.7 %collective-permute-start.19 = (f32[64,2048]{1,0:T(8,128)S(1)}, f32[64,2048]{1,0:T(8,128)S(1)}, u32[]{:S(2)}, u32[]{:S(2)}) collective-permute-start(f32[64,2048]{1,0:T(8,128)S(1)} %get-tuple-element.79), channel_id=1, source_target_pairs={{0,12},{1,13},{2,14},{3,15},{4,0},{5,1},{6,2},{7,3},{8,4},{9,5},{1... | collective-permute-start | bytes 1572872 | tf_op jit(solution)/shard_map/ppermute | solution.py:380
  179.9 0.8 collective-permute-done.24.refs_12_
  180.7 1.9 collective-permute-start.21
  182.6 6.8 %shard_map.80 = (f32[1,64,8192]{2,1,0:T(8,128)}, f32[8,4096]{1,0:T(8,128)S(1)}, f32[8,128]{1,0:T(8,128)S(1)}) custom-call(s32[2]{0:T(128)S(1)} %pad_add_fusion.1.here, bf16[64,131072]{1,0:T(8,128)(2,1)} %bitcast.123, f32[32,16384]{1,0:T(8,128)} %collective-permute-done.refs_4_.refs_5_.refs_6_.refs_7_.refs_21_.refs_2_.refs_3_.refs_12_.refs_13_.refs_1_, ...), custom_call_target="tpu_custom_call" | custom-call | tf_op jit(solution)/shard_map/pallas_call | solution.py:114
  189.5 3.5 %collective-permute-start.31 = (f32[8,4096]{1,0:T(8,128)S(1)}, f32[8,4096]{1,0:T(8,128)S(1)}, u32[]{:S(2)}, u32[]{:S(2)}) collective-permute-start(f32[8,4096]{1,0:T(8,128)S(1)} %get-tuple-element.90.refs_0_), channel_id=1, source_target_pairs={{0,64},{16,80},{32,96},{48,112},{64,0},{80,16},{96,32},{112,48},{1... | collective-permute-start | bytes 393224 | tf_op jit(solution)/shard_map/ppermute | solution.py:384
  193.0 0.4 collective-permute-start.30
  193.4 1.0 collective-permute-start.29
  194.5 6.8 %shard_map.81 = (f32[1,64,8192]{2,1,0:T(8,128)}, f32[8,4096]{1,0:T(8,128)S(1)}, f32[8,128]{1,0:T(8,128)S(1)}) custom-call(s32[2]{0:T(128)S(1)} %pad_add_fusion.1.here, bf16[64,131072]{1,0:T(8,128)(2,1)} %bitcast.125, ...), custom_call_target="tpu_custom_call", output_to_operand_aliasing={{0}: (19, {})} | custom-call | tf_op jit(solution)/shard_map/pallas_call | solution.py:114
  201.3 1.2 collective-permute-start.28
  202.5 2.0 collective-permute-start.27
  204.5 4.8 %shard_map.82 = (f32[64,4096]{1,0:T(8,128)S(1)}, f32[8,128]{1,0:T(8,128)S(1)}) custom-call(s32[2]{0:T(128)S(1)} %pad_add_fusion.1.here, f32[8,4096]{1,0:T(8,128)S(1)} %get-tuple-element.90.refs_0_, f32[8,4096]{1,0:T(8,128)S(1)} %collective-permute-done.29.refs_1_, f32[8,4096]{1,0:T(8,128)S(1)} %collective-permute-done.30.refs_2_, ...), custom_call_target="tpu_custom_call" | custom-call | tf_op jit(solution)/shard_map/pallas_call | solution.py:114
  209.4 6.6 %collective-permute-start.33 = (f32[64,4096]{1,0:T(8,128)S(1)}, f32[64,4096]{1,0:T(8,128)S(1)}, u32[]{:S(2)}, u32[]{:S(2)}) collective-permute-start(f32[64,4096]{1,0:T(8,128)S(1)} %get-tuple-element.94.refs_0_), channel_id=1, source_target_pairs={{0,16},{16,0},{32,48},{48,32},{64,80},{80,64},{96,112},{112,96},{1... | collective-permute-start | bytes 3145736 | tf_op jit(solution)/shard_map/ppermute | solution.py:390
  216.0 4.8 %shard_map.83 = (f32[64,4096]{1,0:T(8,128)S(1)}, f32[8,128]{1,0:T(8,128)S(1)}) custom-call(s32[2]{0:T(128)S(1)} %pad_add_fusion.1.here, f32[8,4096]{1,0:T(8,128)S(1)} %get-tuple-element.89.refs_0_, f32[8,4096]{1,0:T(8,128)S(1)} %collective-permute-done.26.refs_1_, f32[8,4096]{1,0:T(8,128)S(1)} %collective-permute-done.27.refs_2_, ...), custom_call_target="tpu_custom_call" | custom-call | tf_op jit(solution)/shard_map/pallas_call | solution.py:114
  220.8 1.3 collective-permute-start.32
  222.2 1.7 shard_map.84
  223.9 0.5 collective-permute-done.32.refs_1_
  224.4 1.7 shard_map.85
  (32 shorter events, 0.1 us)
Async XLA Ops:
  4.8 48.6 %collective-permute-start.2 = (f32[32,16384]{1,0:T(8,128)}, f32[32,16384]{1,0:T(8,128)}, u32[]{:S(2)}, u32[]{:S(2)}) collective-permute-start(f32[32,16384]{1,0:T(8,128)} %get-tuple-element.55), channel_id=1, source_target_pairs={{0,1},{1,2},{2,3},{3,0},{4,5},{5,6},{6,7},{7,4},{8,9},{9,10},{10,1... | collective-permute-start | bytes 6291464 | tf_op jit(solution)/shard_map/ppermute | solution.py:380
  6.9 48.1 %collective-permute-start.3 = (f32[32,16384]{1,0:T(8,128)}, f32[32,16384]{1,0:T(8,128)}, u32[]{:S(2)}, u32[]{:S(2)}) collective-permute-start(f32[32,16384]{1,0:T(8,128)} %get-tuple-element.56), channel_id=1, source_target_pairs={{0,3},{1,0},{2,1},{3,2},{4,7},{5,4},{6,5},{7,6},{8,11},{9,8},{10,9... | collective-permute-start | bytes 6291464 | tf_op jit(solution)/shard_map/ppermute | solution.py:380
  12.3 47.8 %collective-permute-start.4 = (f32[32,16384]{1,0:T(8,128)}, f32[32,16384]{1,0:T(8,128)}, u32[]{:S(2)}, u32[]{:S(2)}) collective-permute-start(f32[32,16384]{1,0:T(8,128)} %get-tuple-element.57), channel_id=1, source_target_pairs={{0,4},{1,5},{2,6},{3,7},{4,8},{5,9},{6,10},{7,11},{8,12},{9,13},{1... | collective-permute-start | bytes 6291464 | tf_op jit(solution)/shard_map/ppermute | solution.py:380
  13.8 47.6 %collective-permute-start.5 = (f32[32,16384]{1,0:T(8,128)}, f32[32,16384]{1,0:T(8,128)}, u32[]{:S(2)}, u32[]{:S(2)}) collective-permute-start(f32[32,16384]{1,0:T(8,128)} %get-tuple-element.58), channel_id=1, source_target_pairs={{0,12},{1,13},{2,14},{3,15},{4,0},{5,1},{6,2},{7,3},{8,4},{9,5},{1... | collective-permute-start | bytes 6291464 | tf_op jit(solution)/shard_map/ppermute | solution.py:380
  19.4 79.0 %collective-permute-start = (f32[32,16384]{1,0:T(8,128)}, f32[32,16384]{1,0:T(8,128)}, u32[]{:S(2)}, u32[]{:S(2)}) collective-permute-start(f32[32,16384]{1,0:T(8,128)} %get-tuple-element.53), channel_id=1, source_target_pairs={{0,1},{1,2},{2,3},{3,0},{4,5},{5,6},{6,7},{7,4},{8,9},{9,10},{10,1... | collective-permute-start | bytes 6291464 | tf_op jit(solution)/shard_map/ppermute | solution.py:380
  53.4 46.5 %collective-permute-start.1 = (f32[32,16384]{1,0:T(8,128)}, f32[32,16384]{1,0:T(8,128)}, u32[]{:S(2)}, u32[]{:S(2)}) collective-permute-start(f32[32,16384]{1,0:T(8,128)} %get-tuple-element.54), channel_id=1, source_target_pairs={{0,3},{1,0},{2,1},{3,2},{4,7},{5,4},{6,5},{7,6},{8,11},{9,8},{10,9... | collective-permute-start | bytes 6291464 | tf_op jit(solution)/shard_map/ppermute | solution.py:380
  55.0 50.1 %collective-permute-start.8 = (f32[32,16384]{1,0:T(8,128)}, f32[32,16384]{1,0:T(8,128)}, u32[]{:S(2)}, u32[]{:S(2)}) collective-permute-start(f32[32,16384]{1,0:T(8,128)} %get-tuple-element.65), channel_id=1, source_target_pairs={{0,4},{1,5},{2,6},{3,7},{4,8},{5,9},{6,10},{7,11},{8,12},{9,13},{1... | collective-permute-start | bytes 6291464 | tf_op jit(solution)/shard_map/ppermute | solution.py:380
  60.1 47.3 %collective-permute-start.9 = (f32[32,16384]{1,0:T(8,128)}, f32[32,16384]{1,0:T(8,128)}, u32[]{:S(2)}, u32[]{:S(2)}) collective-permute-start(f32[32,16384]{1,0:T(8,128)} %get-tuple-element.66), channel_id=1, source_target_pairs={{0,12},{1,13},{2,14},{3,15},{4,0},{5,1},{6,2},{7,3},{8,4},{9,5},{1... | collective-permute-start | bytes 6291464 | tf_op jit(solution)/shard_map/ppermute | solution.py:380
  61.5 10.1 %collective-permute-start.14 = (s32[1,8,8192]{2,1,0:T(8,128)}, s32[1,8,8192]{2,1,0:T(8,128)}, u32[]{:S(2)}, u32[]{:S(2)}) collective-permute-start(s32[1,8,8192]{2,1,0:T(8,128)} %refs_4_.3), channel_id=1, source_target_pairs={{0,32},{16,48},{32,64},{48,80},{64,96},{80,112},{96,0},{112,16},{1... | collective-permute-start | bytes 786440 | tf_op jit(solution)/shard_map/ppermute | solution.py:384
  71.6 71.7 %collective-permute-start.6 = (f32[32,16384]{1,0:T(8,128)S(1)}, f32[32,16384]{1,0:T(8,128)S(1)}, u32[]{:S(2)}, u32[]{:S(2)}) collective-permute-start(f32[32,16384]{1,0:T(8,128)S(1)} %get-tuple-element.62), channel_id=1, source_target_pairs={{0,1},{1,2},{2,3},{3,0},{4,5},{5,6},{6,7},{7,4},{8,9},{9,10},{10,1... | collective-permute-start | bytes 6291464 | tf_op jit(solution)/shard_map/ppermute | solution.py:380
  98.4 44.9 %collective-permute-start.7 = (f32[32,16384]{1,0:T(8,128)S(1)}, f32[32,16384]{1,0:T(8,128)S(1)}, u32[]{:S(2)}, u32[]{:S(2)}) collective-permute-start(f32[32,16384]{1,0:T(8,128)S(1)} %get-tuple-element.63), channel_id=1, source_target_pairs={{0,3},{1,0},{2,1},{3,2},{4,7},{5,4},{6,5},{7,6},{8,11},{9,8},{10,9... | collective-permute-start | bytes 6291464 | tf_op jit(solution)/shard_map/ppermute | solution.py:380
  99.9 51.0 %collective-permute-start.12 = (f32[32,16384]{1,0:T(8,128)S(1)}, f32[32,16384]{1,0:T(8,128)}, u32[]{:S(2)}, u32[]{:S(2)}) collective-permute-start(f32[32,16384]{1,0:T(8,128)S(1)} %get-tuple-element.69), channel_id=1, source_target_pairs={{0,4},{1,5},{2,6},{3,7},{4,8},{5,9},{6,10},{7,11},{8,12},{9,13},{1... | collective-permute-start | bytes 6291464 | tf_op jit(solution)/shard_map/ppermute | solution.py:380
  105.1 45.9 %collective-permute-start.13 = (f32[32,16384]{1,0:T(8,128)S(1)}, f32[32,16384]{1,0:T(8,128)}, u32[]{:S(2)}, u32[]{:S(2)}) collective-permute-start(f32[32,16384]{1,0:T(8,128)S(1)} %get-tuple-element.70), channel_id=1, source_target_pairs={{0,12},{1,13},{2,14},{3,15},{4,0},{5,1},{6,2},{7,3},{8,4},{9,5},{1... | collective-permute-start | bytes 6291464 | tf_op jit(solution)/shard_map/ppermute | solution.py:380
  107.5 43.5 %collective-permute-start.15 = (s32[1,16,8192]{2,1,0:T(8,128)S(1)}, s32[1,16,8192]{2,1,0:T(8,128)S(1)}, u32[]{:S(2)}, u32[]{:S(2)}) collective-permute-start(s32[1,16,8192]{2,1,0:T(8,128)S(1)} %pad_add_fusion), channel_id=1, source_target_pairs={{0,64},{16,80},{32,96},{48,112},{64,0},{80,16},{96,32},{112,48},{1... | collective-permute-start | bytes 1572872 | tf_op jit(solution)/shard_map/ppermute | solution.py:384
  143.3 1.3 copy-start.2
  143.3 2.0 copy-start.3
  147.7 12.7 %collective-permute-start.10 = (f32[32,4096]{1,0:T(8,128)S(1)}, f32[32,4096]{1,0:T(8,128)S(1)}, u32[]{:S(2)}, u32[]{:S(2)}) collective-permute-start(f32[32,4096]{1,0:T(8,128)S(1)} %get-tuple-element.67), channel_id=1, source_target_pairs={{0,4},{1,5},{2,6},{3,7},{4,8},{5,9},{6,10},{7,11},{8,12},{9,13},{1... | collective-permute-start | bytes 1572872 | tf_op jit(solution)/shard_map/ppermute | solution.py:380
  149.3 12.2 %collective-permute-start.11 = (f32[32,4096]{1,0:T(8,128)S(1)}, f32[32,4096]{1,0:T(8,128)S(1)}, u32[]{:S(2)}, u32[]{:S(2)}) collective-permute-start(f32[32,4096]{1,0:T(8,128)S(1)} %get-tuple-element.68), channel_id=1, source_target_pairs={{0,12},{1,13},{2,14},{3,15},{4,0},{5,1},{6,2},{7,3},{8,4},{9,5},{1... | collective-permute-start | bytes 1572872 | tf_op jit(solution)/shard_map/ppermute | solution.py:380
  153.4 13.5 %collective-permute-start.16 = (f32[32,4096]{1,0:T(8,128)S(1)}, f32[32,4096]{1,0:T(8,128)S(1)}, u32[]{:S(2)}, u32[]{:S(2)}) collective-permute-start(f32[32,4096]{1,0:T(8,128)S(1)} %get-tuple-element.72), channel_id=1, source_target_pairs={{0,1},{1,2},{2,3},{3,0},{4,5},{5,6},{6,7},{7,4},{8,9},{9,10},{10,1... | collective-permute-start | bytes 1572872 | tf_op jit(solution)/shard_map/ppermute | solution.py:380
  153.5 13.4 %collective-permute-start.17 = (f32[32,4096]{1,0:T(8,128)S(1)}, f32[32,4096]{1,0:T(8,128)S(1)}, u32[]{:S(2)}, u32[]{:S(2)}) collective-permute-start(f32[32,4096]{1,0:T(8,128)S(1)} %get-tuple-element.73), channel_id=1, source_target_pairs={{0,3},{1,0},{2,1},{3,2},{4,7},{5,4},{6,5},{7,6},{8,11},{9,8},{10,9... | collective-permute-start | bytes 1572872 | tf_op jit(solution)/shard_map/ppermute | solution.py:380
  164.0 13.2 %collective-permute-start.22 = (f32[64,2048]{1,0:T(8,128)S(1)}, f32[64,2048]{1,0:T(8,128)S(1)}, u32[]{:S(2)}, u32[]{:S(2)}) collective-permute-start(f32[64,2048]{1,0:T(8,128)S(1)} %get-tuple-element.82), channel_id=1, source_target_pairs={{0,4},{1,5},{2,6},{3,7},{4,8},{5,9},{6,10},{7,11},{8,12},{9,13},{1... | collective-permute-start | bytes 1572872 | tf_op jit(solution)/shard_map/ppermute | solution.py:380
  164.1 15.8 %collective-permute-start.23 = (f32[64,2048]{1,0:T(8,128)S(1)}, f32[64,2048]{1,0:T(8,128)S(1)}, u32[]{:S(2)}, u32[]{:S(2)}) collective-permute-start(f32[64,2048]{1,0:T(8,128)S(1)} %get-tuple-element.83), channel_id=1, source_target_pairs={{0,12},{1,13},{2,14},{3,15},{4,0},{5,1},{6,2},{7,3},{8,4},{9,5},{1... | collective-permute-start | bytes 1572872 | tf_op jit(solution)/shard_map/ppermute | solution.py:380
  169.4 11.3 %collective-permute-start.24 = (f32[64,2048]{1,0:T(8,128)S(1)}, f32[64,2048]{1,0:T(8,128)S(1)}, u32[]{:S(2)}, u32[]{:S(2)}) collective-permute-start(f32[64,2048]{1,0:T(8,128)S(1)} %get-tuple-element.84), channel_id=1, source_target_pairs={{0,1},{1,2},{2,3},{3,0},{4,5},{5,6},{6,7},{7,4},{8,9},{9,10},{10,1... | collective-permute-start | bytes 1572872 | tf_op jit(solution)/shard_map/ppermute | solution.py:380
  169.5 13.1 %collective-permute-start.25 = (f32[64,2048]{1,0:T(8,128)S(1)}, f32[64,2048]{1,0:T(8,128)S(1)}, u32[]{:S(2)}, u32[]{:S(2)}) collective-permute-start(f32[64,2048]{1,0:T(8,128)S(1)} %get-tuple-element.85), channel_id=1, source_target_pairs={{0,3},{1,0},{2,1},{3,2},{4,7},{5,4},{6,5},{7,6},{8,11},{9,8},{10,9... | collective-permute-start | bytes 1572872 | tf_op jit(solution)/shard_map/ppermute | solution.py:380
  174.6 8.0 %copy-start = (bf16[64,256]{1,0:T(8,128)(2,1)S(1)}, bf16[64,256]{1,0:T(8,128)(2,1)}, u32[]{:S(2)}) copy-start(bf16[64,256]{1,0:T(8,128)(2,1)} %constant.25.clone.refs_17_.refs_8_) | copy-start | bytes 98308
  174.7 8.0 %copy-start.1 = (bf16[64,256]{1,0:T(8,128)(2,1)S(1)}, bf16[64,256]{1,0:T(8,128)(2,1)}, u32[]{:S(2)}) copy-start(bf16[64,256]{1,0:T(8,128)(2,1)} %constant.24.clone.refs_16_) | copy-start | bytes 98308
  177.2 15.8 %collective-permute-start.18 = (f32[64,2048]{1,0:T(8,128)S(1)}, f32[64,2048]{1,0:T(8,128)S(1)}, u32[]{:S(2)}, u32[]{:S(2)}) collective-permute-start(f32[64,2048]{1,0:T(8,128)S(1)} %get-tuple-element.78), channel_id=1, source_target_pairs={{0,4},{1,5},{2,6},{3,7},{4,8},{5,9},{6,10},{7,11},{8,12},{9,13},{1... | collective-permute-start | bytes 1572872 | tf_op jit(solution)/shard_map/ppermute | solution.py:380
  177.3 16.1 %collective-permute-start.19 = (f32[64,2048]{1,0:T(8,128)S(1)}, f32[64,2048]{1,0:T(8,128)S(1)}, u32[]{:S(2)}, u32[]{:S(2)}) collective-permute-start(f32[64,2048]{1,0:T(8,128)S(1)} %get-tuple-element.79), channel_id=1, source_target_pairs={{0,12},{1,13},{2,14},{3,15},{4,0},{5,1},{6,2},{7,3},{8,4},{9,5},{1... | collective-permute-start | bytes 1572872 | tf_op jit(solution)/shard_map/ppermute | solution.py:380
  179.9 14.5 %collective-permute-start.20 = (f32[64,2048]{1,0:T(8,128)S(1)}, f32[64,2048]{1,0:T(8,128)S(1)}, u32[]{:S(2)}, u32[]{:S(2)}) collective-permute-start(f32[64,2048]{1,0:T(8,128)S(1)} %get-tuple-element.80), channel_id=1, source_target_pairs={{0,1},{1,2},{2,3},{3,0},{4,5},{5,6},{6,7},{7,4},{8,9},{9,10},{10,1... | collective-permute-start | bytes 1572872 | tf_op jit(solution)/shard_map/ppermute | solution.py:380
  180.7 13.7 %collective-permute-start.21 = (f32[64,2048]{1,0:T(8,128)S(1)}, f32[64,2048]{1,0:T(8,128)S(1)}, u32[]{:S(2)}, u32[]{:S(2)}) collective-permute-start(f32[64,2048]{1,0:T(8,128)S(1)} %get-tuple-element.81), channel_id=1, source_target_pairs={{0,3},{1,0},{2,1},{3,2},{4,7},{5,4},{6,5},{7,6},{8,11},{9,8},{10,9... | collective-permute-start | bytes 1572872 | tf_op jit(solution)/shard_map/ppermute | solution.py:380
  189.5 15.0 %collective-permute-start.31 = (f32[8,4096]{1,0:T(8,128)S(1)}, f32[8,4096]{1,0:T(8,128)S(1)}, u32[]{:S(2)}, u32[]{:S(2)}) collective-permute-start(f32[8,4096]{1,0:T(8,128)S(1)} %get-tuple-element.90.refs_0_), channel_id=1, source_target_pairs={{0,64},{16,80},{32,96},{48,112},{64,0},{80,16},{96,32},{112,48},{1... | collective-permute-start | bytes 393224 | tf_op jit(solution)/shard_map/ppermute | solution.py:384
  193.0 11.5 %collective-permute-start.30 = (f32[8,4096]{1,0:T(8,128)S(1)}, f32[8,4096]{1,0:T(8,128)S(1)}, u32[]{:S(2)}, u32[]{:S(2)}) collective-permute-start(f32[8,4096]{1,0:T(8,128)S(1)} %get-tuple-element.90.refs_0_), channel_id=1, source_target_pairs={{0,96},{16,112},{32,0},{48,16},{64,32},{80,48},{96,64},{112,80},{1... | collective-permute-start | bytes 393224 | tf_op jit(solution)/shard_map/ppermute | solution.py:384
  193.4 11.1 %collective-permute-start.29 = (f32[8,4096]{1,0:T(8,128)S(1)}, f32[8,4096]{1,0:T(8,128)S(1)}, u32[]{:S(2)}, u32[]{:S(2)}) collective-permute-start(f32[8,4096]{1,0:T(8,128)S(1)} %get-tuple-element.90.refs_0_), channel_id=1, source_target_pairs={{0,32},{16,48},{32,64},{48,80},{64,96},{80,112},{96,0},{112,16},{1... | collective-permute-start | bytes 393224 | tf_op jit(solution)/shard_map/ppermute | solution.py:384
  201.3 14.7 %collective-permute-start.28 = (f32[8,4096]{1,0:T(8,128)S(1)}, f32[8,4096]{1,0:T(8,128)S(1)}, u32[]{:S(2)}, u32[]{:S(2)}) collective-permute-start(f32[8,4096]{1,0:T(8,128)S(1)} %get-tuple-element.89.refs_0_), channel_id=1, source_target_pairs={{0,64},{16,80},{32,96},{48,112},{64,0},{80,16},{96,32},{112,48},{1... | collective-permute-start | bytes 393224 | tf_op jit(solution)/shard_map/ppermute | solution.py:384
  202.5 13.5 %collective-permute-start.27 = (f32[8,4096]{1,0:T(8,128)S(1)}, f32[8,4096]{1,0:T(8,128)S(1)}, u32[]{:S(2)}, u32[]{:S(2)}) collective-permute-start(f32[8,4096]{1,0:T(8,128)S(1)} %get-tuple-element.89.refs_0_), channel_id=1, source_target_pairs={{0,96},{16,112},{32,0},{48,16},{64,32},{80,48},{96,64},{112,80},{1... | collective-permute-start | bytes 393224 | tf_op jit(solution)/shard_map/ppermute | solution.py:384
  204.5 11.5 %collective-permute-start.26 = (f32[8,4096]{1,0:T(8,128)S(1)}, f32[8,4096]{1,0:T(8,128)S(1)}, u32[]{:S(2)}, u32[]{:S(2)}) collective-permute-start(f32[8,4096]{1,0:T(8,128)S(1)} %get-tuple-element.89.refs_0_), channel_id=1, source_target_pairs={{0,32},{16,48},{32,64},{48,80},{64,96},{80,112},{96,0},{112,16},{1... | collective-permute-start | bytes 393224 | tf_op jit(solution)/shard_map/ppermute | solution.py:384
  209.4 12.8 %collective-permute-start.33 = (f32[64,4096]{1,0:T(8,128)S(1)}, f32[64,4096]{1,0:T(8,128)S(1)}, u32[]{:S(2)}, u32[]{:S(2)}) collective-permute-start(f32[64,4096]{1,0:T(8,128)S(1)} %get-tuple-element.94.refs_0_), channel_id=1, source_target_pairs={{0,16},{16,0},{32,48},{48,32},{64,80},{80,64},{96,112},{112,96},{1... | collective-permute-start | bytes 3145736 | tf_op jit(solution)/shard_map/ppermute | solution.py:390
  220.8 3.6 %collective-permute-start.32 = (f32[64,4096]{1,0:T(8,128)S(1)}, f32[64,4096]{1,0:T(8,128)S(1)}, u32[]{:S(2)}, u32[]{:S(2)}) collective-permute-start(f32[64,4096]{1,0:T(8,128)S(1)} %get-tuple-element.93.refs_0_), channel_id=1, source_target_pairs={{0,16},{16,0},{32,48},{48,32},{64,80},{80,64},{96,112},{112,96},{1... | collective-permute-start | bytes 3145736 | tf_op jit(solution)/shard_map/ppermute | solution.py:390

commit v11 on v10

--- a/solution.py
+++ b/solution.py
@@ -20,7 +20,7 @@
 PLACES_WITH = ((1, 0), (1, 0))
 TAIL = ('f0', 'f1', 's0', 's1', 'j0', 'j1')
 TOGETHER = 2
-VMEM_LIMIT = 48 * 1024 * 1024
+VMEM_LIMIT = 36 * 1024 * 1024
 F32 = jnp.float32
 BF16 = jnp.bfloat16
 

time: 227 us -> 227 us (level)
  transfers between devices with their start and end apart: 34 -> 34, of which waited for: 9 -> 9; matrix products, arithmetic and copies ran while one was open for 0% -> 0% of each run, Pallas kernels for 27% -> 26%
where the time goes in v11:
time: 227 us; the launch traced here: 226 us
  waiting for transfers between devices  105 us (46%)
  Pallas kernels  64.5 us (28%)
  starting transfers between devices  54.3 us (24%)
    ppermute x24, waiting for transfers between devices, along(): lax.ppermute(value, 'fsdp', shift(0, step) if x_first else shift(step, 0))  105 us
    pallas_call x18, Pallas kernels, call(): pl.pallas_call(run, grid_spec=pltpu.PrefetchScalarGridSpec(num_scalar_pre...  64.5 us
    ppermute x24, starting transfers between devices, along(): lax.ppermute(value, 'fsdp', shift(0, step) if x_first else shift(step, 0))  31.1 us
    ppermute x8, starting transfers between devices, along_z(): lax.ppermute(value, 'rep', [(z * 2 + c, (z + step) % SIDE * 2 + c) for z...  13.5 us
    ppermute x2, starting transfers between devices, other_core(): return lax.ppermute(value, 'rep', [(r, r ^ 1) for r in range(2 * SIDE)])  9.65 us
  transfers between devices with their start and end apart: 34, of which 9 were waited for; matrix products, arithmetic and copies ran while one was open for 0% of the time, Pallas kernels for 26%

profile of v11, /device:TPU:1, one launch (start us, length us, event | category | flops | bytes accessed | tf_op | source)
XLA Modules:
  0.0 225.9 jit_solution(5718843800131948162)
XLA Ops:
  0.6 0.1 pad_add_fusion.1.here
  0.7 4.1 %shard_map.68 = (f32[32,16384]{1,0:T(8,128)}, f32[32,16384]{1,0:T(8,128)}, f32[8,128]{1,0:T(8,128)S(1)}) custom-call(s32[2]{0:T(128)S(1)} %pad_add_fusion.1.here, bf16[64,131072]{1,0:T(8,128)(2,1)} %bitcast.3, bf16[64,131072]{1,0:T(8,128)(2,1)} %bitcast.4, bf16[64,131072]{1,0:T(8,128)(2,1)} %bitcast.5, bf16[64,131072]{1,0:T(8,128)(2,1)} %bitcast.6, ...), custom_call_target="tpu_custom_call" | custom-call | tf_op jit(solution)/shard_map/pallas_call | solution.py:114
  4.8 2.1 collective-permute-start.2
  6.9 1.4 collective-permute-start.3
  8.3 4.2 %shard_map.69 = (f32[32,16384]{1,0:T(8,128)}, f32[32,16384]{1,0:T(8,128)}, f32[8,128]{1,0:T(8,128)S(1)}) custom-call(s32[2]{0:T(128)S(1)} %pad_add_fusion.1.here, bf16[64,131072]{1,0:T(8,128)(2,1)} %bitcast.26, bf16[64,131072]{1,0:T(8,128)(2,1)} %bitcast.20, bf16[64,131072]{1,0:T(8,128)(2,1)} %bitcast.21, bf16[64,131072]{1,0:T(8,128)(2,1)} %bitcast.22, ...), custom_call_target="tpu_custom_call" | custom-call | tf_op jit(solution)/shard_map/pallas_call | solution.py:114
  12.5 1.5 collective-permute-start.4
  13.9 1.5 collective-permute-start.5
  15.5 4.2 %shard_map.70 = (f32[32,16384]{1,0:T(8,128)}, f32[32,16384]{1,0:T(8,128)}, f32[8,128]{1,0:T(8,128)S(1)}) custom-call(s32[2]{0:T(128)S(1)} %pad_add_fusion.1.here, bf16[64,131072]{1,0:T(8,128)(2,1)} %bitcast.35, bf16[64,131072]{1,0:T(8,128)(2,1)} %bitcast.36, bf16[64,131072]{1,0:T(8,128)(2,1)} %bitcast.37, bf16[64,131072]{1,0:T(8,128)(2,1)} %bitcast.38, ...), custom_call_target="tpu_custom_call" | custom-call | tf_op jit(solution)/shard_map/pallas_call | solution.py:114
  19.6 0.1 collective-permute-start
  19.7 4.1 %shard_map.71 = (f32[32,16384]{1,0:T(8,128)}, f32[32,16384]{1,0:T(8,128)}, f32[8,128]{1,0:T(8,128)S(1)}) custom-call(s32[2]{0:T(128)S(1)} %pad_add_fusion.1.here, bf16[64,131072]{1,0:T(8,128)(2,1)} %bitcast.64, bf16[64,131072]{1,0:T(8,128)(2,1)} %bitcast.52, bf16[64,131072]{1,0:T(8,128)(2,1)} %bitcast.53, bf16[64,131072]{1,0:T(8,128)(2,1)} %bitcast.54, ...), custom_call_target="tpu_custom_call" | custom-call | tf_op jit(solution)/shard_map/pallas_call | solution.py:114
  23.8 29.6 %collective-permute-done.2.refs_16_.refs_19_ = f32[32,16384]{1,0:T(8,128)} collective-permute-done((f32[32,16384]{1,0:T(8,128)}, f32[32,16384]{1,0:T(8,128)}, u32[]{:S(2)}, u32[]{:S(2)}) %collective-permute-start.2) | collective-permute-done | bytes 2097184 | tf_op jit(solution)/shard_map/ppermute | solution.py:380
  53.4 1.6 collective-permute-start.1
  55.0 1.3 collective-permute-start.8
  56.3 4.0 %collective-permute-done.4.refs_16_.refs_19_ = f32[32,16384]{1,0:T(8,128)} collective-permute-done((f32[32,16384]{1,0:T(8,128)}, f32[32,16384]{1,0:T(8,128)}, u32[]{:S(2)}, u32[]{:S(2)}) %collective-permute-start.4) | collective-permute-done | bytes 2097184 | tf_op jit(solution)/shard_map/ppermute | solution.py:380
  60.3 1.3 collective-permute-start.9
  61.6 1.6 collective-permute-start.14
  63.2 4.2 %shard_map.72 = (f32[32,16384]{1,0:T(8,128)S(1)}, f32[32,16384]{1,0:T(8,128)S(1)}, f32[8,128]{1,0:T(8,128)S(1)}) custom-call(s32[2]{0:T(128)S(1)} %pad_add_fusion.1.here, bf16[64,131072]{1,0:T(8,128)(2,1)} %bitcast.67, bf16[64,131072]{1,0:T(8,128)(2,1)} %bitcast.68, bf16[64,131072]{1,0:T(8,128)(2,1)} %bitcast.69, bf16[64,131072]{1,0:T(8,128)(2,1)} %bitcast.70, ...), custom_call_target="tpu_custom_call" | custom-call | tf_op jit(solution)/shard_map/pallas_call | solution.py:114
  67.4 4.2 %shard_map.73 = (f32[32,16384]{1,0:T(8,128)S(1)}, f32[32,16384]{1,0:T(8,128)S(1)}, f32[8,128]{1,0:T(8,128)S(1)}) custom-call(s32[2]{0:T(128)S(1)} %pad_add_fusion.1.here, bf16[64,131072]{1,0:T(8,128)(2,1)} %bitcast.89, bf16[64,131072]{1,0:T(8,128)(2,1)} %bitcast.84, bf16[64,131072]{1,0:T(8,128)(2,1)} %bitcast.85, bf16[64,131072]{1,0:T(8,128)(2,1)} %bitcast.86, ...), custom_call_target="tpu_custom_call" | custom-call | tf_op jit(solution)/shard_map/pallas_call | solution.py:114
  71.7 0.1 collective-permute-start.6
  71.8 26.6 %collective-permute-done.refs_4_.refs_5_.refs_6_.refs_7_.refs_21_.refs_2_.refs_3_.refs_12_.refs_13_.refs_1_ = f32[32,16384]{1,0:T(8,128)} collective-permute-done((f32[32,16384]{1,0:T(8,128)}, f32[32,16384]{1,0:T(8,128)}, u32[]{:S(2)}, u32[]{:S(2)}) %collective-permute-start) | collective-permute-done | bytes 2097184 | tf_op jit(solution)/shard_map/ppermute | solution.py:380
  98.4 1.6 collective-permute-start.7
  99.9 1.3 collective-permute-start.12
  101.2 4.0 %collective-permute-done.8.refs_21_.refs_4_.refs_5_.refs_6_.refs_7_.refs_2_.refs_3_.refs_12_.refs_13_.refs_8_ = f32[32,16384]{1,0:T(8,128)} collective-permute-done((f32[32,16384]{1,0:T(8,128)}, f32[32,16384]{1,0:T(8,128)}, u32[]{:S(2)}, u32[]{:S(2)}) %collective-permute-start.8) | collective-permute-done | bytes 2097184 | tf_op jit(solution)/shard_map/ppermute | solution.py:380
  105.2 1.3 collective-permute-start.13
  106.5 1.1 pad_add_fusion
  107.6 3.7 %collective-permute-start.15 = (s32[1,16,8192]{2,1,0:T(8,128)S(1)}, s32[1,16,8192]{2,1,0:T(8,128)S(1)}, u32[]{:S(2)}, u32[]{:S(2)}) collective-permute-start(s32[1,16,8192]{2,1,0:T(8,128)S(1)} %pad_add_fusion), channel_id=1, source_target_pairs={{0,64},{16,80},{32,96},{48,112},{64,0},{80,16},{96,32},{112,48},{1... | collective-permute-start | bytes 1572872 | tf_op jit(solution)/shard_map/ppermute | solution.py:384
  111.3 31.9 %collective-permute-done.6.refs_12_.refs_13_.refs_14_.refs_15_.refs_6_.refs_7_.refs_16_.refs_17_.refs_25_.refs_3_ = f32[32,16384]{1,0:T(8,128)S(1)} collective-permute-done((f32[32,16384]{1,0:T(8,128)S(1)}, f32[32,16384]{1,0:T(8,128)S(1)}, u32[]{:S(2)}, u32[]{:S(2)}) %collective-permute-start.6) | collective-permute-done | bytes 2097184 | tf_op jit(solution)/shard_map/ppermute | solution.py:380
  143.2 2.1 shard_map.74
  145.3 1.7 collective-permute-start.10
  147.0 1.5 collective-permute-start.11
  148.5 1.5 collective-permute-done.12.refs_12_.refs_13_.refs_14_.refs_15_.refs_25_.refs_6_.refs_7_.refs_16_.refs_17_.refs_10_
  150.1 2.3 %shard_map.75 = (f32[32,4096]{1,0:T(8,128)S(1)}, f32[32,4096]{1,0:T(8,128)S(1)}, f32[8,128]{1,0:T(8,128)S(1)}) custom-call(s32[2]{0:T(128)S(1)} %pad_add_fusion.1.here, bf16[64,131072]{1,0:T(8,128)(2,1)} %bitcast.105, bf16[64,131072]{1,0:T(8,128)(2,1)} %bitcast.104, bf16[64,131072]{1,0:T(8,128)(2,1)} %bitcast.103, bf16[64,131072]{1,0:T(8,128)(2,1)} %bitcast.106, ...), custom_call_target="tpu_custom_call" | custom-call | tf_op jit(solution)/shard_map/pallas_call | solution.py:114
  152.3 0.1 collective-permute-start.16
  152.4 2.7 %collective-permute-start.17 = (f32[32,4096]{1,0:T(8,128)S(1)}, f32[32,4096]{1,0:T(8,128)S(1)}, u32[]{:S(2)}, u32[]{:S(2)}) collective-permute-start(f32[32,4096]{1,0:T(8,128)S(1)} %get-tuple-element.73), channel_id=1, source_target_pairs={{0,3},{1,0},{2,1},{3,2},{4,7},{5,4},{6,5},{7,6},{8,11},{9,8},{10,9... | collective-permute-start | bytes 1572872 | tf_op jit(solution)/shard_map/ppermute | solution.py:380
  155.1 6.1 %collective-permute-done.10.refs_20_.refs_21_.refs_25_ = f32[32,4096]{1,0:T(8,128)S(1)} collective-permute-done((f32[32,4096]{1,0:T(8,128)S(1)}, f32[32,4096]{1,0:T(8,128)S(1)}, u32[]{:S(2)}, u32[]{:S(2)}) %collective-permute-start.10) | collective-permute-done | bytes 524320 | tf_op jit(solution)/shard_map/ppermute | solution.py:380
  161.2 2.2 shard_map.76
  163.4 0.8 collective-permute-start.22
  164.2 2.0 collective-permute-start.23
  166.2 2.2 shard_map.77
  168.4 0.1 collective-permute-start.24
  168.5 2.7 %collective-permute-start.25 = (f32[64,2048]{1,0:T(8,128)S(1)}, f32[64,2048]{1,0:T(8,128)S(1)}, u32[]{:S(2)}, u32[]{:S(2)}) collective-permute-start(f32[64,2048]{1,0:T(8,128)S(1)} %get-tuple-element.85), channel_id=1, source_target_pairs={{0,3},{1,0},{2,1},{3,2},{4,7},{5,4},{6,5},{7,6},{8,11},{9,8},{10,9... | collective-permute-start | bytes 1572872 | tf_op jit(solution)/shard_map/ppermute | solution.py:380
  171.2 2.2 shard_map.78
  173.3 0.0 copy-start.1
  173.3 0.0 copy-start.2
  173.3 2.2 shard_map.79
  175.5 0.1 collective-permute-start.18
  175.6 2.7 %collective-permute-start.19 = (f32[64,2048]{1,0:T(8,128)S(1)}, f32[64,2048]{1,0:T(8,128)S(1)}, u32[]{:S(2)}, u32[]{:S(2)}) collective-permute-start(f32[64,2048]{1,0:T(8,128)S(1)} %get-tuple-element.79), channel_id=1, source_target_pairs={{0,12},{1,13},{2,14},{3,15},{4,0},{5,1},{6,2},{7,3},{8,4},{9,5},{1... | collective-permute-start | bytes 1572872 | tf_op jit(solution)/shard_map/ppermute | solution.py:380
  178.3 0.9 collective-permute-done.24.refs_12_
  179.2 1.8 collective-permute-start.21
  181.0 6.6 %shard_map.80 = (f32[1,64,8192]{2,1,0:T(8,128)}, f32[8,4096]{1,0:T(8,128)S(1)}, f32[8,128]{1,0:T(8,128)S(1)}) custom-call(s32[2]{0:T(128)S(1)} %pad_add_fusion.1.here, bf16[64,131072]{1,0:T(8,128)(2,1)} %bitcast.123, f32[32,16384]{1,0:T(8,128)} %collective-permute-done.refs_4_.refs_5_.refs_6_.refs_7_.refs_21_.refs_2_.refs_3_.refs_12_.refs_13_.refs_1_, ...), custom_call_target="tpu_custom_call" | custom-call | tf_op jit(solution)/shard_map/pallas_call | solution.py:114
  187.6 3.6 %collective-permute-start.31 = (f32[8,4096]{1,0:T(8,128)S(1)}, f32[8,4096]{1,0:T(8,128)S(1)}, u32[]{:S(2)}, u32[]{:S(2)}) collective-permute-start(f32[8,4096]{1,0:T(8,128)S(1)} %get-tuple-element.90.refs_0_), channel_id=1, source_target_pairs={{0,64},{16,80},{32,96},{48,112},{64,0},{80,16},{96,32},{112,48},{1... | collective-permute-start | bytes 393224 | tf_op jit(solution)/shard_map/ppermute | solution.py:384
  191.2 0.4 collective-permute-start.30
  191.7 1.0 collective-permute-start.29
  192.7 6.6 %shard_map.81 = (f32[1,64,8192]{2,1,0:T(8,128)}, f32[8,4096]{1,0:T(8,128)S(1)}, f32[8,128]{1,0:T(8,128)S(1)}) custom-call(s32[2]{0:T(128)S(1)} %pad_add_fusion.1.here, bf16[64,131072]{1,0:T(8,128)(2,1)} %bitcast.125, ...), custom_call_target="tpu_custom_call", output_to_operand_aliasing={{0}: (19, {})} | custom-call | tf_op jit(solution)/shard_map/pallas_call | solution.py:114
  199.3 1.7 collective-permute-start.28
  201.0 1.4 collective-permute-start.27
  202.5 0.0 collective-permute-start.26
  202.5 4.8 %shard_map.82 = (f32[64,4096]{1,0:T(8,128)S(1)}, f32[8,128]{1,0:T(8,128)S(1)}) custom-call(s32[2]{0:T(128)S(1)} %pad_add_fusion.1.here, f32[8,4096]{1,0:T(8,128)S(1)} %get-tuple-element.90.refs_0_, f32[8,4096]{1,0:T(8,128)S(1)} %collective-permute-done.29.refs_1_, f32[8,4096]{1,0:T(8,128)S(1)} %collective-permute-done.30.refs_2_, ...), custom_call_target="tpu_custom_call" | custom-call | tf_op jit(solution)/shard_map/pallas_call | solution.py:114
  207.4 8.4 %collective-permute-start.33 = (f32[64,4096]{1,0:T(8,128)S(1)}, f32[64,4096]{1,0:T(8,128)S(1)}, u32[]{:S(2)}, u32[]{:S(2)}) collective-permute-start(f32[64,4096]{1,0:T(8,128)S(1)} %get-tuple-element.94.refs_0_), channel_id=1, source_target_pairs={{0,16},{16,0},{32,48},{48,32},{64,80},{80,64},{96,112},{112,96},{1... | collective-permute-start | bytes 3145736 | tf_op jit(solution)/shard_map/ppermute | solution.py:390
  215.7 4.8 %shard_map.83 = (f32[64,4096]{1,0:T(8,128)S(1)}, f32[8,128]{1,0:T(8,128)S(1)}) custom-call(s32[2]{0:T(128)S(1)} %pad_add_fusion.1.here, f32[8,4096]{1,0:T(8,128)S(1)} %get-tuple-element.89.refs_0_, f32[8,4096]{1,0:T(8,128)S(1)} %collective-permute-done.26.refs_1_, f32[8,4096]{1,0:T(8,128)S(1)} %collective-permute-done.27.refs_2_, ...), custom_call_target="tpu_custom_call" | custom-call | tf_op jit(solution)/shard_map/pallas_call | solution.py:114
  220.6 1.3 collective-permute-start.32
  221.9 1.7 shard_map.84
  223.6 0.5 collective-permute-done.32.refs_1_
  224.2 1.7 shard_map.85
  (30 shorter events, 0.1 us)
Async XLA Ops:
  4.8 48.6 %collective-permute-start.2 = (f32[32,16384]{1,0:T(8,128)}, f32[32,16384]{1,0:T(8,128)}, u32[]{:S(2)}, u32[]{:S(2)}) collective-permute-start(f32[32,16384]{1,0:T(8,128)} %get-tuple-element.55), channel_id=1, source_target_pairs={{0,1},{1,2},{2,3},{3,0},{4,5},{5,6},{6,7},{7,4},{8,9},{9,10},{10,1... | collective-permute-start | bytes 6291464 | tf_op jit(solution)/shard_map/ppermute | solution.py:380
  6.9 48.1 %collective-permute-start.3 = (f32[32,16384]{1,0:T(8,128)}, f32[32,16384]{1,0:T(8,128)}, u32[]{:S(2)}, u32[]{:S(2)}) collective-permute-start(f32[32,16384]{1,0:T(8,128)} %get-tuple-element.56), channel_id=1, source_target_pairs={{0,3},{1,0},{2,1},{3,2},{4,7},{5,4},{6,5},{7,6},{8,11},{9,8},{10,9... | collective-permute-start | bytes 6291464 | tf_op jit(solution)/shard_map/ppermute | solution.py:380
  12.5 47.8 %collective-permute-start.4 = (f32[32,16384]{1,0:T(8,128)}, f32[32,16384]{1,0:T(8,128)}, u32[]{:S(2)}, u32[]{:S(2)}) collective-permute-start(f32[32,16384]{1,0:T(8,128)} %get-tuple-element.57), channel_id=1, source_target_pairs={{0,4},{1,5},{2,6},{3,7},{4,8},{5,9},{6,10},{7,11},{8,12},{9,13},{1... | collective-permute-start | bytes 6291464 | tf_op jit(solution)/shard_map/ppermute | solution.py:380
  13.9 47.6 %collective-permute-start.5 = (f32[32,16384]{1,0:T(8,128)}, f32[32,16384]{1,0:T(8,128)}, u32[]{:S(2)}, u32[]{:S(2)}) collective-permute-start(f32[32,16384]{1,0:T(8,128)} %get-tuple-element.58), channel_id=1, source_target_pairs={{0,12},{1,13},{2,14},{3,15},{4,0},{5,1},{6,2},{7,3},{8,4},{9,5},{1... | collective-permute-start | bytes 6291464 | tf_op jit(solution)/shard_map/ppermute | solution.py:380
  19.6 78.7 %collective-permute-start = (f32[32,16384]{1,0:T(8,128)}, f32[32,16384]{1,0:T(8,128)}, u32[]{:S(2)}, u32[]{:S(2)}) collective-permute-start(f32[32,16384]{1,0:T(8,128)} %get-tuple-element.53), channel_id=1, source_target_pairs={{0,1},{1,2},{2,3},{3,0},{4,5},{5,6},{6,7},{7,4},{8,9},{9,10},{10,1... | collective-permute-start | bytes 6291464 | tf_op jit(solution)/shard_map/ppermute | solution.py:380
  53.4 46.5 %collective-permute-start.1 = (f32[32,16384]{1,0:T(8,128)}, f32[32,16384]{1,0:T(8,128)}, u32[]{:S(2)}, u32[]{:S(2)}) collective-permute-start(f32[32,16384]{1,0:T(8,128)} %get-tuple-element.54), channel_id=1, source_target_pairs={{0,3},{1,0},{2,1},{3,2},{4,7},{5,4},{6,5},{7,6},{8,11},{9,8},{10,9... | collective-permute-start | bytes 6291464 | tf_op jit(solution)/shard_map/ppermute | solution.py:380
  55.0 50.2 %collective-permute-start.8 = (f32[32,16384]{1,0:T(8,128)}, f32[32,16384]{1,0:T(8,128)}, u32[]{:S(2)}, u32[]{:S(2)}) collective-permute-start(f32[32,16384]{1,0:T(8,128)} %get-tuple-element.65), channel_id=1, source_target_pairs={{0,4},{1,5},{2,6},{3,7},{4,8},{5,9},{6,10},{7,11},{8,12},{9,13},{1... | collective-permute-start | bytes 6291464 | tf_op jit(solution)/shard_map/ppermute | solution.py:380
  60.3 47.3 %collective-permute-start.9 = (f32[32,16384]{1,0:T(8,128)}, f32[32,16384]{1,0:T(8,128)}, u32[]{:S(2)}, u32[]{:S(2)}) collective-permute-start(f32[32,16384]{1,0:T(8,128)} %get-tuple-element.66), channel_id=1, source_target_pairs={{0,12},{1,13},{2,14},{3,15},{4,0},{5,1},{6,2},{7,3},{8,4},{9,5},{1... | collective-permute-start | bytes 6291464 | tf_op jit(solution)/shard_map/ppermute | solution.py:380
  61.6 10.1 %collective-permute-start.14 = (s32[1,8,8192]{2,1,0:T(8,128)}, s32[1,8,8192]{2,1,0:T(8,128)}, u32[]{:S(2)}, u32[]{:S(2)}) collective-permute-start(s32[1,8,8192]{2,1,0:T(8,128)} %refs_4_.3), channel_id=1, source_target_pairs={{0,32},{16,48},{32,64},{48,80},{64,96},{80,112},{96,0},{112,16},{1... | collective-permute-start | bytes 786440 | tf_op jit(solution)/shard_map/ppermute | solution.py:384
  71.7 71.5 %collective-permute-start.6 = (f32[32,16384]{1,0:T(8,128)S(1)}, f32[32,16384]{1,0:T(8,128)S(1)}, u32[]{:S(2)}, u32[]{:S(2)}) collective-permute-start(f32[32,16384]{1,0:T(8,128)S(1)} %get-tuple-element.62), channel_id=1, source_target_pairs={{0,1},{1,2},{2,3},{3,0},{4,5},{5,6},{6,7},{7,4},{8,9},{9,10},{10,1... | collective-permute-start | bytes 6291464 | tf_op jit(solution)/shard_map/ppermute | solution.py:380
  98.4 44.8 %collective-permute-start.7 = (f32[32,16384]{1,0:T(8,128)S(1)}, f32[32,16384]{1,0:T(8,128)S(1)}, u32[]{:S(2)}, u32[]{:S(2)}) collective-permute-start(f32[32,16384]{1,0:T(8,128)S(1)} %get-tuple-element.63), channel_id=1, source_target_pairs={{0,3},{1,0},{2,1},{3,2},{4,7},{5,4},{6,5},{7,6},{8,11},{9,8},{10,9... | collective-permute-start | bytes 6291464 | tf_op jit(solution)/shard_map/ppermute | solution.py:380
  99.9 50.1 %collective-permute-start.12 = (f32[32,16384]{1,0:T(8,128)S(1)}, f32[32,16384]{1,0:T(8,128)S(1)}, u32[]{:S(2)}, u32[]{:S(2)}) collective-permute-start(f32[32,16384]{1,0:T(8,128)S(1)} %get-tuple-element.69), channel_id=1, source_target_pairs={{0,4},{1,5},{2,6},{3,7},{4,8},{5,9},{6,10},{7,11},{8,12},{9,13},{1... | collective-permute-start | bytes 6291464 | tf_op jit(solution)/shard_map/ppermute | solution.py:380
  105.2 44.8 %collective-permute-start.13 = (f32[32,16384]{1,0:T(8,128)S(1)}, f32[32,16384]{1,0:T(8,128)S(1)}, u32[]{:S(2)}, u32[]{:S(2)}) collective-permute-start(f32[32,16384]{1,0:T(8,128)S(1)} %get-tuple-element.70), channel_id=1, source_target_pairs={{0,12},{1,13},{2,14},{3,15},{4,0},{5,1},{6,2},{7,3},{8,4},{9,5},{1... | collective-permute-start | bytes 6291464 | tf_op jit(solution)/shard_map/ppermute | solution.py:380
  107.6 40.9 %collective-permute-start.15 = (s32[1,16,8192]{2,1,0:T(8,128)S(1)}, s32[1,16,8192]{2,1,0:T(8,128)S(1)}, u32[]{:S(2)}, u32[]{:S(2)}) collective-permute-start(s32[1,16,8192]{2,1,0:T(8,128)S(1)} %pad_add_fusion), channel_id=1, source_target_pairs={{0,64},{16,80},{32,96},{48,112},{64,0},{80,16},{96,32},{112,48},{1... | collective-permute-start | bytes 1572872 | tf_op jit(solution)/shard_map/ppermute | solution.py:384
  145.3 15.9 %collective-permute-start.10 = (f32[32,4096]{1,0:T(8,128)S(1)}, f32[32,4096]{1,0:T(8,128)S(1)}, u32[]{:S(2)}, u32[]{:S(2)}) collective-permute-start(f32[32,4096]{1,0:T(8,128)S(1)} %get-tuple-element.67), channel_id=1, source_target_pairs={{0,4},{1,5},{2,6},{3,7},{4,8},{5,9},{6,10},{7,11},{8,12},{9,13},{1... | collective-permute-start | bytes 1572872 | tf_op jit(solution)/shard_map/ppermute | solution.py:380
  147.0 14.2 %collective-permute-start.11 = (f32[32,4096]{1,0:T(8,128)S(1)}, f32[32,4096]{1,0:T(8,128)S(1)}, u32[]{:S(2)}, u32[]{:S(2)}) collective-permute-start(f32[32,4096]{1,0:T(8,128)S(1)} %get-tuple-element.68), channel_id=1, source_target_pairs={{0,12},{1,13},{2,14},{3,15},{4,0},{5,1},{6,2},{7,3},{8,4},{9,5},{1... | collective-permute-start | bytes 1572872 | tf_op jit(solution)/shard_map/ppermute | solution.py:380
  150.0 21.1 %copy-start = (f32[32,16384]{1,0:T(8,128)}, f32[32,16384]{1,0:T(8,128)S(1)}, u32[]{:S(2)}) copy-start(f32[32,16384]{1,0:T(8,128)S(1)} %collective-permute-done.13.refs_16_.refs_17_.refs_18_.refs_19_.refs_26_.refs_8_.refs_9_.refs_11_) | copy-start | bytes 6291460
  152.3 13.9 %collective-permute-start.16 = (f32[32,4096]{1,0:T(8,128)S(1)}, f32[32,4096]{1,0:T(8,128)S(1)}, u32[]{:S(2)}, u32[]{:S(2)}) collective-permute-start(f32[32,4096]{1,0:T(8,128)S(1)} %get-tuple-element.72), channel_id=1, source_target_pairs={{0,1},{1,2},{2,3},{3,0},{4,5},{5,6},{6,7},{7,4},{8,9},{9,10},{10,1... | collective-permute-start | bytes 1572872 | tf_op jit(solution)/shard_map/ppermute | solution.py:380
  152.4 13.8 %collective-permute-start.17 = (f32[32,4096]{1,0:T(8,128)S(1)}, f32[32,4096]{1,0:T(8,128)S(1)}, u32[]{:S(2)}, u32[]{:S(2)}) collective-permute-start(f32[32,4096]{1,0:T(8,128)S(1)} %get-tuple-element.73), channel_id=1, source_target_pairs={{0,3},{1,0},{2,1},{3,2},{4,7},{5,4},{6,5},{7,6},{8,11},{9,8},{10,9... | collective-permute-start | bytes 1572872 | tf_op jit(solution)/shard_map/ppermute | solution.py:380
  163.4 12.2 %collective-permute-start.22 = (f32[64,2048]{1,0:T(8,128)S(1)}, f32[64,2048]{1,0:T(8,128)S(1)}, u32[]{:S(2)}, u32[]{:S(2)}) collective-permute-start(f32[64,2048]{1,0:T(8,128)S(1)} %get-tuple-element.82), channel_id=1, source_target_pairs={{0,4},{1,5},{2,6},{3,7},{4,8},{5,9},{6,10},{7,11},{8,12},{9,13},{1... | collective-permute-start | bytes 1572872 | tf_op jit(solution)/shard_map/ppermute | solution.py:380
  164.2 14.1 %collective-permute-start.23 = (f32[64,2048]{1,0:T(8,128)S(1)}, f32[64,2048]{1,0:T(8,128)S(1)}, u32[]{:S(2)}, u32[]{:S(2)}) collective-permute-start(f32[64,2048]{1,0:T(8,128)S(1)} %get-tuple-element.83), channel_id=1, source_target_pairs={{0,12},{1,13},{2,14},{3,15},{4,0},{5,1},{6,2},{7,3},{8,4},{9,5},{1... | collective-permute-start | bytes 1572872 | tf_op jit(solution)/shard_map/ppermute | solution.py:380
  168.4 10.8 %collective-permute-start.24 = (f32[64,2048]{1,0:T(8,128)S(1)}, f32[64,2048]{1,0:T(8,128)S(1)}, u32[]{:S(2)}, u32[]{:S(2)}) collective-permute-start(f32[64,2048]{1,0:T(8,128)S(1)} %get-tuple-element.84), channel_id=1, source_target_pairs={{0,1},{1,2},{2,3},{3,0},{4,5},{5,6},{6,7},{7,4},{8,9},{9,10},{10,1... | collective-permute-start | bytes 1572872 | tf_op jit(solution)/shard_map/ppermute | solution.py:380
  168.5 12.5 %collective-permute-start.25 = (f32[64,2048]{1,0:T(8,128)S(1)}, f32[64,2048]{1,0:T(8,128)S(1)}, u32[]{:S(2)}, u32[]{:S(2)}) collective-permute-start(f32[64,2048]{1,0:T(8,128)S(1)} %get-tuple-element.85), channel_id=1, source_target_pairs={{0,3},{1,0},{2,1},{3,2},{4,7},{5,4},{6,5},{7,6},{8,11},{9,8},{10,9... | collective-permute-start | bytes 1572872 | tf_op jit(solution)/shard_map/ppermute | solution.py:380
  173.3 7.7 %copy-start.1 = (bf16[64,256]{1,0:T(8,128)(2,1)S(1)}, bf16[64,256]{1,0:T(8,128)(2,1)}, u32[]{:S(2)}) copy-start(bf16[64,256]{1,0:T(8,128)(2,1)} %constant.25.clone.refs_17_.refs_8_) | copy-start | bytes 98308
  173.3 7.7 %copy-start.2 = (bf16[64,256]{1,0:T(8,128)(2,1)S(1)}, bf16[64,256]{1,0:T(8,128)(2,1)}, u32[]{:S(2)}) copy-start(bf16[64,256]{1,0:T(8,128)(2,1)} %constant.24.clone.refs_16_) | copy-start | bytes 98308
  175.5 15.7 %collective-permute-start.18 = (f32[64,2048]{1,0:T(8,128)S(1)}, f32[64,2048]{1,0:T(8,128)S(1)}, u32[]{:S(2)}, u32[]{:S(2)}) collective-permute-start(f32[64,2048]{1,0:T(8,128)S(1)} %get-tuple-element.78), channel_id=1, source_target_pairs={{0,4},{1,5},{2,6},{3,7},{4,8},{5,9},{6,10},{7,11},{8,12},{9,13},{1... | collective-permute-start | bytes 1572872 | tf_op jit(solution)/shard_map/ppermute | solution.py:380
  175.6 16.0 %collective-permute-start.19 = (f32[64,2048]{1,0:T(8,128)S(1)}, f32[64,2048]{1,0:T(8,128)S(1)}, u32[]{:S(2)}, u32[]{:S(2)}) collective-permute-start(f32[64,2048]{1,0:T(8,128)S(1)} %get-tuple-element.79), channel_id=1, source_target_pairs={{0,12},{1,13},{2,14},{3,15},{4,0},{5,1},{6,2},{7,3},{8,4},{9,5},{1... | collective-permute-start | bytes 1572872 | tf_op jit(solution)/shard_map/ppermute | solution.py:380
  178.3 14.4 %collective-permute-start.20 = (f32[64,2048]{1,0:T(8,128)S(1)}, f32[64,2048]{1,0:T(8,128)S(1)}, u32[]{:S(2)}, u32[]{:S(2)}) collective-permute-start(f32[64,2048]{1,0:T(8,128)S(1)} %get-tuple-element.80), channel_id=1, source_target_pairs={{0,1},{1,2},{2,3},{3,0},{4,5},{5,6},{6,7},{7,4},{8,9},{9,10},{10,1... | collective-permute-start | bytes 1572872 | tf_op jit(solution)/shard_map/ppermute | solution.py:380
  179.2 13.5 %collective-permute-start.21 = (f32[64,2048]{1,0:T(8,128)S(1)}, f32[64,2048]{1,0:T(8,128)S(1)}, u32[]{:S(2)}, u32[]{:S(2)}) collective-permute-start(f32[64,2048]{1,0:T(8,128)S(1)} %get-tuple-element.81), channel_id=1, source_target_pairs={{0,3},{1,0},{2,1},{3,2},{4,7},{5,4},{6,5},{7,6},{8,11},{9,8},{10,9... | collective-permute-start | bytes 1572872 | tf_op jit(solution)/shard_map/ppermute | solution.py:380
  187.6 14.9 %collective-permute-start.31 = (f32[8,4096]{1,0:T(8,128)S(1)}, f32[8,4096]{1,0:T(8,128)S(1)}, u32[]{:S(2)}, u32[]{:S(2)}) collective-permute-start(f32[8,4096]{1,0:T(8,128)S(1)} %get-tuple-element.90.refs_0_), channel_id=1, source_target_pairs={{0,64},{16,80},{32,96},{48,112},{64,0},{80,16},{96,32},{112,48},{1... | collective-permute-start | bytes 393224 | tf_op jit(solution)/shard_map/ppermute | solution.py:384
  191.2 11.3 %collective-permute-start.30 = (f32[8,4096]{1,0:T(8,128)S(1)}, f32[8,4096]{1,0:T(8,128)S(1)}, u32[]{:S(2)}, u32[]{:S(2)}) collective-permute-start(f32[8,4096]{1,0:T(8,128)S(1)} %get-tuple-element.90.refs_0_), channel_id=1, source_target_pairs={{0,96},{16,112},{32,0},{48,16},{64,32},{80,48},{96,64},{112,80},{1... | collective-permute-start | bytes 393224 | tf_op jit(solution)/shard_map/ppermute | solution.py:384
  191.7 10.8 %collective-permute-start.29 = (f32[8,4096]{1,0:T(8,128)S(1)}, f32[8,4096]{1,0:T(8,128)S(1)}, u32[]{:S(2)}, u32[]{:S(2)}) collective-permute-start(f32[8,4096]{1,0:T(8,128)S(1)} %get-tuple-element.90.refs_0_), channel_id=1, source_target_pairs={{0,32},{16,48},{32,64},{48,80},{64,96},{80,112},{96,0},{112,16},{1... | collective-permute-start | bytes 393224 | tf_op jit(solution)/shard_map/ppermute | solution.py:384
  199.3 16.4 %collective-permute-start.28 = (f32[8,4096]{1,0:T(8,128)S(1)}, f32[8,4096]{1,0:T(8,128)S(1)}, u32[]{:S(2)}, u32[]{:S(2)}) collective-permute-start(f32[8,4096]{1,0:T(8,128)S(1)} %get-tuple-element.89.refs_0_), channel_id=1, source_target_pairs={{0,64},{16,80},{32,96},{48,112},{64,0},{80,16},{96,32},{112,48},{1... | collective-permute-start | bytes 393224 | tf_op jit(solution)/shard_map/ppermute | solution.py:384
  201.0 14.7 %collective-permute-start.27 = (f32[8,4096]{1,0:T(8,128)S(1)}, f32[8,4096]{1,0:T(8,128)S(1)}, u32[]{:S(2)}, u32[]{:S(2)}) collective-permute-start(f32[8,4096]{1,0:T(8,128)S(1)} %get-tuple-element.89.refs_0_), channel_id=1, source_target_pairs={{0,96},{16,112},{32,0},{48,16},{64,32},{80,48},{96,64},{112,80},{1... | collective-permute-start | bytes 393224 | tf_op jit(solution)/shard_map/ppermute | solution.py:384
  202.5 13.2 %collective-permute-start.26 = (f32[8,4096]{1,0:T(8,128)S(1)}, f32[8,4096]{1,0:T(8,128)S(1)}, u32[]{:S(2)}, u32[]{:S(2)}) collective-permute-start(f32[8,4096]{1,0:T(8,128)S(1)} %get-tuple-element.89.refs_0_), channel_id=1, source_target_pairs={{0,32},{16,48},{32,64},{48,80},{64,96},{80,112},{96,0},{112,16},{1... | collective-permute-start | bytes 393224 | tf_op jit(solution)/shard_map/ppermute | solution.py:384
  207.4 14.5 %collective-permute-start.33 = (f32[64,4096]{1,0:T(8,128)S(1)}, f32[64,4096]{1,0:T(8,128)S(1)}, u32[]{:S(2)}, u32[]{:S(2)}) collective-permute-start(f32[64,4096]{1,0:T(8,128)S(1)} %get-tuple-element.94.refs_0_), channel_id=1, source_target_pairs={{0,16},{16,0},{32,48},{48,32},{64,80},{80,64},{96,112},{112,96},{1... | collective-permute-start | bytes 3145736 | tf_op jit(solution)/shard_map/ppermute | solution.py:390
  220.6 3.6 %collective-permute-start.32 = (f32[64,4096]{1,0:T(8,128)S(1)}, f32[64,4096]{1,0:T(8,128)S(1)}, u32[]{:S(2)}, u32[]{:S(2)}) collective-permute-start(f32[64,4096]{1,0:T(8,128)S(1)} %get-tuple-element.93.refs_0_), channel_id=1, source_target_pairs={{0,16},{16,0},{32,48},{48,32},{64,80},{80,64},{96,112},{112,96},{1... | collective-permute-start | bytes 3145736 | tf_op jit(solution)/shard_map/ppermute | solution.py:390
